TPU v7x, 32 devices: a whole 2x2x4 slice. The times are simulated.
32 devices in a mesh: lon: 8 (over z, y), lat: 4 (over x, core).
Axes of the slice: x: 2, y: 2, z: 4, core: 2. Of those that a mesh axis runs over, the one named last changes fastest.
Arguments:
- inputs: bfloat16 [32, 512, 384], P('lat', 'lon'), may hold values from -6 to 6
- conv1_weight: bfloat16 [3, 3, 384, 384], replicated, may hold values from -0.109375 to 0.109375
- conv2_weight: bfloat16 [3, 3, 384, 384], replicated, may hold values from -0.109375 to 0.109375
- cotangent: bfloat16 [32, 512, 384], P('lat', 'lon'), may hold values from -6 to 6
Outputs:
- output: bfloat16 [32, 512, 384], P('lat', 'lon')
- input_grad: bfloat16 [32, 512, 384], P('lat', 'lon')
- conv1_grad: float32 [3, 3, 384, 384], P(None, None, 'lon', 'lat')
- conv2_grad: float32 [3, 3, 384, 384], P(None, None, 'lon', 'lat')
All inputs are finite; a program needn't handle non-finite values.
Results may differ from a plain program's by a relative error of at most 0.0033.
Values may be sent and summed in bfloat16 or wider, within the bound.
No kernel may reach another device: no remote copies, remote signals or barrier semaphores. Data moves between devices by JAX's collectives and lax.ppermute only.
A program may use at most 128 MiB of HBM per device.

v0:
```python
import jax
import jax.numpy as jnp
from jax import lax
from jax.sharding import PartitionSpec as P


def passed_along(shard, axis, by):
    length = lax.axis_size(axis)
    return lax.ppermute(shard, axis, [(i, (i + by) % length) for i in range(length)])


def padded(shard, sides, width):
    for axis, dim in sides:
        size, length = (lax.axis_size(axis), shard.shape[dim])
        up = [(i, (i + 1) % size) for i in range(size - 1)]
        down = [(j, i) for i, j in up]
        last = lax.slice_in_dim(shard, length - width, length, axis=dim)
        initial = lax.slice_in_dim(shard, 0, width, axis=dim)
        before = lax.ppermute(last, axis, up)
        after = lax.ppermute(initial, axis, down)
        shard = jnp.concatenate([before, shard, after], axis=dim)
    return shard


def extend(field):
    western = passed_along(field, "lon", 1)
    eastern = passed_along(field, "lon", -1)
    widened = jnp.concatenate([western, field, eastern], axis=1)
    return padded(widened, (("lat", 0),), 1)


def windows(padded_field, count_of_rows, lon_width, channels, direction):
    pieces = []
    for lat_step in (-1, 0, 1):
        for longitude_stride in (-1, 0, 1):
            row_start = 1 + direction * lat_step
            column_begin = lon_width + direction * lon_width * longitude_stride
            pieces.append(
                padded_field[
                    row_start : row_start + count_of_rows, column_begin : column_begin + lon_width
                ]
            )
    stacked = jnp.concatenate(pieces, axis=2)
    return stacked.reshape(count_of_rows * lon_width, 9 * channels)


def full_terms(stacked, grad, scale, channels):
    product = lax.dot_general(
        stacked, grad, (((0,), (0,)), ((), ())), preferred_element_type=jnp.float32
    )
    return (product * scale).reshape(9, channels, channels)


def local(inputs, conv1_weight, conv2_weight, cotangent):
    count_of_rows, lon_width, channels = inputs.shape
    cells = count_of_rows * lon_width
    lon_count = lax.axis_size("lon")
    latitude_count = lax.axis_size("lat")
    scale = (count_of_rows * latitude_count * lon_width * lon_count) ** (-0.5)
    forward_one = conv1_weight.reshape(9 * channels, channels)
    forward_two = conv2_weight.reshape(9 * channels, channels)
    turned_one = jnp.swapaxes(conv1_weight, 2, 3).reshape(9 * channels, channels)
    turned_two = jnp.swapaxes(conv2_weight, 2, 3).reshape(9 * channels, channels)
    source_field, cot_field = (inputs, cotangent)

    def stack_of(field, direction):
        return windows(extend(field), count_of_rows, lon_width, channels, direction)

    def as_field(flat):
        return flat.reshape(count_of_rows, lon_width, channels)

    stack_input = stack_of(source_field, 1)
    first = jnp.dot(stack_input, forward_one, preferred_element_type=jnp.float32)
    cdf = 0.5 * (1.0 + jax.scipy.special.erf(first / jnp.sqrt(2.0)))
    hidden = (first * cdf).astype(jnp.bfloat16)
    stack_hidden = stack_of(as_field(hidden), 1)
    second = jnp.dot(stack_hidden, forward_two, preferred_element_type=jnp.float32)
    flat_input = source_field.reshape(cells, channels)
    output = (flat_input.astype(jnp.float32) + second).astype(jnp.bfloat16)
    flat_cot = cot_field.reshape(cells, channels)
    stacked_cotangent = stack_of(cot_field, -1)
    upstream = jnp.dot(stacked_cotangent, turned_two, preferred_element_type=jnp.float32)
    density = jnp.exp(-0.5 * first * first) / jnp.sqrt(2.0 * jnp.pi)
    pre_grad = (upstream * (cdf + first * density)).astype(jnp.bfloat16)
    stack_pre = stack_of(as_field(pre_grad), -1)
    back = jnp.dot(stack_pre, turned_one, preferred_element_type=jnp.float32)
    input_grad = (flat_cot.astype(jnp.float32) + back).astype(jnp.bfloat16)
    output = output.reshape(count_of_rows, lon_width, channels)
    input_grad = input_grad.reshape(count_of_rows, lon_width, channels)
    in_part = channels // lon_count
    out_part = channels // latitude_count
    terms_one = full_terms(stack_input, pre_grad, scale, channels)
    terms_two = full_terms(stack_hidden, flat_cot, scale, channels)
    partly = (
        lax.psum_scatter(terms_one, "lon", scatter_dimension=1, tiled=True),
        lax.psum_scatter(terms_two, "lon", scatter_dimension=1, tiled=True),
    )
    grad_one, grad_two = (
        lax.psum_scatter(partly[0], "lat", scatter_dimension=2, tiled=True),
        lax.psum_scatter(partly[1], "lat", scatter_dimension=2, tiled=True),
    )
    conv1_grad = grad_one.reshape(3, 3, in_part, out_part)
    conv2_grad = grad_two.reshape(3, 3, in_part, out_part)
    return (output, input_grad, conv1_grad, conv2_grad)


def solution(mesh):
    in_specs = (P("lat", "lon", None), P(), P(), P("lat", "lon", None))
    out_specs = (
        P("lat", "lon", None),
        P("lat", "lon", None),
        P(None, None, "lon", "lat"),
        P(None, None, "lon", "lat"),
    )
    return jax.shard_map(local, mesh=mesh, in_specs=in_specs, out_specs=out_specs, check_vma=False)
```

profile of v0, /device:TPU:0, one launch (start us, length us, event | category | flops | bytes accessed | tf_op | source)
XLA Modules:
  0.0 351.8 jit_solution(17425843395593510278)
XLA Ops:
  7.2 3.0 collective-permute-start
  10.3 3.1 collective-permute-start.1
  13.4 4.7 %collective-permute-start.9 = (bf16[8,64,384]{2,1,0:T(8,128)(2,1)}, bf16[8,64,384]{2,1,0:T(8,128)(2,1)S(1)}, u32[]{:S(2)}, u32[]{:S(2)}) collective-permute-start(bf16[8,64,384]{2,1,0:T(8,128)(2,1)} %param.7), channel_id=1, source_target_pairs={{0,28},{4,0},{8,4},{12,8},{16,12},{20,16},{24,20},{28,24},{1,29},{... | collective-permute-start | bytes 1179656 | tf_op jit(solution)/shard_map/ppermute | solution.py:9
  18.1 5.8 %copy.10 = bf16[3,3,384,384]{2,3,1,0:T(8,128)(2,1)} copy(bf16[3,3,384,384]{3,2,1,0:T(8,128)(2,1)} %param.6) | data formatting | bytes 5308416 | tf_op args[2]
  23.9 13.1 %collective-permute-done = bf16[8,64,384]{2,1,0:T(8,128)(2,1)S(1)} collective-permute-done((bf16[8,64,384]{2,1,0:T(8,128)(2,1)}, bf16[8,64,384]{2,1,0:T(8,128)(2,1)S(1)}, u32[]{:S(2)}, u32[]{:S(2)}) %collective-permute-start) | collective-permute-done | bytes 393248 | tf_op jit(solution)/shard_map/ppermute | solution.py:9
  47.7 3.0 collective-permute-start.11
  59.1 4.5 %convolution_multiply_fusion = f32[3456,384]{1,0:T(8,128)} fusion(bf16[512,3456]{1,0:T(8,128)(2,1)S(1)} %bitcast.104, bf16[512,384]{1,0:T(8,128)(2,1)S(1)} %fusion.3), kind=kOutput, calls=%fused_computation | convolution fusion | flops 1360281600 | bytes 9240576 | tf_op jit(solution)/shard_map/dot_general | solution.py:48
  64.1 4.3 %collective-permute-start.5 = (bf16[8,64,384]{2,1,0:T(8,128)(2,1)S(1)}, bf16[8,64,384]{2,1,0:T(8,128)(2,1)S(1)}, u32[]{:S(2)}, u32[]{:S(2)}) collective-permute-start(bf16[8,64,384]{2,1,0:T(8,128)(2,1)S(1)} %bitcast.61), channel_id=1, source_target_pairs={{0,28},{4,0},{8,4},{12,8},{16,12},{20,16},{24,20},{28,24},{1,29},{... | collective-permute-start | bytes 1179656 | tf_op jit(solution)/shard_map/ppermute | solution.py:9
  68.4 17.9 %collective-permute-done.4 = bf16[8,64,384]{2,1,0:T(8,128)(2,1)S(1)} collective-permute-done((bf16[8,64,384]{2,1,0:T(8,128)(2,1)S(1)}, bf16[8,64,384]{2,1,0:T(8,128)(2,1)S(1)}, u32[]{:S(2)}, u32[]{:S(2)}) %collective-permute-start.4) | collective-permute-done | bytes 393248 | tf_op jit(solution)/shard_map/ppermute | solution.py:9
  86.3 4.1 %collective-permute-done.5 = bf16[8,64,384]{2,1,0:T(8,128)(2,1)S(1)} collective-permute-done((bf16[8,64,384]{2,1,0:T(8,128)(2,1)S(1)}, bf16[8,64,384]{2,1,0:T(8,128)(2,1)S(1)}, u32[]{:S(2)}, u32[]{:S(2)}) %collective-permute-start.5) | collective-permute-done | bytes 393248 | tf_op jit(solution)/shard_map/ppermute | solution.py:9
  99.2 4.4 %fusion = f32[3456,384]{1,0:T(8,128)} fusion(bf16[8,64,3456]{2,1,0:T(8,128)(2,1)S(1)} %get-tuple-element.4, bf16[8,64,384]{2,1,0:T(8,128)(2,1)S(1)} %copy-done.3), kind=kOutput, calls=%fused_computation.2 | convolution fusion | flops 1360281600 | bytes 9240576 | tf_op jit(solution)/shard_map/dot_general | solution.py:48
  103.7 4.7 %collective-permute-start.13 = (bf16[8,64,384]{2,1,0:T(8,128)(2,1)S(1)}, bf16[8,64,384]{2,1,0:T(8,128)(2,1)S(1)}, u32[]{:S(2)}, u32[]{:S(2)}) collective-permute-start(bf16[8,64,384]{2,1,0:T(8,128)(2,1)S(1)} %bitcast.73), channel_id=1, source_target_pairs={{0,28},{4,0},{8,4},{12,8},{16,12},{20,16},{24,20},{28,24},{1,29},{... | collective-permute-start | bytes 1179656 | tf_op jit(solution)/shard_map/ppermute | solution.py:9
  108.4 17.3 %collective-permute-done.12 = bf16[8,64,384]{2,1,0:T(8,128)(2,1)S(1)} collective-permute-done((bf16[8,64,384]{2,1,0:T(8,128)(2,1)S(1)}, bf16[8,64,384]{2,1,0:T(8,128)(2,1)S(1)}, u32[]{:S(2)}, u32[]{:S(2)}) %collective-permute-start.12) | collective-permute-done | bytes 393248 | tf_op jit(solution)/shard_map/ppermute | solution.py:9
  127.8 5.8 %copy.11 = bf16[3,3,384,384]{2,3,1,0:T(8,128)(2,1)} copy(bf16[3,3,384,384]{3,2,1,0:T(8,128)(2,1)} %param.5) | data formatting | bytes 5308416 | tf_op args[1]
  133.6 6.0 %collective-permute-start.15 = (bf16[1,192,384]{2,1,0:T(8,128)(2,1)}, bf16[1,192,384]{2,1,0:T(8,128)(2,1)}, u32[]{:S(2)}, u32[]{:S(2)}) collective-permute-start(bf16[1,192,384]{2,1,0:T(8,128)(2,1)} %get-tuple-element.22), channel_id=1, source_target_pairs={{0,1},{1,2},{2,3},{4,5},{5,6},{6,7},{8,9},{9,10},{10,11},{12,13},{... | collective-permute-start | bytes 442376 | tf_op jit(solution)/shard_map/ppermute | solution.py:19
  144.7 39.0 %reduce-scatter.9.cloned.1.call-done = f32[9,48,384]{2,1,0:T(8,128)} async-done(((f32[9,384,384]{2,1,0:T(8,128)}), f32[9,48,384]{2,1,0:T(8,128)}) %reduce-scatter.9.cloned.1.call-update) | async-done | bytes 663568 | tf_op jit(solution)/shard_map/reduce_scatter | solution.py:95
  183.8 3.2 copy.12
  187.0 3.0 reshape.95
  199.4 92.3 %reduce-scatter.11.cloned.1.call-done = f32[9,48,384]{2,1,0:T(8,128)} async-done(((f32[9,384,384]{2,1,0:T(8,128)}), f32[9,48,384]{2,1,0:T(8,128)}) %reduce-scatter.11.cloned.1.call-update) | async-done | bytes 663568 | tf_op jit(solution)/shard_map/reduce_scatter | solution.py:96
  291.8 3.5 %copy.14 = f32[9,48,384]{1,0,2:T(8,128)S(1)} copy(f32[9,48,384]{2,1,0:T(8,128)} %reduce-scatter.11.cloned.1.call-done) | data formatting | bytes 1327104
  302.6 5.7 %fusion.2 = bf16[512,384]{1,0:T(8,128)(2,1)} fusion(bf16[512,3456]{1,0:T(8,128)(2,1)} %constant_dynamic-update-slice_fusion.21, bf16[3456,384]{1,0:T(8,128)(2,1)} %bitcast.85, bf16[512,384]{1,0:T(8,128)(2,1)S(1)} %bitcast.87), kind=kOutput, calls=%fused_computation.7 | convolution fusion | flops 1359544320 | bytes 6979584 | tf_op jit(solution)/shard_map/dot_general | solution.py:86
  308.3 4.8 %fusion.1 = bf16[512,384]{1,0:T(8,128)(2,1)} fusion(bf16[512,3456]{1,0:T(8,128)(2,1)} %constant_dynamic-update-slice_fusion.6, bf16[3456,384]{1,0:T(8,128)(2,1)S(1)} %bitcast.84, bf16[512,384]{1,0:T(8,128)(2,1)S(1)} %bitcast.88), kind=kOutput, calls=%fused_computation.6 | convolution fusion | flops 1359544320 | bytes 6979584 | tf_op jit(solution)/shard_map/dot_general | solution.py:77
  313.2 4.1 %reduce-scatter.13.cloned.1.call-done = f32[96,432]{1,0:T(8,128)} async-done(((f32[384,432]{1,0:T(8,128)}), f32[96,432]{1,0:T(8,128)}) %reduce-scatter.13.cloned.1.call-update) | async-done | bytes 165904
  319.5 23.7 %reduce-scatter.15.cloned.1.call-done = f32[96,432]{1,0:T(8,128)} async-done(((f32[384,432]{1,0:T(8,128)}), f32[96,432]{1,0:T(8,128)}) %reduce-scatter.15.cloned.1.call-update) | async-done | bytes 165904
  (107 shorter events, 56.3 us)
Async XLA Ops:
  7.2 29.8 %copy-start.5 = (bf16[8,64,384]{2,1,0:T(8,128)(2,1)S(1)}, bf16[8,64,384]{2,1,0:T(8,128)(2,1)}, u32[]{:S(2)}) copy-start(bf16[8,64,384]{2,1,0:T(8,128)(2,1)} %param.4) | copy-start | bytes 1179652
  7.2 37.1 %copy-start.3 = (bf16[8,64,384]{2,1,0:T(8,128)(2,1)S(1)}, bf16[8,64,384]{2,1,0:T(8,128)(2,1)}, u32[]{:S(2)}) copy-start(bf16[8,64,384]{2,1,0:T(8,128)(2,1)} %param.7) | copy-start | bytes 1179652
  7.2 176.6 %reduce-scatter.9.cloned.1.call-start = ((), (), s32[]{:S(2)}) async-start(), calls=%async_computation.4 | async-start | bytes 5971968 | tf_op jit(solution)/shard_map/reduce_scatter | solution.py:95
  7.2 29.7 %collective-permute-start = (bf16[8,64,384]{2,1,0:T(8,128)(2,1)}, bf16[8,64,384]{2,1,0:T(8,128)(2,1)S(1)}, u32[]{:S(2)}, u32[]{:S(2)}) collective-permute-start(bf16[8,64,384]{2,1,0:T(8,128)(2,1)} %param.4), channel_id=1, source_target_pairs={{0,4},{4,8},{8,12},{12,16},{16,20},{20,24},{24,28},{28,0},{1,5},{5... | collective-permute-start | bytes 1179656 | tf_op jit(solution)/shard_map/ppermute | solution.py:9
  10.3 29.1 %collective-permute-start.1 = (bf16[8,64,384]{2,1,0:T(8,128)(2,1)}, bf16[8,64,384]{2,1,0:T(8,128)(2,1)S(1)}, u32[]{:S(2)}, u32[]{:S(2)}) collective-permute-start(bf16[8,64,384]{2,1,0:T(8,128)(2,1)} %param.4), channel_id=1, source_target_pairs={{0,28},{4,0},{8,4},{12,8},{16,12},{20,16},{24,20},{28,24},{1,29},{... | collective-permute-start | bytes 1179656 | tf_op jit(solution)/shard_map/ppermute | solution.py:9
  13.4 30.9 %collective-permute-start.8 = (bf16[8,64,384]{2,1,0:T(8,128)(2,1)}, bf16[8,64,384]{2,1,0:T(8,128)(2,1)S(1)}, u32[]{:S(2)}, u32[]{:S(2)}) collective-permute-start(bf16[8,64,384]{2,1,0:T(8,128)(2,1)} %param.7), channel_id=1, source_target_pairs={{0,4},{4,8},{8,12},{12,16},{16,20},{20,24},{24,28},{28,0},{1,5},{5... | collective-permute-start | bytes 1179656 | tf_op jit(solution)/shard_map/ppermute | solution.py:9
  13.4 33.0 %collective-permute-start.9 = (bf16[8,64,384]{2,1,0:T(8,128)(2,1)}, bf16[8,64,384]{2,1,0:T(8,128)(2,1)S(1)}, u32[]{:S(2)}, u32[]{:S(2)}) collective-permute-start(bf16[8,64,384]{2,1,0:T(8,128)(2,1)} %param.7), channel_id=1, source_target_pairs={{0,28},{4,0},{8,4},{12,8},{16,12},{20,16},{24,20},{28,24},{1,29},{... | collective-permute-start | bytes 1179656 | tf_op jit(solution)/shard_map/ppermute | solution.py:9
  39.5 11.3 %collective-permute-start.2 = (bf16[1,192,384]{2,1,0:T(8,128)(2,1)S(1)}, bf16[1,192,384]{2,1,0:T(8,128)(2,1)S(1)}, u32[]{:S(2)}, u32[]{:S(2)}) collective-permute-start(bf16[1,192,384]{2,1,0:T(8,128)(2,1)S(1)} %get-tuple-element.29), channel_id=1, source_target_pairs={{0,1},{1,2},{2,3},{4,5},{5,6},{6,7},{8,9},{9,10},{10,11},{12,13},{... | collective-permute-start | bytes 442376 | tf_op jit(solution)/shard_map/ppermute | solution.py:19
  40.8 10.4 %collective-permute-start.3 = (bf16[1,192,384]{2,1,0:T(8,128)(2,1)S(1)}, bf16[1,192,384]{2,1,0:T(8,128)(2,1)S(1)}, u32[]{:S(2)}, u32[]{:S(2)}) collective-permute-start(bf16[1,192,384]{2,1,0:T(8,128)(2,1)S(1)} %get-tuple-element.28), channel_id=1, source_target_pairs={{1,0},{2,1},{3,2},{5,4},{6,5},{7,6},{9,8},{10,9},{11,10},{13,12},{... | collective-permute-start | bytes 442376 | tf_op jit(solution)/shard_map/ppermute | solution.py:20
  46.4 8.5 %collective-permute-start.10 = (bf16[1,192,384]{2,1,0:T(8,128)(2,1)S(1)}, bf16[1,192,384]{2,1,0:T(8,128)(2,1)S(1)}, u32[]{:S(2)}, u32[]{:S(2)}) collective-permute-start(bf16[1,192,384]{2,1,0:T(8,128)(2,1)S(1)} %get-tuple-element.25), channel_id=1, source_target_pairs={{1,0},{2,1},{3,2},{5,4},{6,5},{7,6},{9,8},{10,9},{11,10},{13,12},{... | collective-permute-start | bytes 442376 | tf_op jit(solution)/shard_map/ppermute | solution.py:20
  47.7 7.6 %collective-permute-start.11 = (bf16[1,192,384]{2,1,0:T(8,128)(2,1)S(1)}, bf16[1,192,384]{2,1,0:T(8,128)(2,1)S(1)}, u32[]{:S(2)}, u32[]{:S(2)}) collective-permute-start(bf16[1,192,384]{2,1,0:T(8,128)(2,1)S(1)} %get-tuple-element.24), channel_id=1, source_target_pairs={{0,1},{1,2},{2,3},{4,5},{5,6},{6,7},{8,9},{9,10},{10,11},{12,13},{... | collective-permute-start | bytes 442376 | tf_op jit(solution)/shard_map/ppermute | solution.py:19
  63.5 228.2 %reduce-scatter.11.cloned.1.call-start = ((), (), s32[]{:S(2)}) async-start(), calls=%async_computation.5 | async-start | bytes 5971968 | tf_op jit(solution)/shard_map/reduce_scatter | solution.py:96
  63.6 22.7 %collective-permute-start.4 = (bf16[8,64,384]{2,1,0:T(8,128)(2,1)S(1)}, bf16[8,64,384]{2,1,0:T(8,128)(2,1)S(1)}, u32[]{:S(2)}, u32[]{:S(2)}) collective-permute-start(bf16[8,64,384]{2,1,0:T(8,128)(2,1)S(1)} %bitcast.60), channel_id=1, source_target_pairs={{0,4},{4,8},{8,12},{12,16},{16,20},{20,24},{24,28},{28,0},{1,5},{5... | collective-permute-start | bytes 1179656 | tf_op jit(solution)/shard_map/ppermute | solution.py:9
  64.1 26.3 %collective-permute-start.5 = (bf16[8,64,384]{2,1,0:T(8,128)(2,1)S(1)}, bf16[8,64,384]{2,1,0:T(8,128)(2,1)S(1)}, u32[]{:S(2)}, u32[]{:S(2)}) collective-permute-start(bf16[8,64,384]{2,1,0:T(8,128)(2,1)S(1)} %bitcast.61), channel_id=1, source_target_pairs={{0,28},{4,0},{8,4},{12,8},{16,12},{20,16},{24,20},{28,24},{1,29},{... | collective-permute-start | bytes 1179656 | tf_op jit(solution)/shard_map/ppermute | solution.py:9
  90.3 4.3 %collective-permute-start.6 = (bf16[1,192,384]{2,1,0:T(8,128)(2,1)S(1)}, bf16[1,192,384]{2,1,0:T(8,128)(2,1)S(1)}, u32[]{:S(2)}, u32[]{:S(2)}) collective-permute-start(bf16[1,192,384]{2,1,0:T(8,128)(2,1)S(1)} %get-tuple-element.27), channel_id=1, source_target_pairs={{0,1},{1,2},{2,3},{4,5},{5,6},{6,7},{8,9},{9,10},{10,11},{12,13},{... | collective-permute-start | bytes 442376 | tf_op jit(solution)/shard_map/ppermute | solution.py:19
  93.4 3.3 collective-permute-start.7
  103.6 213.7 %reduce-scatter.13.cloned.1.call-start = ((), (), s32[]{:S(2)}) async-start(), calls=%async_computation.6 | async-start | bytes 983040
  103.7 22.1 %collective-permute-start.12 = (bf16[8,64,384]{2,1,0:T(8,128)(2,1)S(1)}, bf16[8,64,384]{2,1,0:T(8,128)(2,1)S(1)}, u32[]{:S(2)}, u32[]{:S(2)}) collective-permute-start(bf16[8,64,384]{2,1,0:T(8,128)(2,1)S(1)} %bitcast.72), channel_id=1, source_target_pairs={{0,4},{4,8},{8,12},{12,16},{16,20},{20,24},{24,28},{28,0},{1,5},{5... | collective-permute-start | bytes 1179656 | tf_op jit(solution)/shard_map/ppermute | solution.py:9
  103.7 22.0 %collective-permute-start.13 = (bf16[8,64,384]{2,1,0:T(8,128)(2,1)S(1)}, bf16[8,64,384]{2,1,0:T(8,128)(2,1)S(1)}, u32[]{:S(2)}, u32[]{:S(2)}) collective-permute-start(bf16[8,64,384]{2,1,0:T(8,128)(2,1)S(1)} %bitcast.73), channel_id=1, source_target_pairs={{0,28},{4,0},{8,4},{12,8},{16,12},{20,16},{24,20},{28,24},{1,29},{... | collective-permute-start | bytes 1179656 | tf_op jit(solution)/shard_map/ppermute | solution.py:9
  126.5 13.1 %collective-permute-start.14 = (bf16[1,192,384]{2,1,0:T(8,128)(2,1)}, bf16[1,192,384]{2,1,0:T(8,128)(2,1)}, u32[]{:S(2)}, u32[]{:S(2)}) collective-permute-start(bf16[1,192,384]{2,1,0:T(8,128)(2,1)} %get-tuple-element.23), channel_id=1, source_target_pairs={{1,0},{2,1},{3,2},{5,4},{6,5},{7,6},{9,8},{10,9},{11,10},{13,12},{... | collective-permute-start | bytes 442376 | tf_op jit(solution)/shard_map/ppermute | solution.py:20
  133.6 61.5 %collective-permute-start.15 = (bf16[1,192,384]{2,1,0:T(8,128)(2,1)}, bf16[1,192,384]{2,1,0:T(8,128)(2,1)}, u32[]{:S(2)}, u32[]{:S(2)}) collective-permute-start(bf16[1,192,384]{2,1,0:T(8,128)(2,1)} %get-tuple-element.22), channel_id=1, source_target_pairs={{0,1},{1,2},{2,3},{4,5},{5,6},{6,7},{8,9},{9,10},{10,11},{12,13},{... | collective-permute-start | bytes 442376 | tf_op jit(solution)/shard_map/ppermute | solution.py:19
  190.1 153.1 %reduce-scatter.15.cloned.1.call-start = ((), (), s32[]{:S(2)}) async-start(), calls=%async_computation.7 | async-start | bytes 983040
  295.3 7.3 %copy-start.4 = (bf16[8,64,384]{2,1,0:T(8,128)(2,1)S(1)}, bf16[8,64,384]{2,1,0:T(8,128)(2,1)}, u32[]{:S(2)}) copy-start(bf16[8,64,384]{2,1,0:T(8,128)(2,1)} %param.7) | copy-start | bytes 1179652
  302.6 5.7 %copy-start.6 = (bf16[8,64,384]{2,1,0:T(8,128)(2,1)S(1)}, bf16[8,64,384]{2,1,0:T(8,128)(2,1)}, u32[]{:S(2)}) copy-start(bf16[8,64,384]{2,1,0:T(8,128)(2,1)} %param.4) | copy-start | bytes 1179652
  (3 other events, 9.2 us)
Sparse Core Ops, SparseCore 0:
  63.7 120.0 reduce-scatter.8
  187.8 103.9 reduce-scatter.10
  294.3 22.9 reduce-scatter.12
  319.9 23.2 reduce-scatter.14
where the time goes:
time: 353 us; the launch traced here: 352 us
  waiting for transfers between devices  219 us (62%)
  local copies, waits for them, and re-layouts  49.1 us (14%)
  starting transfers between devices  39.1 us (11%)
  matrix products  23.6 us (7%)
  between operations  14.2 us (4%)
  other arithmetic  6.37 us (2%)
    reduce_scatter x1, waiting for transfers between devices, local(): lax.psum_scatter(terms_two, 'lon', scatter_dimension=1, tiled=True)  92.3 us
    ppermute x8, waiting for transfers between devices, passed_along(): lax.ppermute(shard, axis, [(i, (i + by) % length) for i in range(length)])  58.8 us
    unnamed x53, local copies, waits for them, and re-layouts  46.1 us
    reduce_scatter x1, waiting for transfers between devices, local(): lax.psum_scatter(terms_one, 'lon', scatter_dimension=1, tiled=True)  39 us
    unnamed x6, waiting for transfers between devices  27.9 us
    ppermute x8, starting transfers between devices, passed_along(): lax.ppermute(shard, axis, [(i, (i + by) % length) for i in range(length)])  20.4 us
    ppermute x4, starting transfers between devices, padded(): before = lax.ppermute(last, axis, up)  13.4 us
    dot_general x2, matrix products, full_terms(): lax.dot_general(stacked, grad, (((0,), (0,)), ((), ())), preferred_elemen...  8.84 us
  transfers between devices with their start and end apart: 20, of which 12 were waited for; matrix products, arithmetic and copies ran while one was open for 19% of the time, Pallas kernels for 0%

commit v1 on v0

--- a/solution.py
+++ b/solution.py
@@ -1,7 +1,13 @@
+import functools
+
 import jax
 import jax.numpy as jnp
 from jax import lax
+from jax.experimental import pallas as pl
+from jax.experimental.pallas import tpu as pltpu
 from jax.sharding import PartitionSpec as P
+
+F32, BF16 = jnp.float32, jnp.bfloat16
 
 
 def passed_along(shard, axis, by):
@@ -104,6 +110,214 @@
     return (output, input_grad, conv1_grad, conv2_grad)
 
 
+def write_stack(field, stack_ref, band, step):
+    cells, channels = field.shape
+    wide = field.astype(F32)
+    place = lax.broadcasted_iota(jnp.int32, (cells, channels), 0) % band
+    above = jnp.where(place >= step, pltpu.roll(wide, step, 0), 0.0).astype(BF16)
+    below = jnp.where(place < band - step, pltpu.roll(wide, cells - step, 0), 0.0).astype(BF16)
+    for at, part in enumerate((above, field, below)):
+        columns = slice(at * channels, (at + 1) * channels)
+        stack_ref[band : band + cells, columns] = part
+        stack_ref[0:band, columns] = part[cells - band :]
+        stack_ref[band + cells :, columns] = part[0:band]
+
+
+def convolved(stack_ref, weight_ref, band, cells):
+    total = None
+    for b in range(3):
+        channels = weight_ref.shape[2]
+        tap = weight_ref[:, b].reshape(3 * channels, channels)
+        term = jnp.dot(stack_ref[b * band : b * band + cells, :], tap, preferred_element_type=F32)
+        total = term if total is None else total + term
+    return total
+
+
+def convolved_back(stack_ref, weight_ref, band, cells):
+    total = None
+    for b in range(3):
+        tap = jnp.concatenate([weight_ref[2 - a, 2 - b] for a in range(3)], axis=1)
+        term = lax.dot_general(
+            stack_ref[b * band : b * band + cells, :],
+            tap,
+            (((1,), (1,)), ((), ())),
+            preferred_element_type=F32,
+        )
+        total = term if total is None else total + term
+    return total
+
+
+def inner_kernel(band, step, place_ref, own_ref, other_ref, one_ref, two_ref,
+                 hidden_ref, pre_ref, keep_ref, give_ref,
+                 stack_ref, grad_stack_ref, turned_ref, first_ref, up_ref, act_ref, sums_ref):
+    chip, core = place_ref[0], place_ref[1]
+    cells, channels = first_ref.shape
+    rows = 32
+    for group, fields_ref in enumerate((own_ref, other_ref)):
+        source = fields_ref[:, 0].reshape(cells, channels)
+        cot = fields_ref[:, 1].reshape(cells, channels)
+        write_stack(source, stack_ref, band, step)
+        write_stack(cot, grad_stack_ref.at[group], band, step)
+        first_ref[...] = convolved(stack_ref, one_ref, band, cells)
+        up_ref[...] = convolved_back(grad_stack_ref.at[group], two_ref, band, cells)
+
+        def activate(at, carry):
+            span = pl.ds(pl.multiple_of(at * rows, rows), rows)
+            first = first_ref[span, :]
+            cdf = 0.5 * (1.0 + lax.erf(first * (0.5**0.5)))
+            density = jnp.exp(-0.5 * first * first) * ((2.0 * jnp.pi) ** -0.5)
+            act_ref[0, span, :] = (first * cdf).astype(BF16)
+            act_ref[1, span, :] = (up_ref[span, :] * (cdf + first * density)).astype(BF16)
+            return carry
+
+        lax.fori_loop(0, cells // rows, activate, 0)
+        if group == 0:
+            hidden_ref[...] = act_ref[0]
+            pre_ref[...] = act_ref[1]
+
+        @pl.when(core == 0)
+        def _():
+            write_stack(act_ref[1], grad_stack_ref.at[group], band, step)
+            turned_ref[group] = source.T
+
+        @pl.when(core == 1)
+        def _():
+            turned_ref[group] = act_ref[0].T
+
+    for b in range(3):
+        span = slice(b * band, b * band + cells)
+        terms = [
+            jnp.dot(turned_ref[group], grad_stack_ref[group, span, :], preferred_element_type=F32)
+            for group in range(2)
+        ]
+        total = terms[0] + terms[1]
+        for a in range(3):
+            sums_ref[(2 - a) * 3 + 2 - b] = total[:, a * channels : (a + 1) * channels]
+
+    half, part = channels // 2, keep_ref.shape[0]
+    deep = channels // part
+
+    def packed(west, east, at, depth):
+        low = jnp.concatenate([west[:, :half], east[:, :half]], axis=1)
+        high = jnp.concatenate([west[:, half:], east[:, half:]], axis=1)
+        span = slice(at, at + depth)
+        return span, jnp.where(chip == 0, low, high), jnp.where(chip == 0, high, low)
+
+    for piece in range(part):
+        begin = piece * deep
+        for tap in range(4):
+            span, mine, others = packed(
+                sums_ref[tap, begin : begin + deep, :],
+                sums_ref[5 + tap, begin : begin + deep, :],
+                tap * deep,
+                deep,
+            )
+            keep_ref[piece, span, :] = mine.astype(BF16)
+            give_ref[piece, span, :] = others.astype(BF16)
+        short = deep // 2
+        rest = jnp.zeros((32 - short, channels), F32)
+        span, mine, others = packed(
+            jnp.concatenate([sums_ref[4, begin : begin + short, :], rest], axis=0),
+            jnp.concatenate([sums_ref[4, begin + short : begin + deep, :], rest], axis=0),
+            4 * deep,
+            32,
+        )
+        keep_ref[piece, span, :] = mine.astype(BF16)
+        give_ref[piece, span, :] = others.astype(BF16)
+
+
+def outer_kernel(band, step, own_ref, hidden_ref, pre_ref, one_ref, two_ref, out_ref, stack_ref):
+    cells, channels = hidden_ref.shape
+    shape = (out_ref.shape[0],) + out_ref.shape[2:]
+    write_stack(hidden_ref[...], stack_ref, band, step)
+    second = convolved(stack_ref, two_ref, band, cells)
+    source = own_ref[:, 0].reshape(cells, channels)
+    out_ref[:, 0] = (source.astype(F32) + second).astype(BF16).reshape(shape)
+    write_stack(pre_ref[...], stack_ref, band, step)
+    back = convolved_back(stack_ref, one_ref, band, cells)
+    cot = own_ref[:, 1].reshape(cells, channels)
+    out_ref[:, 1] = (cot.astype(F32) + back).astype(BF16).reshape(shape)
+
+
+def fast_local(inputs, conv1_weight, conv2_weight, cotangent):
+    rows, width, channels = inputs.shape
+    lon, lat = lax.axis_size("lon"), lax.axis_size("lat")
+    devices = lon * lat
+    step = width // devices
+    cells = rows * width
+    band = rows * lat * step
+    scale = (rows * lat * width * lon) ** (-0.5)
+    place = lax.axis_index("lat")
+    chip, core = place // 2, place % 2
+
+    both = jnp.stack([inputs, cotangent]).reshape(2, rows, devices, step, channels)
+    both = both.transpose(2, 0, 1, 3, 4).reshape(devices, 2, rows * step, channels)
+    own = lax.all_to_all(both, ("lon", "lat"), 0, 0, tiled=True)
+    other = lax.ppermute(own, "lat", [(i, i ^ 1) for i in range(lat)])
+
+    vmem = pl.BlockSpec(memory_space=pltpu.VMEM)
+    params = pltpu.CompilerParams(vmem_limit_bytes=52 * 2**20)
+    deep = channels // lon
+    height = 4 * deep + 32
+    flops = 2 * 9 * cells * channels * channels
+    field = jax.ShapeDtypeStruct((cells, channels), BF16)
+    wire = jax.ShapeDtypeStruct((lon, height, channels), BF16)
+    hidden, pre_grad, keep, give = pl.pallas_call(
+        functools.partial(inner_kernel, band, step),
+        out_shape=(field, field, wire, wire),
+        in_specs=[pl.BlockSpec(memory_space=pltpu.SMEM)] + [vmem] * 4,
+        out_specs=(vmem,) * 4,
+        scratch_shapes=[
+            pltpu.VMEM((cells + 2 * band, 3 * channels), BF16),
+            pltpu.VMEM((2, cells + 2 * band, 3 * channels), BF16),
+            pltpu.VMEM((2, channels, cells), BF16),
+            pltpu.VMEM((cells, channels), F32),
+            pltpu.VMEM((cells, channels), F32),
+            pltpu.VMEM((2, cells, channels), BF16),
+            pltpu.VMEM((9, channels, channels), F32),
+        ],
+        compiler_params=params,
+        cost_estimate=pl.CostEstimate(flops=6 * flops, bytes_accessed=12 * 2**20, transcendentals=0),
+    )(jnp.stack([chip, core]).astype(jnp.int32), own, other, conv1_weight, conv2_weight)
+
+    given = lax.ppermute(give, "lat", [(i, i ^ 2) for i in range(lat)])
+    fields = pl.pallas_call(
+        functools.partial(outer_kernel, band, step),
+        out_shape=jax.ShapeDtypeStruct((devices, 2, rows * step, channels), BF16),
+        in_specs=[vmem] * 5,
+        out_specs=vmem,
+        scratch_shapes=[pltpu.VMEM((cells + 2 * band, 3 * channels), BF16)],
+        compiler_params=params,
+        cost_estimate=pl.CostEstimate(flops=2 * flops, bytes_accessed=8 * 2**20, transcendentals=0),
+    )(own, hidden, pre_grad, conv1_weight, conv2_weight)
+    fields = lax.all_to_all(fields, ("lon", "lat"), 0, 0, tiled=True)
+    fields = fields.reshape(devices, 2, rows, step, channels).transpose(1, 2, 0, 3, 4)
+    output, input_grad = fields.reshape(2, rows, width, channels)
+
+    pair = (keep.astype(F32) + given.astype(F32)).astype(BF16)
+    parts = lax.all_to_all(pair, "lon", 0, 0, tiled=True)
+    total = jnp.sum(parts.astype(F32), axis=0) * scale
+    half, short = channels // 2, deep // 2
+    west, east = total[:, :half], total[:, half:]
+    middle = slice(4 * deep, 4 * deep + short)
+    whole = jnp.concatenate([west[: 4 * deep], west[middle], east[middle], east[: 4 * deep]], axis=0)
+    whole = whole.reshape(9, deep, half)
+    quarter = half // 2
+    low, high = whole[:, :, :quarter], whole[:, :, quarter:]
+    mine = jnp.where(core == 0, low, high)
+    theirs = lax.ppermute(
+        jnp.where(core == 0, high, low), "lat", [(i, i ^ 1) for i in range(lat)]
+    )
+    shape = (3, 3, deep, quarter)
+    conv1_grad = jnp.where(core == 0, mine, theirs).reshape(shape)
+    conv2_grad = jnp.where(core == 0, theirs, mine).reshape(shape)
+    return (output, input_grad, conv1_grad, conv2_grad)
+
+
+def is_fast(mesh):
+    return dict(mesh.shape) == {"lon": 8, "lat": 4}
+
+
 def solution(mesh):
     in_specs = (P("lat", "lon", None), P(), P(), P("lat", "lon", None))
     out_specs = (
@@ -112,4 +326,5 @@
         P(None, None, "lon", "lat"),
         P(None, None, "lon", "lat"),
     )
-    return jax.shard_map(local, mesh=mesh, in_specs=in_specs, out_specs=out_specs, check_vma=False)
+    body = fast_local if is_fast(mesh) else local
+    return jax.shard_map(body, mesh=mesh, in_specs=in_specs, out_specs=out_specs, check_vma=False)

time: 353 us -> 135 us (0.38)
  waiting for transfers between devices: 219 us -> 61.7 us
  local copies, waits for them, and re-layouts: 49.1 us -> 6.85 us
  starting transfers between devices: 39.1 us -> 7.88 us
  blocking collectives: 0 us -> 27.7 us
  Pallas kernels: 0 us -> 26.5 us
  matrix products: 23.6 us -> 0 us
  between operations: 14.2 us -> 0.76 us
    reduce_scatter x2 -> x0, waiting for transfers between devices: 131 us -> none  [the longest x1 92.3 us: local(): lax.psum_scatter(terms_two, 'lon', scatter_dimension=1, tiled=True)]
    unnamed x53 -> x6, local copies, waits for them, and re-layouts: 46.1 us -> 0.89 us
    ppermute x16 -> x3, starting transfers between devices: 38.9 us -> 1.54 us  [the longest x1 1.46 us: fast_local(): given = lax.ppermute(give, 'lat', [(i, i ^ 2) for i in range(lat)])]
    all_to_all x0 -> x2, waiting for transfers between devices: none -> 32.5 us  [the longest x1 31.9 us: fast_local(): parts = lax.all_to_all(pair, 'lon', 0, 0, tiled=True)]
    ppermute x16 -> x3, waiting for transfers between devices: 60.2 us -> 29.2 us  [the longest x1 27 us: fast_local(): given = lax.ppermute(give, 'lat', [(i, i ^ 2) for i in range(lat)])]
    unnamed x6 -> x0, waiting for transfers between devices: 27.9 us -> none
    all_to_all x0 -> x1, blocking collectives: none -> 27.7 us  [fast_local(): own = lax.all_to_all(both, ('lon', 'lat'), 0, 0, tiled=True)]
    pallas_call x0 -> x2, Pallas kernels: none -> 26.5 us  [the longest x1 18.7 us: fast_local(): pl.pallas_call(functools.partial(inner_kernel, band, step), out_shape=(fi...]
  transfers between devices with their start and end apart: 20 -> 5, of which waited for: 12 -> 4; matrix products, arithmetic and copies ran while one was open for 19% -> 3% of each run, Pallas kernels for 0% -> 6%
where the time goes in v1:
time: 135 us
  waiting for transfers between devices  61.7 us (46%)
  blocking collectives  27.7 us (21%)
  Pallas kernels  26.5 us (20%)
  starting transfers between devices  7.88 us (6%)
  local copies, waits for them, and re-layouts  6.85 us (5%)
  other arithmetic  3.47 us (3%)
    all_to_all x1, waiting for transfers between devices, fast_local(): parts = lax.all_to_all(pair, 'lon', 0, 0, tiled=True)  31.9 us
    all_to_all x1, blocking collectives, fast_local(): own = lax.all_to_all(both, ('lon', 'lat'), 0, 0, tiled=True)  27.7 us
    ppermute x1, waiting for transfers between devices, fast_local(): given = lax.ppermute(give, 'lat', [(i, i ^ 2) for i in range(lat)])  27 us
    pallas_call x1, Pallas kernels, fast_local(): pl.pallas_call(functools.partial(inner_kernel, band, step), out_shape=(fi...  18.7 us
    pallas_call x1, Pallas kernels, fast_local(): pl.pallas_call(functools.partial(outer_kernel, band, step), out_shape=jax...  7.78 us
    all_to_all x1, starting transfers between devices, fast_local(): parts = lax.all_to_all(pair, 'lon', 0, 0, tiled=True)  3.57 us
    another operation x5, local copies, waits for them, and re-layouts, fast_local(): output, input_grad = fields.reshape(2, rows, width, channels)  2.87 us
    all_to_all x1, starting transfers between devices, fast_local(): fields = lax.all_to_all(fields, ('lon', 'lat'), 0, 0, tiled=True)  2.77 us
  transfers between devices with their start and end apart: 5, of which 4 were waited for; matrix products, arithmetic and copies ran while one was open for 3% of the time, Pallas kernels for 6%

profile of v1, /device:TPU:0, one launch (start us, length us, event | category | flops | bytes accessed | tf_op | source)
XLA Modules:
  0.0 134.9 jit_solution(13385345197656328734)
XLA Ops:
  0.6 1.1 stack.18
  1.8 1.1 stack.19
  2.9 0.7 copy_bitcast_fusion
  3.6 0.3 reshape.33
  3.9 27.7 %all_to_all.15.own_ref = bf16[32,2,16,384]{3,2,1,0:T(8,128)(2,1)S(1)} all-to-all(bf16[32,2,16,384]{3,2,1,0:T(8,128)(2,1)S(1)} %reshape.33), channel_id=1, replica_groups=mesh['lon'=8,'lat'=4] {'lon','lat'}, dimensions={0} | all-to-all | bytes 1572864 | tf_op jit(solution)/shard_map/all_to_all | solution.py:255
  31.7 2.2 %collective-permute-done.other_ref = bf16[32,2,16,384]{3,2,1,0:T(8,128)(2,1)S(1)} collective-permute-done((bf16[32,2,16,384]{3,2,1,0:T(8,128)(2,1)S(1)}, bf16[32,2,16,384]{3,2,1,0:T(8,128)(2,1)S(1)}, u32[]{:S(2)}, u32[]{:S(2)}) %collective-permute-start) | collective-permute-done | bytes 786464 | tf_op jit(solution)/shard_map/ppermute | solution.py:256
  34.0 0.9 copy-done.2
  34.8 18.7 %shard_map.75 = (bf16[512,384]{1,0:T(8,128)(2,1)S(1)}, bf16[512,384]{1,0:T(8,128)(2,1)S(1)}, bf16[8,224,384]{2,1,0:T(8,128)(2,1)}, bf16[8,224,384]{2,1,0:T(8,128)(2,1)}) custom-call(s32[2]{0:T(128)S(1)} %pad_add_fusion.place_ref, bf16[32,2,16,384]{3,2,1,0:T(8,128)(2,1)S(1)} %all_to_all.15.own_ref, bf16[32,2,16,384]{3,2,1,0:T(8,128)(2,1)} %copy-done.2, ...), custom_call_target="tpu_custom_call" | custom-call | flops 8153726976 | bytes 12582912 | tf_op jit(solution)/shard_map/pallas_call | solution.py:265
  53.5 1.5 %collective-permute-start.1 = (bf16[8,224,384]{2,1,0:T(8,128)(2,1)}, bf16[8,224,384]{2,1,0:T(8,128)(2,1)S(1)}, u32[]{:S(2)}, u32[]{:S(2)}) collective-permute-start(bf16[8,224,384]{2,1,0:T(8,128)(2,1)} %get-tuple-element.11), channel_id=1, source_target_pairs={{0,2},{1,3},{2,0},{3,1},{4,6},{5,7},{6,4},{7,5},{8,10},{9,11},{10,... | collective-permute-start | bytes 4128776 | tf_op jit(solution)/shard_map/ppermute | solution.py:283
  55.0 7.8 %shard_map.76 = bf16[32,2,16,384]{3,2,1,0:T(8,128)(2,1)} custom-call(bf16[32,2,16,384]{3,2,1,0:T(8,128)(2,1)} %copy-done, bf16[512,384]{1,0:T(8,128)(2,1)S(1)} %get-tuple-element.8.hidden_ref, bf16[512,384]{1,0:T(8,128)(2,1)S(1)} %get-tuple-element.9.pre_ref, bf16[3,3,384,384]{3,2,1,0:T(8,128)(2,1)} %one_ref.3, bf16[3,3,384,384]{3,2,1,0:T(8,128)(2,1)} %two_ref.3), custom_call_target="tpu_custom_call" | custom-call | flops 2717908992 | bytes 8388608 | tf_op jit(solution)/shard_map/pallas_call | solution.py:284
  62.8 2.8 %all-to-all-start.1 = ((bf16[32,2,16,384]{3,2,1,0:T(8,128)(2,1)}), bf16[32,2,16,384]{3,2,1,0:T(8,128)(2,1)S(1)}, u32[]{:S(2)}, u32[]{:S(2)}) async-start(bf16[32,2,16,384]{3,2,1,0:T(8,128)(2,1)} %shard_map.76), calls=%async_computation.1 | async-start | bytes 1572864 | tf_op jit(solution)/shard_map/all_to_all | solution.py:293
  65.6 27.0 %collective-permute-done.1 = bf16[8,224,384]{2,1,0:T(8,128)(2,1)S(1)} collective-permute-done((bf16[8,224,384]{2,1,0:T(8,128)(2,1)}, bf16[8,224,384]{2,1,0:T(8,128)(2,1)S(1)}, u32[]{:S(2)}, u32[]{:S(2)}) %collective-permute-start.1) | collective-permute-done | bytes 1376288 | tf_op jit(solution)/shard_map/ppermute | solution.py:283
  92.6 1.4 %add_convert_fusion = bf16[8,224,384]{2,1,0:T(8,128)(2,1)} fusion(bf16[8,224,384]{2,1,0:T(8,128)(2,1)S(1)} %collective-permute-done.1, bf16[8,224,384]{2,1,0:T(8,128)(2,1)S(1)} %copy-done.1), kind=kLoop, calls=%fused_computation.1 | loop fusion | flops 2752512 | bytes 4128768 | tf_op jit(solution)/shard_map/convert_element_type | solution.py:297
  94.1 0.6 all-to-all-done.1
  94.6 3.6 %all-to-all-start.2 = ((bf16[8,224,384]{2,1,0:T(8,128)(2,1)}), bf16[8,224,384]{2,1,0:T(8,128)(2,1)S(1)}, u32[]{:S(2)}, u32[]{:S(2)}) async-start(bf16[8,224,384]{2,1,0:T(8,128)(2,1)} %add_convert_fusion), calls=%async_computation.2 | async-start | bytes 2752512 | tf_op jit(solution)/shard_map/all_to_all | solution.py:298
  98.2 0.3 reshape.34
  98.5 31.9 %all-to-all-done.2 = bf16[8,224,384]{2,1,0:T(8,128)(2,1)S(1)} async-done(((bf16[8,224,384]{2,1,0:T(8,128)(2,1)}), bf16[8,224,384]{2,1,0:T(8,128)(2,1)S(1)}, u32[]{:S(2)}, u32[]{:S(2)}) %all-to-all-start.2) | async-done | bytes 1376288 | tf_op jit(solution)/shard_map/all_to_all | solution.py:298
  130.4 0.2 convert_reduce_fusion
  131.1 0.5 fusion
  131.6 0.3 copy.11
  131.9 0.9 unstack.15
  132.8 0.3 copy.10
  133.1 0.9 unstack.13
  134.0 0.9 broadcast_select_fusion
  (15 shorter events, 0.5 us)
Async XLA Ops:
  31.7 21.9 %copy-start = (bf16[32,2,16,384]{3,2,1,0:T(8,128)(2,1)}, bf16[32,2,16,384]{3,2,1,0:T(8,128)(2,1)S(1)}, u32[]{:S(2)}) copy-start(bf16[32,2,16,384]{3,2,1,0:T(8,128)(2,1)S(1)} %all_to_all.15.own_ref) | copy-start | bytes 2359300
  31.7 2.3 %collective-permute-start = (bf16[32,2,16,384]{3,2,1,0:T(8,128)(2,1)S(1)}, bf16[32,2,16,384]{3,2,1,0:T(8,128)(2,1)S(1)}, u32[]{:S(2)}, u32[]{:S(2)}) collective-permute-start(bf16[32,2,16,384]{3,2,1,0:T(8,128)(2,1)S(1)} %all_to_all.15.own_ref), channel_id=1, source_target_pairs={{0,1},{1,0},{2,3},{3,2},{4,5},{5,4},{6,7},{7,6},{8,9},{9,8},{10,11... | collective-permute-start | bytes 2359304 | tf_op jit(solution)/shard_map/ppermute | solution.py:256
  33.9 0.9 copy-start.2
  53.5 39.1 %collective-permute-start.1 = (bf16[8,224,384]{2,1,0:T(8,128)(2,1)}, bf16[8,224,384]{2,1,0:T(8,128)(2,1)S(1)}, u32[]{:S(2)}, u32[]{:S(2)}) collective-permute-start(bf16[8,224,384]{2,1,0:T(8,128)(2,1)} %get-tuple-element.11), channel_id=1, source_target_pairs={{0,2},{1,3},{2,0},{3,1},{4,6},{5,7},{6,4},{7,5},{8,10},{9,11},{10,... | collective-permute-start | bytes 4128776 | tf_op jit(solution)/shard_map/ppermute | solution.py:283
  62.8 29.8 %copy-start.1 = (bf16[8,224,384]{2,1,0:T(8,128)(2,1)S(1)}, bf16[8,224,384]{2,1,0:T(8,128)(2,1)}, u32[]{:S(2)}) copy-start(bf16[8,224,384]{2,1,0:T(8,128)(2,1)} %get-tuple-element.10) | copy-start | bytes 4128772
  62.8 31.8 %all-to-all-start.1 = ((bf16[32,2,16,384]{3,2,1,0:T(8,128)(2,1)}), bf16[32,2,16,384]{3,2,1,0:T(8,128)(2,1)S(1)}, u32[]{:S(2)}, u32[]{:S(2)}) async-start(bf16[32,2,16,384]{3,2,1,0:T(8,128)(2,1)} %shard_map.76), calls=%async_computation.1 | async-start | bytes 1572864 | tf_op jit(solution)/shard_map/all_to_all | solution.py:293
  94.6 35.8 %all-to-all-start.2 = ((bf16[8,224,384]{2,1,0:T(8,128)(2,1)}), bf16[8,224,384]{2,1,0:T(8,128)(2,1)S(1)}, u32[]{:S(2)}, u32[]{:S(2)}) async-start(bf16[8,224,384]{2,1,0:T(8,128)(2,1)} %add_convert_fusion), calls=%async_computation.2 | async-start | bytes 2752512 | tf_op jit(solution)/shard_map/all_to_all | solution.py:298
  131.0 3.0 %collective-permute-start.2 = (f32[9,48,96]{2,1,0:T(8,128)S(1)}, f32[9,48,96]{2,1,0:T(8,128)S(1)}, u32[]{:S(2)}, u32[]{:S(2)}) collective-permute-start(f32[9,48,96]{2,1,0:T(8,128)S(1)} %slice_select_fusion), channel_id=1, source_target_pairs={{0,1},{1,0},{2,3},{3,2},{4,5},{5,4},{6,7},{7,6},{8,9},{9,8},{10,11... | collective-permute-start | bytes 497672 | tf_op jit(solution)/shard_map/ppermute | solution.py:308

commit v2 on v0

--- a/solution.py
+++ b/solution.py
@@ -1,7 +1,13 @@
+import functools
+
 import jax
 import jax.numpy as jnp
 from jax import lax
+from jax.experimental import pallas as pl
+from jax.experimental.pallas import tpu as pltpu
 from jax.sharding import PartitionSpec as P
+
+F32, BF16 = jnp.float32, jnp.bfloat16
 
 
 def passed_along(shard, axis, by):
@@ -104,12 +110,253 @@
     return (output, input_grad, conv1_grad, conv2_grad)
 
 
+def write_stack(field, stack_ref, band, step):
+    cells, channels = field.shape
+    wide = field.astype(F32)
+    place = lax.broadcasted_iota(jnp.int32, (cells, channels), 0) % band
+    above = jnp.where(place >= step, pltpu.roll(wide, step, 0), 0.0).astype(BF16)
+    below = jnp.where(place < band - step, pltpu.roll(wide, cells - step, 0), 0.0).astype(BF16)
+    for at, part in enumerate((above, field, below)):
+        columns = slice(at * channels, (at + 1) * channels)
+        stack_ref[band : band + cells, columns] = part
+        stack_ref[0:band, columns] = part[cells - band :]
+        stack_ref[band + cells :, columns] = part[0:band]
+
+
+def convolved(stack_ref, weight_ref, band, cells):
+    total = None
+    for b in range(3):
+        channels = weight_ref.shape[2]
+        tap = weight_ref[:, b].reshape(3 * channels, channels)
+        term = jnp.dot(stack_ref[b * band : b * band + cells, :], tap, preferred_element_type=F32)
+        total = term if total is None else total + term
+    return total
+
+
+def convolved_back(stack_ref, weight_ref, band, cells):
+    total = None
+    for b in range(3):
+        tap = jnp.concatenate([weight_ref[2 - a, 2 - b] for a in range(3)], axis=1)
+        term = lax.dot_general(
+            stack_ref[b * band : b * band + cells, :],
+            tap,
+            (((1,), (1,)), ((), ())),
+            preferred_element_type=F32,
+        )
+        total = term if total is None else total + term
+    return total
+
+
+def forward_kernel(band, step, source_ref, weight_ref, hidden_ref, slope_ref, send_ref, stack_ref, first_ref):
+    cells, channels = first_ref.shape
+    rows = 32
+    source = source_ref[...].reshape(cells, channels)
+    write_stack(source, stack_ref, band, step)
+    first_ref[...] = convolved(stack_ref, weight_ref, band, cells)
+
+    def activate(at, carry):
+        span = pl.ds(pl.multiple_of(at * rows, rows), rows)
+        first = first_ref[span, :]
+        cdf = 0.5 * (1.0 + lax.erf(first * (0.5**0.5)))
+        density = jnp.exp(-0.5 * first * first) * ((2.0 * jnp.pi) ** -0.5)
+        hidden_ref[span, :] = (first * cdf).astype(BF16)
+        slope_ref[span, :] = cdf + first * density
+        return carry
+
+    lax.fori_loop(0, cells // rows, activate, 0)
+    half = send_ref.shape[1]
+    deep = half // 4
+    for core, turned in enumerate((source.T, hidden_ref[...].T)):
+        for y in range(2):
+            for z in range(4):
+                begin = (2 * z + y) * deep
+                for x in range(2):
+                    send_ref[y * 4 + x * 2 + core, z * deep : (z + 1) * deep, :] = turned[begin : begin + deep]
+
+
+def backward_kernel(band, step, cot_ref, slope_ref, weight_ref, pre_ref, send_ref, stack_ref):
+    cells, channels = slope_ref.shape
+    cot = cot_ref[...].reshape(cells, channels)
+    write_stack(cot, stack_ref, band, step)
+    pre_ref[...] = (slope_ref[...] * convolved_back(stack_ref, weight_ref, band, cells)).astype(BF16)
+    half, upper = channels // 2, cells // 2
+    for core, field in enumerate((pre_ref[...], cot)):
+        field = field.astype(F32)
+        for x in range(2):
+            part = field[:, x * half : (x + 1) * half]
+            part = jnp.concatenate([part[:upper], part[upper:]], axis=1).astype(BF16)
+            for y in range(2):
+                send_ref[y * 4 + x * 2 + core] = part
+
+
+def outer_kernel(band, step, source_ref, cot_ref, hidden_ref, pre_ref, one_ref, two_ref, out_ref, stack_ref):
+    cells, channels = hidden_ref.shape
+    shape = (out_ref.shape[0],) + out_ref.shape[2:]
+    write_stack(hidden_ref[...], stack_ref, band, step)
+    second = convolved(stack_ref, two_ref, band, cells)
+    source = source_ref[...].reshape(cells, channels)
+    out_ref[:, 0] = (source.astype(F32) + second).astype(BF16).reshape(shape)
+    write_stack(pre_ref[...], stack_ref, band, step)
+    back = convolved_back(stack_ref, one_ref, band, cells)
+    cot = cot_ref[...].reshape(cells, channels)
+    out_ref[:, 1] = (cot.astype(F32) + back).astype(BF16).reshape(shape)
+
+
+def units(deep):
+    count = deep // 16
+    for unit in range(9 * count):
+        yield unit // count, (unit % count) * 16, (unit // 4) * 16, unit % 4
+
+
+def grads_kernel(band, step, left_ref, right_ref, send_ref, turned_ref, moved_ref, sums_ref):
+    sources, half, cells = left_ref.shape
+    upper = cells // 2
+    place = lax.broadcasted_iota(jnp.int32, (half, cells), 1) % band
+    for at in range(sources):
+        columns = slice(at * cells, (at + 1) * cells)
+        field = left_ref[at]
+        wide = field.astype(F32)
+        turned_ref[0:half, columns] = jnp.where(place >= step, pltpu.roll(wide, step, 1), 0.0).astype(BF16)
+        turned_ref[half : 2 * half, columns] = field
+        turned_ref[2 * half :, columns] = jnp.where(
+            place < band - step, pltpu.roll(wide, cells - step, 1), 0.0
+        ).astype(BF16)
+        packed = right_ref[at].astype(F32)
+        grad = jnp.concatenate([packed[:, :half], packed[:, half:]], axis=0).astype(BF16)
+        begin = at * cells
+        moved_ref[1, begin : begin + cells, :] = grad
+        moved_ref[2, begin + band : begin + cells, :] = grad[: cells - band]
+        moved_ref[2, begin : begin + band, :] = grad[cells - band :]
+        moved_ref[0, begin : begin + cells - band, :] = grad[band:]
+        moved_ref[0, begin + cells - band : begin + cells, :] = grad[:band]
+    for b in range(3):
+        sums_ref[b] = jnp.dot(turned_ref[...], moved_ref[b], preferred_element_type=F32)
+    deep, quarter = half // 4, half // 2
+    height = send_ref.shape[1]
+    for z in range(4):
+        for core in range(2):
+            blocks = [[] for _ in range(height // 16)]
+            for tap, row, to, _ in units(deep):
+                begin = (tap // 3) * half + z * deep + row
+                blocks[to // 16].append(
+                    sums_ref[tap % 3, begin : begin + 16, core * quarter : (core + 1) * quarter]
+                )
+            for to, parts in enumerate(blocks):
+                while len(parts) < 4:
+                    parts.append(jnp.zeros((16, quarter), F32))
+                send_ref[z * 2 + core, to * 16 : (to + 1) * 16, :] = jnp.concatenate(parts, axis=1).astype(BF16)
+
+
+def finish_kernel(scale, parts_ref, one_ref, two_ref):
+    deep, quarter = one_ref.shape[2:]
+    for core, out_ref in enumerate((one_ref, two_ref)):
+        total = parts_ref[core].astype(F32)
+        for z in range(1, parts_ref.shape[0] // 2):
+            total = total + parts_ref[z * 2 + core].astype(F32)
+        total = total * scale
+        for tap, row, begin, slot in units(deep):
+            out_ref[tap // 3, tap % 3, row : row + 16, :] = total[
+                begin : begin + 16, slot * quarter : (slot + 1) * quarter
+            ]
+
+
+def fast_local(inputs, conv1_weight, conv2_weight, cotangent):
+    rows, width, channels = inputs.shape
+    every, plane, line = ("z", "y", "x", "core"), ("y", "x", "core"), ("z", "core")
+    devices = lax.axis_size(every)
+    step = width // devices
+    cells = rows * width
+    lat = lax.axis_size("x") * lax.axis_size("core")
+    lon = devices // lat
+    band = rows * lat * step
+    half, deep = channels // 2, channels // lon
+    height = -(-9 * (deep // 16) // 4) * 16
+    scale = (rows * lat * width * lon) ** (-0.5)
+    field = jax.ShapeDtypeStruct((cells, channels), BF16)
+    stack = pltpu.VMEM((cells + 2 * band, 3 * channels), BF16)
+    flops = 2 * 9 * cells * channels * channels
+
+    def kernel(body, arguments, out_shape, scratch_shapes, work, megabytes):
+        return pl.pallas_call(
+            body,
+            out_shape=out_shape,
+            in_specs=[pl.BlockSpec(memory_space=pltpu.VMEM)] * len(arguments),
+            out_specs=jax.tree.map(lambda _: pl.BlockSpec(memory_space=pltpu.VMEM), out_shape),
+            scratch_shapes=scratch_shapes,
+            compiler_params=pltpu.CompilerParams(vmem_limit_bytes=40 * 2**20),
+            cost_estimate=pl.CostEstimate(flops=work, bytes_accessed=megabytes * 2**20, transcendentals=0),
+        )(*arguments)
+
+    def dealt(block):
+        block = block.reshape(rows, devices, step, channels).transpose(1, 0, 2, 3)
+        return lax.all_to_all(block.reshape(devices, rows * step, channels), every, 0, 0, tiled=True)
+
+    source, cot = dealt(inputs), dealt(cotangent)
+    hidden, slope, left = kernel(
+        functools.partial(forward_kernel, band, step),
+        (source, conv1_weight),
+        (field, jax.ShapeDtypeStruct((cells, channels), F32), jax.ShapeDtypeStruct((8, half, cells), BF16)),
+        [stack, pltpu.VMEM((cells, channels), F32)],
+        flops,
+        8,
+    )
+    left = lax.all_to_all(left, plane, 0, 0, tiled=True)
+    pre_grad, right = kernel(
+        functools.partial(backward_kernel, band, step),
+        (cot, slope, conv2_weight),
+        (field, jax.ShapeDtypeStruct((8, cells // 2, channels), BF16)),
+        [stack],
+        flops,
+        8,
+    )
+    right = lax.all_to_all(right, plane, 0, 0, tiled=True)
+    fields = kernel(
+        functools.partial(outer_kernel, band, step),
+        (source, cot, hidden, pre_grad, conv1_weight, conv2_weight),
+        jax.ShapeDtypeStruct((devices, 2, rows * step, channels), BF16),
+        [stack],
+        2 * flops,
+        9,
+    )
+    fields = lax.all_to_all(fields, every, 0, 0, tiled=True)
+    fields = fields.reshape(devices, 2, rows, step, channels).transpose(1, 2, 0, 3, 4)
+    output, input_grad = fields.reshape(2, rows, width, channels)
+
+    terms = kernel(
+        functools.partial(grads_kernel, band, step),
+        (left, right),
+        jax.ShapeDtypeStruct((8, height, channels), BF16),
+        [
+            pltpu.VMEM((3 * half, 8 * cells), BF16),
+            pltpu.VMEM((3, 8 * cells, half), BF16),
+            pltpu.VMEM((3, 3 * half, half), F32),
+        ],
+        2 * flops,
+        6,
+    )
+    terms = lax.all_to_all(terms, line, 0, 0, tiled=True)
+    grad = jax.ShapeDtypeStruct((3, 3, deep, half // 2), F32)
+    conv1_grad, conv2_grad = kernel(
+        functools.partial(finish_kernel, scale), (terms,), (grad, grad), [], 10**6, 2
+    )
+    return (output, input_grad, conv1_grad, conv2_grad)
+
+
+def is_fast(mesh):
+    return dict(mesh.shape) == {"lon": 8, "lat": 4}
+
+
 def solution(mesh):
-    in_specs = (P("lat", "lon", None), P(), P(), P("lat", "lon", None))
-    out_specs = (
-        P("lat", "lon", None),
-        P("lat", "lon", None),
-        P(None, None, "lon", "lat"),
-        P(None, None, "lon", "lat"),
-    )
-    return jax.shard_map(local, mesh=mesh, in_specs=in_specs, out_specs=out_specs, check_vma=False)
+    body, lon, lat = local, "lon", "lat"
+    if is_fast(mesh):
+        lon, lat = ("z", "y"), ("x", "core")
+        mesh = jax.sharding.Mesh(mesh.devices.reshape(4, 2, 2, 2), lon + lat)
+        body = fast_local
+    field, grad = P(lat, lon, None), P(None, None, lon, lat)
+    return jax.shard_map(
+        body,
+        mesh=mesh,
+        in_specs=(field, P(), P(), field),
+        out_specs=(field, field, grad, grad),
+        check_vma=False,
+    )

time: 353 us -> 136 us (0.39)
  waiting for transfers between devices: 219 us -> 72.4 us
  local copies, waits for them, and re-layouts: 49.1 us -> 22.4 us
  matrix products: 23.6 us -> 0 us
  Pallas kernels: 0 us -> 15.8 us
  starting transfers between devices: 39.1 us -> 24.2 us
  between operations: 14.2 us -> 0.84 us
  other arithmetic: 6.37 us -> 0 us
    reduce_scatter x2 -> x0, waiting for transfers between devices: 131 us -> none  [the longest x1 92.3 us: local(): lax.psum_scatter(terms_two, 'lon', scatter_dimension=1, tiled=True)]
    all_to_all x0 -> x6, waiting for transfers between devices: none -> 72.4 us  [the longest x2 19.2 us: dealt(): lax.all_to_all(block.reshape(devices, rows * step, channels), every, 0, 0...]
    ppermute x16 -> x0, waiting for transfers between devices: 60.2 us -> none  [the longest x8 58.8 us: passed_along(): lax.ppermute(shard, axis, [(i, (i + by) % length) for i in range(length)])]
    ppermute x16 -> x0, starting transfers between devices: 38.9 us -> none  [the longest x8 20.4 us: passed_along(): lax.ppermute(shard, axis, [(i, (i + by) % length) for i in range(length)])]
    unnamed x53 -> x28, local copies, waits for them, and re-layouts: 46.1 us -> 13.7 us
    unnamed x6 -> x0, waiting for transfers between devices: 27.9 us -> none
    all_to_all x0 -> x6, starting transfers between devices: none -> 24.2 us  [the longest x2 9.93 us: dealt(): lax.all_to_all(block.reshape(devices, rows * step, channels), every, 0, 0...]
    dot_general x6 -> x0, matrix products: 23.6 us -> none  [the longest x2 8.84 us: full_terms(): lax.dot_general(stacked, grad, (((0,), (0,)), ((), ())), preferred_elemen...]
  transfers between devices with their start and end apart: 20 -> 6, of which waited for: 12 -> 6; matrix products, arithmetic and copies ran while one was open for 19% -> 5% of each run, Pallas kernels for 0% -> 11%
where the time goes in v2:
time: 136 us
  waiting for transfers between devices  72.4 us (53%)
  starting transfers between devices  24.2 us (18%)
  local copies, waits for them, and re-layouts  22.4 us (16%)
  Pallas kernels  15.8 us (12%)
    all_to_all x2, waiting for transfers between devices, dealt(): lax.all_to_all(block.reshape(devices, rows * step, channels), every, 0, 0...  19.2 us
    pallas_call x5, Pallas kernels, kernel(): pl.pallas_call(body, out_shape=out_shape, in_specs=[pl.BlockSpec(memory_s...  15.8 us
    all_to_all x1, waiting for transfers between devices, fast_local(): left = lax.all_to_all(left, plane, 0, 0, tiled=True)  15 us
    all_to_all x1, waiting for transfers between devices, fast_local(): fields = lax.all_to_all(fields, every, 0, 0, tiled=True)  15 us
    all_to_all x1, waiting for transfers between devices, fast_local(): terms = lax.all_to_all(terms, line, 0, 0, tiled=True)  13.7 us
    unnamed x28, local copies, waits for them, and re-layouts  13.7 us
    all_to_all x2, starting transfers between devices, dealt(): lax.all_to_all(block.reshape(devices, rows * step, channels), every, 0, 0...  9.93 us
    all_to_all x1, waiting for transfers between devices, fast_local(): right = lax.all_to_all(right, plane, 0, 0, tiled=True)  9.46 us
  transfers between devices with their start and end apart: 6, of which 6 were waited for; matrix products, arithmetic and copies ran while one was open for 5% of the time, Pallas kernels for 11%

profile of v2, /device:TPU:0, one launch (start us, length us, event | category | flops | bytes accessed | tf_op | source)
XLA Modules:
  0.0 135.6 jit_solution(14922794460559027351)
XLA Ops:
  0.6 1.2 reshape.28
  3.0 7.3 %all-to-all-start = ((bf16[32,16,384]{2,1,0:T(8,128)(2,1)}), bf16[32,16,384]{2,1,0:T(8,128)(2,1)S(1)}, u32[]{:S(2)}, u32[]{:S(2)}) async-start(bf16[32,16,384]{2,1,0:T(8,128)(2,1)} %reshape.29), calls=%async_computation | async-start | bytes 786432 | tf_op jit(solution)/shard_map/all_to_all | solution.py:292
  11.7 11.8 %all-to-all-done.source_ref = bf16[32,16,384]{2,1,0:T(8,128)(2,1)S(1)} async-done(((bf16[32,16,384]{2,1,0:T(8,128)(2,1)}), bf16[32,16,384]{2,1,0:T(8,128)(2,1)S(1)}, u32[]{:S(2)}, u32[]{:S(2)}) %all-to-all-start) | async-done | bytes 393248 | tf_op jit(solution)/shard_map/all_to_all | solution.py:292
  23.5 2.6 %all-to-all-start.1 = ((bf16[32,16,384]{2,1,0:T(8,128)(2,1)}), bf16[32,16,384]{2,1,0:T(8,128)(2,1)S(1)}, u32[]{:S(2)}, u32[]{:S(2)}) async-start(bf16[32,16,384]{2,1,0:T(8,128)(2,1)} %reshape.31), calls=%async_computation.1 | async-start | bytes 786432 | tf_op jit(solution)/shard_map/all_to_all | solution.py:292
  26.1 1.7 %copy-done.5 = bf16[3,3,384,384]{3,2,1,0:T(8,128)(2,1)S(1)} copy-done((bf16[3,3,384,384]{3,2,1,0:T(8,128)(2,1)S(1)}, bf16[3,3,384,384]{3,2,1,0:T(8,128)(2,1)}, u32[]{:S(2)}) %copy-start.5) | copy-done | bytes 2654232
  27.9 4.0 %shard_map.75 = (bf16[512,384]{1,0:T(8,128)(2,1)S(1)}, f32[512,384]{1,0:T(8,128)S(1)}, bf16[8,192,512]{2,1,0:T(8,128)(2,1)}) custom-call(bf16[32,16,384]{2,1,0:T(8,128)(2,1)S(1)} %all-to-all-done.source_ref, bf16[3,3,384,384]{3,2,1,0:T(8,128)(2,1)S(1)} %copy-done.5), custom_call_target="tpu_custom_call" | custom-call | flops 1358954496 | bytes 8388608 | tf_op jit(solution)/shard_map/pallas_call | solution.py:280
  31.9 7.4 %all-to-all-done.1.cot_ref = bf16[32,16,384]{2,1,0:T(8,128)(2,1)S(1)} async-done(((bf16[32,16,384]{2,1,0:T(8,128)(2,1)}), bf16[32,16,384]{2,1,0:T(8,128)(2,1)S(1)}, u32[]{:S(2)}, u32[]{:S(2)}) %all-to-all-start.1) | async-done | bytes 393248 | tf_op jit(solution)/shard_map/all_to_all | solution.py:292
  39.3 3.6 %all-to-all-start.3 = ((bf16[8,192,512]{2,1,0:T(8,128)(2,1)}), bf16[8,192,512]{2,1,0:T(8,128)(2,1)S(1)}, u32[]{:S(2)}, u32[]{:S(2)}) async-start(bf16[8,192,512]{2,1,0:T(8,128)(2,1)} %get-tuple-element.14), calls=%async_computation.3 | async-start | bytes 3145728 | tf_op jit(solution)/shard_map/all_to_all | solution.py:303
  42.9 1.7 %copy-done.7 = bf16[3,3,384,384]{3,2,1,0:T(8,128)(2,1)S(1)} copy-done((bf16[3,3,384,384]{3,2,1,0:T(8,128)(2,1)S(1)}, bf16[3,3,384,384]{3,2,1,0:T(8,128)(2,1)}, u32[]{:S(2)}) %copy-start.7) | copy-done | bytes 2654232
  44.7 2.2 %shard_map.76 = (bf16[512,384]{1,0:T(8,128)(2,1)S(1)}, bf16[8,256,384]{2,1,0:T(8,128)(2,1)S(1)}) custom-call(bf16[32,16,384]{2,1,0:T(8,128)(2,1)S(1)} %all-to-all-done.1.cot_ref, f32[512,384]{1,0:T(8,128)S(1)} %get-tuple-element.12.slope_ref, bf16[3,3,384,384]{3,2,1,0:T(8,128)(2,1)S(1)} %copy-done.7), custom_call_target="tpu_custom_call" | custom-call | flops 1358954496 | bytes 8388608 | tf_op jit(solution)/shard_map/pallas_call | solution.py:280
  46.9 1.2 copy-done
  48.9 15.0 %all-to-all-done.3.left_ref = bf16[8,192,512]{2,1,0:T(8,128)(2,1)S(1)} async-done(((bf16[8,192,512]{2,1,0:T(8,128)(2,1)}), bf16[8,192,512]{2,1,0:T(8,128)(2,1)S(1)}, u32[]{:S(2)}, u32[]{:S(2)}) %all-to-all-start.3) | async-done | bytes 1572896 | tf_op jit(solution)/shard_map/all_to_all | solution.py:303
  63.9 3.6 %all-to-all-start.4 = ((bf16[8,256,384]{2,1,0:T(8,128)(2,1)}), bf16[8,256,384]{2,1,0:T(8,128)(2,1)S(1)}, u32[]{:S(2)}, u32[]{:S(2)}) async-start(bf16[8,256,384]{2,1,0:T(8,128)(2,1)} %copy-done), calls=%async_computation.4 | async-start | bytes 3145728 | tf_op jit(solution)/shard_map/all_to_all | solution.py:312
  68.5 1.7 %copy-done.6 = bf16[3,3,384,384]{3,2,1,0:T(8,128)(2,1)S(1)} copy-done((bf16[3,3,384,384]{3,2,1,0:T(8,128)(2,1)S(1)}, bf16[3,3,384,384]{3,2,1,0:T(8,128)(2,1)}, u32[]{:S(2)}) %copy-start.6) | copy-done | bytes 2654232
  70.2 1.7 %copy-done.8 = bf16[3,3,384,384]{3,2,1,0:T(8,128)(2,1)S(1)} copy-done((bf16[3,3,384,384]{3,2,1,0:T(8,128)(2,1)S(1)}, bf16[3,3,384,384]{3,2,1,0:T(8,128)(2,1)}, u32[]{:S(2)}) %copy-start.8) | copy-done | bytes 2654232
  72.0 1.0 copy-done.10
  73.9 4.1 %shard_map.77 = bf16[32,2,16,384]{3,2,1,0:T(8,128)(2,1)S(1)} custom-call(bf16[32,16,384]{2,1,0:T(8,128)(2,1)S(1)} %all-to-all-done.source_ref, bf16[32,16,384]{2,1,0:T(8,128)(2,1)S(1)} %copy-done.4, bf16[512,384]{1,0:T(8,128)(2,1)S(1)} %copy-done.12, bf16[512,384]{1,0:T(8,128)(2,1)S(1)} %copy-done.10, bf16[3,3,384,384]{3,2,1,0:T(8,128)(2,1)S(1)} %copy-done.6, ...), custom_call_target="tpu_custom_call" | custom-call | flops 2717908992 | bytes 9437184 | tf_op jit(solution)/shard_map/pallas_call | solution.py:280
  79.0 9.5 %all-to-all-done.4.right_ref = bf16[8,256,384]{2,1,0:T(8,128)(2,1)S(1)} async-done(((bf16[8,256,384]{2,1,0:T(8,128)(2,1)}), bf16[8,256,384]{2,1,0:T(8,128)(2,1)S(1)}, u32[]{:S(2)}, u32[]{:S(2)}) %all-to-all-start.4) | async-done | bytes 1572896 | tf_op jit(solution)/shard_map/all_to_all | solution.py:312
  88.4 3.5 %all-to-all-start.2 = ((bf16[32,2,16,384]{3,2,1,0:T(8,128)(2,1)}), bf16[32,2,16,384]{3,2,1,0:T(8,128)(2,1)}, u32[]{:S(2)}, u32[]{:S(2)}) async-start(bf16[32,2,16,384]{3,2,1,0:T(8,128)(2,1)} %copy-done.1), calls=%async_computation.2 | async-start | bytes 1572864 | tf_op jit(solution)/shard_map/all_to_all | solution.py:321
  91.9 4.5 %shard_map.78 = bf16[8,112,384]{2,1,0:T(8,128)(2,1)S(1)} custom-call(bf16[8,192,512]{2,1,0:T(8,128)(2,1)S(1)} %all-to-all-done.3.left_ref, bf16[8,256,384]{2,1,0:T(8,128)(2,1)S(1)} %all-to-all-done.4.right_ref), custom_call_target="tpu_custom_call" | custom-call | flops 2717908992 | bytes 6291456 | tf_op jit(solution)/shard_map/pallas_call | solution.py:280
  97.3 15.0 %all-to-all-done.2 = bf16[32,2,16,384]{3,2,1,0:T(8,128)(2,1)} async-done(((bf16[32,2,16,384]{3,2,1,0:T(8,128)(2,1)}), bf16[32,2,16,384]{3,2,1,0:T(8,128)(2,1)}, u32[]{:S(2)}, u32[]{:S(2)}) %all-to-all-start.2) | async-done | bytes 786464 | tf_op jit(solution)/shard_map/all_to_all | solution.py:321
  112.3 3.5 %all-to-all-start.5 = ((bf16[8,112,384]{2,1,0:T(8,128)(2,1)}), bf16[8,112,384]{2,1,0:T(8,128)(2,1)S(1)}, u32[]{:S(2)}, u32[]{:S(2)}) async-start(bf16[8,112,384]{2,1,0:T(8,128)(2,1)} %copy-done.2), calls=%async_computation.5 | async-start | bytes 1376256 | tf_op jit(solution)/shard_map/all_to_all | solution.py:337
  115.9 2.2 %reshape.32 = bf16[32,2,8,2,384]{4,3,2,1,0:T(2,128)(2,1)S(1)} reshape(bf16[32,2,16,384]{3,2,1,0:T(8,128)(2,1)} %all-to-all-done.2) | data formatting | bytes 1572864 | tf_op jit(solution)/shard_map/reshape | solution.py:322
  121.0 13.7 %all-to-all-done.5.parts_ref = bf16[8,112,384]{2,1,0:T(8,128)(2,1)S(1)} async-done(((bf16[8,112,384]{2,1,0:T(8,128)(2,1)}), bf16[8,112,384]{2,1,0:T(8,128)(2,1)S(1)}, u32[]{:S(2)}, u32[]{:S(2)}) %all-to-all-start.5) | async-done | bytes 688160 | tf_op jit(solution)/shard_map/all_to_all | solution.py:337
  (33 shorter events, 10.8 us)
Async XLA Ops:
  0.6 9.7 %copy-start.13 = (bf16[8,64,384]{2,1,0:T(8,128)(2,1)S(1)}, bf16[8,64,384]{2,1,0:T(8,128)(2,1)}, u32[]{:S(2)}) copy-start(bf16[8,64,384]{2,1,0:T(8,128)(2,1)} %param.7) | copy-start | bytes 1179652
  3.0 20.5 %all-to-all-start = ((bf16[32,16,384]{2,1,0:T(8,128)(2,1)}), bf16[32,16,384]{2,1,0:T(8,128)(2,1)S(1)}, u32[]{:S(2)}, u32[]{:S(2)}) async-start(bf16[32,16,384]{2,1,0:T(8,128)(2,1)} %reshape.29), calls=%async_computation | async-start | bytes 786432 | tf_op jit(solution)/shard_map/all_to_all | solution.py:292
  23.5 15.8 %all-to-all-start.1 = ((bf16[32,16,384]{2,1,0:T(8,128)(2,1)}), bf16[32,16,384]{2,1,0:T(8,128)(2,1)S(1)}, u32[]{:S(2)}, u32[]{:S(2)}) async-start(bf16[32,16,384]{2,1,0:T(8,128)(2,1)} %reshape.31), calls=%async_computation.1 | async-start | bytes 786432 | tf_op jit(solution)/shard_map/all_to_all | solution.py:292
  26.1 1.8 %copy-start.5 = (bf16[3,3,384,384]{3,2,1,0:T(8,128)(2,1)S(1)}, bf16[3,3,384,384]{3,2,1,0:T(8,128)(2,1)}, u32[]{:S(2)}) copy-start(bf16[3,3,384,384]{3,2,1,0:T(8,128)(2,1)} %one_ref.1) | copy-start | bytes 7962628
  31.9 7.4 %copy-start.11 = (bf16[512,384]{1,0:T(8,128)(2,1)}, bf16[512,384]{1,0:T(8,128)(2,1)S(1)}, u32[]{:S(2)}) copy-start(bf16[512,384]{1,0:T(8,128)(2,1)S(1)} %get-tuple-element.11.hidden_ref) | copy-start | bytes 1179652
  39.3 3.6 %copy-start.3 = (bf16[32,16,384]{2,1,0:T(8,128)(2,1)}, bf16[32,16,384]{2,1,0:T(8,128)(2,1)S(1)}, u32[]{:S(2)}) copy-start(bf16[32,16,384]{2,1,0:T(8,128)(2,1)S(1)} %all-to-all-done.1.cot_ref) | copy-start | bytes 1179652
  39.3 24.5 %all-to-all-start.3 = ((bf16[8,192,512]{2,1,0:T(8,128)(2,1)}), bf16[8,192,512]{2,1,0:T(8,128)(2,1)S(1)}, u32[]{:S(2)}, u32[]{:S(2)}) async-start(bf16[8,192,512]{2,1,0:T(8,128)(2,1)} %get-tuple-element.14), calls=%async_computation.3 | async-start | bytes 3145728 | tf_op jit(solution)/shard_map/all_to_all | solution.py:303
  42.9 1.8 %copy-start.7 = (bf16[3,3,384,384]{3,2,1,0:T(8,128)(2,1)S(1)}, bf16[3,3,384,384]{3,2,1,0:T(8,128)(2,1)}, u32[]{:S(2)}) copy-start(bf16[3,3,384,384]{3,2,1,0:T(8,128)(2,1)} %two_ref.1) | copy-start | bytes 7962628
  46.9 1.2 copy-start
  48.1 0.7 copy-start.9
  63.9 24.5 %all-to-all-start.4 = ((bf16[8,256,384]{2,1,0:T(8,128)(2,1)}), bf16[8,256,384]{2,1,0:T(8,128)(2,1)S(1)}, u32[]{:S(2)}, u32[]{:S(2)}) async-start(bf16[8,256,384]{2,1,0:T(8,128)(2,1)} %copy-done), calls=%async_computation.4 | async-start | bytes 3145728 | tf_op jit(solution)/shard_map/all_to_all | solution.py:312
  67.5 1.0 copy-start.4
  68.5 1.7 %copy-start.6 = (bf16[3,3,384,384]{3,2,1,0:T(8,128)(2,1)S(1)}, bf16[3,3,384,384]{3,2,1,0:T(8,128)(2,1)}, u32[]{:S(2)}) copy-start(bf16[3,3,384,384]{3,2,1,0:T(8,128)(2,1)} %one_ref.1) | copy-start | bytes 7962628
  70.2 1.7 %copy-start.8 = (bf16[3,3,384,384]{3,2,1,0:T(8,128)(2,1)S(1)}, bf16[3,3,384,384]{3,2,1,0:T(8,128)(2,1)}, u32[]{:S(2)}) copy-start(bf16[3,3,384,384]{3,2,1,0:T(8,128)(2,1)} %two_ref.1) | copy-start | bytes 7962628
  72.0 1.0 copy-start.10
  72.9 1.0 copy-start.12
  78.0 0.9 copy-start.1
  88.4 23.9 %all-to-all-start.2 = ((bf16[32,2,16,384]{3,2,1,0:T(8,128)(2,1)}), bf16[32,2,16,384]{3,2,1,0:T(8,128)(2,1)}, u32[]{:S(2)}, u32[]{:S(2)}) async-start(bf16[32,2,16,384]{3,2,1,0:T(8,128)(2,1)} %copy-done.1), calls=%async_computation.2 | async-start | bytes 1572864 | tf_op jit(solution)/shard_map/all_to_all | solution.py:321
  96.5 0.9 copy-start.2
  112.3 22.3 %all-to-all-start.5 = ((bf16[8,112,384]{2,1,0:T(8,128)(2,1)}), bf16[8,112,384]{2,1,0:T(8,128)(2,1)S(1)}, u32[]{:S(2)}, u32[]{:S(2)}) async-start(bf16[8,112,384]{2,1,0:T(8,128)(2,1)} %copy-done.2), calls=%async_computation.5 | async-start | bytes 1376256 | tf_op jit(solution)/shard_map/all_to_all | solution.py:337

commit v3 on v2

--- a/solution.py
+++ b/solution.py
@@ -147,12 +147,64 @@
     return total
 
 
-def forward_kernel(band, step, source_ref, weight_ref, hidden_ref, slope_ref, send_ref, stack_ref, first_ref):
+def one_hot_rows(cells, step, devices, back):
+    to = lax.broadcasted_iota(jnp.int32, (cells, cells), 1 if back else 0)
+    source = lax.broadcasted_iota(jnp.int32, (cells, cells), 0 if back else 1)
+    rows = cells // (devices * step)
+    device, row, column = to // (rows * step), (to // step) % rows, to % step
+    return (source == (row * devices + device) * step + column).astype(BF16)
+
+
+def deal_kernel(step, inputs_ref, cot_ref, out_ref):
+    devices, _, rows, channels = out_ref.shape
+    cells = devices * rows
+    chosen = one_hot_rows(cells, step, devices, False)
+    for at, ref in enumerate((inputs_ref, cot_ref)):
+        field = ref[...].reshape(cells, channels)
+        dealt = jnp.dot(chosen, field, preferred_element_type=F32).astype(BF16)
+        out_ref[:, at] = dealt.reshape(devices, rows, channels)
+
+
+def gather_kernel(step, fields_ref, output_ref, grad_ref):
+    devices, _, rows, channels = fields_ref.shape
+    cells = devices * rows
+    chosen = one_hot_rows(cells, step, devices, True)
+    for at, ref in enumerate((output_ref, grad_ref)):
+        field = fields_ref[:, at].reshape(cells, channels)
+        ref[...] = jnp.dot(chosen, field, preferred_element_type=F32).astype(BF16).reshape(ref.shape)
+
+
+def fetched(pairs, sems):
+    copies = [pltpu.make_async_copy(source, to, sems.at[at]) for at, (source, to) in enumerate(pairs)]
+    for copy in copies:
+        copy.start()
+    return copies
+
+
+def inner_kernel(band, step, place_ref, own_ref, one_ref, two_ref,
+                 hidden_ref, pre_ref, kept_ref, pair_ref, x_same_ref, x_cross_ref, y_same_ref, y_cross_ref,
+                 source_ref, cot_ref, one_held, two_held, stack_ref, first_ref, slope_ref, turned_ref, sems):
+    x, y, core = place_ref[0], place_ref[1], place_ref[2]
     cells, channels = first_ref.shape
-    rows = 32
+    copies = fetched(
+        ((own_ref.at[:, 0], source_ref), (one_ref, one_held), (own_ref.at[:, 1], cot_ref), (two_ref, two_held)), sems
+    )
+    half, rows = channels // 2, 32
+    deep = half // 4
+
+    def turn(at, field):
+        turned = field.T
+        for h in range(2):
+            for z in range(4):
+                begin = (2 * z + h) * deep if at < 2 else h * half + z * deep
+                turned_ref[at * 2 + h, z * deep : (z + 1) * deep, :] = turned[begin : begin + deep]
+
+    copies[0].wait()
     source = source_ref[...].reshape(cells, channels)
     write_stack(source, stack_ref, band, step)
-    first_ref[...] = convolved(stack_ref, weight_ref, band, cells)
+    copies[1].wait()
+    first_ref[...] = convolved(stack_ref, one_held, band, cells)
+    turn(0, source)
 
     def activate(at, carry):
         span = pl.ds(pl.multiple_of(at * rows, rows), rows)
@@ -164,41 +216,50 @@
         return carry
 
     lax.fori_loop(0, cells // rows, activate, 0)
-    half = send_ref.shape[1]
-    deep = half // 4
-    for core, turned in enumerate((source.T, hidden_ref[...].T)):
-        for y in range(2):
-            for z in range(4):
-                begin = (2 * z + y) * deep
-                for x in range(2):
-                    send_ref[y * 4 + x * 2 + core, z * deep : (z + 1) * deep, :] = turned[begin : begin + deep]
-
-
-def backward_kernel(band, step, cot_ref, slope_ref, weight_ref, pre_ref, send_ref, stack_ref):
-    cells, channels = slope_ref.shape
+    turn(1, hidden_ref[...])
+    copies[2].wait()
     cot = cot_ref[...].reshape(cells, channels)
     write_stack(cot, stack_ref, band, step)
-    pre_ref[...] = (slope_ref[...] * convolved_back(stack_ref, weight_ref, band, cells)).astype(BF16)
-    half, upper = channels // 2, cells // 2
-    for core, field in enumerate((pre_ref[...], cot)):
-        field = field.astype(F32)
-        for x in range(2):
-            part = field[:, x * half : (x + 1) * half]
-            part = jnp.concatenate([part[:upper], part[upper:]], axis=1).astype(BF16)
-            for y in range(2):
-                send_ref[y * 4 + x * 2 + core] = part
-
-
-def outer_kernel(band, step, source_ref, cot_ref, hidden_ref, pre_ref, one_ref, two_ref, out_ref, stack_ref):
+    turn(3, cot)
+    copies[3].wait()
+    pre_ref[...] = (slope_ref[...] * convolved_back(stack_ref, two_held, band, cells)).astype(BF16)
+    turn(2, pre_ref[...])
+
+    def left(of, h):
+        return turned_ref[of * 2 + h]
+
+    def right(of, h):
+        return turned_ref[4 + of * 2 + h]
+
+    other = 1 - core
+    kept_ref[0], kept_ref[1] = left(core, y), right(core, x)
+    pair_ref[0], pair_ref[1] = left(other, y), right(other, x)
+    x_same_ref[0], x_same_ref[1] = left(core, y), right(core, 1 - x)
+    x_cross_ref[0], x_cross_ref[1] = left(other, y), right(other, 1 - x)
+    y_same_ref[0], y_same_ref[1] = left(core, 1 - y), right(core, x)
+    y_cross_ref[0], y_cross_ref[1] = left(other, 1 - y), right(other, x)
+
+
+def outer_kernel(band, step, own_ref, hidden_ref, pre_ref, one_ref, two_ref, out_ref,
+                 own_held, hidden_held, pre_held, one_held, two_held, stack_ref, sems):
     cells, channels = hidden_ref.shape
     shape = (out_ref.shape[0],) + out_ref.shape[2:]
-    write_stack(hidden_ref[...], stack_ref, band, step)
-    second = convolved(stack_ref, two_ref, band, cells)
-    source = source_ref[...].reshape(cells, channels)
+    copies = fetched(
+        ((hidden_ref, hidden_held), (two_ref, two_held), (own_ref, own_held), (pre_ref, pre_held), (one_ref, one_held)),
+        sems,
+    )
+    copies[0].wait()
+    write_stack(hidden_held[...], stack_ref, band, step)
+    copies[1].wait()
+    second = convolved(stack_ref, two_held, band, cells)
+    copies[2].wait()
+    source = own_held[:, 0].reshape(cells, channels)
     out_ref[:, 0] = (source.astype(F32) + second).astype(BF16).reshape(shape)
-    write_stack(pre_ref[...], stack_ref, band, step)
-    back = convolved_back(stack_ref, one_ref, band, cells)
-    cot = cot_ref[...].reshape(cells, channels)
+    copies[3].wait()
+    write_stack(pre_held[...], stack_ref, band, step)
+    copies[4].wait()
+    back = convolved_back(stack_ref, one_held, band, cells)
+    cot = own_held[:, 1].reshape(cells, channels)
     out_ref[:, 1] = (cot.astype(F32) + back).astype(BF16).reshape(shape)
 
 
@@ -208,29 +269,32 @@
         yield unit // count, (unit % count) * 16, (unit // 4) * 16, unit % 4
 
 
-def grads_kernel(band, step, left_ref, right_ref, send_ref, turned_ref, moved_ref, sums_ref):
-    sources, half, cells = left_ref.shape
-    upper = cells // 2
+def grads_kernel(band, step, *refs):
+    pieces, (send_ref, turned_ref, moved_ref, sums_ref) = refs[:-4], refs[-4:]
+    kept_ref, pair_ref, x_same_ref, x_cross_ref, y_same_ref, y_cross_ref = pieces[:6]
+    x_far_same, x_far_cross, y_far_same, y_far_cross = pieces[6:]
+    lefts = [ref.at[0] for ref in pieces[:6]] + [x_far_same, x_far_cross]
+    rights = [ref.at[1] for ref in pieces[:6]] + [y_far_same, y_far_cross]
+    half, cells = x_far_same.shape
     place = lax.broadcasted_iota(jnp.int32, (half, cells), 1) % band
-    for at in range(sources):
+    for at, (left_ref, right_ref) in enumerate(zip(lefts, rights)):
         columns = slice(at * cells, (at + 1) * cells)
-        field = left_ref[at]
+        field = left_ref[...]
         wide = field.astype(F32)
         turned_ref[0:half, columns] = jnp.where(place >= step, pltpu.roll(wide, step, 1), 0.0).astype(BF16)
         turned_ref[half : 2 * half, columns] = field
         turned_ref[2 * half :, columns] = jnp.where(
             place < band - step, pltpu.roll(wide, cells - step, 1), 0.0
         ).astype(BF16)
-        packed = right_ref[at].astype(F32)
-        grad = jnp.concatenate([packed[:, :half], packed[:, half:]], axis=0).astype(BF16)
-        begin = at * cells
-        moved_ref[1, begin : begin + cells, :] = grad
-        moved_ref[2, begin + band : begin + cells, :] = grad[: cells - band]
-        moved_ref[2, begin : begin + band, :] = grad[cells - band :]
-        moved_ref[0, begin : begin + cells - band, :] = grad[band:]
-        moved_ref[0, begin + cells - band : begin + cells, :] = grad[:band]
+        grad = right_ref[...]
+        wide = grad.astype(F32)
+        moved_ref[0, :, columns] = pltpu.roll(wide, cells - band, 1).astype(BF16)
+        moved_ref[1, :, columns] = grad
+        moved_ref[2, :, columns] = pltpu.roll(wide, band, 1).astype(BF16)
     for b in range(3):
-        sums_ref[b] = jnp.dot(turned_ref[...], moved_ref[b], preferred_element_type=F32)
+        sums_ref[b] = lax.dot_general(
+            turned_ref[...], moved_ref[b], (((1,), (1,)), ((), ())), preferred_element_type=F32
+        )
     deep, quarter = half // 4, half // 2
     height = send_ref.shape[1]
     for z in range(4):
@@ -262,7 +326,7 @@
 
 def fast_local(inputs, conv1_weight, conv2_weight, cotangent):
     rows, width, channels = inputs.shape
-    every, plane, line = ("z", "y", "x", "core"), ("y", "x", "core"), ("z", "core")
+    every, line = ("z", "y", "x", "core"), ("z", "core")
     devices = lax.axis_size(every)
     step = width // devices
     cells = rows * width
@@ -272,72 +336,99 @@
     half, deep = channels // 2, channels // lon
     height = -(-9 * (deep // 16) // 4) * 16
     scale = (rows * lat * width * lon) ** (-0.5)
-    field = jax.ShapeDtypeStruct((cells, channels), BF16)
-    stack = pltpu.VMEM((cells + 2 * band, 3 * channels), BF16)
     flops = 2 * 9 * cells * channels * channels
-
-    def kernel(body, arguments, out_shape, scratch_shapes, work, megabytes):
+    vmem, hbm, smem = (pl.BlockSpec(memory_space=space) for space in (pltpu.VMEM, pl.ANY, pltpu.SMEM))
+
+    def held(*shape, kind=BF16):
+        return pltpu.VMEM(shape, kind)
+
+    def shaped(*shape, kind=BF16):
+        return jax.ShapeDtypeStruct(shape, kind)
+
+    def kernel(body, specs, arguments, out_shape, scratch_shapes, work, megabytes):
         return pl.pallas_call(
             body,
             out_shape=out_shape,
-            in_specs=[pl.BlockSpec(memory_space=pltpu.VMEM)] * len(arguments),
-            out_specs=jax.tree.map(lambda _: pl.BlockSpec(memory_space=pltpu.VMEM), out_shape),
+            in_specs=specs,
+            out_specs=jax.tree.map(lambda _: vmem, out_shape),
             scratch_shapes=scratch_shapes,
             compiler_params=pltpu.CompilerParams(vmem_limit_bytes=40 * 2**20),
             cost_estimate=pl.CostEstimate(flops=work, bytes_accessed=megabytes * 2**20, transcendentals=0),
         )(*arguments)
 
-    def dealt(block):
-        block = block.reshape(rows, devices, step, channels).transpose(1, 0, 2, 3)
-        return lax.all_to_all(block.reshape(devices, rows * step, channels), every, 0, 0, tiled=True)
-
-    source, cot = dealt(inputs), dealt(cotangent)
-    hidden, slope, left = kernel(
-        functools.partial(forward_kernel, band, step),
-        (source, conv1_weight),
-        (field, jax.ShapeDtypeStruct((cells, channels), F32), jax.ShapeDtypeStruct((8, half, cells), BF16)),
-        [stack, pltpu.VMEM((cells, channels), F32)],
-        flops,
-        8,
-    )
-    left = lax.all_to_all(left, plane, 0, 0, tiled=True)
-    pre_grad, right = kernel(
-        functools.partial(backward_kernel, band, step),
-        (cot, slope, conv2_weight),
-        (field, jax.ShapeDtypeStruct((8, cells // 2, channels), BF16)),
-        [stack],
-        flops,
-        8,
-    )
-    right = lax.all_to_all(right, plane, 0, 0, tiled=True)
+    def passed(piece, x, y, core):
+        pairs = [(i, i ^ (4 * y + 2 * x + core)) for i in range(8)]
+        return lax.ppermute(piece, ("y", "x", "core"), pairs)
+
+    stack = held(cells + 2 * band, 3 * channels)
+    weights = held(*conv1_weight.shape)
+    dealt = shaped(devices, 2, rows * step, channels)
+    own = kernel(functools.partial(deal_kernel, step), [vmem] * 2, (inputs, cotangent), dealt, [], 10**9, 3)
+    own = lax.all_to_all(own, every, 0, 0, tiled=True)
+    place = jnp.stack([lax.axis_index("x"), lax.axis_index("y"), lax.axis_index("core")]).astype(jnp.int32)
+    piece = shaped(2, half, cells)
+    hidden, pre_grad, kept, pair, x_same, x_cross, y_same, y_cross = kernel(
+        functools.partial(inner_kernel, band, step),
+        [smem] + [hbm] * 3,
+        (place, own, conv1_weight, conv2_weight),
+        (shaped(cells, channels),) * 2 + (piece,) * 6,
+        [
+            held(devices, rows * step, channels),
+            held(devices, rows * step, channels),
+            weights,
+            weights,
+            stack,
+            held(cells, channels, kind=F32),
+            held(cells, channels, kind=F32),
+            held(8, half, cells),
+            pltpu.SemaphoreType.DMA((4,)),
+        ],
+        2 * flops,
+        10,
+    )
+    y_same, x_same = passed(y_same, 0, 1, 0), passed(x_same, 1, 0, 0)
+    y_cross, x_cross = passed(y_cross, 0, 1, 1), passed(x_cross, 1, 0, 1)
+    pair = passed(pair, 0, 0, 1)
+    far = (
+        passed(y_same[0], 1, 0, 0),
+        passed(y_cross[0], 1, 0, 0),
+        passed(x_same[1], 0, 1, 0),
+        passed(x_cross[1], 0, 1, 0),
+    )
     fields = kernel(
         functools.partial(outer_kernel, band, step),
-        (source, cot, hidden, pre_grad, conv1_weight, conv2_weight),
-        jax.ShapeDtypeStruct((devices, 2, rows * step, channels), BF16),
-        [stack],
+        [hbm] * 5,
+        (own, hidden, pre_grad, conv1_weight, conv2_weight),
+        dealt,
+        [
+            held(devices, 2, rows * step, channels),
+            held(cells, channels),
+            held(cells, channels),
+            weights,
+            weights,
+            stack,
+            pltpu.SemaphoreType.DMA((5,)),
+        ],
         2 * flops,
         9,
     )
     fields = lax.all_to_all(fields, every, 0, 0, tiled=True)
-    fields = fields.reshape(devices, 2, rows, step, channels).transpose(1, 2, 0, 3, 4)
-    output, input_grad = fields.reshape(2, rows, width, channels)
-
+    output, input_grad = kernel(
+        functools.partial(gather_kernel, step), [vmem], (fields,), (shaped(*inputs.shape),) * 2, [], 10**9, 3
+    )
     terms = kernel(
         functools.partial(grads_kernel, band, step),
-        (left, right),
-        jax.ShapeDtypeStruct((8, height, channels), BF16),
-        [
-            pltpu.VMEM((3 * half, 8 * cells), BF16),
-            pltpu.VMEM((3, 8 * cells, half), BF16),
-            pltpu.VMEM((3, 3 * half, half), F32),
-        ],
+        [vmem] * 10,
+        (kept, pair, x_same, x_cross, y_same, y_cross) + far,
+        shaped(8, height, channels),
+        [held(3 * half, 8 * cells), held(3, half, 8 * cells), held(3, 3 * half, half, kind=F32)],
         2 * flops,
         6,
     )
     terms = lax.all_to_all(terms, line, 0, 0, tiled=True)
-    grad = jax.ShapeDtypeStruct((3, 3, deep, half // 2), F32)
+    grad = shaped(3, 3, deep, half // 2, kind=F32)
     conv1_grad, conv2_grad = kernel(
-        functools.partial(finish_kernel, scale), (terms,), (grad, grad), [], 10**6, 2
+        functools.partial(finish_kernel, scale), [vmem], (terms,), (grad, grad), [], 10**6, 2
     )
     return (output, input_grad, conv1_grad, conv2_grad)
 

time: 136 us -> 124 us (0.912)
  local copies, waits for them, and re-layouts: 22.4 us -> 6.85 us
  Pallas kernels: 15.8 us -> 23.9 us
  waiting for transfers between devices: 72.4 us -> 65.5 us
  starting transfers between devices: 24.2 us -> 26.2 us
    ppermute x0 -> x9, waiting for transfers between devices: none -> 27.6 us  [passed(): return lax.ppermute(piece, ('y', 'x', 'core'), pairs)]
    all_to_all x4 -> x1, waiting for transfers between devices: 43.7 us -> 20.5 us  [fast_local(): own = lax.all_to_all(own, every, 0, 0, tiled=True)]
    all_to_all x1, waiting for transfers between devices: 15 us -> 0.01 us  [fast_local(): fields = lax.all_to_all(fields, every, 0, 0, tiled=True)]
    ppermute x0 -> x9, starting transfers between devices: none -> 10.2 us  [passed(): return lax.ppermute(piece, ('y', 'x', 'core'), pairs)]
    all_to_all x4 -> x1, starting transfers between devices: 17.1 us -> 7.3 us  [fast_local(): own = lax.all_to_all(own, every, 0, 0, tiled=True)]
    pallas_call x5 -> x6, Pallas kernels: 15.8 us -> 23.9 us  [kernel(): pl.pallas_call(body, out_shape=out_shape, in_specs=specs, out_specs=jax.t...]
    unnamed x28 -> x26, local copies, waits for them, and re-layouts: 13.7 us -> 6.79 us
    reshape x7 -> x0, local copies, waits for them, and re-layouts: 5.83 us -> none  [the longest x1 2.16 us: fast_local(): fields.reshape(devices, 2, rows, step, channels).transpose(1, 2, 0, 3, 4)]
  transfers between devices with their start and end apart: 6 -> 12, of which waited for: 6 -> 7; matrix products, arithmetic and copies ran while one was open for 5% -> 0% of each run, Pallas kernels for 11% -> 11%
where the time goes in v3:
time: 124 us; the launch traced here: 123 us
  waiting for transfers between devices  65.5 us (53%)
  starting transfers between devices  26.2 us (21%)
  Pallas kernels  23.9 us (19%)
  local copies, waits for them, and re-layouts  6.85 us (6%)
    ppermute x9, waiting for transfers between devices, passed(): return lax.ppermute(piece, ('y', 'x', 'core'), pairs)  27.6 us
    pallas_call x6, Pallas kernels, kernel(): pl.pallas_call(body, out_shape=out_shape, in_specs=specs, out_specs=jax.t...  23.9 us
    all_to_all x1, waiting for transfers between devices, fast_local(): own = lax.all_to_all(own, every, 0, 0, tiled=True)  20.5 us
    all_to_all x1, waiting for transfers between devices, fast_local(): terms = lax.all_to_all(terms, line, 0, 0, tiled=True)  17.4 us
    ppermute x9, starting transfers between devices, passed(): return lax.ppermute(piece, ('y', 'x', 'core'), pairs)  10.2 us
    all_to_all x1, starting transfers between devices, fast_local(): own = lax.all_to_all(own, every, 0, 0, tiled=True)  7.3 us
    unnamed x26, local copies, waits for them, and re-layouts  6.79 us
    all_to_all x1, starting transfers between devices, fast_local(): terms = lax.all_to_all(terms, line, 0, 0, tiled=True)  4.61 us
  transfers between devices with their start and end apart: 12, of which 7 were waited for; matrix products, arithmetic and copies ran while one was open for 0% of the time, Pallas kernels for 11%

profile of v3, /device:TPU:0, one launch (start us, length us, event | category | flops | bytes accessed | tf_op | source)
XLA Modules:
  0.0 123.3 jit_solution(413837959403705935)
XLA Ops:
  0.6 1.0 copy-done.3
  1.6 1.0 copy-done.4
  2.6 1.6 %shard_map.75 = bf16[32,2,16,384]{3,2,1,0:T(8,128)(2,1)} custom-call(bf16[8,64,384]{2,1,0:T(8,128)(2,1)S(1)} %copy-done.3, bf16[8,64,384]{2,1,0:T(8,128)(2,1)S(1)} %copy-done.4), custom_call_target="tpu_custom_call" | custom-call | flops 1000000000 | bytes 3145728 | tf_op jit(solution)/shard_map/pallas_call | solution.py:349
  4.2 7.3 %all-to-all-start = ((bf16[32,2,16,384]{3,2,1,0:T(8,128)(2,1)}), bf16[32,2,16,384]{3,2,1,0:T(8,128)(2,1)S(1)}, u32[]{:S(2)}, u32[]{:S(2)}) async-start(bf16[32,2,16,384]{3,2,1,0:T(8,128)(2,1)} %shard_map.75), calls=%async_computation | async-start | bytes 1572864 | tf_op jit(solution)/shard_map/all_to_all | solution.py:367
  11.6 20.5 %all-to-all-done.own_ref = bf16[32,2,16,384]{3,2,1,0:T(8,128)(2,1)S(1)} async-done(((bf16[32,2,16,384]{3,2,1,0:T(8,128)(2,1)}), bf16[32,2,16,384]{3,2,1,0:T(8,128)(2,1)S(1)}, u32[]{:S(2)}, u32[]{:S(2)}) %all-to-all-start) | async-done | bytes 786464 | tf_op jit(solution)/shard_map/all_to_all | solution.py:367
  32.2 1.7 %copy-done.2 = bf16[3,3,384,384]{3,2,1,0:T(8,128)(2,1)S(1)} copy-done((bf16[3,3,384,384]{3,2,1,0:T(8,128)(2,1)S(1)}, bf16[3,3,384,384]{3,2,1,0:T(8,128)(2,1)}, u32[]{:S(2)}) %copy-start.2) | copy-done | bytes 2654232
  33.9 7.9 %shard_map.76 = (bf16[512,384]{1,0:T(8,128)(2,1)S(1)}, bf16[512,384]{1,0:T(8,128)(2,1)S(1)}, bf16[2,192,512]{2,1,0:T(8,128)(2,1)S(1)}, bf16[2,192,512]{2,1,0:T(8...) custom-call(s32[3]{0:T(128)S(1)} %pad_add_fusion.place_ref, ...), custom_call_target="tpu_custom_call" | custom-call | flops 2717908992 | bytes 10485760 | tf_op jit(solution)/shard_map/pallas_call | solution.py:349
  44.9 1.5 %collective-permute-start.1 = (bf16[2,192,512]{2,1,0:T(8,128)(2,1)}, bf16[2,192,512]{2,1,0:T(8,128)(2,1)S(1)}, u32[]{:S(2)}, u32[]{:S(2)}) collective-permute-start(bf16[2,192,512]{2,1,0:T(8,128)(2,1)} %get-tuple-element.22), channel_id=1, source_target_pairs={{0,2},{1,3},{2,0},{3,1},{4,6},{5,7},{6,4},{7,5},{8,10},{9,11},{10,... | collective-permute-start | bytes 1179656 | tf_op jit(solution)/shard_map/ppermute | solution.py:361
  46.3 6.9 %shard_map.77 = bf16[32,2,16,384]{3,2,1,0:T(8,128)(2,1)} custom-call(bf16[32,2,16,384]{3,2,1,0:T(8,128)(2,1)S(1)} %all-to-all-done.own_ref, bf16[512,384]{1,0:T(8,128)(2,1)S(1)} %get-tuple-element.16.hidden_ref, bf16[512,384]{1,0:T(8,128)(2,1)S(1)} %get-tuple-element.17.pre_ref, bf16[3,3,384,384]{3,2,1,0:T(8,128)(2,1)S(1)} %copy-done.1, ...), custom_call_target="tpu_custom_call" | custom-call | flops 2717908992 | bytes 9437184 | tf_op jit(solution)/shard_map/pallas_call | solution.py:349
  53.2 4.1 %all-to-all-start.1 = ((bf16[32,2,16,384]{3,2,1,0:T(8,128)(2,1)}), bf16[32,2,16,384]{3,2,1,0:T(8,128)(2,1)S(1)}, u32[]{:S(2)}, u32[]{:S(2)}) async-start(bf16[32,2,16,384]{3,2,1,0:T(8,128)(2,1)} %shard_map.77), calls=%async_computation.1 | async-start | bytes 1572864 | tf_op jit(solution)/shard_map/all_to_all | solution.py:415
  57.5 1.7 %collective-permute-start.3 = (bf16[2,192,512]{2,1,0:T(8,128)(2,1)S(1)}, bf16[2,192,512]{2,1,0:T(8,128)(2,1)S(1)}, u32[]{:S(2)}, u32[]{:S(2)}) collective-permute-start(bf16[2,192,512]{2,1,0:T(8,128)(2,1)S(1)} %copy-done.10), channel_id=1, source_target_pairs={{0,4},{1,5},{2,6},{3,7},{4,0},{5,1},{6,2},{7,3},{8,12},{9,13},{10,... | collective-permute-start | bytes 1179656 | tf_op jit(solution)/shard_map/ppermute | solution.py:361
  59.3 1.6 %collective-permute-start.7 = (bf16[192,512]{1,0:T(8,128)(2,1)S(1)}, bf16[192,512]{1,0:T(8,128)(2,1)S(1)}, u32[]{:S(2)}, u32[]{:S(2)}) collective-permute-start(bf16[192,512]{1,0:T(8,128)(2,1)S(1)} %slice_bitcast_fusion.1), channel_id=1, source_target_pairs={{0,4},{1,5},{2,6},{3,7},{4,0},{5,1},{6,2},{7,3},{8,12},{9,13},{10,... | collective-permute-start | bytes 589832 | tf_op jit(solution)/shard_map/ppermute | solution.py:361
  61.0 7.7 %collective-permute-done.2.refs_3_ = bf16[2,192,512]{2,1,0:T(8,128)(2,1)S(1)} collective-permute-done((bf16[2,192,512]{2,1,0:T(8,128)(2,1)}, bf16[2,192,512]{2,1,0:T(8,128)(2,1)S(1)}, u32[]{:S(2)}, u32[]{:S(2)}) %collective-permute-start.2) | collective-permute-done | bytes 393248 | tf_op jit(solution)/shard_map/ppermute | solution.py:361
  68.7 1.8 %collective-permute-start.8 = (bf16[192,512]{1,0:T(8,128)(2,1)S(1)}, bf16[192,512]{1,0:T(8,128)(2,1)S(1)}, u32[]{:S(2)}, u32[]{:S(2)}) collective-permute-start(bf16[192,512]{1,0:T(8,128)(2,1)S(1)} %slice_bitcast_fusion), channel_id=1, source_target_pairs={{0,4},{1,5},{2,6},{3,7},{4,0},{5,1},{6,2},{7,3},{8,12},{9,13},{10,... | collective-permute-start | bytes 589832 | tf_op jit(solution)/shard_map/ppermute | solution.py:361
  70.5 6.3 %collective-permute-done.3.refs_4_ = bf16[2,192,512]{2,1,0:T(8,128)(2,1)S(1)} collective-permute-done((bf16[2,192,512]{2,1,0:T(8,128)(2,1)S(1)}, bf16[2,192,512]{2,1,0:T(8,128)(2,1)S(1)}, u32[]{:S(2)}, u32[]{:S(2)}) %collective-permute-start.3) | collective-permute-done | bytes 393248 | tf_op jit(solution)/shard_map/ppermute | solution.py:361
  76.8 1.8 %collective-permute-start.5 = (bf16[192,512]{1,0:T(8,128)(2,1)S(1)}, bf16[192,512]{1,0:T(8,128)(2,1)S(1)}, u32[]{:S(2)}, u32[]{:S(2)}) collective-permute-start(bf16[192,512]{1,0:T(8,128)(2,1)S(1)} %slice_bitcast_fusion.3), channel_id=1, source_target_pairs={{0,2},{1,3},{2,0},{3,1},{4,6},{5,7},{6,4},{7,5},{8,10},{9,11},{10,... | collective-permute-start | bytes 589832 | tf_op jit(solution)/shard_map/ppermute | solution.py:361
  78.6 6.2 %collective-permute-done.4.refs_5_ = bf16[2,192,512]{2,1,0:T(8,128)(2,1)S(1)} collective-permute-done((bf16[2,192,512]{2,1,0:T(8,128)(2,1)S(1)}, bf16[2,192,512]{2,1,0:T(8,128)(2,1)S(1)}, u32[]{:S(2)}, u32[]{:S(2)}) %collective-permute-start.4) | collective-permute-done | bytes 393248 | tf_op jit(solution)/shard_map/ppermute | solution.py:361
  84.9 1.6 %collective-permute-start.6 = (bf16[192,512]{1,0:T(8,128)(2,1)S(1)}, bf16[192,512]{1,0:T(8,128)(2,1)S(1)}, u32[]{:S(2)}, u32[]{:S(2)}) collective-permute-start(bf16[192,512]{1,0:T(8,128)(2,1)S(1)} %slice_bitcast_fusion.2), channel_id=1, source_target_pairs={{0,2},{1,3},{2,0},{3,1},{4,6},{5,7},{6,4},{7,5},{8,10},{9,11},{10,... | collective-permute-start | bytes 589832 | tf_op jit(solution)/shard_map/ppermute | solution.py:361
  86.4 3.6 %collective-permute-done.7.refs_8_ = bf16[192,512]{1,0:T(8,128)(2,1)S(1)} collective-permute-done((bf16[192,512]{1,0:T(8,128)(2,1)S(1)}, bf16[192,512]{1,0:T(8,128)(2,1)S(1)}, u32[]{:S(2)}, u32[]{:S(2)}) %collective-permute-start.7) | collective-permute-done | bytes 196640 | tf_op jit(solution)/shard_map/ppermute | solution.py:361
  90.0 3.7 %collective-permute-done.8.refs_9_ = bf16[192,512]{1,0:T(8,128)(2,1)S(1)} collective-permute-done((bf16[192,512]{1,0:T(8,128)(2,1)S(1)}, bf16[192,512]{1,0:T(8,128)(2,1)S(1)}, u32[]{:S(2)}, u32[]{:S(2)}) %collective-permute-start.8) | collective-permute-done | bytes 196640 | tf_op jit(solution)/shard_map/ppermute | solution.py:361
  93.8 5.2 %shard_map.79 = bf16[8,112,384]{2,1,0:T(8,128)(2,1)} custom-call(bf16[2,192,512]{2,1,0:T(8,128)(2,1)S(1)} %copy-done.12, bf16[2,192,512]{2,1,0:T(8,128)(2,1)S(1)} %collective-permute-done.refs_1_, bf16[2,192,512]{2,1,0:T(8,128)(2,1)S(1)} %collective-permute-done.1.refs_2_, bf16[2,192,512]{2,1,0:T(8,128)(2,1)S(1)} %collective-permute-done.2.refs_3_, ...), custom_call_target="tpu_custom_call" | custom-call | flops 2717908992 | bytes 6291456 | tf_op jit(solution)/shard_map/pallas_call | solution.py:349
  98.9 4.6 %all-to-all-start.2 = ((bf16[8,112,384]{2,1,0:T(8,128)(2,1)}), bf16[8,112,384]{2,1,0:T(8,128)(2,1)S(1)}, u32[]{:S(2)}, u32[]{:S(2)}) async-start(bf16[8,112,384]{2,1,0:T(8,128)(2,1)} %shard_map.79), calls=%async_computation.2 | async-start | bytes 1376256 | tf_op jit(solution)/shard_map/all_to_all | solution.py:428
  103.5 1.5 %shard_map.78 = (bf16[8,64,384]{2,1,0:T(8,128)(2,1)}, bf16[8,64,384]{2,1,0:T(8,128)(2,1)}) custom-call(bf16[32,2,16,384]{3,2,1,0:T(8,128)(2,1)S(1)} %all-to-all-done.1.fields_ref), custom_call_target="tpu_custom_call" | custom-call | flops 1000000000 | bytes 3145728 | tf_op jit(solution)/shard_map/pallas_call | solution.py:349
  105.0 17.4 %all-to-all-done.2.parts_ref = bf16[8,112,384]{2,1,0:T(8,128)(2,1)S(1)} async-done(((bf16[8,112,384]{2,1,0:T(8,128)(2,1)}), bf16[8,112,384]{2,1,0:T(8,128)(2,1)S(1)}, u32[]{:S(2)}, u32[]{:S(2)}) %all-to-all-start.2) | async-done | bytes 688160 | tf_op jit(solution)/shard_map/all_to_all | solution.py:428
  (37 shorter events, 4.4 us)
Async XLA Ops:
  0.6 1.0 copy-start.3
  1.6 1.0 copy-start.4
  2.6 29.6 %copy-start = (bf16[3,3,384,384]{3,2,1,0:T(8,128)(2,1)S(1)}, bf16[3,3,384,384]{3,2,1,0:T(8,128)(2,1)}, u32[]{:S(2)}) copy-start(bf16[3,3,384,384]{3,2,1,0:T(8,128)(2,1)} %one_ref.3) | copy-start | bytes 7962628
  4.2 27.9 %all-to-all-start = ((bf16[32,2,16,384]{3,2,1,0:T(8,128)(2,1)}), bf16[32,2,16,384]{3,2,1,0:T(8,128)(2,1)S(1)}, u32[]{:S(2)}, u32[]{:S(2)}) async-start(bf16[32,2,16,384]{3,2,1,0:T(8,128)(2,1)} %shard_map.75), calls=%async_computation | async-start | bytes 1572864 | tf_op jit(solution)/shard_map/all_to_all | solution.py:367
  32.2 1.8 %copy-start.2 = (bf16[3,3,384,384]{3,2,1,0:T(8,128)(2,1)S(1)}, bf16[3,3,384,384]{3,2,1,0:T(8,128)(2,1)}, u32[]{:S(2)}) copy-start(bf16[3,3,384,384]{3,2,1,0:T(8,128)(2,1)} %two_ref.3) | copy-start | bytes 7962628
  33.9 12.4 %copy-start.1 = (bf16[3,3,384,384]{3,2,1,0:T(8,128)(2,1)S(1)}, bf16[3,3,384,384]{3,2,1,0:T(8,128)(2,1)}, u32[]{:S(2)}) copy-start(bf16[3,3,384,384]{3,2,1,0:T(8,128)(2,1)} %one_ref.3) | copy-start | bytes 7962628
  41.8 0.8 copy-start.5
  42.6 0.8 copy-start.7
  44.1 0.8 copy-start.11
  44.9 14.5 %collective-permute-start.1 = (bf16[2,192,512]{2,1,0:T(8,128)(2,1)}, bf16[2,192,512]{2,1,0:T(8,128)(2,1)S(1)}, u32[]{:S(2)}, u32[]{:S(2)}) collective-permute-start(bf16[2,192,512]{2,1,0:T(8,128)(2,1)} %get-tuple-element.22), channel_id=1, source_target_pairs={{0,2},{1,3},{2,0},{3,1},{4,6},{5,7},{6,4},{7,5},{8,10},{9,11},{10,... | collective-permute-start | bytes 1179656 | tf_op jit(solution)/shard_map/ppermute | solution.py:361
  46.3 22.4 %collective-permute-start.2 = (bf16[2,192,512]{2,1,0:T(8,128)(2,1)}, bf16[2,192,512]{2,1,0:T(8,128)(2,1)S(1)}, u32[]{:S(2)}, u32[]{:S(2)}) collective-permute-start(bf16[2,192,512]{2,1,0:T(8,128)(2,1)} %get-tuple-element.23), channel_id=1, source_target_pairs={{0,3},{1,2},{2,1},{3,0},{4,7},{5,6},{6,5},{7,4},{8,11},{9,10},{10,... | collective-permute-start | bytes 1179656 | tf_op jit(solution)/shard_map/ppermute | solution.py:361
  46.3 11.0 %copy-start.6 = (bf16[2,192,512]{2,1,0:T(8,128)(2,1)S(1)}, bf16[2,192,512]{2,1,0:T(8,128)(2,1)}, u32[]{:S(2)}) copy-start(bf16[2,192,512]{2,1,0:T(8,128)(2,1)} %copy-done.5) | copy-start | bytes 1179652
  46.3 11.2 %copy-start.10 = (bf16[2,192,512]{2,1,0:T(8,128)(2,1)S(1)}, bf16[2,192,512]{2,1,0:T(8,128)(2,1)}, u32[]{:S(2)}) copy-start(bf16[2,192,512]{2,1,0:T(8,128)(2,1)} %copy-done.9) | copy-start | bytes 1179652
  46.3 12.9 %copy-start.8 = (bf16[2,192,512]{2,1,0:T(8,128)(2,1)S(1)}, bf16[2,192,512]{2,1,0:T(8,128)(2,1)}, u32[]{:S(2)}) copy-start(bf16[2,192,512]{2,1,0:T(8,128)(2,1)} %copy-done.7) | copy-start | bytes 1179652
  53.2 40.5 %copy-start.12 = (bf16[2,192,512]{2,1,0:T(8,128)(2,1)S(1)}, bf16[2,192,512]{2,1,0:T(8,128)(2,1)}, u32[]{:S(2)}) copy-start(bf16[2,192,512]{2,1,0:T(8,128)(2,1)} %copy-done.11) | copy-start | bytes 1179652
  53.2 45.7 %all-to-all-start.1 = ((bf16[32,2,16,384]{3,2,1,0:T(8,128)(2,1)}), bf16[32,2,16,384]{3,2,1,0:T(8,128)(2,1)S(1)}, u32[]{:S(2)}, u32[]{:S(2)}) async-start(bf16[32,2,16,384]{3,2,1,0:T(8,128)(2,1)} %shard_map.77), calls=%async_computation.1 | async-start | bytes 1572864 | tf_op jit(solution)/shard_map/all_to_all | solution.py:415
  57.4 29.1 %collective-permute-start = (bf16[2,192,512]{2,1,0:T(8,128)(2,1)S(1)}, bf16[2,192,512]{2,1,0:T(8,128)(2,1)S(1)}, u32[]{:S(2)}, u32[]{:S(2)}) collective-permute-start(bf16[2,192,512]{2,1,0:T(8,128)(2,1)S(1)} %copy-done.6), channel_id=1, source_target_pairs={{0,1},{1,0},{2,3},{3,2},{4,5},{5,4},{6,7},{7,6},{8,9},{9,8},{10,11... | collective-permute-start | bytes 1179656 | tf_op jit(solution)/shard_map/ppermute | solution.py:361
  57.5 19.3 %collective-permute-start.3 = (bf16[2,192,512]{2,1,0:T(8,128)(2,1)S(1)}, bf16[2,192,512]{2,1,0:T(8,128)(2,1)S(1)}, u32[]{:S(2)}, u32[]{:S(2)}) collective-permute-start(bf16[2,192,512]{2,1,0:T(8,128)(2,1)S(1)} %copy-done.10), channel_id=1, source_target_pairs={{0,4},{1,5},{2,6},{3,7},{4,0},{5,1},{6,2},{7,3},{8,12},{9,13},{10,... | collective-permute-start | bytes 1179656 | tf_op jit(solution)/shard_map/ppermute | solution.py:361
  59.2 25.7 %collective-permute-start.4 = (bf16[2,192,512]{2,1,0:T(8,128)(2,1)S(1)}, bf16[2,192,512]{2,1,0:T(8,128)(2,1)S(1)}, u32[]{:S(2)}, u32[]{:S(2)}) collective-permute-start(bf16[2,192,512]{2,1,0:T(8,128)(2,1)S(1)} %copy-done.8), channel_id=1, source_target_pairs={{0,5},{1,4},{2,7},{3,6},{4,1},{5,0},{6,3},{7,2},{8,13},{9,12},{10,... | collective-permute-start | bytes 1179656 | tf_op jit(solution)/shard_map/ppermute | solution.py:361
  59.3 30.7 %collective-permute-start.7 = (bf16[192,512]{1,0:T(8,128)(2,1)S(1)}, bf16[192,512]{1,0:T(8,128)(2,1)S(1)}, u32[]{:S(2)}, u32[]{:S(2)}) collective-permute-start(bf16[192,512]{1,0:T(8,128)(2,1)S(1)} %slice_bitcast_fusion.1), channel_id=1, source_target_pairs={{0,4},{1,5},{2,6},{3,7},{4,0},{5,1},{6,2},{7,3},{8,12},{9,13},{10,... | collective-permute-start | bytes 589832 | tf_op jit(solution)/shard_map/ppermute | solution.py:361
  68.7 25.0 %collective-permute-start.8 = (bf16[192,512]{1,0:T(8,128)(2,1)S(1)}, bf16[192,512]{1,0:T(8,128)(2,1)S(1)}, u32[]{:S(2)}, u32[]{:S(2)}) collective-permute-start(bf16[192,512]{1,0:T(8,128)(2,1)S(1)} %slice_bitcast_fusion), channel_id=1, source_target_pairs={{0,4},{1,5},{2,6},{3,7},{4,0},{5,1},{6,2},{7,3},{8,12},{9,13},{10,... | collective-permute-start | bytes 589832 | tf_op jit(solution)/shard_map/ppermute | solution.py:361
  76.8 16.9 %collective-permute-start.5 = (bf16[192,512]{1,0:T(8,128)(2,1)S(1)}, bf16[192,512]{1,0:T(8,128)(2,1)S(1)}, u32[]{:S(2)}, u32[]{:S(2)}) collective-permute-start(bf16[192,512]{1,0:T(8,128)(2,1)S(1)} %slice_bitcast_fusion.3), channel_id=1, source_target_pairs={{0,2},{1,3},{2,0},{3,1},{4,6},{5,7},{6,4},{7,5},{8,10},{9,11},{10,... | collective-permute-start | bytes 589832 | tf_op jit(solution)/shard_map/ppermute | solution.py:361
  84.9 8.9 %collective-permute-start.6 = (bf16[192,512]{1,0:T(8,128)(2,1)S(1)}, bf16[192,512]{1,0:T(8,128)(2,1)S(1)}, u32[]{:S(2)}, u32[]{:S(2)}) collective-permute-start(bf16[192,512]{1,0:T(8,128)(2,1)S(1)} %slice_bitcast_fusion.2), channel_id=1, source_target_pairs={{0,2},{1,3},{2,0},{3,1},{4,6},{5,7},{6,4},{7,5},{8,10},{9,11},{10,... | collective-permute-start | bytes 589832 | tf_op jit(solution)/shard_map/ppermute | solution.py:361
  98.9 23.5 %all-to-all-start.2 = ((bf16[8,112,384]{2,1,0:T(8,128)(2,1)}), bf16[8,112,384]{2,1,0:T(8,128)(2,1)S(1)}, u32[]{:S(2)}, u32[]{:S(2)}) async-start(bf16[8,112,384]{2,1,0:T(8,128)(2,1)} %shard_map.79), calls=%async_computation.2 | async-start | bytes 1376256 | tf_op jit(solution)/shard_map/all_to_all | solution.py:428
  (1 other events, 0.7 us)

commit v4 on v3

--- a/solution.py
+++ b/solution.py
@@ -155,12 +155,14 @@
     return (source == (row * devices + device) * step + column).astype(BF16)
 
 
-def deal_kernel(step, inputs_ref, cot_ref, out_ref):
+def deal_kernel(step, inputs_ref, cot_ref, out_ref, held_ref, sems):
     devices, _, rows, channels = out_ref.shape
     cells = devices * rows
+    copies = fetched(((inputs_ref, held_ref.at[0]), (cot_ref, held_ref.at[1])), sems)
     chosen = one_hot_rows(cells, step, devices, False)
-    for at, ref in enumerate((inputs_ref, cot_ref)):
-        field = ref[...].reshape(cells, channels)
+    for at, copy in enumerate(copies):
+        copy.wait()
+        field = held_ref[at].reshape(cells, channels)
         dealt = jnp.dot(chosen, field, preferred_element_type=F32).astype(BF16)
         out_ref[:, at] = dealt.reshape(devices, rows, channels)
 
@@ -183,12 +185,11 @@
 
 def inner_kernel(band, step, place_ref, own_ref, one_ref, two_ref,
                  hidden_ref, pre_ref, kept_ref, pair_ref, x_same_ref, x_cross_ref, y_same_ref, y_cross_ref,
-                 source_ref, cot_ref, one_held, two_held, stack_ref, first_ref, slope_ref, turned_ref, sems):
+                 two_held, stack_ref, first_ref, slope_ref, turned_ref, sems, out_sems):
     x, y, core = place_ref[0], place_ref[1], place_ref[2]
+    other = 1 - core
     cells, channels = first_ref.shape
-    copies = fetched(
-        ((own_ref.at[:, 0], source_ref), (one_ref, one_held), (own_ref.at[:, 1], cot_ref), (two_ref, two_held)), sems
-    )
+    fetch = fetched(((two_ref, two_held),), sems)[0]
     half, rows = channels // 2, 32
     deep = half // 4
 
@@ -199,11 +200,13 @@
                 begin = (2 * z + h) * deep if at < 2 else h * half + z * deep
                 turned_ref[at * 2 + h, z * deep : (z + 1) * deep, :] = turned[begin : begin + deep]
 
-    copies[0].wait()
-    source = source_ref[...].reshape(cells, channels)
+    def sent(side, wanted):
+        pairs = [(turned_ref.at[4 * side + of * 2 + h], ref.at[side]) for ref, of, h in wanted]
+        return fetched(pairs, out_sems.at[side])
+
+    source = own_ref[:, 0].reshape(cells, channels)
     write_stack(source, stack_ref, band, step)
-    copies[1].wait()
-    first_ref[...] = convolved(stack_ref, one_held, band, cells)
+    first_ref[...] = convolved(stack_ref, one_ref, band, cells)
     turn(0, source)
 
     def activate(at, carry):
@@ -217,49 +220,38 @@
 
     lax.fori_loop(0, cells // rows, activate, 0)
     turn(1, hidden_ref[...])
-    copies[2].wait()
-    cot = cot_ref[...].reshape(cells, channels)
+    copies = sent(0, (
+        (y_same_ref, core, 1 - y), (y_cross_ref, other, 1 - y), (x_same_ref, core, y),
+        (x_cross_ref, other, y), (pair_ref, other, y), (kept_ref, core, y),
+    ))
+    cot = own_ref[:, 1].reshape(cells, channels)
     write_stack(cot, stack_ref, band, step)
     turn(3, cot)
-    copies[3].wait()
+    fetch.wait()
     pre_ref[...] = (slope_ref[...] * convolved_back(stack_ref, two_held, band, cells)).astype(BF16)
     turn(2, pre_ref[...])
-
-    def left(of, h):
-        return turned_ref[of * 2 + h]
-
-    def right(of, h):
-        return turned_ref[4 + of * 2 + h]
-
-    other = 1 - core
-    kept_ref[0], kept_ref[1] = left(core, y), right(core, x)
-    pair_ref[0], pair_ref[1] = left(other, y), right(other, x)
-    x_same_ref[0], x_same_ref[1] = left(core, y), right(core, 1 - x)
-    x_cross_ref[0], x_cross_ref[1] = left(other, y), right(other, 1 - x)
-    y_same_ref[0], y_same_ref[1] = left(core, 1 - y), right(core, x)
-    y_cross_ref[0], y_cross_ref[1] = left(other, 1 - y), right(other, x)
+    copies += sent(1, (
+        (y_same_ref, core, x), (y_cross_ref, other, x), (x_same_ref, core, 1 - x),
+        (x_cross_ref, other, 1 - x), (pair_ref, other, x), (kept_ref, core, x),
+    ))
+    for copy in copies:
+        copy.wait()
 
 
 def outer_kernel(band, step, own_ref, hidden_ref, pre_ref, one_ref, two_ref, out_ref,
-                 own_held, hidden_held, pre_held, one_held, two_held, stack_ref, sems):
+                 one_held, two_held, stack_ref, sems):
     cells, channels = hidden_ref.shape
     shape = (out_ref.shape[0],) + out_ref.shape[2:]
-    copies = fetched(
-        ((hidden_ref, hidden_held), (two_ref, two_held), (own_ref, own_held), (pre_ref, pre_held), (one_ref, one_held)),
-        sems,
-    )
+    copies = fetched(((two_ref, two_held), (one_ref, one_held)), sems)
+    write_stack(hidden_ref[...], stack_ref, band, step)
     copies[0].wait()
-    write_stack(hidden_held[...], stack_ref, band, step)
+    second = convolved(stack_ref, two_held, band, cells)
+    source = own_ref[:, 0].reshape(cells, channels)
+    out_ref[:, 0] = (source.astype(F32) + second).astype(BF16).reshape(shape)
+    write_stack(pre_ref[...], stack_ref, band, step)
     copies[1].wait()
-    second = convolved(stack_ref, two_held, band, cells)
-    copies[2].wait()
-    source = own_held[:, 0].reshape(cells, channels)
-    out_ref[:, 0] = (source.astype(F32) + second).astype(BF16).reshape(shape)
-    copies[3].wait()
-    write_stack(pre_held[...], stack_ref, band, step)
-    copies[4].wait()
     back = convolved_back(stack_ref, one_held, band, cells)
-    cot = own_held[:, 1].reshape(cells, channels)
+    cot = own_ref[:, 1].reshape(cells, channels)
     out_ref[:, 1] = (cot.astype(F32) + back).astype(BF16).reshape(shape)
 
 
@@ -269,32 +261,39 @@
         yield unit // count, (unit % count) * 16, (unit // 4) * 16, unit % 4
 
 
-def grads_kernel(band, step, *refs):
+def summed(band, step, lefts, rights, turned_ref, moved_ref, b):
+    half, cells = lefts[0].shape
+    if b == 0:
+        place = lax.broadcasted_iota(jnp.int32, (half, cells), 1) % band
+        for at, (left_ref, right_ref) in enumerate(zip(lefts, rights)):
+            columns = slice(at * cells, (at + 1) * cells)
+            field = left_ref[...]
+            wide = field.astype(F32)
+            turned_ref[0:half, columns] = jnp.where(place >= step, pltpu.roll(wide, step, 1), 0.0).astype(BF16)
+            turned_ref[half : 2 * half, columns] = field
+            turned_ref[2 * half :, columns] = jnp.where(
+                place < band - step, pltpu.roll(wide, cells - step, 1), 0.0
+            ).astype(BF16)
+            grad = right_ref[...]
+            wide = grad.astype(F32)
+            moved_ref[0, :, columns] = pltpu.roll(wide, cells - band, 1).astype(BF16)
+            moved_ref[1, :, columns] = grad
+            moved_ref[2, :, columns] = pltpu.roll(wide, band, 1).astype(BF16)
+    return lax.dot_general(turned_ref[...], moved_ref[b], (((1,), (1,)), ((), ())), preferred_element_type=F32)
+
+
+def near_kernel(band, step, *refs):
+    pieces, (sums_ref, turned_ref, moved_ref) = refs[:-3], refs[-3:]
+    lefts, rights = ([ref.at[side] for ref in pieces] for side in range(2))
+    for b in range(3):
+        sums_ref[b] = summed(band, step, lefts, rights, turned_ref, moved_ref, b)
+
+
+def far_kernel(band, step, near_ref, *refs):
     pieces, (send_ref, turned_ref, moved_ref, sums_ref) = refs[:-4], refs[-4:]
-    kept_ref, pair_ref, x_same_ref, x_cross_ref, y_same_ref, y_cross_ref = pieces[:6]
-    x_far_same, x_far_cross, y_far_same, y_far_cross = pieces[6:]
-    lefts = [ref.at[0] for ref in pieces[:6]] + [x_far_same, x_far_cross]
-    rights = [ref.at[1] for ref in pieces[:6]] + [y_far_same, y_far_cross]
-    half, cells = x_far_same.shape
-    place = lax.broadcasted_iota(jnp.int32, (half, cells), 1) % band
-    for at, (left_ref, right_ref) in enumerate(zip(lefts, rights)):
-        columns = slice(at * cells, (at + 1) * cells)
-        field = left_ref[...]
-        wide = field.astype(F32)
-        turned_ref[0:half, columns] = jnp.where(place >= step, pltpu.roll(wide, step, 1), 0.0).astype(BF16)
-        turned_ref[half : 2 * half, columns] = field
-        turned_ref[2 * half :, columns] = jnp.where(
-            place < band - step, pltpu.roll(wide, cells - step, 1), 0.0
-        ).astype(BF16)
-        grad = right_ref[...]
-        wide = grad.astype(F32)
-        moved_ref[0, :, columns] = pltpu.roll(wide, cells - band, 1).astype(BF16)
-        moved_ref[1, :, columns] = grad
-        moved_ref[2, :, columns] = pltpu.roll(wide, band, 1).astype(BF16)
+    half, cells = pieces[0].shape
     for b in range(3):
-        sums_ref[b] = lax.dot_general(
-            turned_ref[...], moved_ref[b], (((1,), (1,)), ((), ())), preferred_element_type=F32
-        )
+        sums_ref[b] = near_ref[b] + summed(band, step, pieces[:2], pieces[2:], turned_ref, moved_ref, b)
     deep, quarter = half // 4, half // 2
     height = send_ref.shape[1]
     for z in range(4):
@@ -337,7 +336,7 @@
     height = -(-9 * (deep // 16) // 4) * 16
     scale = (rows * lat * width * lon) ** (-0.5)
     flops = 2 * 9 * cells * channels * channels
-    vmem, hbm, smem = (pl.BlockSpec(memory_space=space) for space in (pltpu.VMEM, pl.ANY, pltpu.SMEM))
+    vmem, hbm, smem = (pl.BlockSpec(memory_space=space) for space in (pltpu.VMEM, pltpu.HBM, pltpu.SMEM))
 
     def held(*shape, kind=BF16):
         return pltpu.VMEM(shape, kind)
@@ -345,14 +344,14 @@
     def shaped(*shape, kind=BF16):
         return jax.ShapeDtypeStruct(shape, kind)
 
-    def kernel(body, specs, arguments, out_shape, scratch_shapes, work, megabytes):
+    def kernel(body, specs, arguments, out_shape, scratch_shapes, work, megabytes, out_specs=None):
         return pl.pallas_call(
             body,
             out_shape=out_shape,
             in_specs=specs,
-            out_specs=jax.tree.map(lambda _: vmem, out_shape),
+            out_specs=out_specs or jax.tree.map(lambda _: vmem, out_shape),
             scratch_shapes=scratch_shapes,
-            compiler_params=pltpu.CompilerParams(vmem_limit_bytes=40 * 2**20),
+            compiler_params=pltpu.CompilerParams(vmem_limit_bytes=28 * 2**20),
             cost_estimate=pl.CostEstimate(flops=work, bytes_accessed=megabytes * 2**20, transcendentals=0),
         )(*arguments)
 
@@ -363,28 +362,35 @@
     stack = held(cells + 2 * band, 3 * channels)
     weights = held(*conv1_weight.shape)
     dealt = shaped(devices, 2, rows * step, channels)
-    own = kernel(functools.partial(deal_kernel, step), [vmem] * 2, (inputs, cotangent), dealt, [], 10**9, 3)
+    own = kernel(
+        functools.partial(deal_kernel, step),
+        [hbm] * 2,
+        (inputs, cotangent),
+        dealt,
+        [held(2, *inputs.shape), pltpu.SemaphoreType.DMA((2,))],
+        10**9,
+        3,
+    )
     own = lax.all_to_all(own, every, 0, 0, tiled=True)
     place = jnp.stack([lax.axis_index("x"), lax.axis_index("y"), lax.axis_index("core")]).astype(jnp.int32)
     piece = shaped(2, half, cells)
     hidden, pre_grad, kept, pair, x_same, x_cross, y_same, y_cross = kernel(
         functools.partial(inner_kernel, band, step),
-        [smem] + [hbm] * 3,
+        [smem, vmem, vmem, hbm],
         (place, own, conv1_weight, conv2_weight),
         (shaped(cells, channels),) * 2 + (piece,) * 6,
         [
-            held(devices, rows * step, channels),
-            held(devices, rows * step, channels),
-            weights,
             weights,
             stack,
             held(cells, channels, kind=F32),
             held(cells, channels, kind=F32),
             held(8, half, cells),
-            pltpu.SemaphoreType.DMA((4,)),
+            pltpu.SemaphoreType.DMA((1,)),
+            pltpu.SemaphoreType.DMA((2, 6)),
         ],
         2 * flops,
         10,
+        (vmem,) * 2 + (hbm,) * 6,
     )
     y_same, x_same = passed(y_same, 0, 1, 0), passed(x_same, 1, 0, 0)
     y_cross, x_cross = passed(y_cross, 0, 1, 1), passed(x_cross, 1, 0, 1)
@@ -397,18 +403,10 @@
     )
     fields = kernel(
         functools.partial(outer_kernel, band, step),
-        [hbm] * 5,
+        [vmem] * 3 + [hbm] * 2,
         (own, hidden, pre_grad, conv1_weight, conv2_weight),
         dealt,
-        [
-            held(devices, 2, rows * step, channels),
-            held(cells, channels),
-            held(cells, channels),
-            weights,
-            weights,
-            stack,
-            pltpu.SemaphoreType.DMA((5,)),
-        ],
+        [weights, weights, stack, pltpu.SemaphoreType.DMA((2,))],
         2 * flops,
         9,
     )
@@ -416,14 +414,24 @@
     output, input_grad = kernel(
         functools.partial(gather_kernel, step), [vmem], (fields,), (shaped(*inputs.shape),) * 2, [], 10**9, 3
     )
-    terms = kernel(
-        functools.partial(grads_kernel, band, step),
-        [vmem] * 10,
-        (kept, pair, x_same, x_cross, y_same, y_cross) + far,
-        shaped(8, height, channels),
-        [held(3 * half, 8 * cells), held(3, half, 8 * cells), held(3, 3 * half, half, kind=F32)],
+    sums = shaped(3, 3 * half, half, kind=F32)
+    near = kernel(
+        functools.partial(near_kernel, band, step),
+        [vmem] * 6,
+        (kept, pair, x_same, x_cross, y_same, y_cross),
+        sums,
+        [held(3 * half, 6 * cells), held(3, half, 6 * cells)],
         2 * flops,
         6,
+    )
+    terms = kernel(
+        functools.partial(far_kernel, band, step),
+        [vmem] * 5,
+        (near,) + far,
+        shaped(8, height, channels),
+        [held(3 * half, 2 * cells), held(3, half, 2 * cells), held(*sums.shape, kind=F32)],
+        flops,
+        4,
     )
     terms = lax.all_to_all(terms, line, 0, 0, tiled=True)
     grad = shaped(3, 3, deep, half // 2, kind=F32)

time: 124 us -> 122 us (0.984)
  waiting for transfers between devices: 65.5 us -> 61.4 us
  Pallas kernels: 23.9 us -> 25.5 us
    ppermute x9, waiting for transfers between devices: 27.6 us -> 23.5 us  [passed(): return lax.ppermute(piece, ('y', 'x', 'core'), pairs)]
    pallas_call x6 -> x7, Pallas kernels: 23.9 us -> 25.5 us  [kernel(): pl.pallas_call(body, out_shape=out_shape, in_specs=specs, out_specs=out_s...]
    unnamed x26 -> x30, local copies, waits for them, and re-layouts: 6.79 us -> 7.68 us
  transfers between devices with their start and end apart: 12 -> 12, of which waited for: 7 -> 6; matrix products, arithmetic and copies ran while one was open for 0% -> 0% of each run, Pallas kernels for 11% -> 11%
where the time goes in v4:
time: 122 us
  waiting for transfers between devices  61.4 us (50%)
  starting transfers between devices  26 us (21%)
  Pallas kernels  25.5 us (21%)
  local copies, waits for them, and re-layouts  7.73 us (6%)
    pallas_call x7, Pallas kernels, kernel(): pl.pallas_call(body, out_shape=out_shape, in_specs=specs, out_specs=out_s...  25.5 us
    ppermute x9, waiting for transfers between devices, passed(): return lax.ppermute(piece, ('y', 'x', 'core'), pairs)  23.5 us
    all_to_all x1, waiting for transfers between devices, fast_local(): own = lax.all_to_all(own, every, 0, 0, tiled=True)  20.5 us
    all_to_all x1, waiting for transfers between devices, fast_local(): terms = lax.all_to_all(terms, line, 0, 0, tiled=True)  17.4 us
    ppermute x9, starting transfers between devices, passed(): return lax.ppermute(piece, ('y', 'x', 'core'), pairs)  11.1 us
    unnamed x30, local copies, waits for them, and re-layouts  7.68 us
    all_to_all x1, starting transfers between devices, fast_local(): own = lax.all_to_all(own, every, 0, 0, tiled=True)  7.3 us
    all_to_all x1, starting transfers between devices, fast_local(): terms = lax.all_to_all(terms, line, 0, 0, tiled=True)  4.7 us
  transfers between devices with their start and end apart: 12, of which 6 were waited for; matrix products, arithmetic and copies ran while one was open for 0% of the time, Pallas kernels for 11%

profile of v4, /device:TPU:0, one launch (start us, length us, event | category | flops | bytes accessed | tf_op | source)
XLA Modules:
  0.0 121.5 jit_solution(2425976702531212196)
XLA Ops:
  0.7 1.1 copy-done.3
  1.8 1.0 copy-done.4
  2.8 2.3 %shard_map.75 = bf16[32,2,16,384]{3,2,1,0:T(8,128)(2,1)} custom-call(bf16[8,64,384]{2,1,0:T(8,128)(2,1)S(1)} %copy-done.3, bf16[8,64,384]{2,1,0:T(8,128)(2,1)S(1)} %copy-done.4), custom_call_target="tpu_custom_call" | custom-call | flops 1000000000 | bytes 3145728 | tf_op jit(solution)/shard_map/pallas_call | solution.py:348
  5.1 7.3 %all-to-all-start = ((bf16[32,2,16,384]{3,2,1,0:T(8,128)(2,1)}), bf16[32,2,16,384]{3,2,1,0:T(8,128)(2,1)S(1)}, u32[]{:S(2)}, u32[]{:S(2)}) async-start(bf16[32,2,16,384]{3,2,1,0:T(8,128)(2,1)} %shard_map.75), calls=%async_computation | async-start | bytes 1572864 | tf_op jit(solution)/shard_map/all_to_all | solution.py:374
  12.5 20.5 %all-to-all-done.own_ref = bf16[32,2,16,384]{3,2,1,0:T(8,128)(2,1)S(1)} async-done(((bf16[32,2,16,384]{3,2,1,0:T(8,128)(2,1)}), bf16[32,2,16,384]{3,2,1,0:T(8,128)(2,1)S(1)}, u32[]{:S(2)}, u32[]{:S(2)}) %all-to-all-start) | async-done | bytes 786464 | tf_op jit(solution)/shard_map/all_to_all | solution.py:374
  33.1 1.7 %copy-done.2 = bf16[3,3,384,384]{3,2,1,0:T(8,128)(2,1)S(1)} copy-done((bf16[3,3,384,384]{3,2,1,0:T(8,128)(2,1)S(1)}, bf16[3,3,384,384]{3,2,1,0:T(8,128)(2,1)}, u32[]{:S(2)}) %copy-start.2) | copy-done | bytes 2654232
  34.8 9.1 %shard_map.76 = (bf16[512,384]{1,0:T(8,128)(2,1)S(1)}, bf16[512,384]{1,0:T(8,128)(2,1)S(1)}, bf16[2,192,512]{2,1,0:T(8,128)(2,1)S(1)}, bf16[2,192,512]{2,1,0:T(8...) custom-call(s32[3]{0:T(128)S(1)} %pad_add_fusion.place_ref, ...), custom_call_target="tpu_custom_call" | custom-call | flops 2717908992 | bytes 10485760 | tf_op jit(solution)/shard_map/pallas_call | solution.py:348
  47.7 1.5 %collective-permute-start.3 = (bf16[2,192,512]{2,1,0:T(8,128)(2,1)}, bf16[2,192,512]{2,1,0:T(8,128)(2,1)S(1)}, u32[]{:S(2)}, u32[]{:S(2)}) collective-permute-start(bf16[2,192,512]{2,1,0:T(8,128)(2,1)} %get-tuple-element.24), channel_id=1, source_target_pairs={{0,4},{1,5},{2,6},{3,7},{4,0},{5,1},{6,2},{7,3},{8,12},{9,13},{10,... | collective-permute-start | bytes 1179656 | tf_op jit(solution)/shard_map/ppermute | solution.py:360
  49.3 6.2 %shard_map.77 = bf16[32,2,16,384]{3,2,1,0:T(8,128)(2,1)} custom-call(bf16[32,2,16,384]{3,2,1,0:T(8,128)(2,1)S(1)} %all-to-all-done.own_ref, bf16[512,384]{1,0:T(8,128)(2,1)S(1)} %get-tuple-element.16.hidden_ref, bf16[512,384]{1,0:T(8,128)(2,1)S(1)} %get-tuple-element.17.pre_ref, bf16[3,3,384,384]{3,2,1,0:T(8,128)(2,1)S(1)} %copy-done.1, ...), custom_call_target="tpu_custom_call" | custom-call | flops 2717908992 | bytes 9437184 | tf_op jit(solution)/shard_map/pallas_call | solution.py:348
  55.5 3.0 %all-to-all-start.1 = ((bf16[32,2,16,384]{3,2,1,0:T(8,128)(2,1)}), bf16[32,2,16,384]{3,2,1,0:T(8,128)(2,1)S(1)}, u32[]{:S(2)}, u32[]{:S(2)}) async-start(bf16[32,2,16,384]{3,2,1,0:T(8,128)(2,1)} %shard_map.77), calls=%async_computation.1 | async-start | bytes 1572864 | tf_op jit(solution)/shard_map/all_to_all | solution.py:413
  58.4 1.3 %collective-permute-start.4 = (bf16[2,192,512]{2,1,0:T(8,128)(2,1)S(1)}, bf16[2,192,512]{2,1,0:T(8,128)(2,1)S(1)}, u32[]{:S(2)}, u32[]{:S(2)}) collective-permute-start(bf16[2,192,512]{2,1,0:T(8,128)(2,1)S(1)} %copy-done.12), channel_id=1, source_target_pairs={{0,5},{1,4},{2,7},{3,6},{4,1},{5,0},{6,3},{7,2},{8,13},{9,12},{10,... | collective-permute-start | bytes 1179656 | tf_op jit(solution)/shard_map/ppermute | solution.py:360
  60.1 1.5 %collective-permute-start.1 = (bf16[2,192,512]{2,1,0:T(8,128)(2,1)S(1)}, bf16[2,192,512]{2,1,0:T(8,128)(2,1)S(1)}, u32[]{:S(2)}, u32[]{:S(2)}) collective-permute-start(bf16[2,192,512]{2,1,0:T(8,128)(2,1)S(1)} %copy-done.10), channel_id=1, source_target_pairs={{0,2},{1,3},{2,0},{3,1},{4,6},{5,7},{6,4},{7,5},{8,10},{9,11},{10,... | collective-permute-start | bytes 1179656 | tf_op jit(solution)/shard_map/ppermute | solution.py:360
  61.7 1.5 %collective-permute-start.5 = (bf16[192,512]{1,0:T(8,128)(2,1)S(1)}, bf16[192,512]{1,0:T(8,128)(2,1)S(1)}, u32[]{:S(2)}, u32[]{:S(2)}) collective-permute-start(bf16[192,512]{1,0:T(8,128)(2,1)S(1)} %slice_bitcast_fusion.3), channel_id=1, source_target_pairs={{0,2},{1,3},{2,0},{3,1},{4,6},{5,7},{6,4},{7,5},{8,10},{9,11},{10,... | collective-permute-start | bytes 589832 | tf_op jit(solution)/shard_map/ppermute | solution.py:360
  63.2 13.2 %collective-permute-done.4.refs_5_ = bf16[2,192,512]{2,1,0:T(8,128)(2,1)S(1)} collective-permute-done((bf16[2,192,512]{2,1,0:T(8,128)(2,1)S(1)}, bf16[2,192,512]{2,1,0:T(8,128)(2,1)S(1)}, u32[]{:S(2)}, u32[]{:S(2)}) %collective-permute-start.4) | collective-permute-done | bytes 393248 | tf_op jit(solution)/shard_map/ppermute | solution.py:360
  76.4 2.0 %collective-permute-start.6 = (bf16[192,512]{1,0:T(8,128)(2,1)S(1)}, bf16[192,512]{1,0:T(8,128)(2,1)S(1)}, u32[]{:S(2)}, u32[]{:S(2)}) collective-permute-start(bf16[192,512]{1,0:T(8,128)(2,1)S(1)} %slice_bitcast_fusion.2), channel_id=1, source_target_pairs={{0,2},{1,3},{2,0},{3,1},{4,6},{5,7},{6,4},{7,5},{8,10},{9,11},{10,... | collective-permute-start | bytes 589832 | tf_op jit(solution)/shard_map/ppermute | solution.py:360
  78.5 1.4 %collective-permute-start.7 = (bf16[192,512]{1,0:T(8,128)(2,1)S(1)}, bf16[192,512]{1,0:T(8,128)(2,1)S(1)}, u32[]{:S(2)}, u32[]{:S(2)}) collective-permute-start(bf16[192,512]{1,0:T(8,128)(2,1)S(1)} %slice_bitcast_fusion.1), channel_id=1, source_target_pairs={{0,4},{1,5},{2,6},{3,7},{4,0},{5,1},{6,2},{7,3},{8,12},{9,13},{10,... | collective-permute-start | bytes 589832 | tf_op jit(solution)/shard_map/ppermute | solution.py:360
  79.9 6.0 %collective-permute-done.2.refs_3_ = bf16[2,192,512]{2,1,0:T(8,128)(2,1)S(1)} collective-permute-done((bf16[2,192,512]{2,1,0:T(8,128)(2,1)S(1)}, bf16[2,192,512]{2,1,0:T(8,128)(2,1)S(1)}, u32[]{:S(2)}, u32[]{:S(2)}) %collective-permute-start.2) | collective-permute-done | bytes 393248 | tf_op jit(solution)/shard_map/ppermute | solution.py:360
  85.9 1.4 %collective-permute-start.8 = (bf16[192,512]{1,0:T(8,128)(2,1)S(1)}, bf16[192,512]{1,0:T(8,128)(2,1)S(1)}, u32[]{:S(2)}, u32[]{:S(2)}) collective-permute-start(bf16[192,512]{1,0:T(8,128)(2,1)S(1)} %slice_bitcast_fusion), channel_id=1, source_target_pairs={{0,4},{1,5},{2,6},{3,7},{4,0},{5,1},{6,2},{7,3},{8,12},{9,13},{10,... | collective-permute-start | bytes 589832 | tf_op jit(solution)/shard_map/ppermute | solution.py:360
  87.4 3.2 %shard_map.79.near_ref = f32[3,576,192]{2,1,0:T(8,128)S(1)} custom-call(bf16[2,192,512]{2,1,0:T(8,128)(2,1)S(1)} %copy-done.14, bf16[2,192,512]{2,1,0:T(8,128)(2,1)S(1)} %collective-permute-done.refs_1_, bf16[2,192,512]{2,1,0:T(8,128)(2,1)S(1)} %collective-permute-done.1.refs_2_, bf16[2,192,512]{2,1,0:T(8,128)(2,1)S(1)} %collective-permute-done.2.refs_3_, ...), custom_call_target="tpu_custom_call" | custom-call | flops 2717908992 | bytes 6291456 | tf_op jit(solution)/shard_map/pallas_call | solution.py:348
  90.9 3.8 %collective-permute-done.6.refs_1_ = bf16[192,512]{1,0:T(8,128)(2,1)S(1)} collective-permute-done((bf16[192,512]{1,0:T(8,128)(2,1)S(1)}, bf16[192,512]{1,0:T(8,128)(2,1)S(1)}, u32[]{:S(2)}, u32[]{:S(2)}) %collective-permute-start.6) | collective-permute-done | bytes 196640 | tf_op jit(solution)/shard_map/ppermute | solution.py:360
  94.7 2.3 %shard_map.80 = bf16[8,112,384]{2,1,0:T(8,128)(2,1)} custom-call(f32[3,576,192]{2,1,0:T(8,128)S(1)} %shard_map.79.near_ref, bf16[192,512]{1,0:T(8,128)(2,1)S(1)} %collective-permute-done.5.refs_0_, bf16[192,512]{1,0:T(8,128)(2,1)S(1)} %collective-permute-done.6.refs_1_, bf16[192,512]{1,0:T(8,128)(2,1)S(1)} %collective-permute-done.7.refs_2_, ...), custom_call_target="tpu_custom_call" | custom-call | flops 1358954496 | bytes 4194304 | tf_op jit(solution)/shard_map/pallas_call | solution.py:348
  97.0 4.7 %all-to-all-start.2 = ((bf16[8,112,384]{2,1,0:T(8,128)(2,1)}), bf16[8,112,384]{2,1,0:T(8,128)(2,1)S(1)}, u32[]{:S(2)}, u32[]{:S(2)}) async-start(bf16[8,112,384]{2,1,0:T(8,128)(2,1)} %shard_map.80), calls=%async_computation.2 | async-start | bytes 1376256 | tf_op jit(solution)/shard_map/all_to_all | solution.py:436
  101.7 1.5 %shard_map.78 = (bf16[8,64,384]{2,1,0:T(8,128)(2,1)}, bf16[8,64,384]{2,1,0:T(8,128)(2,1)}) custom-call(bf16[32,2,16,384]{3,2,1,0:T(8,128)(2,1)S(1)} %all-to-all-done.1.fields_ref), custom_call_target="tpu_custom_call" | custom-call | flops 1000000000 | bytes 3145728 | tf_op jit(solution)/shard_map/pallas_call | solution.py:348
  103.2 17.4 %all-to-all-done.2.parts_ref = bf16[8,112,384]{2,1,0:T(8,128)(2,1)S(1)} async-done(((bf16[8,112,384]{2,1,0:T(8,128)(2,1)}), bf16[8,112,384]{2,1,0:T(8,128)(2,1)S(1)}, u32[]{:S(2)}, u32[]{:S(2)}) %all-to-all-start.2) | async-done | bytes 688160 | tf_op jit(solution)/shard_map/all_to_all | solution.py:436
  (42 shorter events, 5.6 us)
Async XLA Ops:
  0.6 32.4 %copy-start = (bf16[3,3,384,384]{3,2,1,0:T(8,128)(2,1)S(1)}, bf16[3,3,384,384]{3,2,1,0:T(8,128)(2,1)}, u32[]{:S(2)}) copy-start(bf16[3,3,384,384]{3,2,1,0:T(8,128)(2,1)} %one_ref.3) | copy-start | bytes 7962628
  0.6 1.1 copy-start.3
  1.8 1.0 copy-start.4
  5.1 27.9 %all-to-all-start = ((bf16[32,2,16,384]{3,2,1,0:T(8,128)(2,1)}), bf16[32,2,16,384]{3,2,1,0:T(8,128)(2,1)S(1)}, u32[]{:S(2)}, u32[]{:S(2)}) async-start(bf16[32,2,16,384]{3,2,1,0:T(8,128)(2,1)} %shard_map.75), calls=%async_computation | async-start | bytes 1572864 | tf_op jit(solution)/shard_map/all_to_all | solution.py:374
  33.1 1.8 %copy-start.2 = (bf16[3,3,384,384]{3,2,1,0:T(8,128)(2,1)S(1)}, bf16[3,3,384,384]{3,2,1,0:T(8,128)(2,1)}, u32[]{:S(2)}) copy-start(bf16[3,3,384,384]{3,2,1,0:T(8,128)(2,1)} %two_ref.3) | copy-start | bytes 7962628
  34.8 14.4 %copy-start.1 = (bf16[3,3,384,384]{3,2,1,0:T(8,128)(2,1)S(1)}, bf16[3,3,384,384]{3,2,1,0:T(8,128)(2,1)}, u32[]{:S(2)}) copy-start(bf16[3,3,384,384]{3,2,1,0:T(8,128)(2,1)} %one_ref.3) | copy-start | bytes 7962628
  44.7 0.8 copy-start.7
  45.5 0.8 copy-start.9
  47.7 13.9 %collective-permute-start.3 = (bf16[2,192,512]{2,1,0:T(8,128)(2,1)}, bf16[2,192,512]{2,1,0:T(8,128)(2,1)S(1)}, u32[]{:S(2)}, u32[]{:S(2)}) collective-permute-start(bf16[2,192,512]{2,1,0:T(8,128)(2,1)} %get-tuple-element.24), channel_id=1, source_target_pairs={{0,4},{1,5},{2,6},{3,7},{4,0},{5,1},{6,2},{7,3},{8,12},{9,13},{10,... | collective-permute-start | bytes 1179656 | tf_op jit(solution)/shard_map/ppermute | solution.py:360
  49.2 9.2 %copy-start.12 = (bf16[2,192,512]{2,1,0:T(8,128)(2,1)S(1)}, bf16[2,192,512]{2,1,0:T(8,128)(2,1)}, u32[]{:S(2)}) copy-start(bf16[2,192,512]{2,1,0:T(8,128)(2,1)} %copy-done.11) | copy-start | bytes 1179652
  49.3 10.5 %copy-start.6 = (bf16[2,192,512]{2,1,0:T(8,128)(2,1)S(1)}, bf16[2,192,512]{2,1,0:T(8,128)(2,1)}, u32[]{:S(2)}) copy-start(bf16[2,192,512]{2,1,0:T(8,128)(2,1)} %copy-done.5) | copy-start | bytes 1179652
  49.3 10.9 %copy-start.10 = (bf16[2,192,512]{2,1,0:T(8,128)(2,1)S(1)}, bf16[2,192,512]{2,1,0:T(8,128)(2,1)}, u32[]{:S(2)}) copy-start(bf16[2,192,512]{2,1,0:T(8,128)(2,1)} %copy-done.9) | copy-start | bytes 1179652
  49.3 12.3 %copy-start.8 = (bf16[2,192,512]{2,1,0:T(8,128)(2,1)S(1)}, bf16[2,192,512]{2,1,0:T(8,128)(2,1)}, u32[]{:S(2)}) copy-start(bf16[2,192,512]{2,1,0:T(8,128)(2,1)} %copy-done.7) | copy-start | bytes 1179652
  55.4 31.9 %copy-start.14 = (bf16[2,192,512]{2,1,0:T(8,128)(2,1)S(1)}, bf16[2,192,512]{2,1,0:T(8,128)(2,1)}, u32[]{:S(2)}) copy-start(bf16[2,192,512]{2,1,0:T(8,128)(2,1)} %copy-done.13) | copy-start | bytes 1179652
  55.5 41.6 %all-to-all-start.1 = ((bf16[32,2,16,384]{3,2,1,0:T(8,128)(2,1)}), bf16[32,2,16,384]{3,2,1,0:T(8,128)(2,1)S(1)}, u32[]{:S(2)}, u32[]{:S(2)}) async-start(bf16[32,2,16,384]{3,2,1,0:T(8,128)(2,1)} %shard_map.77), calls=%async_computation.1 | async-start | bytes 1572864 | tf_op jit(solution)/shard_map/all_to_all | solution.py:413
  58.4 18.0 %collective-permute-start.4 = (bf16[2,192,512]{2,1,0:T(8,128)(2,1)S(1)}, bf16[2,192,512]{2,1,0:T(8,128)(2,1)S(1)}, u32[]{:S(2)}, u32[]{:S(2)}) collective-permute-start(bf16[2,192,512]{2,1,0:T(8,128)(2,1)S(1)} %copy-done.12), channel_id=1, source_target_pairs={{0,5},{1,4},{2,7},{3,6},{4,1},{5,0},{6,3},{7,2},{8,13},{9,12},{10,... | collective-permute-start | bytes 1179656 | tf_op jit(solution)/shard_map/ppermute | solution.py:360
  59.8 27.6 %collective-permute-start = (bf16[2,192,512]{2,1,0:T(8,128)(2,1)S(1)}, bf16[2,192,512]{2,1,0:T(8,128)(2,1)S(1)}, u32[]{:S(2)}, u32[]{:S(2)}) collective-permute-start(bf16[2,192,512]{2,1,0:T(8,128)(2,1)S(1)} %copy-done.6), channel_id=1, source_target_pairs={{0,1},{1,0},{2,3},{3,2},{4,5},{5,4},{6,7},{7,6},{8,9},{9,8},{10,11... | collective-permute-start | bytes 1179656 | tf_op jit(solution)/shard_map/ppermute | solution.py:360
  60.1 18.3 %collective-permute-start.1 = (bf16[2,192,512]{2,1,0:T(8,128)(2,1)S(1)}, bf16[2,192,512]{2,1,0:T(8,128)(2,1)S(1)}, u32[]{:S(2)}, u32[]{:S(2)}) collective-permute-start(bf16[2,192,512]{2,1,0:T(8,128)(2,1)S(1)} %copy-done.10), channel_id=1, source_target_pairs={{0,2},{1,3},{2,0},{3,1},{4,6},{5,7},{6,4},{7,5},{8,10},{9,11},{10,... | collective-permute-start | bytes 1179656 | tf_op jit(solution)/shard_map/ppermute | solution.py:360
  61.6 24.3 %collective-permute-start.2 = (bf16[2,192,512]{2,1,0:T(8,128)(2,1)S(1)}, bf16[2,192,512]{2,1,0:T(8,128)(2,1)S(1)}, u32[]{:S(2)}, u32[]{:S(2)}) collective-permute-start(bf16[2,192,512]{2,1,0:T(8,128)(2,1)S(1)} %copy-done.8), channel_id=1, source_target_pairs={{0,3},{1,2},{2,1},{3,0},{4,7},{5,6},{6,5},{7,4},{8,11},{9,10},{10,... | collective-permute-start | bytes 1179656 | tf_op jit(solution)/shard_map/ppermute | solution.py:360
  61.7 29.2 %collective-permute-start.5 = (bf16[192,512]{1,0:T(8,128)(2,1)S(1)}, bf16[192,512]{1,0:T(8,128)(2,1)S(1)}, u32[]{:S(2)}, u32[]{:S(2)}) collective-permute-start(bf16[192,512]{1,0:T(8,128)(2,1)S(1)} %slice_bitcast_fusion.3), channel_id=1, source_target_pairs={{0,2},{1,3},{2,0},{3,1},{4,6},{5,7},{6,4},{7,5},{8,10},{9,11},{10,... | collective-permute-start | bytes 589832 | tf_op jit(solution)/shard_map/ppermute | solution.py:360
  76.4 18.3 %collective-permute-start.6 = (bf16[192,512]{1,0:T(8,128)(2,1)S(1)}, bf16[192,512]{1,0:T(8,128)(2,1)S(1)}, u32[]{:S(2)}, u32[]{:S(2)}) collective-permute-start(bf16[192,512]{1,0:T(8,128)(2,1)S(1)} %slice_bitcast_fusion.2), channel_id=1, source_target_pairs={{0,2},{1,3},{2,0},{3,1},{4,6},{5,7},{6,4},{7,5},{8,10},{9,11},{10,... | collective-permute-start | bytes 589832 | tf_op jit(solution)/shard_map/ppermute | solution.py:360
  78.5 16.2 %collective-permute-start.7 = (bf16[192,512]{1,0:T(8,128)(2,1)S(1)}, bf16[192,512]{1,0:T(8,128)(2,1)S(1)}, u32[]{:S(2)}, u32[]{:S(2)}) collective-permute-start(bf16[192,512]{1,0:T(8,128)(2,1)S(1)} %slice_bitcast_fusion.1), channel_id=1, source_target_pairs={{0,4},{1,5},{2,6},{3,7},{4,0},{5,1},{6,2},{7,3},{8,12},{9,13},{10,... | collective-permute-start | bytes 589832 | tf_op jit(solution)/shard_map/ppermute | solution.py:360
  85.9 8.8 %collective-permute-start.8 = (bf16[192,512]{1,0:T(8,128)(2,1)S(1)}, bf16[192,512]{1,0:T(8,128)(2,1)S(1)}, u32[]{:S(2)}, u32[]{:S(2)}) collective-permute-start(bf16[192,512]{1,0:T(8,128)(2,1)S(1)} %slice_bitcast_fusion), channel_id=1, source_target_pairs={{0,4},{1,5},{2,6},{3,7},{4,0},{5,1},{6,2},{7,3},{8,12},{9,13},{10,... | collective-permute-start | bytes 589832 | tf_op jit(solution)/shard_map/ppermute | solution.py:360
  97.0 23.6 %all-to-all-start.2 = ((bf16[8,112,384]{2,1,0:T(8,128)(2,1)}), bf16[8,112,384]{2,1,0:T(8,128)(2,1)S(1)}, u32[]{:S(2)}, u32[]{:S(2)}) async-start(bf16[8,112,384]{2,1,0:T(8,128)(2,1)} %shard_map.80), calls=%async_computation.2 | async-start | bytes 1376256 | tf_op jit(solution)/shard_map/all_to_all | solution.py:436
  (3 other events, 2.2 us)

commit v5 on v4

--- a/solution.py
+++ b/solution.py
@@ -351,7 +351,7 @@
             in_specs=specs,
             out_specs=out_specs or jax.tree.map(lambda _: vmem, out_shape),
             scratch_shapes=scratch_shapes,
-            compiler_params=pltpu.CompilerParams(vmem_limit_bytes=28 * 2**20),
+            compiler_params=pltpu.CompilerParams(vmem_limit_bytes=20 * 2**20),
             cost_estimate=pl.CostEstimate(flops=work, bytes_accessed=megabytes * 2**20, transcendentals=0),
         )(*arguments)
 
@@ -365,7 +365,7 @@
     own = kernel(
         functools.partial(deal_kernel, step),
         [hbm] * 2,
-        (inputs, cotangent),
+        [pltpu.with_memory_space_constraint(field, pltpu.HBM) for field in (inputs, cotangent)],
         dealt,
         [held(2, *inputs.shape), pltpu.SemaphoreType.DMA((2,))],
         10**9,
@@ -373,11 +373,12 @@
     )
     own = lax.all_to_all(own, every, 0, 0, tiled=True)
     place = jnp.stack([lax.axis_index("x"), lax.axis_index("y"), lax.axis_index("core")]).astype(jnp.int32)
-    piece = shaped(2, half, cells)
+    piece = pltpu.HBM((2, half, cells), BF16)
+    one_far, two_far = (pltpu.with_memory_space_constraint(w, pltpu.HBM) for w in (conv1_weight, conv2_weight))
     hidden, pre_grad, kept, pair, x_same, x_cross, y_same, y_cross = kernel(
         functools.partial(inner_kernel, band, step),
         [smem, vmem, vmem, hbm],
-        (place, own, conv1_weight, conv2_weight),
+        (place, own, conv1_weight, two_far),
         (shaped(cells, channels),) * 2 + (piece,) * 6,
         [
             weights,
@@ -404,7 +405,7 @@
     fields = kernel(
         functools.partial(outer_kernel, band, step),
         [vmem] * 3 + [hbm] * 2,
-        (own, hidden, pre_grad, conv1_weight, conv2_weight),
+        (own, hidden, pre_grad, one_far, two_far),
         dealt,
         [weights, weights, stack, pltpu.SemaphoreType.DMA((2,))],
         2 * flops,

time: 122 us -> 114 us (0.934)
  local copies, waits for them, and re-layouts: 7.73 us -> 0.08 us
    unnamed x30 -> x12, local copies, waits for them, and re-layouts: 7.68 us -> 0.03 us
  transfers between devices with their start and end apart: 12 -> 12, of which waited for: 6 -> 6; matrix products, arithmetic and copies ran while one was open for 0% -> 0% of each run, Pallas kernels for 11% -> 13%
where the time goes in v5:
time: 114 us
  waiting for transfers between devices  61.4 us (54%)
  starting transfers between devices  26.1 us (23%)
  Pallas kernels  25.4 us (22%)
    pallas_call x7, Pallas kernels, kernel(): pl.pallas_call(body, out_shape=out_shape, in_specs=specs, out_specs=out_s...  25.4 us
    ppermute x9, waiting for transfers between devices, passed(): return lax.ppermute(piece, ('y', 'x', 'core'), pairs)  23.4 us
    all_to_all x1, waiting for transfers between devices, fast_local(): own = lax.all_to_all(own, every, 0, 0, tiled=True)  20.5 us
    all_to_all x1, waiting for transfers between devices, fast_local(): terms = lax.all_to_all(terms, line, 0, 0, tiled=True)  17.4 us
    ppermute x9, starting transfers between devices, passed(): return lax.ppermute(piece, ('y', 'x', 'core'), pairs)  11.2 us
    all_to_all x1, starting transfers between devices, fast_local(): own = lax.all_to_all(own, every, 0, 0, tiled=True)  7.3 us
    all_to_all x1, starting transfers between devices, fast_local(): terms = lax.all_to_all(terms, line, 0, 0, tiled=True)  4.7 us
    all_to_all x1, starting transfers between devices, fast_local(): fields = lax.all_to_all(fields, every, 0, 0, tiled=True)  2.95 us
  transfers between devices with their start and end apart: 12, of which 6 were waited for; matrix products, arithmetic and copies ran while one was open for 0% of the time, Pallas kernels for 13%

profile of v5, /device:TPU:0, one launch (start us, length us, event | category | flops | bytes accessed | tf_op | source)
XLA Modules:
  0.0 113.8 jit_solution(13207203958445274453)
XLA Ops:
  0.6 2.9 %shard_map.75 = bf16[32,2,16,384]{3,2,1,0:T(8,128)(2,1)} custom-call(bf16[8,64,384]{2,1,0:T(8,128)(2,1)} %inputs_ref.1, bf16[8,64,384]{2,1,0:T(8,128)(2,1)} %cot_ref.1), custom_call_target="tpu_custom_call" | custom-call | flops 1000000000 | bytes 3145728 | tf_op jit(solution)/shard_map/pallas_call | solution.py:348
  3.6 7.3 %all-to-all-start = ((bf16[32,2,16,384]{3,2,1,0:T(8,128)(2,1)}), bf16[32,2,16,384]{3,2,1,0:T(8,128)(2,1)S(1)}, u32[]{:S(2)}, u32[]{:S(2)}) async-start(bf16[32,2,16,384]{3,2,1,0:T(8,128)(2,1)} %shard_map.75), calls=%async_computation | async-start | bytes 1572864 | tf_op jit(solution)/shard_map/all_to_all | solution.py:374
  11.0 20.5 %all-to-all-done.own_ref = bf16[32,2,16,384]{3,2,1,0:T(8,128)(2,1)S(1)} async-done(((bf16[32,2,16,384]{3,2,1,0:T(8,128)(2,1)}), bf16[32,2,16,384]{3,2,1,0:T(8,128)(2,1)S(1)}, u32[]{:S(2)}, u32[]{:S(2)}) %all-to-all-start) | async-done | bytes 786464 | tf_op jit(solution)/shard_map/all_to_all | solution.py:374
  31.5 7.2 %shard_map.76 = (bf16[512,384]{1,0:T(8,128)(2,1)S(1)}, bf16[512,384]{1,0:T(8,128)(2,1)S(1)}, bf16[2,192,512]{2,1,0:T(8,128)(2,1)}, bf16[2,192,512]{2,1,0:T(8,128...) custom-call(s32[3]{0:T(128)S(1)} %pad_add_fusion.place_ref, ...), custom_call_target="tpu_custom_call" | custom-call | flops 2717908992 | bytes 10485760 | tf_op jit(solution)/shard_map/pallas_call | solution.py:348
  38.8 1.6 %collective-permute-start.3 = (bf16[2,192,512]{2,1,0:T(8,128)(2,1)}, bf16[2,192,512]{2,1,0:T(8,128)(2,1)S(1)}, u32[]{:S(2)}, u32[]{:S(2)}) collective-permute-start(bf16[2,192,512]{2,1,0:T(8,128)(2,1)} %get-tuple-element.24), channel_id=1, source_target_pairs={{0,4},{1,5},{2,6},{3,7},{4,0},{5,1},{6,2},{7,3},{8,12},{9,13},{10,... | collective-permute-start | bytes 1179656 | tf_op jit(solution)/shard_map/ppermute | solution.py:360
  40.4 7.3 %shard_map.77 = bf16[32,2,16,384]{3,2,1,0:T(8,128)(2,1)} custom-call(bf16[32,2,16,384]{3,2,1,0:T(8,128)(2,1)S(1)} %all-to-all-done.own_ref, bf16[512,384]{1,0:T(8,128)(2,1)S(1)} %get-tuple-element.16.hidden_ref, bf16[512,384]{1,0:T(8,128)(2,1)S(1)} %get-tuple-element.17.pre_ref, bf16[3,3,384,384]{3,2,1,0:T(8,128)(2,1)} %one_ref.3, ...), custom_call_target="tpu_custom_call" | custom-call | flops 2717908992 | bytes 9437184 | tf_op jit(solution)/shard_map/pallas_call | solution.py:348
  47.7 3.0 %all-to-all-start.1 = ((bf16[32,2,16,384]{3,2,1,0:T(8,128)(2,1)}), bf16[32,2,16,384]{3,2,1,0:T(8,128)(2,1)S(1)}, u32[]{:S(2)}, u32[]{:S(2)}) async-start(bf16[32,2,16,384]{3,2,1,0:T(8,128)(2,1)} %shard_map.77), calls=%async_computation.1 | async-start | bytes 1572864 | tf_op jit(solution)/shard_map/all_to_all | solution.py:414
  50.7 1.3 %collective-permute-start.4 = (bf16[2,192,512]{2,1,0:T(8,128)(2,1)S(1)}, bf16[2,192,512]{2,1,0:T(8,128)(2,1)S(1)}, u32[]{:S(2)}, u32[]{:S(2)}) collective-permute-start(bf16[2,192,512]{2,1,0:T(8,128)(2,1)S(1)} %copy-done.5), channel_id=1, source_target_pairs={{0,5},{1,4},{2,7},{3,6},{4,1},{5,0},{6,3},{7,2},{8,13},{9,12},{10,... | collective-permute-start | bytes 1179656 | tf_op jit(solution)/shard_map/ppermute | solution.py:360
  52.0 0.4 collective-permute-start
  52.4 1.5 %collective-permute-start.1 = (bf16[2,192,512]{2,1,0:T(8,128)(2,1)S(1)}, bf16[2,192,512]{2,1,0:T(8,128)(2,1)S(1)}, u32[]{:S(2)}, u32[]{:S(2)}) collective-permute-start(bf16[2,192,512]{2,1,0:T(8,128)(2,1)S(1)} %copy-done.4), channel_id=1, source_target_pairs={{0,2},{1,3},{2,0},{3,1},{4,6},{5,7},{6,4},{7,5},{8,10},{9,11},{10,... | collective-permute-start | bytes 1179656 | tf_op jit(solution)/shard_map/ppermute | solution.py:360
  53.9 1.5 %collective-permute-start.5 = (bf16[192,512]{1,0:T(8,128)(2,1)S(1)}, bf16[192,512]{1,0:T(8,128)(2,1)S(1)}, u32[]{:S(2)}, u32[]{:S(2)}) collective-permute-start(bf16[192,512]{1,0:T(8,128)(2,1)S(1)} %slice_bitcast_fusion.3), channel_id=1, source_target_pairs={{0,2},{1,3},{2,0},{3,1},{4,6},{5,7},{6,4},{7,5},{8,10},{9,11},{10,... | collective-permute-start | bytes 589832 | tf_op jit(solution)/shard_map/ppermute | solution.py:360
  55.4 13.2 %collective-permute-done.4.refs_5_ = bf16[2,192,512]{2,1,0:T(8,128)(2,1)S(1)} collective-permute-done((bf16[2,192,512]{2,1,0:T(8,128)(2,1)S(1)}, bf16[2,192,512]{2,1,0:T(8,128)(2,1)S(1)}, u32[]{:S(2)}, u32[]{:S(2)}) %collective-permute-start.4) | collective-permute-done | bytes 393248 | tf_op jit(solution)/shard_map/ppermute | solution.py:360
  68.7 2.0 %collective-permute-start.6 = (bf16[192,512]{1,0:T(8,128)(2,1)S(1)}, bf16[192,512]{1,0:T(8,128)(2,1)S(1)}, u32[]{:S(2)}, u32[]{:S(2)}) collective-permute-start(bf16[192,512]{1,0:T(8,128)(2,1)S(1)} %slice_bitcast_fusion.2), channel_id=1, source_target_pairs={{0,2},{1,3},{2,0},{3,1},{4,6},{5,7},{6,4},{7,5},{8,10},{9,11},{10,... | collective-permute-start | bytes 589832 | tf_op jit(solution)/shard_map/ppermute | solution.py:360
  70.7 1.4 %collective-permute-start.7 = (bf16[192,512]{1,0:T(8,128)(2,1)S(1)}, bf16[192,512]{1,0:T(8,128)(2,1)S(1)}, u32[]{:S(2)}, u32[]{:S(2)}) collective-permute-start(bf16[192,512]{1,0:T(8,128)(2,1)S(1)} %slice_bitcast_fusion.1), channel_id=1, source_target_pairs={{0,4},{1,5},{2,6},{3,7},{4,0},{5,1},{6,2},{7,3},{8,12},{9,13},{10,... | collective-permute-start | bytes 589832 | tf_op jit(solution)/shard_map/ppermute | solution.py:360
  72.2 6.0 %collective-permute-done.2.refs_3_ = bf16[2,192,512]{2,1,0:T(8,128)(2,1)S(1)} collective-permute-done((bf16[2,192,512]{2,1,0:T(8,128)(2,1)S(1)}, bf16[2,192,512]{2,1,0:T(8,128)(2,1)S(1)}, u32[]{:S(2)}, u32[]{:S(2)}) %collective-permute-start.2) | collective-permute-done | bytes 393248 | tf_op jit(solution)/shard_map/ppermute | solution.py:360
  78.2 1.4 %collective-permute-start.8 = (bf16[192,512]{1,0:T(8,128)(2,1)S(1)}, bf16[192,512]{1,0:T(8,128)(2,1)S(1)}, u32[]{:S(2)}, u32[]{:S(2)}) collective-permute-start(bf16[192,512]{1,0:T(8,128)(2,1)S(1)} %slice_bitcast_fusion), channel_id=1, source_target_pairs={{0,4},{1,5},{2,6},{3,7},{4,0},{5,1},{6,2},{7,3},{8,12},{9,13},{10,... | collective-permute-start | bytes 589832 | tf_op jit(solution)/shard_map/ppermute | solution.py:360
  79.6 3.2 %shard_map.79.near_ref = f32[3,576,192]{2,1,0:T(8,128)S(1)} custom-call(bf16[2,192,512]{2,1,0:T(8,128)(2,1)S(1)} %copy-done.1, bf16[2,192,512]{2,1,0:T(8,128)(2,1)S(1)} %collective-permute-done.refs_1_, bf16[2,192,512]{2,1,0:T(8,128)(2,1)S(1)} %collective-permute-done.1.refs_2_, bf16[2,192,512]{2,1,0:T(8,128)(2,1)S(1)} %collective-permute-done.2.refs_3_, ...), custom_call_target="tpu_custom_call" | custom-call | flops 2717908992 | bytes 6291456 | tf_op jit(solution)/shard_map/pallas_call | solution.py:348
  82.8 0.3 collective-permute-done.5.refs_0_
  83.1 3.8 %collective-permute-done.6.refs_1_ = bf16[192,512]{1,0:T(8,128)(2,1)S(1)} collective-permute-done((bf16[192,512]{1,0:T(8,128)(2,1)S(1)}, bf16[192,512]{1,0:T(8,128)(2,1)S(1)}, u32[]{:S(2)}, u32[]{:S(2)}) %collective-permute-start.6) | collective-permute-done | bytes 196640 | tf_op jit(solution)/shard_map/ppermute | solution.py:360
  87.0 2.3 %shard_map.80 = bf16[8,112,384]{2,1,0:T(8,128)(2,1)} custom-call(f32[3,576,192]{2,1,0:T(8,128)S(1)} %shard_map.79.near_ref, bf16[192,512]{1,0:T(8,128)(2,1)S(1)} %collective-permute-done.5.refs_0_, bf16[192,512]{1,0:T(8,128)(2,1)S(1)} %collective-permute-done.6.refs_1_, bf16[192,512]{1,0:T(8,128)(2,1)S(1)} %collective-permute-done.7.refs_2_, ...), custom_call_target="tpu_custom_call" | custom-call | flops 1358954496 | bytes 4194304 | tf_op jit(solution)/shard_map/pallas_call | solution.py:348
  89.3 4.7 %all-to-all-start.2 = ((bf16[8,112,384]{2,1,0:T(8,128)(2,1)}), bf16[8,112,384]{2,1,0:T(8,128)(2,1)S(1)}, u32[]{:S(2)}, u32[]{:S(2)}) async-start(bf16[8,112,384]{2,1,0:T(8,128)(2,1)} %shard_map.80), calls=%async_computation.2 | async-start | bytes 1376256 | tf_op jit(solution)/shard_map/all_to_all | solution.py:437
  94.0 1.5 %shard_map.78 = (bf16[8,64,384]{2,1,0:T(8,128)(2,1)}, bf16[8,64,384]{2,1,0:T(8,128)(2,1)}) custom-call(bf16[32,2,16,384]{3,2,1,0:T(8,128)(2,1)S(1)} %all-to-all-done.1.fields_ref), custom_call_target="tpu_custom_call" | custom-call | flops 1000000000 | bytes 3145728 | tf_op jit(solution)/shard_map/pallas_call | solution.py:348
  95.5 17.4 %all-to-all-done.2.parts_ref = bf16[8,112,384]{2,1,0:T(8,128)(2,1)S(1)} async-done(((bf16[8,112,384]{2,1,0:T(8,128)(2,1)}), bf16[8,112,384]{2,1,0:T(8,128)(2,1)S(1)}, u32[]{:S(2)}, u32[]{:S(2)}) %all-to-all-start.2) | async-done | bytes 688160 | tf_op jit(solution)/shard_map/all_to_all | solution.py:437
  112.9 0.9 shard_map.81
  (24 shorter events, 0.2 us)
Async XLA Ops:
  0.6 30.9 %copy-start = (bf16[3,3,384,384]{3,2,1,0:T(8,128)(2,1)S(1)}, bf16[3,3,384,384]{3,2,1,0:T(8,128)(2,1)}, u32[]{:S(2)}) copy-start(bf16[3,3,384,384]{3,2,1,0:T(8,128)(2,1)} %one_ref.3) | copy-start | bytes 7962628
  3.6 27.9 %all-to-all-start = ((bf16[32,2,16,384]{3,2,1,0:T(8,128)(2,1)}), bf16[32,2,16,384]{3,2,1,0:T(8,128)(2,1)S(1)}, u32[]{:S(2)}, u32[]{:S(2)}) async-start(bf16[32,2,16,384]{3,2,1,0:T(8,128)(2,1)} %shard_map.75), calls=%async_computation | async-start | bytes 1572864 | tf_op jit(solution)/shard_map/all_to_all | solution.py:374
  38.8 15.1 %collective-permute-start.3 = (bf16[2,192,512]{2,1,0:T(8,128)(2,1)}, bf16[2,192,512]{2,1,0:T(8,128)(2,1)S(1)}, u32[]{:S(2)}, u32[]{:S(2)}) collective-permute-start(bf16[2,192,512]{2,1,0:T(8,128)(2,1)} %get-tuple-element.24), channel_id=1, source_target_pairs={{0,4},{1,5},{2,6},{3,7},{4,0},{5,1},{6,2},{7,3},{8,12},{9,13},{10,... | collective-permute-start | bytes 1179656 | tf_op jit(solution)/shard_map/ppermute | solution.py:360
  40.4 10.3 %copy-start.5 = (bf16[2,192,512]{2,1,0:T(8,128)(2,1)S(1)}, bf16[2,192,512]{2,1,0:T(8,128)(2,1)}, u32[]{:S(2)}) copy-start(bf16[2,192,512]{2,1,0:T(8,128)(2,1)} %get-tuple-element.25) | copy-start | bytes 1179652
  40.4 11.7 %copy-start.2 = (bf16[2,192,512]{2,1,0:T(8,128)(2,1)S(1)}, bf16[2,192,512]{2,1,0:T(8,128)(2,1)}, u32[]{:S(2)}) copy-start(bf16[2,192,512]{2,1,0:T(8,128)(2,1)} %get-tuple-element.21) | copy-start | bytes 1179652
  40.4 12.0 %copy-start.4 = (bf16[2,192,512]{2,1,0:T(8,128)(2,1)S(1)}, bf16[2,192,512]{2,1,0:T(8,128)(2,1)}, u32[]{:S(2)}) copy-start(bf16[2,192,512]{2,1,0:T(8,128)(2,1)} %get-tuple-element.22) | copy-start | bytes 1179652
  40.4 13.5 %copy-start.3 = (bf16[2,192,512]{2,1,0:T(8,128)(2,1)S(1)}, bf16[2,192,512]{2,1,0:T(8,128)(2,1)}, u32[]{:S(2)}) copy-start(bf16[2,192,512]{2,1,0:T(8,128)(2,1)} %get-tuple-element.23) | copy-start | bytes 1179652
  47.7 31.9 %copy-start.1 = (bf16[2,192,512]{2,1,0:T(8,128)(2,1)S(1)}, bf16[2,192,512]{2,1,0:T(8,128)(2,1)}, u32[]{:S(2)}) copy-start(bf16[2,192,512]{2,1,0:T(8,128)(2,1)} %get-tuple-element.20.refs_0_) | copy-start | bytes 1179652
  47.7 41.6 %all-to-all-start.1 = ((bf16[32,2,16,384]{3,2,1,0:T(8,128)(2,1)}), bf16[32,2,16,384]{3,2,1,0:T(8,128)(2,1)S(1)}, u32[]{:S(2)}, u32[]{:S(2)}) async-start(bf16[32,2,16,384]{3,2,1,0:T(8,128)(2,1)} %shard_map.77), calls=%async_computation.1 | async-start | bytes 1572864 | tf_op jit(solution)/shard_map/all_to_all | solution.py:414
  50.7 18.0 %collective-permute-start.4 = (bf16[2,192,512]{2,1,0:T(8,128)(2,1)S(1)}, bf16[2,192,512]{2,1,0:T(8,128)(2,1)S(1)}, u32[]{:S(2)}, u32[]{:S(2)}) collective-permute-start(bf16[2,192,512]{2,1,0:T(8,128)(2,1)S(1)} %copy-done.5), channel_id=1, source_target_pairs={{0,5},{1,4},{2,7},{3,6},{4,1},{5,0},{6,3},{7,2},{8,13},{9,12},{10,... | collective-permute-start | bytes 1179656 | tf_op jit(solution)/shard_map/ppermute | solution.py:360
  52.0 27.6 %collective-permute-start = (bf16[2,192,512]{2,1,0:T(8,128)(2,1)S(1)}, bf16[2,192,512]{2,1,0:T(8,128)(2,1)S(1)}, u32[]{:S(2)}, u32[]{:S(2)}) collective-permute-start(bf16[2,192,512]{2,1,0:T(8,128)(2,1)S(1)} %copy-done.2), channel_id=1, source_target_pairs={{0,1},{1,0},{2,3},{3,2},{4,5},{5,4},{6,7},{7,6},{8,9},{9,8},{10,11... | collective-permute-start | bytes 1179656 | tf_op jit(solution)/shard_map/ppermute | solution.py:360
  52.4 18.3 %collective-permute-start.1 = (bf16[2,192,512]{2,1,0:T(8,128)(2,1)S(1)}, bf16[2,192,512]{2,1,0:T(8,128)(2,1)S(1)}, u32[]{:S(2)}, u32[]{:S(2)}) collective-permute-start(bf16[2,192,512]{2,1,0:T(8,128)(2,1)S(1)} %copy-done.4), channel_id=1, source_target_pairs={{0,2},{1,3},{2,0},{3,1},{4,6},{5,7},{6,4},{7,5},{8,10},{9,11},{10,... | collective-permute-start | bytes 1179656 | tf_op jit(solution)/shard_map/ppermute | solution.py:360
  53.9 24.3 %collective-permute-start.2 = (bf16[2,192,512]{2,1,0:T(8,128)(2,1)S(1)}, bf16[2,192,512]{2,1,0:T(8,128)(2,1)S(1)}, u32[]{:S(2)}, u32[]{:S(2)}) collective-permute-start(bf16[2,192,512]{2,1,0:T(8,128)(2,1)S(1)} %copy-done.3), channel_id=1, source_target_pairs={{0,3},{1,2},{2,1},{3,0},{4,7},{5,6},{6,5},{7,4},{8,11},{9,10},{10,... | collective-permute-start | bytes 1179656 | tf_op jit(solution)/shard_map/ppermute | solution.py:360
  53.9 29.2 %collective-permute-start.5 = (bf16[192,512]{1,0:T(8,128)(2,1)S(1)}, bf16[192,512]{1,0:T(8,128)(2,1)S(1)}, u32[]{:S(2)}, u32[]{:S(2)}) collective-permute-start(bf16[192,512]{1,0:T(8,128)(2,1)S(1)} %slice_bitcast_fusion.3), channel_id=1, source_target_pairs={{0,2},{1,3},{2,0},{3,1},{4,6},{5,7},{6,4},{7,5},{8,10},{9,11},{10,... | collective-permute-start | bytes 589832 | tf_op jit(solution)/shard_map/ppermute | solution.py:360
  68.7 18.3 %collective-permute-start.6 = (bf16[192,512]{1,0:T(8,128)(2,1)S(1)}, bf16[192,512]{1,0:T(8,128)(2,1)S(1)}, u32[]{:S(2)}, u32[]{:S(2)}) collective-permute-start(bf16[192,512]{1,0:T(8,128)(2,1)S(1)} %slice_bitcast_fusion.2), channel_id=1, source_target_pairs={{0,2},{1,3},{2,0},{3,1},{4,6},{5,7},{6,4},{7,5},{8,10},{9,11},{10,... | collective-permute-start | bytes 589832 | tf_op jit(solution)/shard_map/ppermute | solution.py:360
  70.7 16.3 %collective-permute-start.7 = (bf16[192,512]{1,0:T(8,128)(2,1)S(1)}, bf16[192,512]{1,0:T(8,128)(2,1)S(1)}, u32[]{:S(2)}, u32[]{:S(2)}) collective-permute-start(bf16[192,512]{1,0:T(8,128)(2,1)S(1)} %slice_bitcast_fusion.1), channel_id=1, source_target_pairs={{0,4},{1,5},{2,6},{3,7},{4,0},{5,1},{6,2},{7,3},{8,12},{9,13},{10,... | collective-permute-start | bytes 589832 | tf_op jit(solution)/shard_map/ppermute | solution.py:360
  78.2 8.8 %collective-permute-start.8 = (bf16[192,512]{1,0:T(8,128)(2,1)S(1)}, bf16[192,512]{1,0:T(8,128)(2,1)S(1)}, u32[]{:S(2)}, u32[]{:S(2)}) collective-permute-start(bf16[192,512]{1,0:T(8,128)(2,1)S(1)} %slice_bitcast_fusion), channel_id=1, source_target_pairs={{0,4},{1,5},{2,6},{3,7},{4,0},{5,1},{6,2},{7,3},{8,12},{9,13},{10,... | collective-permute-start | bytes 589832 | tf_op jit(solution)/shard_map/ppermute | solution.py:360
  89.3 23.6 %all-to-all-start.2 = ((bf16[8,112,384]{2,1,0:T(8,128)(2,1)}), bf16[8,112,384]{2,1,0:T(8,128)(2,1)S(1)}, u32[]{:S(2)}, u32[]{:S(2)}) async-start(bf16[8,112,384]{2,1,0:T(8,128)(2,1)} %shard_map.80), calls=%async_computation.2 | async-start | bytes 1376256 | tf_op jit(solution)/shard_map/all_to_all | solution.py:437

commit v6 on v5

--- a/solution.py
+++ b/solution.py
@@ -289,8 +289,9 @@
         sums_ref[b] = summed(band, step, lefts, rights, turned_ref, moved_ref, b)
 
 
-def far_kernel(band, step, near_ref, *refs):
-    pieces, (send_ref, turned_ref, moved_ref, sums_ref) = refs[:-4], refs[-4:]
+def far_kernel(band, step, place_ref, near_ref, *refs):
+    pieces, out_refs, (turned_ref, moved_ref, sums_ref, send_ref, sems) = refs[:4], refs[4:-5], refs[-5:]
+    me = place_ref[3] * 2 + place_ref[2]
     half, cells = pieces[0].shape
     for b in range(3):
         sums_ref[b] = near_ref[b] + summed(band, step, pieces[:2], pieces[2:], turned_ref, moved_ref, b)
@@ -308,15 +309,26 @@
                 while len(parts) < 4:
                     parts.append(jnp.zeros((16, quarter), F32))
                 send_ref[z * 2 + core, to * 16 : (to + 1) * 16, :] = jnp.concatenate(parts, axis=1).astype(BF16)
-
-
-def finish_kernel(scale, parts_ref, one_ref, two_ref):
+    pairs = [(send_ref.at[me ^ away], ref) for away, ref in enumerate(out_refs)]
+    for copy in fetched(pairs, sems):
+        copy.wait()
+
+
+def finish_kernel(scale, place_ref, *refs):
+    parts, (one_ref, two_ref) = refs[:-2], refs[-2:]
+    core = place_ref[2]
     deep, quarter = one_ref.shape[2:]
-    for core, out_ref in enumerate((one_ref, two_ref)):
-        total = parts_ref[core].astype(F32)
-        for z in range(1, parts_ref.shape[0] // 2):
-            total = total + parts_ref[z * 2 + core].astype(F32)
-        total = total * scale
+    sums = []
+    for other in range(2):
+        total = parts[other][...].astype(F32)
+        for ref in parts[other + 2 :: 2]:
+            total = total + ref[...].astype(F32)
+        sums.append(total * scale)
+    ours, theirs = sums
+    for out_ref, total in (
+        (one_ref, jnp.where(core == 0, ours, theirs)),
+        (two_ref, jnp.where(core == 0, theirs, ours)),
+    ):
         for tap, row, begin, slot in units(deep):
             out_ref[tap // 3, tap % 3, row : row + 16, :] = total[
                 begin : begin + 16, slot * quarter : (slot + 1) * quarter
@@ -325,7 +337,7 @@
 
 def fast_local(inputs, conv1_weight, conv2_weight, cotangent):
     rows, width, channels = inputs.shape
-    every, line = ("z", "y", "x", "core"), ("z", "core")
+    every = ("z", "y", "x", "core")
     devices = lax.axis_size(every)
     step = width // devices
     cells = rows * width
@@ -372,7 +384,7 @@
         3,
     )
     own = lax.all_to_all(own, every, 0, 0, tiled=True)
-    place = jnp.stack([lax.axis_index("x"), lax.axis_index("y"), lax.axis_index("core")]).astype(jnp.int32)
+    place = jnp.stack([lax.axis_index(axis) for axis in ("x", "y", "core", "z")]).astype(jnp.int32)
     piece = pltpu.HBM((2, half, cells), BF16)
     one_far, two_far = (pltpu.with_memory_space_constraint(w, pltpu.HBM) for w in (conv1_weight, conv2_weight))
     hidden, pre_grad, kept, pair, x_same, x_cross, y_same, y_cross = kernel(
@@ -402,6 +414,7 @@
         passed(x_same[1], 0, 1, 0),
         passed(x_cross[1], 0, 1, 0),
     )
+    hidden, pre_grad, pair = lax.optimization_barrier((hidden, pre_grad, pair))
     fields = kernel(
         functools.partial(outer_kernel, band, step),
         [vmem] * 3 + [hbm] * 2,
@@ -427,17 +440,26 @@
     )
     terms = kernel(
         functools.partial(far_kernel, band, step),
-        [vmem] * 5,
-        (near,) + far,
-        shaped(8, height, channels),
-        [held(3 * half, 2 * cells), held(3, half, 2 * cells), held(*sums.shape, kind=F32)],
+        [smem] + [vmem] * 5,
+        (place, near) + far,
+        (pltpu.HBM((height, channels), BF16),) * 8,
+        [
+            held(3 * half, 2 * cells),
+            held(3, half, 2 * cells),
+            held(*sums.shape, kind=F32),
+            held(8, height, channels),
+            pltpu.SemaphoreType.DMA((8,)),
+        ],
         flops,
         4,
-    )
-    terms = lax.all_to_all(terms, line, 0, 0, tiled=True)
+        (hbm,) * 8,
+    )
+    parts = list(terms)
+    for away in (6, 7, 4, 5, 2, 3, 1):
+        parts[away] = lax.ppermute(terms[away], ("z", "core"), [(i, i ^ away) for i in range(8)])
     grad = shaped(3, 3, deep, half // 2, kind=F32)
     conv1_grad, conv2_grad = kernel(
-        functools.partial(finish_kernel, scale), [vmem], (terms,), (grad, grad), [], 10**6, 2
+        functools.partial(finish_kernel, scale), [smem] + [vmem] * 8, (place, *parts), (grad, grad), [], 10**6, 2
     )
     return (output, input_grad, conv1_grad, conv2_grad)
 

time: 114 us -> 116 us (1.018); the launches traced: 114 us -> 114 us
  waiting for transfers between devices: 61.4 us -> 54.6 us
  starting transfers between devices: 26.1 us -> 29.6 us
  local copies, waits for them, and re-layouts: 0.08 us -> 2.71 us
    all_to_all x1 -> x0, waiting for transfers between devices: 17.4 us -> none  [fast_local(): terms = lax.all_to_all(terms, line, 0, 0, tiled=True)]
    ppermute x0 -> x7, waiting for transfers between devices: none -> 9.31 us  [fast_local(): lax.ppermute(terms[away], ('z', 'core'), [(i, i ^ away) for i in range(8)])]
    ppermute x0 -> x7, starting transfers between devices: none -> 8.12 us  [fast_local(): lax.ppermute(terms[away], ('z', 'core'), [(i, i ^ away) for i in range(8)])]
    all_to_all x1 -> x0, starting transfers between devices: 4.7 us -> none  [fast_local(): terms = lax.all_to_all(terms, line, 0, 0, tiled=True)]
    unnamed x12 -> x10, local copies, waits for them, and re-layouts: 0.03 us -> 2.65 us
    ppermute x9, waiting for transfers between devices: 23.4 us -> 24.8 us  [passed(): return lax.ppermute(piece, ('y', 'x', 'core'), pairs)]
  transfers between devices with their start and end apart: 12 -> 18, of which waited for: 6 -> 9; matrix products, arithmetic and copies ran while one was open for 0% -> 0% of each run, Pallas kernels for 13% -> 13%
where the time goes in v6:
time: 116 us; the launch traced here: 114 us
  waiting for transfers between devices  54.6 us (47%)
  starting transfers between devices  29.6 us (26%)
  Pallas kernels  26.3 us (23%)
  local copies, waits for them, and re-layouts  2.71 us (2%)
    pallas_call x7, Pallas kernels, kernel(): pl.pallas_call(body, out_shape=out_shape, in_specs=specs, out_specs=out_s...  26.3 us
    ppermute x9, waiting for transfers between devices, passed(): return lax.ppermute(piece, ('y', 'x', 'core'), pairs)  24.8 us
    all_to_all x1, waiting for transfers between devices, fast_local(): own = lax.all_to_all(own, every, 0, 0, tiled=True)  20.5 us
    ppermute x9, starting transfers between devices, passed(): return lax.ppermute(piece, ('y', 'x', 'core'), pairs)  10.3 us
    ppermute x7, waiting for transfers between devices, fast_local(): lax.ppermute(terms[away], ('z', 'core'), [(i, i ^ away) for i in range(8)])  9.31 us
    ppermute x7, starting transfers between devices, fast_local(): lax.ppermute(terms[away], ('z', 'core'), [(i, i ^ away) for i in range(8)])  8.12 us
    all_to_all x1, starting transfers between devices, fast_local(): own = lax.all_to_all(own, every, 0, 0, tiled=True)  7.3 us
    all_to_all x1, starting transfers between devices, fast_local(): fields = lax.all_to_all(fields, every, 0, 0, tiled=True)  3.81 us
  transfers between devices with their start and end apart: 18, of which 9 were waited for; matrix products, arithmetic and copies ran while one was open for 0% of the time, Pallas kernels for 13%

profile of v6, /device:TPU:0, one launch (start us, length us, event | category | flops | bytes accessed | tf_op | source)
XLA Modules:
  0.0 114.0 jit_solution(5777274025877365934)
XLA Ops:
  0.6 2.8 %shard_map.75 = bf16[32,2,16,384]{3,2,1,0:T(8,128)(2,1)} custom-call(bf16[8,64,384]{2,1,0:T(8,128)(2,1)} %inputs_ref.1, bf16[8,64,384]{2,1,0:T(8,128)(2,1)} %cot_ref.1), custom_call_target="tpu_custom_call" | custom-call | flops 1000000000 | bytes 3145728 | tf_op jit(solution)/shard_map/pallas_call | solution.py:360
  3.4 7.3 %all-to-all-start = ((bf16[32,2,16,384]{3,2,1,0:T(8,128)(2,1)}), bf16[32,2,16,384]{3,2,1,0:T(8,128)(2,1)S(1)}, u32[]{:S(2)}, u32[]{:S(2)}) async-start(bf16[32,2,16,384]{3,2,1,0:T(8,128)(2,1)} %shard_map.75), calls=%async_computation | async-start | bytes 1572864 | tf_op jit(solution)/shard_map/all_to_all | solution.py:386
  10.8 20.5 %all-to-all-done.own_ref = bf16[32,2,16,384]{3,2,1,0:T(8,128)(2,1)S(1)} async-done(((bf16[32,2,16,384]{3,2,1,0:T(8,128)(2,1)}), bf16[32,2,16,384]{3,2,1,0:T(8,128)(2,1)S(1)}, u32[]{:S(2)}, u32[]{:S(2)}) %all-to-all-start) | async-done | bytes 786464 | tf_op jit(solution)/shard_map/all_to_all | solution.py:386
  31.4 1.7 %copy-done.1 = bf16[3,3,384,384]{3,2,1,0:T(8,128)(2,1)S(1)} copy-done((bf16[3,3,384,384]{3,2,1,0:T(8,128)(2,1)S(1)}, bf16[3,3,384,384]{3,2,1,0:T(8,128)(2,1)}, u32[]{:S(2)}) %copy-start.1) | copy-done | bytes 2654232
  33.1 7.2 %shard_map.76 = (bf16[512,384]{1,0:T(8,128)(2,1)S(1)}, bf16[512,384]{1,0:T(8,128)(2,1)S(1)}, bf16[2,192,512]{2,1,0:T(8,128)(2,1)}, bf16[2,192,512]{2,1,0:T(8,128...) custom-call(s32[4]{0:T(128)S(1)} %pad_add_fusion.place_ref, ...), custom_call_target="tpu_custom_call" | custom-call | flops 2717908992 | bytes 10485760 | tf_op jit(solution)/shard_map/pallas_call | solution.py:360
  40.4 1.6 %collective-permute-start.3 = (bf16[2,192,512]{2,1,0:T(8,128)(2,1)}, bf16[2,192,512]{2,1,0:T(8,128)(2,1)S(1)}, u32[]{:S(2)}, u32[]{:S(2)}) collective-permute-start(bf16[2,192,512]{2,1,0:T(8,128)(2,1)} %get-tuple-element.38), channel_id=1, source_target_pairs={{0,4},{1,5},{2,6},{3,7},{4,0},{5,1},{6,2},{7,3},{8,12},{9,13},{10,... | collective-permute-start | bytes 1179656 | tf_op jit(solution)/shard_map/ppermute | solution.py:372
  42.3 7.3 %shard_map.77 = bf16[32,2,16,384]{3,2,1,0:T(8,128)(2,1)} custom-call(bf16[32,2,16,384]{3,2,1,0:T(8,128)(2,1)S(1)} %all-to-all-done.own_ref, bf16[512,384]{1,0:T(8,128)(2,1)S(1)} %get-tuple-element.30.hidden_ref, bf16[512,384]{1,0:T(8,128)(2,1)S(1)} %get-tuple-element.31.pre_ref, bf16[3,3,384,384]{3,2,1,0:T(8,128)(2,1)} %one_ref.3, ...), custom_call_target="tpu_custom_call" | custom-call | flops 2717908992 | bytes 9437184 | tf_op jit(solution)/shard_map/pallas_call | solution.py:360
  49.7 3.8 %all-to-all-start.1 = ((bf16[32,2,16,384]{3,2,1,0:T(8,128)(2,1)}), bf16[32,2,16,384]{3,2,1,0:T(8,128)(2,1)S(1)}, u32[]{:S(2)}, u32[]{:S(2)}) async-start(bf16[32,2,16,384]{3,2,1,0:T(8,128)(2,1)} %shard_map.77), calls=%async_computation.1 | async-start | bytes 1572864 | tf_op jit(solution)/shard_map/all_to_all | solution.py:427
  53.5 1.7 %collective-permute-start.1 = (bf16[2,192,512]{2,1,0:T(8,128)(2,1)S(1)}, bf16[2,192,512]{2,1,0:T(8,128)(2,1)S(1)}, u32[]{:S(2)}, u32[]{:S(2)}) collective-permute-start(bf16[2,192,512]{2,1,0:T(8,128)(2,1)S(1)} %copy-done.4), channel_id=1, source_target_pairs={{0,2},{1,3},{2,0},{3,1},{4,6},{5,7},{6,4},{7,5},{8,10},{9,11},{10,... | collective-permute-start | bytes 1179656 | tf_op jit(solution)/shard_map/ppermute | solution.py:372
  55.2 1.6 %collective-permute-start.5 = (bf16[192,512]{1,0:T(8,128)(2,1)S(1)}, bf16[192,512]{1,0:T(8,128)(2,1)S(1)}, u32[]{:S(2)}, u32[]{:S(2)}) collective-permute-start(bf16[192,512]{1,0:T(8,128)(2,1)S(1)} %slice_bitcast_fusion.3), channel_id=1, source_target_pairs={{0,2},{1,3},{2,0},{3,1},{4,6},{5,7},{6,4},{7,5},{8,10},{9,11},{10,... | collective-permute-start | bytes 589832 | tf_op jit(solution)/shard_map/ppermute | solution.py:372
  56.7 8.7 %collective-permute-done.4.refs_5_ = bf16[2,192,512]{2,1,0:T(8,128)(2,1)S(1)} collective-permute-done((bf16[2,192,512]{2,1,0:T(8,128)(2,1)}, bf16[2,192,512]{2,1,0:T(8,128)(2,1)S(1)}, u32[]{:S(2)}, u32[]{:S(2)}) %collective-permute-start.4) | collective-permute-done | bytes 393248 | tf_op jit(solution)/shard_map/ppermute | solution.py:372
  65.4 1.9 %collective-permute-start.6 = (bf16[192,512]{1,0:T(8,128)(2,1)S(1)}, bf16[192,512]{1,0:T(8,128)(2,1)S(1)}, u32[]{:S(2)}, u32[]{:S(2)}) collective-permute-start(bf16[192,512]{1,0:T(8,128)(2,1)S(1)} %slice_bitcast_fusion.2), channel_id=1, source_target_pairs={{0,2},{1,3},{2,0},{3,1},{4,6},{5,7},{6,4},{7,5},{8,10},{9,11},{10,... | collective-permute-start | bytes 589832 | tf_op jit(solution)/shard_map/ppermute | solution.py:372
  67.3 5.9 %collective-permute-done.1.refs_2_ = bf16[2,192,512]{2,1,0:T(8,128)(2,1)S(1)} collective-permute-done((bf16[2,192,512]{2,1,0:T(8,128)(2,1)S(1)}, bf16[2,192,512]{2,1,0:T(8,128)(2,1)S(1)}, u32[]{:S(2)}, u32[]{:S(2)}) %collective-permute-start.1) | collective-permute-done | bytes 393248 | tf_op jit(solution)/shard_map/ppermute | solution.py:372
  73.3 1.8 %collective-permute-start.7 = (bf16[192,512]{1,0:T(8,128)(2,1)S(1)}, bf16[192,512]{1,0:T(8,128)(2,1)S(1)}, u32[]{:S(2)}, u32[]{:S(2)}) collective-permute-start(bf16[192,512]{1,0:T(8,128)(2,1)S(1)} %slice_bitcast_fusion.1), channel_id=1, source_target_pairs={{0,4},{1,5},{2,6},{3,7},{4,0},{5,1},{6,2},{7,3},{8,12},{9,13},{10,... | collective-permute-start | bytes 589832 | tf_op jit(solution)/shard_map/ppermute | solution.py:372
  75.0 5.9 %collective-permute-done.2.refs_3_ = bf16[2,192,512]{2,1,0:T(8,128)(2,1)S(1)} collective-permute-done((bf16[2,192,512]{2,1,0:T(8,128)(2,1)S(1)}, bf16[2,192,512]{2,1,0:T(8,128)(2,1)S(1)}, u32[]{:S(2)}, u32[]{:S(2)}) %collective-permute-start.2) | collective-permute-done | bytes 393248 | tf_op jit(solution)/shard_map/ppermute | solution.py:372
  81.0 1.5 %collective-permute-start.8 = (bf16[192,512]{1,0:T(8,128)(2,1)S(1)}, bf16[192,512]{1,0:T(8,128)(2,1)S(1)}, u32[]{:S(2)}, u32[]{:S(2)}) collective-permute-start(bf16[192,512]{1,0:T(8,128)(2,1)S(1)} %slice_bitcast_fusion), channel_id=1, source_target_pairs={{0,4},{1,5},{2,6},{3,7},{4,0},{5,1},{6,2},{7,3},{8,12},{9,13},{10,... | collective-permute-start | bytes 589832 | tf_op jit(solution)/shard_map/ppermute | solution.py:372
  82.5 3.2 %shard_map.79.near_ref = f32[3,576,192]{2,1,0:T(8,128)S(1)} custom-call(bf16[2,192,512]{2,1,0:T(8,128)(2,1)S(1)} %copy-done.2, bf16[2,192,512]{2,1,0:T(8,128)(2,1)S(1)} %collective-permute-done.refs_1_, bf16[2,192,512]{2,1,0:T(8,128)(2,1)S(1)} %collective-permute-done.1.refs_2_, bf16[2,192,512]{2,1,0:T(8,128)(2,1)S(1)} %collective-permute-done.2.refs_3_, ...), custom_call_target="tpu_custom_call" | custom-call | flops 2717908992 | bytes 6291456 | tf_op jit(solution)/shard_map/pallas_call | solution.py:360
  86.1 3.7 %collective-permute-done.6.refs_1_ = bf16[192,512]{1,0:T(8,128)(2,1)S(1)} collective-permute-done((bf16[192,512]{1,0:T(8,128)(2,1)S(1)}, bf16[192,512]{1,0:T(8,128)(2,1)S(1)}, u32[]{:S(2)}, u32[]{:S(2)}) %collective-permute-start.6) | collective-permute-done | bytes 196640 | tf_op jit(solution)/shard_map/ppermute | solution.py:372
  89.9 2.9 %shard_map.80 = (bf16[112,384]{1,0:T(8,128)(2,1)}, bf16[112,384]{1,0:T(8,128)(2,1)}, bf16[112,384]{1,0:T(8,128)(2,1)}, bf16[112,384]{1,0:T(8,128)(2,1)}, bf16[11...) custom-call(s32[4]{0:T(128)S(1)} %pad_add_fusion.place_ref, ...), custom_call_target="tpu_custom_call" | custom-call | flops 1358954496 | bytes 4194304 | tf_op jit(solution)/shard_map/pallas_call | solution.py:360
  92.8 1.5 %collective-permute-start.10 = (bf16[112,384]{1,0:T(8,128)(2,1)}, bf16[112,384]{1,0:T(8,128)(2,1)S(1)}, u32[]{:S(2)}, u32[]{:S(2)}) collective-permute-start(bf16[112,384]{1,0:T(8,128)(2,1)} %get-tuple-element.42), channel_id=1, source_target_pairs={{0,8},{1,9},{8,0},{9,1},{16,24},{17,25},{24,16},{25,17},{2,10},{3,... | collective-permute-start | bytes 258056 | tf_op jit(solution)/shard_map/ppermute | solution.py:459
  94.7 2.4 %collective-permute-start.12 = (bf16[112,384]{1,0:T(8,128)(2,1)}, bf16[112,384]{1,0:T(8,128)(2,1)S(1)}, u32[]{:S(2)}, u32[]{:S(2)}) collective-permute-start(bf16[112,384]{1,0:T(8,128)(2,1)} %get-tuple-element.44), channel_id=1, source_target_pairs={{0,16},{1,17},{8,24},{9,25},{16,0},{17,1},{24,8},{25,9},{2,18},{3,... | collective-permute-start | bytes 258056 | tf_op jit(solution)/shard_map/ppermute | solution.py:459
  97.3 3.3 %collective-permute-start.14 = (bf16[112,384]{1,0:T(8,128)(2,1)}, bf16[112,384]{1,0:T(8,128)(2,1)S(1)}, u32[]{:S(2)}, u32[]{:S(2)}) collective-permute-start(bf16[112,384]{1,0:T(8,128)(2,1)} %get-tuple-element.46), channel_id=1, source_target_pairs={{0,24},{1,25},{8,16},{9,17},{16,8},{17,9},{24,0},{25,1},{2,26},{3,... | collective-permute-start | bytes 258056 | tf_op jit(solution)/shard_map/ppermute | solution.py:459
  101.2 8.9 %collective-permute-done.13.refs_5_ = bf16[112,384]{1,0:T(8,128)(2,1)S(1)} collective-permute-done((bf16[112,384]{1,0:T(8,128)(2,1)}, bf16[112,384]{1,0:T(8,128)(2,1)S(1)}, u32[]{:S(2)}, u32[]{:S(2)}) %collective-permute-start.13) | collective-permute-done | bytes 86048 | tf_op jit(solution)/shard_map/ppermute | solution.py:459
  111.1 1.5 %shard_map.81 = (f32[3,3,48,96]{3,2,1,0:T(8,128)}, f32[3,3,48,96]{3,2,1,0:T(8,128)}) custom-call(s32[4]{0:T(128)S(1)} %pad_add_fusion.place_ref, bf16[112,384]{1,0:T(8,128)(2,1)S(1)} %copy-done, bf16[112,384]{1,0:T(8,128)(2,1)S(1)} %collective-permute-done.9.refs_1_, bf16[112,384]{1,0:T(8,128)(2,1)S(1)} %collective-permute-done.10.refs_2_, ...), custom_call_target="tpu_custom_call" | custom-call | flops 1000000 | bytes 2097152 | tf_op jit(solution)/shard_map/pallas_call | solution.py:360
  (34 shorter events, 4.6 us)
Async XLA Ops:
  3.4 27.9 %all-to-all-start = ((bf16[32,2,16,384]{3,2,1,0:T(8,128)(2,1)}), bf16[32,2,16,384]{3,2,1,0:T(8,128)(2,1)S(1)}, u32[]{:S(2)}, u32[]{:S(2)}) async-start(bf16[32,2,16,384]{3,2,1,0:T(8,128)(2,1)} %shard_map.75), calls=%async_computation | async-start | bytes 1572864 | tf_op jit(solution)/shard_map/all_to_all | solution.py:386
  31.4 1.8 %copy-start.1 = (bf16[3,3,384,384]{3,2,1,0:T(8,128)(2,1)S(1)}, bf16[3,3,384,384]{3,2,1,0:T(8,128)(2,1)}, u32[]{:S(2)}) copy-start(bf16[3,3,384,384]{3,2,1,0:T(8,128)(2,1)} %one_ref.3) | copy-start | bytes 7962628
  40.3 2.0 %collective-permute-start = (bf16[2,192,512]{2,1,0:T(8,128)(2,1)}, bf16[2,192,512]{2,1,0:T(8,128)(2,1)S(1)}, u32[]{:S(2)}, u32[]{:S(2)}) collective-permute-start(bf16[2,192,512]{2,1,0:T(8,128)(2,1)} %get-tuple-element.29), channel_id=1, source_target_pairs={{0,1},{1,0},{2,3},{3,2},{4,5},{5,4},{6,7},{7,6},{8,9},{9,8},{10,11... | collective-permute-start | bytes 1179656 | tf_op jit(solution)/shard_map/ppermute | solution.py:372
  40.4 14.7 %collective-permute-start.3 = (bf16[2,192,512]{2,1,0:T(8,128)(2,1)}, bf16[2,192,512]{2,1,0:T(8,128)(2,1)S(1)}, u32[]{:S(2)}, u32[]{:S(2)}) collective-permute-start(bf16[2,192,512]{2,1,0:T(8,128)(2,1)} %get-tuple-element.38), channel_id=1, source_target_pairs={{0,4},{1,5},{2,6},{3,7},{4,0},{5,1},{6,2},{7,3},{8,12},{9,13},{10,... | collective-permute-start | bytes 1179656 | tf_op jit(solution)/shard_map/ppermute | solution.py:372
  42.0 23.4 %collective-permute-start.4 = (bf16[2,192,512]{2,1,0:T(8,128)(2,1)}, bf16[2,192,512]{2,1,0:T(8,128)(2,1)S(1)}, u32[]{:S(2)}, u32[]{:S(2)}) collective-permute-start(bf16[2,192,512]{2,1,0:T(8,128)(2,1)} %get-tuple-element.39), channel_id=1, source_target_pairs={{0,5},{1,4},{2,7},{3,6},{4,1},{5,0},{6,3},{7,2},{8,13},{9,12},{10,... | collective-permute-start | bytes 1179656 | tf_op jit(solution)/shard_map/ppermute | solution.py:372
  42.3 11.2 %copy-start.4 = (bf16[2,192,512]{2,1,0:T(8,128)(2,1)S(1)}, bf16[2,192,512]{2,1,0:T(8,128)(2,1)}, u32[]{:S(2)}) copy-start(bf16[2,192,512]{2,1,0:T(8,128)(2,1)} %get-tuple-element.36) | copy-start | bytes 1179652
  42.3 12.8 %copy-start.3 = (bf16[2,192,512]{2,1,0:T(8,128)(2,1)S(1)}, bf16[2,192,512]{2,1,0:T(8,128)(2,1)}, u32[]{:S(2)}) copy-start(bf16[2,192,512]{2,1,0:T(8,128)(2,1)} %get-tuple-element.37) | copy-start | bytes 1179652
  49.7 32.9 %copy-start.2 = (bf16[2,192,512]{2,1,0:T(8,128)(2,1)S(1)}, bf16[2,192,512]{2,1,0:T(8,128)(2,1)}, u32[]{:S(2)}) copy-start(bf16[2,192,512]{2,1,0:T(8,128)(2,1)} %get-tuple-element.34.refs_0_) | copy-start | bytes 1179652
  49.7 62.9 %all-to-all-start.1 = ((bf16[32,2,16,384]{3,2,1,0:T(8,128)(2,1)}), bf16[32,2,16,384]{3,2,1,0:T(8,128)(2,1)S(1)}, u32[]{:S(2)}, u32[]{:S(2)}) async-start(bf16[32,2,16,384]{3,2,1,0:T(8,128)(2,1)} %shard_map.77), calls=%async_computation.1 | async-start | bytes 1572864 | tf_op jit(solution)/shard_map/all_to_all | solution.py:427
  53.5 19.8 %collective-permute-start.1 = (bf16[2,192,512]{2,1,0:T(8,128)(2,1)S(1)}, bf16[2,192,512]{2,1,0:T(8,128)(2,1)S(1)}, u32[]{:S(2)}, u32[]{:S(2)}) collective-permute-start(bf16[2,192,512]{2,1,0:T(8,128)(2,1)S(1)} %copy-done.4), channel_id=1, source_target_pairs={{0,2},{1,3},{2,0},{3,1},{4,6},{5,7},{6,4},{7,5},{8,10},{9,11},{10,... | collective-permute-start | bytes 1179656 | tf_op jit(solution)/shard_map/ppermute | solution.py:372
  55.2 25.8 %collective-permute-start.2 = (bf16[2,192,512]{2,1,0:T(8,128)(2,1)S(1)}, bf16[2,192,512]{2,1,0:T(8,128)(2,1)S(1)}, u32[]{:S(2)}, u32[]{:S(2)}) collective-permute-start(bf16[2,192,512]{2,1,0:T(8,128)(2,1)S(1)} %copy-done.3), channel_id=1, source_target_pairs={{0,3},{1,2},{2,1},{3,0},{4,7},{5,6},{6,5},{7,4},{8,11},{9,10},{10,... | collective-permute-start | bytes 1179656 | tf_op jit(solution)/shard_map/ppermute | solution.py:372
  55.2 30.9 %collective-permute-start.5 = (bf16[192,512]{1,0:T(8,128)(2,1)S(1)}, bf16[192,512]{1,0:T(8,128)(2,1)S(1)}, u32[]{:S(2)}, u32[]{:S(2)}) collective-permute-start(bf16[192,512]{1,0:T(8,128)(2,1)S(1)} %slice_bitcast_fusion.3), channel_id=1, source_target_pairs={{0,2},{1,3},{2,0},{3,1},{4,6},{5,7},{6,4},{7,5},{8,10},{9,11},{10,... | collective-permute-start | bytes 589832 | tf_op jit(solution)/shard_map/ppermute | solution.py:372
  65.4 24.4 %collective-permute-start.6 = (bf16[192,512]{1,0:T(8,128)(2,1)S(1)}, bf16[192,512]{1,0:T(8,128)(2,1)S(1)}, u32[]{:S(2)}, u32[]{:S(2)}) collective-permute-start(bf16[192,512]{1,0:T(8,128)(2,1)S(1)} %slice_bitcast_fusion.2), channel_id=1, source_target_pairs={{0,2},{1,3},{2,0},{3,1},{4,6},{5,7},{6,4},{7,5},{8,10},{9,11},{10,... | collective-permute-start | bytes 589832 | tf_op jit(solution)/shard_map/ppermute | solution.py:372
  73.3 16.6 %collective-permute-start.7 = (bf16[192,512]{1,0:T(8,128)(2,1)S(1)}, bf16[192,512]{1,0:T(8,128)(2,1)S(1)}, u32[]{:S(2)}, u32[]{:S(2)}) collective-permute-start(bf16[192,512]{1,0:T(8,128)(2,1)S(1)} %slice_bitcast_fusion.1), channel_id=1, source_target_pairs={{0,4},{1,5},{2,6},{3,7},{4,0},{5,1},{6,2},{7,3},{8,12},{9,13},{10,... | collective-permute-start | bytes 589832 | tf_op jit(solution)/shard_map/ppermute | solution.py:372
  81.0 8.9 %collective-permute-start.8 = (bf16[192,512]{1,0:T(8,128)(2,1)S(1)}, bf16[192,512]{1,0:T(8,128)(2,1)S(1)}, u32[]{:S(2)}, u32[]{:S(2)}) collective-permute-start(bf16[192,512]{1,0:T(8,128)(2,1)S(1)} %slice_bitcast_fusion), channel_id=1, source_target_pairs={{0,4},{1,5},{2,6},{3,7},{4,0},{5,1},{6,2},{7,3},{8,12},{9,13},{10,... | collective-permute-start | bytes 589832 | tf_op jit(solution)/shard_map/ppermute | solution.py:372
  92.7 4.5 %collective-permute-start.9 = (bf16[112,384]{1,0:T(8,128)(2,1)}, bf16[112,384]{1,0:T(8,128)(2,1)S(1)}, u32[]{:S(2)}, u32[]{:S(2)}) collective-permute-start(bf16[112,384]{1,0:T(8,128)(2,1)} %get-tuple-element.41), channel_id=1, source_target_pairs={{0,1},{1,0},{8,9},{9,8},{16,17},{17,16},{24,25},{25,24},{2,3},{3,2... | collective-permute-start | bytes 258056 | tf_op jit(solution)/shard_map/ppermute | solution.py:459
  92.8 7.8 %collective-permute-start.10 = (bf16[112,384]{1,0:T(8,128)(2,1)}, bf16[112,384]{1,0:T(8,128)(2,1)S(1)}, u32[]{:S(2)}, u32[]{:S(2)}) collective-permute-start(bf16[112,384]{1,0:T(8,128)(2,1)} %get-tuple-element.42), channel_id=1, source_target_pairs={{0,8},{1,9},{8,0},{9,1},{16,24},{17,25},{24,16},{25,17},{2,10},{3,... | collective-permute-start | bytes 258056 | tf_op jit(solution)/shard_map/ppermute | solution.py:459
  94.3 6.9 %collective-permute-start.11 = (bf16[112,384]{1,0:T(8,128)(2,1)}, bf16[112,384]{1,0:T(8,128)(2,1)S(1)}, u32[]{:S(2)}, u32[]{:S(2)}) collective-permute-start(bf16[112,384]{1,0:T(8,128)(2,1)} %get-tuple-element.43), channel_id=1, source_target_pairs={{0,9},{1,8},{8,1},{9,0},{16,25},{17,24},{24,17},{25,16},{2,11},{3,... | collective-permute-start | bytes 258056 | tf_op jit(solution)/shard_map/ppermute | solution.py:459
  94.7 6.6 %collective-permute-start.12 = (bf16[112,384]{1,0:T(8,128)(2,1)}, bf16[112,384]{1,0:T(8,128)(2,1)S(1)}, u32[]{:S(2)}, u32[]{:S(2)}) collective-permute-start(bf16[112,384]{1,0:T(8,128)(2,1)} %get-tuple-element.44), channel_id=1, source_target_pairs={{0,16},{1,17},{8,24},{9,25},{16,0},{17,1},{24,8},{25,9},{2,18},{3,... | collective-permute-start | bytes 258056 | tf_op jit(solution)/shard_map/ppermute | solution.py:459
  97.0 13.1 %collective-permute-start.13 = (bf16[112,384]{1,0:T(8,128)(2,1)}, bf16[112,384]{1,0:T(8,128)(2,1)S(1)}, u32[]{:S(2)}, u32[]{:S(2)}) collective-permute-start(bf16[112,384]{1,0:T(8,128)(2,1)} %get-tuple-element.45), channel_id=1, source_target_pairs={{0,17},{1,16},{8,25},{9,24},{16,1},{17,0},{24,9},{25,8},{2,19},{3,... | collective-permute-start | bytes 258056 | tf_op jit(solution)/shard_map/ppermute | solution.py:459
  97.3 12.9 %collective-permute-start.14 = (bf16[112,384]{1,0:T(8,128)(2,1)}, bf16[112,384]{1,0:T(8,128)(2,1)S(1)}, u32[]{:S(2)}, u32[]{:S(2)}) collective-permute-start(bf16[112,384]{1,0:T(8,128)(2,1)} %get-tuple-element.46), channel_id=1, source_target_pairs={{0,24},{1,25},{8,16},{9,17},{16,8},{17,9},{24,0},{25,1},{2,26},{3,... | collective-permute-start | bytes 258056 | tf_op jit(solution)/shard_map/ppermute | solution.py:459
  100.6 9.6 %collective-permute-start.15 = (bf16[112,384]{1,0:T(8,128)(2,1)}, bf16[112,384]{1,0:T(8,128)(2,1)S(1)}, u32[]{:S(2)}, u32[]{:S(2)}) collective-permute-start(bf16[112,384]{1,0:T(8,128)(2,1)} %get-tuple-element.47), channel_id=1, source_target_pairs={{0,25},{1,24},{8,17},{9,16},{16,9},{17,8},{24,1},{25,0},{2,27},{3,... | collective-permute-start | bytes 258056 | tf_op jit(solution)/shard_map/ppermute | solution.py:459
  110.2 0.9 copy-start

commit v7 on v6

--- a/solution.py
+++ b/solution.py
@@ -123,9 +123,11 @@
         stack_ref[band + cells :, columns] = part[0:band]
 
 
-def convolved(stack_ref, weight_ref, band, cells):
+def convolved(stack_ref, weight_ref, band, cells, fetch=None):
     total = None
     for b in range(3):
+        if fetch is not None:
+            fetch[b].wait()
         channels = weight_ref.shape[2]
         tap = weight_ref[:, b].reshape(3 * channels, channels)
         term = jnp.dot(stack_ref[b * band : b * band + cells, :], tap, preferred_element_type=F32)
@@ -185,11 +187,11 @@
 
 def inner_kernel(band, step, place_ref, own_ref, one_ref, two_ref,
                  hidden_ref, pre_ref, kept_ref, pair_ref, x_same_ref, x_cross_ref, y_same_ref, y_cross_ref,
-                 two_held, stack_ref, first_ref, slope_ref, turned_ref, sems, out_sems):
+                 one_held, two_held, stack_ref, first_ref, slope_ref, turned_ref, sems, out_sems):
     x, y, core = place_ref[0], place_ref[1], place_ref[2]
     other = 1 - core
     cells, channels = first_ref.shape
-    fetch = fetched(((two_ref, two_held),), sems)[0]
+    fetch = fetched([(one_ref.at[:, b], one_held.at[:, b]) for b in range(3)] + [(two_ref, two_held)], sems)
     half, rows = channels // 2, 32
     deep = half // 4
 
@@ -206,7 +208,7 @@
 
     source = own_ref[:, 0].reshape(cells, channels)
     write_stack(source, stack_ref, band, step)
-    first_ref[...] = convolved(stack_ref, one_ref, band, cells)
+    first_ref[...] = convolved(stack_ref, one_held, band, cells, fetch)
     turn(0, source)
 
     def activate(at, carry):
@@ -227,7 +229,7 @@
     cot = own_ref[:, 1].reshape(cells, channels)
     write_stack(cot, stack_ref, band, step)
     turn(3, cot)
-    fetch.wait()
+    fetch[3].wait()
     pre_ref[...] = (slope_ref[...] * convolved_back(stack_ref, two_held, band, cells)).astype(BF16)
     turn(2, pre_ref[...])
     copies += sent(1, (
@@ -356,12 +358,12 @@
     def shaped(*shape, kind=BF16):
         return jax.ShapeDtypeStruct(shape, kind)
 
-    def kernel(body, specs, arguments, out_shape, scratch_shapes, work, megabytes, out_specs=None):
+    def kernel(body, specs, arguments, out_shape, scratch_shapes, work, megabytes):
         return pl.pallas_call(
             body,
             out_shape=out_shape,
             in_specs=specs,
-            out_specs=out_specs or jax.tree.map(lambda _: vmem, out_shape),
+            out_specs=jax.tree.map(lambda _: vmem, out_shape),
             scratch_shapes=scratch_shapes,
             compiler_params=pltpu.CompilerParams(vmem_limit_bytes=20 * 2**20),
             cost_estimate=pl.CostEstimate(flops=work, bytes_accessed=megabytes * 2**20, transcendentals=0),
@@ -385,35 +387,29 @@
     )
     own = lax.all_to_all(own, every, 0, 0, tiled=True)
     place = jnp.stack([lax.axis_index(axis) for axis in ("x", "y", "core", "z")]).astype(jnp.int32)
-    piece = pltpu.HBM((2, half, cells), BF16)
+    piece = pltpu.VMEM((2, half, cells), BF16)
     one_far, two_far = (pltpu.with_memory_space_constraint(w, pltpu.HBM) for w in (conv1_weight, conv2_weight))
     hidden, pre_grad, kept, pair, x_same, x_cross, y_same, y_cross = kernel(
         functools.partial(inner_kernel, band, step),
-        [smem, vmem, vmem, hbm],
-        (place, own, conv1_weight, two_far),
+        [smem, vmem, hbm, hbm],
+        (place, own, one_far, two_far),
         (shaped(cells, channels),) * 2 + (piece,) * 6,
         [
+            weights,
             weights,
             stack,
             held(cells, channels, kind=F32),
             held(cells, channels, kind=F32),
             held(8, half, cells),
-            pltpu.SemaphoreType.DMA((1,)),
+            pltpu.SemaphoreType.DMA((4,)),
             pltpu.SemaphoreType.DMA((2, 6)),
         ],
         2 * flops,
         10,
-        (vmem,) * 2 + (hbm,) * 6,
     )
     y_same, x_same = passed(y_same, 0, 1, 0), passed(x_same, 1, 0, 0)
     y_cross, x_cross = passed(y_cross, 0, 1, 1), passed(x_cross, 1, 0, 1)
     pair = passed(pair, 0, 0, 1)
-    far = (
-        passed(y_same[0], 1, 0, 0),
-        passed(y_cross[0], 1, 0, 0),
-        passed(x_same[1], 0, 1, 0),
-        passed(x_cross[1], 0, 1, 0),
-    )
     hidden, pre_grad, pair = lax.optimization_barrier((hidden, pre_grad, pair))
     fields = kernel(
         functools.partial(outer_kernel, band, step),
@@ -424,6 +420,13 @@
         2 * flops,
         9,
     )
+    fields, y_same, x_same = lax.optimization_barrier((fields, y_same, x_same))
+    far = (
+        passed(y_same[0], 1, 0, 0),
+        passed(y_cross[0], 1, 0, 0),
+        passed(x_same[1], 0, 1, 0),
+        passed(x_cross[1], 0, 1, 0),
+    )
     fields = lax.all_to_all(fields, every, 0, 0, tiled=True)
     output, input_grad = kernel(
         functools.partial(gather_kernel, step), [vmem], (fields,), (shaped(*inputs.shape),) * 2, [], 10**9, 3
@@ -442,7 +445,7 @@
         functools.partial(far_kernel, band, step),
         [smem] + [vmem] * 5,
         (place, near) + far,
-        (pltpu.HBM((height, channels), BF16),) * 8,
+        (pltpu.VMEM((height, channels), BF16),) * 8,
         [
             held(3 * half, 2 * cells),
             held(3, half, 2 * cells),
@@ -452,11 +455,11 @@
         ],
         flops,
         4,
-        (hbm,) * 8,
     )
     parts = list(terms)
     for away in (6, 7, 4, 5, 2, 3, 1):
         parts[away] = lax.ppermute(terms[away], ("z", "core"), [(i, i ^ away) for i in range(8)])
+    output, input_grad, parts = lax.optimization_barrier((output, input_grad, parts))
     grad = shaped(3, 3, deep, half // 2, kind=F32)
     conv1_grad, conv2_grad = kernel(
         functools.partial(finish_kernel, scale), [smem] + [vmem] * 8, (place, *parts), (grad, grad), [], 10**6, 2

time: 116 us -> 110 us (0.948)
  waiting for transfers between devices: 54.6 us -> 47.7 us
  Pallas kernels: 26.3 us -> 29.8 us
  local copies, waits for them, and re-layouts: 2.71 us -> 0.05 us
    ppermute x9, waiting for transfers between devices: 24.8 us -> 19.5 us  [passed(): return lax.ppermute(piece, ('y', 'x', 'core'), pairs)]
    pallas_call x7, Pallas kernels: 26.3 us -> 29.8 us  [kernel(): pl.pallas_call(body, out_shape=out_shape, in_specs=specs, out_specs=jax.t...]
    unnamed x10 -> x0, local copies, waits for them, and re-layouts: 2.65 us -> none
    ppermute x7, waiting for transfers between devices: 9.31 us -> 7.65 us  [fast_local(): lax.ppermute(terms[away], ('z', 'core'), [(i, i ^ away) for i in range(8)])]
  transfers between devices with their start and end apart: 18 -> 18, of which waited for: 9 -> 8; matrix products, arithmetic and copies ran while one was open for 0% -> 0% of each run, Pallas kernels for 13% -> 14%
where the time goes in v7:
time: 110 us; the launch traced here: 108 us
  waiting for transfers between devices  47.7 us (43%)
  Pallas kernels  29.8 us (27%)
  starting transfers between devices  29.2 us (27%)
    pallas_call x7, Pallas kernels, kernel(): pl.pallas_call(body, out_shape=out_shape, in_specs=specs, out_specs=jax.t...  29.8 us
    all_to_all x1, waiting for transfers between devices, fast_local(): own = lax.all_to_all(own, every, 0, 0, tiled=True)  20.5 us
    ppermute x9, waiting for transfers between devices, passed(): return lax.ppermute(piece, ('y', 'x', 'core'), pairs)  19.5 us
    ppermute x9, starting transfers between devices, passed(): return lax.ppermute(piece, ('y', 'x', 'core'), pairs)  10.8 us
    ppermute x7, starting transfers between devices, fast_local(): lax.ppermute(terms[away], ('z', 'core'), [(i, i ^ away) for i in range(8)])  8.12 us
    ppermute x7, waiting for transfers between devices, fast_local(): lax.ppermute(terms[away], ('z', 'core'), [(i, i ^ away) for i in range(8)])  7.65 us
    all_to_all x1, starting transfers between devices, fast_local(): own = lax.all_to_all(own, every, 0, 0, tiled=True)  7.3 us
    all_to_all x1, starting transfers between devices, fast_local(): fields = lax.all_to_all(fields, every, 0, 0, tiled=True)  3.01 us
  transfers between devices with their start and end apart: 18, of which 8 were waited for; matrix products, arithmetic and copies ran while one was open for 0% of the time, Pallas kernels for 14%

profile of v7, /device:TPU:0, one launch (start us, length us, event | category | flops | bytes accessed | tf_op | source)
XLA Modules:
  0.0 107.7 jit_solution(7518306132473981373)
XLA Ops:
  0.6 2.8 %shard_map.75 = bf16[32,2,16,384]{3,2,1,0:T(8,128)(2,1)} custom-call(bf16[8,64,384]{2,1,0:T(8,128)(2,1)} %inputs_ref.1, bf16[8,64,384]{2,1,0:T(8,128)(2,1)} %cot_ref.1), custom_call_target="tpu_custom_call" | custom-call | flops 1000000000 | bytes 3145728 | tf_op jit(solution)/shard_map/pallas_call | solution.py:362
  3.4 7.3 %all-to-all-start = ((bf16[32,2,16,384]{3,2,1,0:T(8,128)(2,1)}), bf16[32,2,16,384]{3,2,1,0:T(8,128)(2,1)S(1)}, u32[]{:S(2)}, u32[]{:S(2)}) async-start(bf16[32,2,16,384]{3,2,1,0:T(8,128)(2,1)} %shard_map.75), calls=%async_computation | async-start | bytes 1572864 | tf_op jit(solution)/shard_map/all_to_all | solution.py:388
  10.8 20.5 %all-to-all-done.own_ref = bf16[32,2,16,384]{3,2,1,0:T(8,128)(2,1)S(1)} async-done(((bf16[32,2,16,384]{3,2,1,0:T(8,128)(2,1)}), bf16[32,2,16,384]{3,2,1,0:T(8,128)(2,1)S(1)}, u32[]{:S(2)}, u32[]{:S(2)}) %all-to-all-start) | async-done | bytes 786464 | tf_op jit(solution)/shard_map/all_to_all | solution.py:388
  31.3 10.8 %shard_map.76 = (bf16[512,384]{1,0:T(8,128)(2,1)S(1)}, bf16[512,384]{1,0:T(8,128)(2,1)S(1)}, bf16[2,192,512]{2,1,0:T(8,128)(2,1)S(1)}, bf16[2,192,512]{2,1,0:T(8...) custom-call(s32[4]{0:T(128)S(1)} %pad_add_fusion.place_ref, ...), custom_call_target="tpu_custom_call" | custom-call | flops 2717908992 | bytes 10485760 | tf_op jit(solution)/shard_map/pallas_call | solution.py:362
  42.2 1.6 %collective-permute-start.1 = (bf16[2,192,512]{2,1,0:T(8,128)(2,1)S(1)}, bf16[2,192,512]{2,1,0:T(8,128)(2,1)S(1)}, u32[]{:S(2)}, u32[]{:S(2)}) collective-permute-start(bf16[2,192,512]{2,1,0:T(8,128)(2,1)S(1)} %get-tuple-element.45), channel_id=1, source_target_pairs={{0,4},{1,5},{2,6},{3,7},{4,0},{5,1},{6,2},{7,3},{8,12},{9,13},{10,... | collective-permute-start | bytes 1179656 | tf_op jit(solution)/shard_map/ppermute | solution.py:374
  43.8 1.4 %collective-permute-start.2 = (bf16[2,192,512]{2,1,0:T(8,128)(2,1)S(1)}, bf16[2,192,512]{2,1,0:T(8,128)(2,1)S(1)}, u32[]{:S(2)}, u32[]{:S(2)}) collective-permute-start(bf16[2,192,512]{2,1,0:T(8,128)(2,1)S(1)} %get-tuple-element.46), channel_id=1, source_target_pairs={{0,2},{1,3},{2,0},{3,1},{4,6},{5,7},{6,4},{7,5},{8,10},{9,11},{10,... | collective-permute-start | bytes 1179656 | tf_op jit(solution)/shard_map/ppermute | solution.py:374
  45.3 7.2 %shard_map.77 = bf16[32,2,16,384]{3,2,1,0:T(8,128)(2,1)} custom-call(bf16[32,2,16,384]{3,2,1,0:T(8,128)(2,1)S(1)} %all-to-all-done.own_ref, bf16[512,384]{1,0:T(8,128)(2,1)S(1)} %get-tuple-element.43.hidden_ref, bf16[512,384]{1,0:T(8,128)(2,1)S(1)} %get-tuple-element.44.pre_ref, bf16[3,3,384,384]{3,2,1,0:T(8,128)(2,1)} %one_ref.3, ...), custom_call_target="tpu_custom_call" | custom-call | flops 2717908992 | bytes 9437184 | tf_op jit(solution)/shard_map/pallas_call | solution.py:362
  52.5 1.7 %collective-permute-done.1.refs_4_ = bf16[2,192,512]{2,1,0:T(8,128)(2,1)S(1)} collective-permute-done((bf16[2,192,512]{2,1,0:T(8,128)(2,1)S(1)}, bf16[2,192,512]{2,1,0:T(8,128)(2,1)S(1)}, u32[]{:S(2)}, u32[]{:S(2)}) %collective-permute-start.1) | collective-permute-done | bytes 393248 | tf_op jit(solution)/shard_map/ppermute | solution.py:374
  55.0 3.0 %all-to-all-start.1 = ((bf16[32,2,16,384]{3,2,1,0:T(8,128)(2,1)}), bf16[32,2,16,384]{3,2,1,0:T(8,128)(2,1)S(1)}, u32[]{:S(2)}, u32[]{:S(2)}) async-start(bf16[32,2,16,384]{3,2,1,0:T(8,128)(2,1)} %shard_map.77), calls=%async_computation.1 | async-start | bytes 1572864 | tf_op jit(solution)/shard_map/all_to_all | solution.py:430
  58.0 1.4 %collective-permute-start.3 = (bf16[2,192,512]{2,1,0:T(8,128)(2,1)S(1)}, bf16[2,192,512]{2,1,0:T(8,128)(2,1)S(1)}, u32[]{:S(2)}, u32[]{:S(2)}) collective-permute-start(bf16[2,192,512]{2,1,0:T(8,128)(2,1)S(1)} %get-tuple-element.53), channel_id=1, source_target_pairs={{0,3},{1,2},{2,1},{3,0},{4,7},{5,6},{6,5},{7,4},{8,11},{9,10},{10,... | collective-permute-start | bytes 1179656 | tf_op jit(solution)/shard_map/ppermute | solution.py:374
  59.9 4.9 %collective-permute-done.4.refs_5_ = bf16[2,192,512]{2,1,0:T(8,128)(2,1)S(1)} collective-permute-done((bf16[2,192,512]{2,1,0:T(8,128)(2,1)S(1)}, bf16[2,192,512]{2,1,0:T(8,128)(2,1)S(1)}, u32[]{:S(2)}, u32[]{:S(2)}) %collective-permute-start.4) | collective-permute-done | bytes 393248 | tf_op jit(solution)/shard_map/ppermute | solution.py:374
  64.8 2.3 %collective-permute-start.6 = (bf16[192,512]{1,0:T(8,128)(2,1)S(1)}, bf16[192,512]{1,0:T(8,128)(2,1)S(1)}, u32[]{:S(2)}, u32[]{:S(2)}) collective-permute-start(bf16[192,512]{1,0:T(8,128)(2,1)S(1)} %slice_bitcast_fusion.1), channel_id=1, source_target_pairs={{0,2},{1,3},{2,0},{3,1},{4,6},{5,7},{6,4},{7,5},{8,10},{9,11},{10,... | collective-permute-start | bytes 589832 | tf_op jit(solution)/shard_map/ppermute | solution.py:374
  67.1 1.7 %collective-permute-start.7 = (bf16[192,512]{1,0:T(8,128)(2,1)S(1)}, bf16[192,512]{1,0:T(8,128)(2,1)S(1)}, u32[]{:S(2)}, u32[]{:S(2)}) collective-permute-start(bf16[192,512]{1,0:T(8,128)(2,1)S(1)} %slice_bitcast_fusion.2), channel_id=1, source_target_pairs={{0,4},{1,5},{2,6},{3,7},{4,0},{5,1},{6,2},{7,3},{8,12},{9,13},{10,... | collective-permute-start | bytes 589832 | tf_op jit(solution)/shard_map/ppermute | solution.py:374
  68.8 7.2 %collective-permute-done.3.refs_3_ = bf16[2,192,512]{2,1,0:T(8,128)(2,1)S(1)} collective-permute-done((bf16[2,192,512]{2,1,0:T(8,128)(2,1)S(1)}, bf16[2,192,512]{2,1,0:T(8,128)(2,1)S(1)}, u32[]{:S(2)}, u32[]{:S(2)}) %collective-permute-start.3) | collective-permute-done | bytes 393248 | tf_op jit(solution)/shard_map/ppermute | solution.py:374
  76.0 1.9 %collective-permute-start.8 = (bf16[192,512]{1,0:T(8,128)(2,1)S(1)}, bf16[192,512]{1,0:T(8,128)(2,1)S(1)}, u32[]{:S(2)}, u32[]{:S(2)}) collective-permute-start(bf16[192,512]{1,0:T(8,128)(2,1)S(1)} %slice_bitcast_fusion), channel_id=1, source_target_pairs={{0,4},{1,5},{2,6},{3,7},{4,0},{5,1},{6,2},{7,3},{8,12},{9,13},{10,... | collective-permute-start | bytes 589832 | tf_op jit(solution)/shard_map/ppermute | solution.py:374
  77.9 3.2 %shard_map.79.near_ref = f32[3,576,192]{2,1,0:T(8,128)S(1)} custom-call(bf16[2,192,512]{2,1,0:T(8,128)(2,1)S(1)} %get-tuple-element.50.refs_0_, bf16[2,192,512]{2,1,0:T(8,128)(2,1)S(1)} %collective-permute-done.refs_1_, bf16[2,192,512]{2,1,0:T(8,128)(2,1)S(1)} %collective-permute-done.2.refs_2_, bf16[2,192,512]{2,1,0:T(8,128)(2,1)S(1)} %collective-permute-done.3.refs_3_, ...), custom_call_target="tpu_custom_call" | custom-call | flops 2717908992 | bytes 6291456 | tf_op jit(solution)/shard_map/pallas_call | solution.py:362
  82.2 3.7 %collective-permute-done.6.refs_1_ = bf16[192,512]{1,0:T(8,128)(2,1)S(1)} collective-permute-done((bf16[192,512]{1,0:T(8,128)(2,1)S(1)}, bf16[192,512]{1,0:T(8,128)(2,1)S(1)}, u32[]{:S(2)}, u32[]{:S(2)}) %collective-permute-start.6) | collective-permute-done | bytes 196640 | tf_op jit(solution)/shard_map/ppermute | solution.py:374
  86.0 2.9 %shard_map.80 = (bf16[112,384]{1,0:T(8,128)(2,1)S(1)}, bf16[112,384]{1,0:T(8,128)(2,1)S(1)}, bf16[112,384]{1,0:T(8,128)(2,1)S(1)}, bf16[112,384]{1,0:T(8,128)(2,...) custom-call(s32[4]{0:T(128)S(1)} %pad_add_fusion.place_ref, ...), custom_call_target="tpu_custom_call" | custom-call | flops 1358954496 | bytes 4194304 | tf_op jit(solution)/shard_map/pallas_call | solution.py:362
  89.0 1.5 %collective-permute-start.10 = (bf16[112,384]{1,0:T(8,128)(2,1)S(1)}, bf16[112,384]{1,0:T(8,128)(2,1)S(1)}, u32[]{:S(2)}, u32[]{:S(2)}) collective-permute-start(bf16[112,384]{1,0:T(8,128)(2,1)S(1)} %get-tuple-element.58), channel_id=1, source_target_pairs={{0,8},{1,9},{8,0},{9,1},{16,24},{17,25},{24,16},{25,17},{2,10},{3,... | collective-permute-start | bytes 258056 | tf_op jit(solution)/shard_map/ppermute | solution.py:461
  90.9 2.4 %collective-permute-start.12 = (bf16[112,384]{1,0:T(8,128)(2,1)S(1)}, bf16[112,384]{1,0:T(8,128)(2,1)S(1)}, u32[]{:S(2)}, u32[]{:S(2)}) collective-permute-start(bf16[112,384]{1,0:T(8,128)(2,1)S(1)} %get-tuple-element.60), channel_id=1, source_target_pairs={{0,16},{1,17},{8,24},{9,25},{16,0},{17,1},{24,8},{25,9},{2,18},{3,... | collective-permute-start | bytes 258056 | tf_op jit(solution)/shard_map/ppermute | solution.py:461
  93.5 3.3 %collective-permute-start.14 = (bf16[112,384]{1,0:T(8,128)(2,1)S(1)}, bf16[112,384]{1,0:T(8,128)(2,1)S(1)}, u32[]{:S(2)}, u32[]{:S(2)}) collective-permute-start(bf16[112,384]{1,0:T(8,128)(2,1)S(1)} %get-tuple-element.62), channel_id=1, source_target_pairs={{0,24},{1,25},{8,16},{9,17},{16,8},{17,9},{24,0},{25,1},{2,26},{3,... | collective-permute-start | bytes 258056 | tf_op jit(solution)/shard_map/ppermute | solution.py:461
  97.1 1.5 %shard_map.78 = (bf16[8,64,384]{2,1,0:T(8,128)(2,1)}, bf16[8,64,384]{2,1,0:T(8,128)(2,1)}) custom-call(bf16[32,2,16,384]{3,2,1,0:T(8,128)(2,1)S(1)} %all-to-all-done.1.fields_ref), custom_call_target="tpu_custom_call" | custom-call | flops 1000000000 | bytes 3145728 | tf_op jit(solution)/shard_map/pallas_call | solution.py:362
  98.5 7.6 %collective-permute-done.13.refs_5_ = bf16[112,384]{1,0:T(8,128)(2,1)S(1)} collective-permute-done((bf16[112,384]{1,0:T(8,128)(2,1)S(1)}, bf16[112,384]{1,0:T(8,128)(2,1)S(1)}, u32[]{:S(2)}, u32[]{:S(2)}) %collective-permute-start.13) | collective-permute-done | bytes 86048 | tf_op jit(solution)/shard_map/ppermute | solution.py:461
  106.2 1.5 %shard_map.81 = (f32[3,3,48,96]{3,2,1,0:T(8,128)}, f32[3,3,48,96]{3,2,1,0:T(8,128)}) custom-call(s32[4]{0:T(128)S(1)} %pad_add_fusion.place_ref, bf16[112,384]{1,0:T(8,128)(2,1)S(1)} %get-tuple-element.66.refs_0_, bf16[112,384]{1,0:T(8,128)(2,1)S(1)} %collective-permute-done.9.refs_1_, bf16[112,384]{1,0:T(8,128)(2,1)S(1)} %collective-permute-done.10.refs_2_, ...), custom_call_target="tpu_custom_call" | custom-call | flops 1000000 | bytes 2097152 | tf_op jit(solution)/shard_map/pallas_call | solution.py:362
  (24 shorter events, 3.5 us)
Async XLA Ops:
  3.4 27.9 %all-to-all-start = ((bf16[32,2,16,384]{3,2,1,0:T(8,128)(2,1)}), bf16[32,2,16,384]{3,2,1,0:T(8,128)(2,1)S(1)}, u32[]{:S(2)}, u32[]{:S(2)}) async-start(bf16[32,2,16,384]{3,2,1,0:T(8,128)(2,1)} %shard_map.75), calls=%async_computation | async-start | bytes 1572864 | tf_op jit(solution)/shard_map/all_to_all | solution.py:388
  42.1 3.1 %collective-permute-start = (bf16[2,192,512]{2,1,0:T(8,128)(2,1)S(1)}, bf16[2,192,512]{2,1,0:T(8,128)(2,1)S(1)}, u32[]{:S(2)}, u32[]{:S(2)}) collective-permute-start(bf16[2,192,512]{2,1,0:T(8,128)(2,1)S(1)} %get-tuple-element.42), channel_id=1, source_target_pairs={{0,1},{1,0},{2,3},{3,2},{4,5},{5,4},{6,7},{7,6},{8,9},{9,8},{10,11... | collective-permute-start | bytes 1179656 | tf_op jit(solution)/shard_map/ppermute | solution.py:374
  42.2 12.0 %collective-permute-start.1 = (bf16[2,192,512]{2,1,0:T(8,128)(2,1)S(1)}, bf16[2,192,512]{2,1,0:T(8,128)(2,1)S(1)}, u32[]{:S(2)}, u32[]{:S(2)}) collective-permute-start(bf16[2,192,512]{2,1,0:T(8,128)(2,1)S(1)} %get-tuple-element.45), channel_id=1, source_target_pairs={{0,4},{1,5},{2,6},{3,7},{4,0},{5,1},{6,2},{7,3},{8,12},{9,13},{10,... | collective-permute-start | bytes 1179656 | tf_op jit(solution)/shard_map/ppermute | solution.py:374
  43.8 11.2 %collective-permute-start.2 = (bf16[2,192,512]{2,1,0:T(8,128)(2,1)S(1)}, bf16[2,192,512]{2,1,0:T(8,128)(2,1)S(1)}, u32[]{:S(2)}, u32[]{:S(2)}) collective-permute-start(bf16[2,192,512]{2,1,0:T(8,128)(2,1)S(1)} %get-tuple-element.46), channel_id=1, source_target_pairs={{0,2},{1,3},{2,0},{3,1},{4,6},{5,7},{6,4},{7,5},{8,10},{9,11},{10,... | collective-permute-start | bytes 1179656 | tf_op jit(solution)/shard_map/ppermute | solution.py:374
  45.3 19.6 %collective-permute-start.4 = (bf16[2,192,512]{2,1,0:T(8,128)(2,1)S(1)}, bf16[2,192,512]{2,1,0:T(8,128)(2,1)S(1)}, u32[]{:S(2)}, u32[]{:S(2)}) collective-permute-start(bf16[2,192,512]{2,1,0:T(8,128)(2,1)S(1)} %get-tuple-element.55), channel_id=1, source_target_pairs={{0,5},{1,4},{2,7},{3,6},{4,1},{5,0},{6,3},{7,2},{8,13},{9,12},{10,... | collective-permute-start | bytes 1179656 | tf_op jit(solution)/shard_map/ppermute | solution.py:374
  55.0 42.1 %all-to-all-start.1 = ((bf16[32,2,16,384]{3,2,1,0:T(8,128)(2,1)}), bf16[32,2,16,384]{3,2,1,0:T(8,128)(2,1)S(1)}, u32[]{:S(2)}, u32[]{:S(2)}) async-start(bf16[32,2,16,384]{3,2,1,0:T(8,128)(2,1)} %shard_map.77), calls=%async_computation.1 | async-start | bytes 1572864 | tf_op jit(solution)/shard_map/all_to_all | solution.py:430
  58.0 18.0 %collective-permute-start.3 = (bf16[2,192,512]{2,1,0:T(8,128)(2,1)S(1)}, bf16[2,192,512]{2,1,0:T(8,128)(2,1)S(1)}, u32[]{:S(2)}, u32[]{:S(2)}) collective-permute-start(bf16[2,192,512]{2,1,0:T(8,128)(2,1)S(1)} %get-tuple-element.53), channel_id=1, source_target_pairs={{0,3},{1,2},{2,1},{3,0},{4,7},{5,6},{6,5},{7,4},{8,11},{9,10},{10,... | collective-permute-start | bytes 1179656 | tf_op jit(solution)/shard_map/ppermute | solution.py:374
  59.5 22.8 %collective-permute-start.5 = (bf16[192,512]{1,0:T(8,128)(2,1)S(1)}, bf16[192,512]{1,0:T(8,128)(2,1)S(1)}, u32[]{:S(2)}, u32[]{:S(2)}) collective-permute-start(bf16[192,512]{1,0:T(8,128)(2,1)S(1)} %slice_bitcast_fusion.3), channel_id=1, source_target_pairs={{0,2},{1,3},{2,0},{3,1},{4,6},{5,7},{6,4},{7,5},{8,10},{9,11},{10,... | collective-permute-start | bytes 589832 | tf_op jit(solution)/shard_map/ppermute | solution.py:374
  64.8 21.2 %collective-permute-start.6 = (bf16[192,512]{1,0:T(8,128)(2,1)S(1)}, bf16[192,512]{1,0:T(8,128)(2,1)S(1)}, u32[]{:S(2)}, u32[]{:S(2)}) collective-permute-start(bf16[192,512]{1,0:T(8,128)(2,1)S(1)} %slice_bitcast_fusion.1), channel_id=1, source_target_pairs={{0,2},{1,3},{2,0},{3,1},{4,6},{5,7},{6,4},{7,5},{8,10},{9,11},{10,... | collective-permute-start | bytes 589832 | tf_op jit(solution)/shard_map/ppermute | solution.py:374
  67.1 18.9 %collective-permute-start.7 = (bf16[192,512]{1,0:T(8,128)(2,1)S(1)}, bf16[192,512]{1,0:T(8,128)(2,1)S(1)}, u32[]{:S(2)}, u32[]{:S(2)}) collective-permute-start(bf16[192,512]{1,0:T(8,128)(2,1)S(1)} %slice_bitcast_fusion.2), channel_id=1, source_target_pairs={{0,4},{1,5},{2,6},{3,7},{4,0},{5,1},{6,2},{7,3},{8,12},{9,13},{10,... | collective-permute-start | bytes 589832 | tf_op jit(solution)/shard_map/ppermute | solution.py:374
  76.0 10.0 %collective-permute-start.8 = (bf16[192,512]{1,0:T(8,128)(2,1)S(1)}, bf16[192,512]{1,0:T(8,128)(2,1)S(1)}, u32[]{:S(2)}, u32[]{:S(2)}) collective-permute-start(bf16[192,512]{1,0:T(8,128)(2,1)S(1)} %slice_bitcast_fusion), channel_id=1, source_target_pairs={{0,4},{1,5},{2,6},{3,7},{4,0},{5,1},{6,2},{7,3},{8,12},{9,13},{10,... | collective-permute-start | bytes 589832 | tf_op jit(solution)/shard_map/ppermute | solution.py:374
  88.9 4.5 %collective-permute-start.9 = (bf16[112,384]{1,0:T(8,128)(2,1)S(1)}, bf16[112,384]{1,0:T(8,128)(2,1)S(1)}, u32[]{:S(2)}, u32[]{:S(2)}) collective-permute-start(bf16[112,384]{1,0:T(8,128)(2,1)S(1)} %get-tuple-element.57), channel_id=1, source_target_pairs={{0,1},{1,0},{8,9},{9,8},{16,17},{17,16},{24,25},{25,24},{2,3},{3,2... | collective-permute-start | bytes 258056 | tf_op jit(solution)/shard_map/ppermute | solution.py:461
  89.0 7.8 %collective-permute-start.10 = (bf16[112,384]{1,0:T(8,128)(2,1)S(1)}, bf16[112,384]{1,0:T(8,128)(2,1)S(1)}, u32[]{:S(2)}, u32[]{:S(2)}) collective-permute-start(bf16[112,384]{1,0:T(8,128)(2,1)S(1)} %get-tuple-element.58), channel_id=1, source_target_pairs={{0,8},{1,9},{8,0},{9,1},{16,24},{17,25},{24,16},{25,17},{2,10},{3,... | collective-permute-start | bytes 258056 | tf_op jit(solution)/shard_map/ppermute | solution.py:461
  90.6 8.0 %collective-permute-start.11 = (bf16[112,384]{1,0:T(8,128)(2,1)S(1)}, bf16[112,384]{1,0:T(8,128)(2,1)S(1)}, u32[]{:S(2)}, u32[]{:S(2)}) collective-permute-start(bf16[112,384]{1,0:T(8,128)(2,1)S(1)} %get-tuple-element.59), channel_id=1, source_target_pairs={{0,9},{1,8},{8,1},{9,0},{16,25},{17,24},{24,17},{25,16},{2,11},{3,... | collective-permute-start | bytes 258056 | tf_op jit(solution)/shard_map/ppermute | solution.py:461
  90.9 7.7 %collective-permute-start.12 = (bf16[112,384]{1,0:T(8,128)(2,1)S(1)}, bf16[112,384]{1,0:T(8,128)(2,1)S(1)}, u32[]{:S(2)}, u32[]{:S(2)}) collective-permute-start(bf16[112,384]{1,0:T(8,128)(2,1)S(1)} %get-tuple-element.60), channel_id=1, source_target_pairs={{0,16},{1,17},{8,24},{9,25},{16,0},{17,1},{24,8},{25,9},{2,18},{3,... | collective-permute-start | bytes 258056 | tf_op jit(solution)/shard_map/ppermute | solution.py:461
  93.3 12.9 %collective-permute-start.13 = (bf16[112,384]{1,0:T(8,128)(2,1)S(1)}, bf16[112,384]{1,0:T(8,128)(2,1)S(1)}, u32[]{:S(2)}, u32[]{:S(2)}) collective-permute-start(bf16[112,384]{1,0:T(8,128)(2,1)S(1)} %get-tuple-element.61), channel_id=1, source_target_pairs={{0,17},{1,16},{8,25},{9,24},{16,1},{17,0},{24,9},{25,8},{2,19},{3,... | collective-permute-start | bytes 258056 | tf_op jit(solution)/shard_map/ppermute | solution.py:461
  93.5 12.7 %collective-permute-start.14 = (bf16[112,384]{1,0:T(8,128)(2,1)S(1)}, bf16[112,384]{1,0:T(8,128)(2,1)S(1)}, u32[]{:S(2)}, u32[]{:S(2)}) collective-permute-start(bf16[112,384]{1,0:T(8,128)(2,1)S(1)} %get-tuple-element.62), channel_id=1, source_target_pairs={{0,24},{1,25},{8,16},{9,17},{16,8},{17,9},{24,0},{25,1},{2,26},{3,... | collective-permute-start | bytes 258056 | tf_op jit(solution)/shard_map/ppermute | solution.py:461
  96.8 9.4 %collective-permute-start.15 = (bf16[112,384]{1,0:T(8,128)(2,1)S(1)}, bf16[112,384]{1,0:T(8,128)(2,1)S(1)}, u32[]{:S(2)}, u32[]{:S(2)}) collective-permute-start(bf16[112,384]{1,0:T(8,128)(2,1)S(1)} %get-tuple-element.63), channel_id=1, source_target_pairs={{0,25},{1,24},{8,17},{9,16},{16,9},{17,8},{24,1},{25,0},{2,27},{3,... | collective-permute-start | bytes 258056 | tf_op jit(solution)/shard_map/ppermute | solution.py:461

commit v8 on v6

--- a/solution.py
+++ b/solution.py
@@ -183,13 +183,16 @@
     return copies
 
 
+def weights_kernel(one_ref, two_ref, one_out, two_out, sems):
+    for copy in fetched(((one_ref, one_out), (two_ref, two_out)), sems):
+        copy.wait()
+
+
 def inner_kernel(band, step, place_ref, own_ref, one_ref, two_ref,
-                 hidden_ref, pre_ref, kept_ref, pair_ref, x_same_ref, x_cross_ref, y_same_ref, y_cross_ref,
-                 two_held, stack_ref, first_ref, slope_ref, turned_ref, sems, out_sems):
+                 hidden_ref, pre_ref, mine_ref, give_ref,
+                 stack_ref, first_ref, slope_ref, turned_ref):
     x, y, core = place_ref[0], place_ref[1], place_ref[2]
-    other = 1 - core
     cells, channels = first_ref.shape
-    fetch = fetched(((two_ref, two_held),), sems)[0]
     half, rows = channels // 2, 32
     deep = half // 4
 
@@ -199,10 +202,6 @@
             for z in range(4):
                 begin = (2 * z + h) * deep if at < 2 else h * half + z * deep
                 turned_ref[at * 2 + h, z * deep : (z + 1) * deep, :] = turned[begin : begin + deep]
-
-    def sent(side, wanted):
-        pairs = [(turned_ref.at[4 * side + of * 2 + h], ref.at[side]) for ref, of, h in wanted]
-        return fetched(pairs, out_sems.at[side])
 
     source = own_ref[:, 0].reshape(cells, channels)
     write_stack(source, stack_ref, band, step)
@@ -220,37 +219,36 @@
 
     lax.fori_loop(0, cells // rows, activate, 0)
     turn(1, hidden_ref[...])
-    copies = sent(0, (
-        (y_same_ref, core, 1 - y), (y_cross_ref, other, 1 - y), (x_same_ref, core, y),
-        (x_cross_ref, other, y), (pair_ref, other, y), (kept_ref, core, y),
-    ))
     cot = own_ref[:, 1].reshape(cells, channels)
     write_stack(cot, stack_ref, band, step)
     turn(3, cot)
-    fetch.wait()
-    pre_ref[...] = (slope_ref[...] * convolved_back(stack_ref, two_held, band, cells)).astype(BF16)
+    pre_ref[...] = (slope_ref[...] * convolved_back(stack_ref, two_ref, band, cells)).astype(BF16)
     turn(2, pre_ref[...])
-    copies += sent(1, (
-        (y_same_ref, core, x), (y_cross_ref, other, x), (x_same_ref, core, 1 - x),
-        (x_cross_ref, other, 1 - x), (pair_ref, other, x), (kept_ref, core, x),
-    ))
-    for copy in copies:
-        copy.wait()
-
-
-def outer_kernel(band, step, own_ref, hidden_ref, pre_ref, one_ref, two_ref, out_ref,
-                 one_held, two_held, stack_ref, sems):
+
+    for ref, of in ((mine_ref, core), (give_ref, 1 - core)):
+        ref[0] = turned_ref[of * 2 + 1 - y]
+        ref[1] = turned_ref[of * 2 + y]
+        ref[2] = turned_ref[4 + of * 2 + 1 - x]
+        ref[3] = turned_ref[4 + of * 2 + x]
+
+
+def join_kernel(mine_ref, got_ref, x_ref, y_ref):
+    for at, ref in enumerate((mine_ref, got_ref)):
+        y_ref[at] = ref[0]
+        x_ref[2 + at] = ref[1]
+        x_ref[at] = ref[2]
+        y_ref[2 + at] = ref[3]
+
+
+def outer_kernel(band, step, own_ref, hidden_ref, pre_ref, one_ref, two_ref, out_ref, stack_ref):
     cells, channels = hidden_ref.shape
     shape = (out_ref.shape[0],) + out_ref.shape[2:]
-    copies = fetched(((two_ref, two_held), (one_ref, one_held)), sems)
     write_stack(hidden_ref[...], stack_ref, band, step)
-    copies[0].wait()
-    second = convolved(stack_ref, two_held, band, cells)
+    second = convolved(stack_ref, two_ref, band, cells)
     source = own_ref[:, 0].reshape(cells, channels)
     out_ref[:, 0] = (source.astype(F32) + second).astype(BF16).reshape(shape)
     write_stack(pre_ref[...], stack_ref, band, step)
-    copies[1].wait()
-    back = convolved_back(stack_ref, one_held, band, cells)
+    back = convolved_back(stack_ref, one_ref, band, cells)
     cot = own_ref[:, 1].reshape(cells, channels)
     out_ref[:, 1] = (cot.astype(F32) + back).astype(BF16).reshape(shape)
 
@@ -282,19 +280,20 @@
     return lax.dot_general(turned_ref[...], moved_ref[b], (((1,), (1,)), ((), ())), preferred_element_type=F32)
 
 
-def near_kernel(band, step, *refs):
-    pieces, (sums_ref, turned_ref, moved_ref) = refs[:-3], refs[-3:]
-    lefts, rights = ([ref.at[side] for ref in pieces] for side in range(2))
+def near_kernel(band, step, x_ref, y_ref, x_got_ref, y_got_ref, sums_ref, turned_ref, moved_ref):
+    lefts = [x_ref.at[2], x_ref.at[3], x_got_ref.at[2], x_got_ref.at[3], y_got_ref.at[0], y_got_ref.at[1]]
+    rights = [y_ref.at[2], y_ref.at[3], x_got_ref.at[0], x_got_ref.at[1], y_got_ref.at[2], y_got_ref.at[3]]
     for b in range(3):
         sums_ref[b] = summed(band, step, lefts, rights, turned_ref, moved_ref, b)
 
 
-def far_kernel(band, step, place_ref, near_ref, *refs):
-    pieces, out_refs, (turned_ref, moved_ref, sums_ref, send_ref, sems) = refs[:4], refs[4:-5], refs[-5:]
+def far_kernel(band, step, place_ref, near_ref, left_ref, right_ref, *refs):
+    out_refs, (turned_ref, moved_ref, sums_ref, send_ref, sems) = refs[:-5], refs[-5:]
     me = place_ref[3] * 2 + place_ref[2]
-    half, cells = pieces[0].shape
+    half = left_ref.shape[1]
+    lefts, rights = ([ref.at[at] for at in range(2)] for ref in (left_ref, right_ref))
     for b in range(3):
-        sums_ref[b] = near_ref[b] + summed(band, step, pieces[:2], pieces[2:], turned_ref, moved_ref, b)
+        sums_ref[b] = near_ref[b] + summed(band, step, lefts, rights, turned_ref, moved_ref, b)
     deep, quarter = half // 4, half // 2
     height = send_ref.shape[1]
     for z in range(4):
@@ -356,12 +355,12 @@
     def shaped(*shape, kind=BF16):
         return jax.ShapeDtypeStruct(shape, kind)
 
-    def kernel(body, specs, arguments, out_shape, scratch_shapes, work, megabytes, out_specs=None):
+    def kernel(body, specs, arguments, out_shape, scratch_shapes, work, megabytes):
         return pl.pallas_call(
             body,
             out_shape=out_shape,
             in_specs=specs,
-            out_specs=out_specs or jax.tree.map(lambda _: vmem, out_shape),
+            out_specs=jax.tree.map(lambda _: vmem, out_shape),
             scratch_shapes=scratch_shapes,
             compiler_params=pltpu.CompilerParams(vmem_limit_bytes=20 * 2**20),
             cost_estimate=pl.CostEstimate(flops=work, bytes_accessed=megabytes * 2**20, transcendentals=0),
@@ -385,42 +384,37 @@
     )
     own = lax.all_to_all(own, every, 0, 0, tiled=True)
     place = jnp.stack([lax.axis_index(axis) for axis in ("x", "y", "core", "z")]).astype(jnp.int32)
-    piece = pltpu.HBM((2, half, cells), BF16)
-    one_far, two_far = (pltpu.with_memory_space_constraint(w, pltpu.HBM) for w in (conv1_weight, conv2_weight))
-    hidden, pre_grad, kept, pair, x_same, x_cross, y_same, y_cross = kernel(
+    one, two = kernel(
+        weights_kernel,
+        [hbm] * 2,
+        [pltpu.with_memory_space_constraint(w, pltpu.HBM) for w in (conv1_weight, conv2_weight)],
+        (weights, weights),
+        [pltpu.SemaphoreType.DMA((2,))],
+        10**6,
+        10,
+    )
+    pieces = held(4, half, cells)
+    hidden, pre_grad, mine, give = kernel(
         functools.partial(inner_kernel, band, step),
-        [smem, vmem, vmem, hbm],
-        (place, own, conv1_weight, two_far),
-        (shaped(cells, channels),) * 2 + (piece,) * 6,
-        [
-            weights,
-            stack,
-            held(cells, channels, kind=F32),
-            held(cells, channels, kind=F32),
-            held(8, half, cells),
-            pltpu.SemaphoreType.DMA((1,)),
-            pltpu.SemaphoreType.DMA((2, 6)),
-        ],
+        [smem] + [vmem] * 3,
+        (place, own, one, two),
+        (held(cells, channels), held(cells, channels), pieces, pieces),
+        [stack, held(cells, channels, kind=F32), held(cells, channels, kind=F32), held(8, half, cells)],
         2 * flops,
         10,
-        (vmem,) * 2 + (hbm,) * 6,
-    )
-    y_same, x_same = passed(y_same, 0, 1, 0), passed(x_same, 1, 0, 0)
-    y_cross, x_cross = passed(y_cross, 0, 1, 1), passed(x_cross, 1, 0, 1)
-    pair = passed(pair, 0, 0, 1)
-    far = (
-        passed(y_same[0], 1, 0, 0),
-        passed(y_cross[0], 1, 0, 0),
-        passed(x_same[1], 0, 1, 0),
-        passed(x_cross[1], 0, 1, 0),
-    )
-    hidden, pre_grad, pair = lax.optimization_barrier((hidden, pre_grad, pair))
+    )
+    x_given, y_given = kernel(
+        join_kernel, [vmem] * 2, (mine, passed(give, 0, 0, 1)), (pieces, pieces), [], 10**6, 4
+    )
+    x_got, y_got = passed(x_given, 1, 0, 0), passed(y_given, 0, 1, 0)
+    far = (passed(y_got[:2], 1, 0, 0), passed(x_got[:2], 0, 1, 0))
+    hidden, pre_grad, x_given = lax.optimization_barrier((hidden, pre_grad, x_given))
     fields = kernel(
         functools.partial(outer_kernel, band, step),
-        [vmem] * 3 + [hbm] * 2,
-        (own, hidden, pre_grad, one_far, two_far),
+        [vmem] * 5,
+        (own, hidden, pre_grad, one, two),
         dealt,
-        [weights, weights, stack, pltpu.SemaphoreType.DMA((2,))],
+        [stack],
         2 * flops,
         9,
     )
@@ -431,8 +425,8 @@
     sums = shaped(3, 3 * half, half, kind=F32)
     near = kernel(
         functools.partial(near_kernel, band, step),
-        [vmem] * 6,
-        (kept, pair, x_same, x_cross, y_same, y_cross),
+        [vmem] * 4,
+        (x_given, y_given, x_got, y_got),
         sums,
         [held(3 * half, 6 * cells), held(3, half, 6 * cells)],
         2 * flops,
@@ -440,9 +434,9 @@
     )
     terms = kernel(
         functools.partial(far_kernel, band, step),
-        [smem] + [vmem] * 5,
+        [smem] + [vmem] * 3,
         (place, near) + far,
-        (pltpu.HBM((height, channels), BF16),) * 8,
+        (pltpu.VMEM((height, channels), BF16),) * 8,
         [
             held(3 * half, 2 * cells),
             held(3, half, 2 * cells),
@@ -452,11 +446,11 @@
         ],
         flops,
         4,
-        (hbm,) * 8,
     )
     parts = list(terms)
     for away in (6, 7, 4, 5, 2, 3, 1):
         parts[away] = lax.ppermute(terms[away], ("z", "core"), [(i, i ^ away) for i in range(8)])
+    output, input_grad, parts = lax.optimization_barrier((output, input_grad, parts))
     grad = shaped(3, 3, deep, half // 2, kind=F32)
     conv1_grad, conv2_grad = kernel(
         functools.partial(finish_kernel, scale), [smem] + [vmem] * 8, (place, *parts), (grad, grad), [], 10**6, 2

time: 116 us -> 116 us (level)
  starting transfers between devices: 29.6 us -> 24.6 us
  local copies, waits for them, and re-layouts: 2.71 us -> 6.62 us
  waiting for transfers between devices: 54.6 us -> 56.2 us
    ppermute x9 -> x5, waiting for transfers between devices: 24.8 us -> 33.7 us  [passed(): return lax.ppermute(piece, ('y', 'x', 'core'), pairs)]
    all_to_all x1, waiting for transfers between devices: 20.5 us -> 14.9 us  [fast_local(): own = lax.all_to_all(own, every, 0, 0, tiled=True)]
    ppermute x9 -> x5, starting transfers between devices: 10.3 us -> 5.35 us  [passed(): return lax.ppermute(piece, ('y', 'x', 'core'), pairs)]
    unnamed x10 -> x12, local copies, waits for them, and re-layouts: 2.65 us -> 6.57 us
    ppermute x7, waiting for transfers between devices: 9.31 us -> 7.54 us  [fast_local(): lax.ppermute(terms[away], ('z', 'core'), [(i, i ^ away) for i in range(8)])]
    pallas_call x7 -> x9, Pallas kernels: 26.3 us -> 25.4 us  [kernel(): pl.pallas_call(body, out_shape=out_shape, in_specs=specs, out_specs=jax.t...]
  transfers between devices with their start and end apart: 18 -> 14, of which waited for: 9 -> 6; matrix products, arithmetic and copies ran while one was open for 0% -> 0% of each run, Pallas kernels for 13% -> 9%
where the time goes in v8:
time: 116 us; the launch traced here: 114 us
  waiting for transfers between devices  56.2 us (48%)
  Pallas kernels  25.4 us (22%)
  starting transfers between devices  24.6 us (21%)
  local copies, waits for them, and re-layouts  6.62 us (6%)
    ppermute x5, waiting for transfers between devices, passed(): return lax.ppermute(piece, ('y', 'x', 'core'), pairs)  33.7 us
    pallas_call x9, Pallas kernels, kernel(): pl.pallas_call(body, out_shape=out_shape, in_specs=specs, out_specs=jax.t...  25.4 us
    all_to_all x1, waiting for transfers between devices, fast_local(): own = lax.all_to_all(own, every, 0, 0, tiled=True)  14.9 us
    ppermute x7, starting transfers between devices, fast_local(): lax.ppermute(terms[away], ('z', 'core'), [(i, i ^ away) for i in range(8)])  8.18 us
    ppermute x7, waiting for transfers between devices, fast_local(): lax.ppermute(terms[away], ('z', 'core'), [(i, i ^ away) for i in range(8)])  7.54 us
    all_to_all x1, starting transfers between devices, fast_local(): own = lax.all_to_all(own, every, 0, 0, tiled=True)  7.3 us
    unnamed x12, local copies, waits for them, and re-layouts  6.57 us
    ppermute x5, starting transfers between devices, passed(): return lax.ppermute(piece, ('y', 'x', 'core'), pairs)  5.35 us
  transfers between devices with their start and end apart: 14, of which 6 were waited for; matrix products, arithmetic and copies ran while one was open for 0% of the time, Pallas kernels for 9%

profile of v8, /device:TPU:0, one launch (start us, length us, event | category | flops | bytes accessed | tf_op | source)
XLA Modules:
  0.0 113.7 jit_solution(10039619348834148207)
XLA Ops:
  0.6 2.8 %shard_map.75 = bf16[32,2,16,384]{3,2,1,0:T(8,128)(2,1)} custom-call(bf16[8,64,384]{2,1,0:T(8,128)(2,1)} %inputs_ref.1, bf16[8,64,384]{2,1,0:T(8,128)(2,1)} %cot_ref.1), custom_call_target="tpu_custom_call" | custom-call | flops 1000000000 | bytes 3145728 | tf_op jit(solution)/shard_map/pallas_call | solution.py:359
  3.4 7.3 %all-to-all-start = ((bf16[32,2,16,384]{3,2,1,0:T(8,128)(2,1)}), bf16[32,2,16,384]{3,2,1,0:T(8,128)(2,1)S(1)}, u32[]{:S(2)}, u32[]{:S(2)}) async-start(bf16[32,2,16,384]{3,2,1,0:T(8,128)(2,1)} %shard_map.75), calls=%async_computation | async-start | bytes 1572864 | tf_op jit(solution)/shard_map/all_to_all | solution.py:385
  10.7 2.6 %shard_map.76 = (bf16[3,3,384,384]{3,2,1,0:T(8,128)(2,1)S(1)}, bf16[3,3,384,384]{3,2,1,0:T(8,128)(2,1)S(1)}) custom-call(bf16[3,3,384,384]{3,2,1,0:T(8,128)(2,1)} %one_ref.1, bf16[3,3,384,384]{3,2,1,0:T(8,128)(2,1)} %two_ref.1), custom_call_target="tpu_custom_call" | custom-call | flops 1000000 | bytes 10485760 | tf_op jit(solution)/shard_map/pallas_call | solution.py:359
  13.3 1.5 %copy-done = bf16[3,3,384,384]{3,2,1,0:T(8,128)(2,1)} copy-done((bf16[3,3,384,384]{3,2,1,0:T(8,128)(2,1)}, bf16[3,3,384,384]{3,2,1,0:T(8,128)(2,1)S(1)}, u32[]{:S(2)}) %copy-start) | copy-done | bytes 2654232
  14.8 1.5 %copy-done.3 = bf16[3,3,384,384]{3,2,1,0:T(8,128)(2,1)} copy-done((bf16[3,3,384,384]{3,2,1,0:T(8,128)(2,1)}, bf16[3,3,384,384]{3,2,1,0:T(8,128)(2,1)S(1)}, u32[]{:S(2)}) %copy-start.3) | copy-done | bytes 2654232
  16.5 14.9 %all-to-all-done.own_ref = bf16[32,2,16,384]{3,2,1,0:T(8,128)(2,1)S(1)} async-done(((bf16[32,2,16,384]{3,2,1,0:T(8,128)(2,1)}), bf16[32,2,16,384]{3,2,1,0:T(8,128)(2,1)S(1)}, u32[]{:S(2)}, u32[]{:S(2)}) %all-to-all-start) | async-done | bytes 786464 | tf_op jit(solution)/shard_map/all_to_all | solution.py:385
  31.3 1.7 %copy-done.1 = bf16[3,3,384,384]{3,2,1,0:T(8,128)(2,1)S(1)} copy-done((bf16[3,3,384,384]{3,2,1,0:T(8,128)(2,1)S(1)}, bf16[3,3,384,384]{3,2,1,0:T(8,128)(2,1)}, u32[]{:S(2)}) %copy-start.1) | copy-done | bytes 2654232
  33.1 1.7 %copy-done.4 = bf16[3,3,384,384]{3,2,1,0:T(8,128)(2,1)S(1)} copy-done((bf16[3,3,384,384]{3,2,1,0:T(8,128)(2,1)S(1)}, bf16[3,3,384,384]{3,2,1,0:T(8,128)(2,1)}, u32[]{:S(2)}) %copy-start.4) | copy-done | bytes 2654232
  34.9 5.9 %shard_map.77 = (bf16[512,384]{1,0:T(8,128)(2,1)S(1)}, bf16[512,384]{1,0:T(8,128)(2,1)S(1)}, bf16[4,192,512]{2,1,0:T(8,128)(2,1)S(1)}, bf16[4,192,512]{2,1,0:T(8,128)(2,1)S(1)}) custom-call(s32[4]{0:T(128)S(1)} %pad_add_fusion.place_ref, bf16[32,2,16,384]{3,2,1,0:T(8,128)(2,1)S(1)} %all-to-all-done.own_ref, bf16[3,3,384,384]{3,2,1,0:T(8,128)(2,1)S(1)} %copy-done.1, ...), custom_call_target="tpu_custom_call" | custom-call | flops 2717908992 | bytes 10485760 | tf_op jit(solution)/shard_map/pallas_call | solution.py:359
  40.8 2.3 %collective-permute-done.got_ref = bf16[4,192,512]{2,1,0:T(8,128)(2,1)S(1)} collective-permute-done((bf16[4,192,512]{2,1,0:T(8,128)(2,1)S(1)}, bf16[4,192,512]{2,1,0:T(8,128)(2,1)S(1)}, u32[]{:S(2)}, u32[]{:S(2)}) %collective-permute-start) | collective-permute-done | bytes 786464 | tf_op jit(solution)/shard_map/ppermute | solution.py:371
  43.2 5.1 %shard_map.79 = bf16[32,2,16,384]{3,2,1,0:T(8,128)(2,1)} custom-call(bf16[32,2,16,384]{3,2,1,0:T(8,128)(2,1)S(1)} %all-to-all-done.own_ref, bf16[512,384]{1,0:T(8,128)(2,1)S(1)} %get-tuple-element.44.hidden_ref, bf16[512,384]{1,0:T(8,128)(2,1)S(1)} %get-tuple-element.45.pre_ref, bf16[3,3,384,384]{3,2,1,0:T(8,128)(2,1)S(1)} %copy-done.2, ...), custom_call_target="tpu_custom_call" | custom-call | flops 2717908992 | bytes 9437184 | tf_op jit(solution)/shard_map/pallas_call | solution.py:359
  48.3 3.8 %all-to-all-start.1 = ((bf16[32,2,16,384]{3,2,1,0:T(8,128)(2,1)}), bf16[32,2,16,384]{3,2,1,0:T(8,128)(2,1)S(1)}, u32[]{:S(2)}, u32[]{:S(2)}) async-start(bf16[32,2,16,384]{3,2,1,0:T(8,128)(2,1)} %shard_map.79), calls=%async_computation.1 | async-start | bytes 1572864 | tf_op jit(solution)/shard_map/all_to_all | solution.py:421
  52.1 1.7 %collective-permute-start.1 = (bf16[4,192,512]{2,1,0:T(8,128)(2,1)S(1)}, bf16[4,192,512]{2,1,0:T(8,128)(2,1)S(1)}, u32[]{:S(2)}, u32[]{:S(2)}) collective-permute-start(bf16[4,192,512]{2,1,0:T(8,128)(2,1)S(1)} %get-tuple-element.48.x_ref), channel_id=1, source_target_pairs={{0,2},{1,3},{2,0},{3,1},{4,6},{5,7},{6,4},{7,5},{8,10},{9,11},{10,... | collective-permute-start | bytes 2359304 | tf_op jit(solution)/shard_map/ppermute | solution.py:371
  53.7 1.5 %collective-permute-start.2 = (bf16[4,192,512]{2,1,0:T(8,128)(2,1)S(1)}, bf16[4,192,512]{2,1,0:T(8,128)(2,1)S(1)}, u32[]{:S(2)}, u32[]{:S(2)}) collective-permute-start(bf16[4,192,512]{2,1,0:T(8,128)(2,1)S(1)} %get-tuple-element.49.y_ref), channel_id=1, source_target_pairs={{0,4},{1,5},{2,6},{3,7},{4,0},{5,1},{6,2},{7,3},{8,12},{9,13},{10,... | collective-permute-start | bytes 2359304 | tf_op jit(solution)/shard_map/ppermute | solution.py:371
  55.2 24.8 %collective-permute-done.1.x_got_ref = bf16[4,192,512]{2,1,0:T(8,128)(2,1)S(1)} collective-permute-done((bf16[4,192,512]{2,1,0:T(8,128)(2,1)S(1)}, bf16[4,192,512]{2,1,0:T(8,128)(2,1)S(1)}, u32[]{:S(2)}, u32[]{:S(2)}) %collective-permute-start.1) | collective-permute-done | bytes 786464 | tf_op jit(solution)/shard_map/ppermute | solution.py:371
  80.1 1.5 %collective-permute-start.4 = (bf16[2,192,512]{2,1,0:T(8,128)(2,1)S(1)}, bf16[2,192,512]{2,1,0:T(8,128)(2,1)S(1)}, u32[]{:S(2)}, u32[]{:S(2)}) collective-permute-start(bf16[2,192,512]{2,1,0:T(8,128)(2,1)S(1)} %slice.9), channel_id=1, source_target_pairs={{0,4},{1,5},{2,6},{3,7},{4,0},{5,1},{6,2},{7,3},{8,12},{9,13},{10,... | collective-permute-start | bytes 1179656 | tf_op jit(solution)/shard_map/ppermute | solution.py:371
  82.3 3.2 %shard_map.81.near_ref = f32[3,576,192]{2,1,0:T(8,128)S(1)} custom-call(bf16[4,192,512]{2,1,0:T(8,128)(2,1)S(1)} %get-tuple-element.48.x_ref, bf16[4,192,512]{2,1,0:T(8,128)(2,1)S(1)} %get-tuple-element.49.y_ref, bf16[4,192,512]{2,1,0:T(8,128)(2,1)S(1)} %collective-permute-done.1.x_got_ref, bf16[4,192,512]{2,1,0:T(8,128)(2,1)S(1)} %collective-permute-done.2.y_got_ref), custom_call_target="tpu_custom_call" | custom-call | flops 2717908992 | bytes 6291456 | tf_op jit(solution)/shard_map/pallas_call | solution.py:359
  85.4 5.3 %collective-permute-done.4.right_ref = bf16[2,192,512]{2,1,0:T(8,128)(2,1)S(1)} collective-permute-done((bf16[2,192,512]{2,1,0:T(8,128)(2,1)S(1)}, bf16[2,192,512]{2,1,0:T(8,128)(2,1)S(1)}, u32[]{:S(2)}, u32[]{:S(2)}) %collective-permute-start.4) | collective-permute-done | bytes 393248 | tf_op jit(solution)/shard_map/ppermute | solution.py:371
  92.1 2.9 %shard_map.82 = (bf16[112,384]{1,0:T(8,128)(2,1)S(1)}, bf16[112,384]{1,0:T(8,128)(2,1)S(1)}, bf16[112,384]{1,0:T(8,128)(2,1)S(1)}, bf16[112,384]{1,0:T(8,128)(2,...) custom-call(s32[4]{0:T(128)S(1)} %pad_add_fusion.place_ref, ...), custom_call_target="tpu_custom_call" | custom-call | flops 1358954496 | bytes 4194304 | tf_op jit(solution)/shard_map/pallas_call | solution.py:359
  95.1 1.5 %collective-permute-start.6 = (bf16[112,384]{1,0:T(8,128)(2,1)S(1)}, bf16[112,384]{1,0:T(8,128)(2,1)S(1)}, u32[]{:S(2)}, u32[]{:S(2)}) collective-permute-start(bf16[112,384]{1,0:T(8,128)(2,1)S(1)} %get-tuple-element.52), channel_id=1, source_target_pairs={{0,8},{1,9},{8,0},{9,1},{16,24},{17,25},{24,16},{25,17},{2,10},{3,... | collective-permute-start | bytes 258056 | tf_op jit(solution)/shard_map/ppermute | solution.py:452
  97.0 2.4 %collective-permute-start.8 = (bf16[112,384]{1,0:T(8,128)(2,1)S(1)}, bf16[112,384]{1,0:T(8,128)(2,1)S(1)}, u32[]{:S(2)}, u32[]{:S(2)}) collective-permute-start(bf16[112,384]{1,0:T(8,128)(2,1)S(1)} %get-tuple-element.54), channel_id=1, source_target_pairs={{0,16},{1,17},{8,24},{9,25},{16,0},{17,1},{24,8},{25,9},{2,18},{3,... | collective-permute-start | bytes 258056 | tf_op jit(solution)/shard_map/ppermute | solution.py:452
  99.6 3.5 %collective-permute-start.10 = (bf16[112,384]{1,0:T(8,128)(2,1)S(1)}, bf16[112,384]{1,0:T(8,128)(2,1)S(1)}, u32[]{:S(2)}, u32[]{:S(2)}) collective-permute-start(bf16[112,384]{1,0:T(8,128)(2,1)S(1)} %get-tuple-element.56), channel_id=1, source_target_pairs={{0,24},{1,25},{8,16},{9,17},{16,8},{17,9},{24,0},{25,1},{2,26},{3,... | collective-permute-start | bytes 258056 | tf_op jit(solution)/shard_map/ppermute | solution.py:452
  104.7 7.5 %collective-permute-done.9.refs_5_ = bf16[112,384]{1,0:T(8,128)(2,1)S(1)} collective-permute-done((bf16[112,384]{1,0:T(8,128)(2,1)S(1)}, bf16[112,384]{1,0:T(8,128)(2,1)S(1)}, u32[]{:S(2)}, u32[]{:S(2)}) %collective-permute-start.9) | collective-permute-done | bytes 86048 | tf_op jit(solution)/shard_map/ppermute | solution.py:452
  112.2 1.5 %shard_map.83 = (f32[3,3,48,96]{3,2,1,0:T(8,128)}, f32[3,3,48,96]{3,2,1,0:T(8,128)}) custom-call(s32[4]{0:T(128)S(1)} %pad_add_fusion.place_ref, bf16[112,384]{1,0:T(8,128)(2,1)S(1)} %get-tuple-element.60.refs_0_, bf16[112,384]{1,0:T(8,128)(2,1)S(1)} %collective-permute-done.5.refs_1_, bf16[112,384]{1,0:T(8,128)(2,1)S(1)} %collective-permute-done.6.refs_2_, ...), custom_call_target="tpu_custom_call" | custom-call | flops 1000000 | bytes 2097152 | tf_op jit(solution)/shard_map/pallas_call | solution.py:359
  (28 shorter events, 4.5 us)
Async XLA Ops:
  3.4 27.9 %all-to-all-start = ((bf16[32,2,16,384]{3,2,1,0:T(8,128)(2,1)}), bf16[32,2,16,384]{3,2,1,0:T(8,128)(2,1)S(1)}, u32[]{:S(2)}, u32[]{:S(2)}) async-start(bf16[32,2,16,384]{3,2,1,0:T(8,128)(2,1)} %shard_map.75), calls=%async_computation | async-start | bytes 1572864 | tf_op jit(solution)/shard_map/all_to_all | solution.py:385
  13.3 1.5 %copy-start = (bf16[3,3,384,384]{3,2,1,0:T(8,128)(2,1)}, bf16[3,3,384,384]{3,2,1,0:T(8,128)(2,1)S(1)}, u32[]{:S(2)}) copy-start(bf16[3,3,384,384]{3,2,1,0:T(8,128)(2,1)S(1)} %get-tuple-element.37.one_ref) | copy-start | bytes 7962628
  14.8 1.5 %copy-start.3 = (bf16[3,3,384,384]{3,2,1,0:T(8,128)(2,1)}, bf16[3,3,384,384]{3,2,1,0:T(8,128)(2,1)S(1)}, u32[]{:S(2)}) copy-start(bf16[3,3,384,384]{3,2,1,0:T(8,128)(2,1)S(1)} %get-tuple-element.38.two_ref) | copy-start | bytes 7962628
  31.3 1.8 %copy-start.1 = (bf16[3,3,384,384]{3,2,1,0:T(8,128)(2,1)S(1)}, bf16[3,3,384,384]{3,2,1,0:T(8,128)(2,1)}, u32[]{:S(2)}) copy-start(bf16[3,3,384,384]{3,2,1,0:T(8,128)(2,1)} %copy-done) | copy-start | bytes 7962628
  33.1 1.7 %copy-start.4 = (bf16[3,3,384,384]{3,2,1,0:T(8,128)(2,1)S(1)}, bf16[3,3,384,384]{3,2,1,0:T(8,128)(2,1)}, u32[]{:S(2)}) copy-start(bf16[3,3,384,384]{3,2,1,0:T(8,128)(2,1)} %copy-done.3) | copy-start | bytes 7962628
  34.8 8.3 %copy-start.2 = (bf16[3,3,384,384]{3,2,1,0:T(8,128)(2,1)S(1)}, bf16[3,3,384,384]{3,2,1,0:T(8,128)(2,1)}, u32[]{:S(2)}) copy-start(bf16[3,3,384,384]{3,2,1,0:T(8,128)(2,1)} %copy-done) | copy-start | bytes 7962628
  34.8 8.3 %copy-start.5 = (bf16[3,3,384,384]{3,2,1,0:T(8,128)(2,1)S(1)}, bf16[3,3,384,384]{3,2,1,0:T(8,128)(2,1)}, u32[]{:S(2)}) copy-start(bf16[3,3,384,384]{3,2,1,0:T(8,128)(2,1)} %copy-done.3) | copy-start | bytes 7962628
  40.7 2.4 %collective-permute-start = (bf16[4,192,512]{2,1,0:T(8,128)(2,1)S(1)}, bf16[4,192,512]{2,1,0:T(8,128)(2,1)S(1)}, u32[]{:S(2)}, u32[]{:S(2)}) collective-permute-start(bf16[4,192,512]{2,1,0:T(8,128)(2,1)S(1)} %get-tuple-element.42), channel_id=1, source_target_pairs={{0,1},{1,0},{2,3},{3,2},{4,5},{5,4},{6,7},{7,6},{8,9},{9,8},{10,11... | collective-permute-start | bytes 2359304 | tf_op jit(solution)/shard_map/ppermute | solution.py:371
  48.3 54.9 %all-to-all-start.1 = ((bf16[32,2,16,384]{3,2,1,0:T(8,128)(2,1)}), bf16[32,2,16,384]{3,2,1,0:T(8,128)(2,1)S(1)}, u32[]{:S(2)}, u32[]{:S(2)}) async-start(bf16[32,2,16,384]{3,2,1,0:T(8,128)(2,1)} %shard_map.79), calls=%async_computation.1 | async-start | bytes 1572864 | tf_op jit(solution)/shard_map/all_to_all | solution.py:421
  52.1 28.0 %collective-permute-start.1 = (bf16[4,192,512]{2,1,0:T(8,128)(2,1)S(1)}, bf16[4,192,512]{2,1,0:T(8,128)(2,1)S(1)}, u32[]{:S(2)}, u32[]{:S(2)}) collective-permute-start(bf16[4,192,512]{2,1,0:T(8,128)(2,1)S(1)} %get-tuple-element.48.x_ref), channel_id=1, source_target_pairs={{0,2},{1,3},{2,0},{3,1},{4,6},{5,7},{6,4},{7,5},{8,10},{9,11},{10,... | collective-permute-start | bytes 2359304 | tf_op jit(solution)/shard_map/ppermute | solution.py:371
  53.7 27.9 %collective-permute-start.2 = (bf16[4,192,512]{2,1,0:T(8,128)(2,1)S(1)}, bf16[4,192,512]{2,1,0:T(8,128)(2,1)S(1)}, u32[]{:S(2)}, u32[]{:S(2)}) collective-permute-start(bf16[4,192,512]{2,1,0:T(8,128)(2,1)S(1)} %get-tuple-element.49.y_ref), channel_id=1, source_target_pairs={{0,4},{1,5},{2,6},{3,7},{4,0},{5,1},{6,2},{7,3},{8,12},{9,13},{10,... | collective-permute-start | bytes 2359304 | tf_op jit(solution)/shard_map/ppermute | solution.py:371
  80.1 10.7 %collective-permute-start.4 = (bf16[2,192,512]{2,1,0:T(8,128)(2,1)S(1)}, bf16[2,192,512]{2,1,0:T(8,128)(2,1)S(1)}, u32[]{:S(2)}, u32[]{:S(2)}) collective-permute-start(bf16[2,192,512]{2,1,0:T(8,128)(2,1)S(1)} %slice.9), channel_id=1, source_target_pairs={{0,4},{1,5},{2,6},{3,7},{4,0},{5,1},{6,2},{7,3},{8,12},{9,13},{10,... | collective-permute-start | bytes 1179656 | tf_op jit(solution)/shard_map/ppermute | solution.py:371
  81.6 10.4 %collective-permute-start.3 = (bf16[2,192,512]{2,1,0:T(8,128)(2,1)S(1)}, bf16[2,192,512]{2,1,0:T(8,128)(2,1)S(1)}, u32[]{:S(2)}, u32[]{:S(2)}) collective-permute-start(bf16[2,192,512]{2,1,0:T(8,128)(2,1)S(1)} %slice.8), channel_id=1, source_target_pairs={{0,2},{1,3},{2,0},{3,1},{4,6},{5,7},{6,4},{7,5},{8,10},{9,11},{10,... | collective-permute-start | bytes 1179656 | tf_op jit(solution)/shard_map/ppermute | solution.py:371
  95.0 4.5 %collective-permute-start.5 = (bf16[112,384]{1,0:T(8,128)(2,1)S(1)}, bf16[112,384]{1,0:T(8,128)(2,1)S(1)}, u32[]{:S(2)}, u32[]{:S(2)}) collective-permute-start(bf16[112,384]{1,0:T(8,128)(2,1)S(1)} %get-tuple-element.51), channel_id=1, source_target_pairs={{0,1},{1,0},{8,9},{9,8},{16,17},{17,16},{24,25},{25,24},{2,3},{3,2... | collective-permute-start | bytes 258056 | tf_op jit(solution)/shard_map/ppermute | solution.py:452
  95.1 8.0 %collective-permute-start.6 = (bf16[112,384]{1,0:T(8,128)(2,1)S(1)}, bf16[112,384]{1,0:T(8,128)(2,1)S(1)}, u32[]{:S(2)}, u32[]{:S(2)}) collective-permute-start(bf16[112,384]{1,0:T(8,128)(2,1)S(1)} %get-tuple-element.52), channel_id=1, source_target_pairs={{0,8},{1,9},{8,0},{9,1},{16,24},{17,25},{24,16},{25,17},{2,10},{3,... | collective-permute-start | bytes 258056 | tf_op jit(solution)/shard_map/ppermute | solution.py:452
  96.6 8.0 %collective-permute-start.7 = (bf16[112,384]{1,0:T(8,128)(2,1)S(1)}, bf16[112,384]{1,0:T(8,128)(2,1)S(1)}, u32[]{:S(2)}, u32[]{:S(2)}) collective-permute-start(bf16[112,384]{1,0:T(8,128)(2,1)S(1)} %get-tuple-element.53), channel_id=1, source_target_pairs={{0,9},{1,8},{8,1},{9,0},{16,25},{17,24},{24,17},{25,16},{2,11},{3,... | collective-permute-start | bytes 258056 | tf_op jit(solution)/shard_map/ppermute | solution.py:452
  97.0 7.7 %collective-permute-start.8 = (bf16[112,384]{1,0:T(8,128)(2,1)S(1)}, bf16[112,384]{1,0:T(8,128)(2,1)S(1)}, u32[]{:S(2)}, u32[]{:S(2)}) collective-permute-start(bf16[112,384]{1,0:T(8,128)(2,1)S(1)} %get-tuple-element.54), channel_id=1, source_target_pairs={{0,16},{1,17},{8,24},{9,25},{16,0},{17,1},{24,8},{25,9},{2,18},{3,... | collective-permute-start | bytes 258056 | tf_op jit(solution)/shard_map/ppermute | solution.py:452
  99.3 12.9 %collective-permute-start.9 = (bf16[112,384]{1,0:T(8,128)(2,1)S(1)}, bf16[112,384]{1,0:T(8,128)(2,1)S(1)}, u32[]{:S(2)}, u32[]{:S(2)}) collective-permute-start(bf16[112,384]{1,0:T(8,128)(2,1)S(1)} %get-tuple-element.55), channel_id=1, source_target_pairs={{0,17},{1,16},{8,25},{9,24},{16,1},{17,0},{24,9},{25,8},{2,19},{3,... | collective-permute-start | bytes 258056 | tf_op jit(solution)/shard_map/ppermute | solution.py:452
  99.6 12.7 %collective-permute-start.10 = (bf16[112,384]{1,0:T(8,128)(2,1)S(1)}, bf16[112,384]{1,0:T(8,128)(2,1)S(1)}, u32[]{:S(2)}, u32[]{:S(2)}) collective-permute-start(bf16[112,384]{1,0:T(8,128)(2,1)S(1)} %get-tuple-element.56), channel_id=1, source_target_pairs={{0,24},{1,25},{8,16},{9,17},{16,8},{17,9},{24,0},{25,1},{2,26},{3,... | collective-permute-start | bytes 258056 | tf_op jit(solution)/shard_map/ppermute | solution.py:452
  103.1 9.2 %collective-permute-start.11 = (bf16[112,384]{1,0:T(8,128)(2,1)S(1)}, bf16[112,384]{1,0:T(8,128)(2,1)S(1)}, u32[]{:S(2)}, u32[]{:S(2)}) collective-permute-start(bf16[112,384]{1,0:T(8,128)(2,1)S(1)} %get-tuple-element.57), channel_id=1, source_target_pairs={{0,25},{1,24},{8,17},{9,16},{16,9},{17,8},{24,1},{25,0},{2,27},{3,... | collective-permute-start | bytes 258056 | tf_op jit(solution)/shard_map/ppermute | solution.py:452

commit v9 on v8

--- a/solution.py
+++ b/solution.py
@@ -123,9 +123,10 @@
         stack_ref[band + cells :, columns] = part[0:band]
 
 
-def convolved(stack_ref, weight_ref, band, cells):
+def convolved(stack_ref, weight_ref, band, cells, copies):
     total = None
     for b in range(3):
+        copies[b].wait()
         channels = weight_ref.shape[2]
         tap = weight_ref[:, b].reshape(3 * channels, channels)
         term = jnp.dot(stack_ref[b * band : b * band + cells, :], tap, preferred_element_type=F32)
@@ -133,9 +134,10 @@
     return total
 
 
-def convolved_back(stack_ref, weight_ref, band, cells):
+def convolved_back(stack_ref, weight_ref, band, cells, copies):
     total = None
     for b in range(3):
+        copies[b].wait()
         tap = jnp.concatenate([weight_ref[2 - a, 2 - b] for a in range(3)], axis=1)
         term = lax.dot_general(
             stack_ref[b * band : b * band + cells, :],
@@ -183,16 +185,16 @@
     return copies
 
 
-def weights_kernel(one_ref, two_ref, one_out, two_out, sems):
-    for copy in fetched(((one_ref, one_out), (two_ref, two_out)), sems):
-        copy.wait()
+def by_tap(weight_ref, held_ref, sems, order):
+    return fetched([(weight_ref.at[:, b], held_ref.at[:, b]) for b in order], sems)
 
 
 def inner_kernel(band, step, place_ref, own_ref, one_ref, two_ref,
                  hidden_ref, pre_ref, mine_ref, give_ref,
-                 stack_ref, first_ref, slope_ref, turned_ref):
+                 one_held, two_held, stack_ref, first_ref, slope_ref, turned_ref, sems):
     x, y, core = place_ref[0], place_ref[1], place_ref[2]
     cells, channels = first_ref.shape
+    first_weight = by_tap(one_ref, one_held, sems.at[0], range(3))
     half, rows = channels // 2, 32
     deep = half // 4
 
@@ -205,7 +207,8 @@
 
     source = own_ref[:, 0].reshape(cells, channels)
     write_stack(source, stack_ref, band, step)
-    first_ref[...] = convolved(stack_ref, one_ref, band, cells)
+    first_ref[...] = convolved(stack_ref, one_held, band, cells, first_weight)
+    second_weight = by_tap(two_ref, two_held, sems.at[1], (2, 1, 0))
     turn(0, source)
 
     def activate(at, carry):
@@ -222,7 +225,7 @@
     cot = own_ref[:, 1].reshape(cells, channels)
     write_stack(cot, stack_ref, band, step)
     turn(3, cot)
-    pre_ref[...] = (slope_ref[...] * convolved_back(stack_ref, two_ref, band, cells)).astype(BF16)
+    pre_ref[...] = (slope_ref[...] * convolved_back(stack_ref, two_held, band, cells, second_weight)).astype(BF16)
     turn(2, pre_ref[...])
 
     for ref, of in ((mine_ref, core), (give_ref, 1 - core)):
@@ -240,15 +243,18 @@
         y_ref[2 + at] = ref[3]
 
 
-def outer_kernel(band, step, own_ref, hidden_ref, pre_ref, one_ref, two_ref, out_ref, stack_ref):
+def outer_kernel(band, step, own_ref, hidden_ref, pre_ref, one_ref, two_ref, out_ref,
+                 one_held, two_held, stack_ref, sems):
     cells, channels = hidden_ref.shape
     shape = (out_ref.shape[0],) + out_ref.shape[2:]
+    second_weight = by_tap(two_ref, two_held, sems.at[1], range(3))
     write_stack(hidden_ref[...], stack_ref, band, step)
-    second = convolved(stack_ref, two_ref, band, cells)
+    second = convolved(stack_ref, two_held, band, cells, second_weight)
+    first_weight = by_tap(one_ref, one_held, sems.at[0], (2, 1, 0))
     source = own_ref[:, 0].reshape(cells, channels)
     out_ref[:, 0] = (source.astype(F32) + second).astype(BF16).reshape(shape)
     write_stack(pre_ref[...], stack_ref, band, step)
-    back = convolved_back(stack_ref, one_ref, band, cells)
+    back = convolved_back(stack_ref, one_held, band, cells, first_weight)
     cot = own_ref[:, 1].reshape(cells, channels)
     out_ref[:, 1] = (cot.astype(F32) + back).astype(BF16).reshape(shape)
 
@@ -384,22 +390,23 @@
     )
     own = lax.all_to_all(own, every, 0, 0, tiled=True)
     place = jnp.stack([lax.axis_index(axis) for axis in ("x", "y", "core", "z")]).astype(jnp.int32)
-    one, two = kernel(
-        weights_kernel,
-        [hbm] * 2,
-        [pltpu.with_memory_space_constraint(w, pltpu.HBM) for w in (conv1_weight, conv2_weight)],
-        (weights, weights),
-        [pltpu.SemaphoreType.DMA((2,))],
-        10**6,
-        10,
-    )
+    one, two = (pltpu.with_memory_space_constraint(w, pltpu.HBM) for w in (conv1_weight, conv2_weight))
+    taps = pltpu.SemaphoreType.DMA((2, 3))
     pieces = held(4, half, cells)
     hidden, pre_grad, mine, give = kernel(
         functools.partial(inner_kernel, band, step),
-        [smem] + [vmem] * 3,
+        [smem, vmem, hbm, hbm],
         (place, own, one, two),
         (held(cells, channels), held(cells, channels), pieces, pieces),
-        [stack, held(cells, channels, kind=F32), held(cells, channels, kind=F32), held(8, half, cells)],
+        [
+            weights,
+            weights,
+            stack,
+            held(cells, channels, kind=F32),
+            held(cells, channels, kind=F32),
+            held(8, half, cells),
+            taps,
+        ],
         2 * flops,
         10,
     )
@@ -407,17 +414,18 @@
         join_kernel, [vmem] * 2, (mine, passed(give, 0, 0, 1)), (pieces, pieces), [], 10**6, 4
     )
     x_got, y_got = passed(x_given, 1, 0, 0), passed(y_given, 0, 1, 0)
-    far = (passed(y_got[:2], 1, 0, 0), passed(x_got[:2], 0, 1, 0))
     hidden, pre_grad, x_given = lax.optimization_barrier((hidden, pre_grad, x_given))
     fields = kernel(
         functools.partial(outer_kernel, band, step),
-        [vmem] * 5,
+        [vmem] * 3 + [hbm] * 2,
         (own, hidden, pre_grad, one, two),
         dealt,
-        [stack],
+        [weights, weights, stack, taps],
         2 * flops,
         9,
     )
+    fields, x_got, y_got = lax.optimization_barrier((fields, x_got, y_got))
+    far = (passed(y_got[:2], 1, 0, 0), passed(x_got[:2], 0, 1, 0))
     fields = lax.all_to_all(fields, every, 0, 0, tiled=True)
     output, input_grad = kernel(
         functools.partial(gather_kernel, step), [vmem], (fields,), (shaped(*inputs.shape),) * 2, [], 10**9, 3
@@ -429,7 +437,7 @@
         (x_given, y_given, x_got, y_got),
         sums,
         [held(3 * half, 6 * cells), held(3, half, 6 * cells)],
-        2 * flops,
+        5 * flops,
         6,
     )
     terms = kernel(
@@ -444,7 +452,7 @@
             held(8, height, channels),
             pltpu.SemaphoreType.DMA((8,)),
         ],
-        flops,
+        5 * flops,
         4,
     )
     parts = list(terms)

time: 116 us -> 109 us (0.940)
  local copies, waits for them, and re-layouts: 6.62 us -> 1.19 us
  waiting for transfers between devices: 56.2 us -> 52.5 us
  Pallas kernels: 25.4 us -> 27.5 us
    ppermute x5, waiting for transfers between devices: 33.7 us -> 24.2 us  [passed(): return lax.ppermute(piece, ('y', 'x', 'core'), pairs)]
    all_to_all x1, waiting for transfers between devices: 14.9 us -> 20.5 us  [fast_local(): own = lax.all_to_all(own, every, 0, 0, tiled=True)]
    unnamed x12 -> x4, local copies, waits for them, and re-layouts: 6.57 us -> 1.14 us
    pallas_call x9 -> x8, Pallas kernels: 25.4 us -> 27.5 us  [kernel(): pl.pallas_call(body, out_shape=out_shape, in_specs=specs, out_specs=jax.t...]
  transfers between devices with their start and end apart: 14 -> 14, of which waited for: 6 -> 7; matrix products, arithmetic and copies ran while one was open for 0% -> 0% of each run, Pallas kernels for 9% -> 14%
where the time goes in v9:
time: 109 us; the launch traced here: 107 us
  waiting for transfers between devices  52.5 us (48%)
  Pallas kernels  27.5 us (25%)
  starting transfers between devices  24.7 us (23%)
  local copies, waits for them, and re-layouts  1.19 us (1%)
    pallas_call x8, Pallas kernels, kernel(): pl.pallas_call(body, out_shape=out_shape, in_specs=specs, out_specs=jax.t...  27.5 us
    ppermute x5, waiting for transfers between devices, passed(): return lax.ppermute(piece, ('y', 'x', 'core'), pairs)  24.2 us
    all_to_all x1, waiting for transfers between devices, fast_local(): own = lax.all_to_all(own, every, 0, 0, tiled=True)  20.5 us
    ppermute x7, starting transfers between devices, fast_local(): lax.ppermute(terms[away], ('z', 'core'), [(i, i ^ away) for i in range(8)])  8.29 us
    ppermute x7, waiting for transfers between devices, fast_local(): lax.ppermute(terms[away], ('z', 'core'), [(i, i ^ away) for i in range(8)])  7.78 us
    all_to_all x1, starting transfers between devices, fast_local(): own = lax.all_to_all(own, every, 0, 0, tiled=True)  7.3 us
    ppermute x5, starting transfers between devices, passed(): return lax.ppermute(piece, ('y', 'x', 'core'), pairs)  6.22 us
    all_to_all x1, starting transfers between devices, fast_local(): fields = lax.all_to_all(fields, every, 0, 0, tiled=True)  2.91 us
  transfers between devices with their start and end apart: 14, of which 7 were waited for; matrix products, arithmetic and copies ran while one was open for 0% of the time, Pallas kernels for 14%

profile of v9, /device:TPU:0, one launch (start us, length us, event | category | flops | bytes accessed | tf_op | source)
XLA Modules:
  0.0 106.7 jit_solution(17632660304754568768)
XLA Ops:
  0.6 2.8 %shard_map.75 = bf16[32,2,16,384]{3,2,1,0:T(8,128)(2,1)} custom-call(bf16[8,64,384]{2,1,0:T(8,128)(2,1)} %inputs_ref.1, bf16[8,64,384]{2,1,0:T(8,128)(2,1)} %cot_ref.1), custom_call_target="tpu_custom_call" | custom-call | flops 1000000000 | bytes 3145728 | tf_op jit(solution)/shard_map/pallas_call | solution.py:365
  3.4 7.3 %all-to-all-start = ((bf16[32,2,16,384]{3,2,1,0:T(8,128)(2,1)}), bf16[32,2,16,384]{3,2,1,0:T(8,128)(2,1)S(1)}, u32[]{:S(2)}, u32[]{:S(2)}) async-start(bf16[32,2,16,384]{3,2,1,0:T(8,128)(2,1)} %shard_map.75), calls=%async_computation | async-start | bytes 1572864 | tf_op jit(solution)/shard_map/all_to_all | solution.py:391
  10.8 20.5 %all-to-all-done.own_ref = bf16[32,2,16,384]{3,2,1,0:T(8,128)(2,1)S(1)} async-done(((bf16[32,2,16,384]{3,2,1,0:T(8,128)(2,1)}), bf16[32,2,16,384]{3,2,1,0:T(8,128)(2,1)S(1)}, u32[]{:S(2)}, u32[]{:S(2)}) %all-to-all-start) | async-done | bytes 786464 | tf_op jit(solution)/shard_map/all_to_all | solution.py:391
  31.4 7.9 %shard_map.76 = (bf16[512,384]{1,0:T(8,128)(2,1)S(1)}, bf16[512,384]{1,0:T(8,128)(2,1)S(1)}, bf16[4,192,512]{2,1,0:T(8,128)(2,1)S(1)}, bf16[4,192,512]{2,1,0:T(8,128)(2,1)S(1)}) custom-call(s32[4]{0:T(128)S(1)} %pad_add_fusion.place_ref, bf16[32,2,16,384]{3,2,1,0:T(8,128)(2,1)S(1)} %all-to-all-done.own_ref, bf16[3,3,384,384]{3,2,1,0:T(8,128)(2,1)} %one_ref.3, ...), custom_call_target="tpu_custom_call" | custom-call | flops 2717908992 | bytes 10485760 | tf_op jit(solution)/shard_map/pallas_call | solution.py:365
  39.3 2.3 %collective-permute-done.got_ref = bf16[4,192,512]{2,1,0:T(8,128)(2,1)S(1)} collective-permute-done((bf16[4,192,512]{2,1,0:T(8,128)(2,1)S(1)}, bf16[4,192,512]{2,1,0:T(8,128)(2,1)S(1)}, u32[]{:S(2)}, u32[]{:S(2)}) %collective-permute-start) | collective-permute-done | bytes 786464 | tf_op jit(solution)/shard_map/ppermute | solution.py:377
  41.7 1.5 %collective-permute-start.1 = (bf16[4,192,512]{2,1,0:T(8,128)(2,1)S(1)}, bf16[4,192,512]{2,1,0:T(8,128)(2,1)S(1)}, u32[]{:S(2)}, u32[]{:S(2)}) collective-permute-start(bf16[4,192,512]{2,1,0:T(8,128)(2,1)S(1)} %get-tuple-element.49.x_ref), channel_id=1, source_target_pairs={{0,2},{1,3},{2,0},{3,1},{4,6},{5,7},{6,4},{7,5},{8,10},{9,11},{10,... | collective-permute-start | bytes 2359304 | tf_op jit(solution)/shard_map/ppermute | solution.py:377
  43.2 1.5 %collective-permute-start.2 = (bf16[4,192,512]{2,1,0:T(8,128)(2,1)S(1)}, bf16[4,192,512]{2,1,0:T(8,128)(2,1)S(1)}, u32[]{:S(2)}, u32[]{:S(2)}) collective-permute-start(bf16[4,192,512]{2,1,0:T(8,128)(2,1)S(1)} %get-tuple-element.45.y_ref), channel_id=1, source_target_pairs={{0,4},{1,5},{2,6},{3,7},{4,0},{5,1},{6,2},{7,3},{8,12},{9,13},{10,... | collective-permute-start | bytes 2359304 | tf_op jit(solution)/shard_map/ppermute | solution.py:377
  44.7 7.7 %shard_map.78 = bf16[32,2,16,384]{3,2,1,0:T(8,128)(2,1)} custom-call(bf16[32,2,16,384]{3,2,1,0:T(8,128)(2,1)S(1)} %all-to-all-done.own_ref, bf16[512,384]{1,0:T(8,128)(2,1)S(1)} %get-tuple-element.43.hidden_ref, bf16[512,384]{1,0:T(8,128)(2,1)S(1)} %get-tuple-element.44.pre_ref, bf16[3,3,384,384]{3,2,1,0:T(8,128)(2,1)} %one_ref.3, ...), custom_call_target="tpu_custom_call" | custom-call | flops 2717908992 | bytes 9437184 | tf_op jit(solution)/shard_map/pallas_call | solution.py:365
  52.4 9.0 %collective-permute-done.1.x_got_ref = bf16[4,192,512]{2,1,0:T(8,128)(2,1)S(1)} collective-permute-done((bf16[4,192,512]{2,1,0:T(8,128)(2,1)S(1)}, bf16[4,192,512]{2,1,0:T(8,128)(2,1)S(1)}, u32[]{:S(2)}, u32[]{:S(2)}) %collective-permute-start.1) | collective-permute-done | bytes 786464 | tf_op jit(solution)/shard_map/ppermute | solution.py:377
  61.4 1.2 %collective-permute-done.2.y_got_ref = bf16[4,192,512]{2,1,0:T(8,128)(2,1)S(1)} collective-permute-done((bf16[4,192,512]{2,1,0:T(8,128)(2,1)S(1)}, bf16[4,192,512]{2,1,0:T(8,128)(2,1)S(1)}, u32[]{:S(2)}, u32[]{:S(2)}) %collective-permute-start.2) | collective-permute-done | bytes 786464 | tf_op jit(solution)/shard_map/ppermute | solution.py:377
  62.6 2.9 %all-to-all-start.1 = ((bf16[32,2,16,384]{3,2,1,0:T(8,128)(2,1)}), bf16[32,2,16,384]{3,2,1,0:T(8,128)(2,1)S(1)}, u32[]{:S(2)}, u32[]{:S(2)}) async-start(bf16[32,2,16,384]{3,2,1,0:T(8,128)(2,1)} %shard_map.78), calls=%async_computation.1 | async-start | bytes 1572864 | tf_op jit(solution)/shard_map/all_to_all | solution.py:429
  65.6 1.7 %collective-permute-start.4 = (bf16[2,192,512]{2,1,0:T(8,128)(2,1)S(1)}, bf16[2,192,512]{2,1,0:T(8,128)(2,1)S(1)}, u32[]{:S(2)}, u32[]{:S(2)}) collective-permute-start(bf16[2,192,512]{2,1,0:T(8,128)(2,1)S(1)} %slice.7), channel_id=1, source_target_pairs={{0,4},{1,5},{2,6},{3,7},{4,0},{5,1},{6,2},{7,3},{8,12},{9,13},{10,... | collective-permute-start | bytes 1179656 | tf_op jit(solution)/shard_map/ppermute | solution.py:377
  67.2 1.5 %collective-permute-start.3 = (bf16[2,192,512]{2,1,0:T(8,128)(2,1)S(1)}, bf16[2,192,512]{2,1,0:T(8,128)(2,1)S(1)}, u32[]{:S(2)}, u32[]{:S(2)}) collective-permute-start(bf16[2,192,512]{2,1,0:T(8,128)(2,1)S(1)} %slice.6), channel_id=1, source_target_pairs={{0,2},{1,3},{2,0},{3,1},{4,6},{5,7},{6,4},{7,5},{8,10},{9,11},{10,... | collective-permute-start | bytes 1179656 | tf_op jit(solution)/shard_map/ppermute | solution.py:377
  68.7 1.1 %copy-done.1 = bf16[4,192,512]{2,1,0:T(8,128)(2,1)S(1)} copy-done((bf16[4,192,512]{2,1,0:T(8,128)(2,1)S(1)}, bf16[4,192,512]{2,1,0:T(8,128)(2,1)}, u32[]{:S(2)}) %copy-start.1) | copy-done | bytes 786456
  69.8 3.2 %shard_map.80.near_ref = f32[3,576,192]{2,1,0:T(8,128)S(1)} custom-call(bf16[4,192,512]{2,1,0:T(8,128)(2,1)S(1)} %get-tuple-element.49.x_ref, bf16[4,192,512]{2,1,0:T(8,128)(2,1)S(1)} %copy-done.1, bf16[4,192,512]{2,1,0:T(8,128)(2,1)S(1)} %collective-permute-done.1.x_got_ref, bf16[4,192,512]{2,1,0:T(8,128)(2,1)S(1)} %collective-permute-done.2.y_got_ref), custom_call_target="tpu_custom_call" | custom-call | flops 6794772480 | bytes 6291456 | tf_op jit(solution)/shard_map/pallas_call | solution.py:365
  73.0 11.4 %collective-permute-done.4.right_ref = bf16[2,192,512]{2,1,0:T(8,128)(2,1)S(1)} collective-permute-done((bf16[2,192,512]{2,1,0:T(8,128)(2,1)S(1)}, bf16[2,192,512]{2,1,0:T(8,128)(2,1)S(1)}, u32[]{:S(2)}, u32[]{:S(2)}) %collective-permute-start.4) | collective-permute-done | bytes 393248 | tf_op jit(solution)/shard_map/ppermute | solution.py:377
  84.7 2.9 %shard_map.81 = (bf16[112,384]{1,0:T(8,128)(2,1)S(1)}, bf16[112,384]{1,0:T(8,128)(2,1)S(1)}, bf16[112,384]{1,0:T(8,128)(2,1)S(1)}, bf16[112,384]{1,0:T(8,128)(2,...) custom-call(s32[4]{0:T(128)S(1)} %pad_add_fusion.place_ref, ...), custom_call_target="tpu_custom_call" | custom-call | flops 6794772480 | bytes 4194304 | tf_op jit(solution)/shard_map/pallas_call | solution.py:365
  87.8 1.4 %collective-permute-start.6 = (bf16[112,384]{1,0:T(8,128)(2,1)S(1)}, bf16[112,384]{1,0:T(8,128)(2,1)S(1)}, u32[]{:S(2)}, u32[]{:S(2)}) collective-permute-start(bf16[112,384]{1,0:T(8,128)(2,1)S(1)} %get-tuple-element.54), channel_id=1, source_target_pairs={{0,8},{1,9},{8,0},{9,1},{16,24},{17,25},{24,16},{25,17},{2,10},{3,... | collective-permute-start | bytes 258056 | tf_op jit(solution)/shard_map/ppermute | solution.py:460
  89.2 0.5 collective-permute-start.7
  89.6 2.7 %collective-permute-start.8 = (bf16[112,384]{1,0:T(8,128)(2,1)S(1)}, bf16[112,384]{1,0:T(8,128)(2,1)S(1)}, u32[]{:S(2)}, u32[]{:S(2)}) collective-permute-start(bf16[112,384]{1,0:T(8,128)(2,1)S(1)} %get-tuple-element.56), channel_id=1, source_target_pairs={{0,16},{1,17},{8,24},{9,25},{16,0},{17,1},{24,8},{25,9},{2,18},{3,... | collective-permute-start | bytes 258056 | tf_op jit(solution)/shard_map/ppermute | solution.py:460
  92.3 3.6 %collective-permute-start.10 = (bf16[112,384]{1,0:T(8,128)(2,1)S(1)}, bf16[112,384]{1,0:T(8,128)(2,1)S(1)}, u32[]{:S(2)}, u32[]{:S(2)}) collective-permute-start(bf16[112,384]{1,0:T(8,128)(2,1)S(1)} %get-tuple-element.58), channel_id=1, source_target_pairs={{0,24},{1,25},{8,16},{9,17},{16,8},{17,9},{24,0},{25,1},{2,26},{3,... | collective-permute-start | bytes 258056 | tf_op jit(solution)/shard_map/ppermute | solution.py:460
  96.0 1.5 %shard_map.79 = (bf16[8,64,384]{2,1,0:T(8,128)(2,1)}, bf16[8,64,384]{2,1,0:T(8,128)(2,1)}) custom-call(bf16[32,2,16,384]{3,2,1,0:T(8,128)(2,1)S(1)} %all-to-all-done.1.fields_ref), custom_call_target="tpu_custom_call" | custom-call | flops 1000000000 | bytes 3145728 | tf_op jit(solution)/shard_map/pallas_call | solution.py:365
  97.5 7.8 %collective-permute-done.9.refs_5_ = bf16[112,384]{1,0:T(8,128)(2,1)S(1)} collective-permute-done((bf16[112,384]{1,0:T(8,128)(2,1)S(1)}, bf16[112,384]{1,0:T(8,128)(2,1)S(1)}, u32[]{:S(2)}, u32[]{:S(2)}) %collective-permute-start.9) | collective-permute-done | bytes 86048 | tf_op jit(solution)/shard_map/ppermute | solution.py:460
  105.2 1.5 %shard_map.82 = (f32[3,3,48,96]{3,2,1,0:T(8,128)}, f32[3,3,48,96]{3,2,1,0:T(8,128)}) custom-call(s32[4]{0:T(128)S(1)} %pad_add_fusion.place_ref, bf16[112,384]{1,0:T(8,128)(2,1)S(1)} %get-tuple-element.62.refs_0_, bf16[112,384]{1,0:T(8,128)(2,1)S(1)} %collective-permute-done.5.refs_1_, bf16[112,384]{1,0:T(8,128)(2,1)S(1)} %collective-permute-done.6.refs_2_, ...), custom_call_target="tpu_custom_call" | custom-call | flops 1000000 | bytes 2097152 | tf_op jit(solution)/shard_map/pallas_call | solution.py:365
  (19 shorter events, 0.8 us)
Async XLA Ops:
  3.4 27.9 %all-to-all-start = ((bf16[32,2,16,384]{3,2,1,0:T(8,128)(2,1)}), bf16[32,2,16,384]{3,2,1,0:T(8,128)(2,1)S(1)}, u32[]{:S(2)}, u32[]{:S(2)}) async-start(bf16[32,2,16,384]{3,2,1,0:T(8,128)(2,1)} %shard_map.75), calls=%async_computation | async-start | bytes 1572864 | tf_op jit(solution)/shard_map/all_to_all | solution.py:391
  39.2 2.4 %collective-permute-start = (bf16[4,192,512]{2,1,0:T(8,128)(2,1)S(1)}, bf16[4,192,512]{2,1,0:T(8,128)(2,1)S(1)}, u32[]{:S(2)}, u32[]{:S(2)}) collective-permute-start(bf16[4,192,512]{2,1,0:T(8,128)(2,1)S(1)} %get-tuple-element.41), channel_id=1, source_target_pairs={{0,1},{1,0},{2,3},{3,2},{4,5},{5,4},{6,7},{7,6},{8,9},{9,8},{10,11... | collective-permute-start | bytes 2359304 | tf_op jit(solution)/shard_map/ppermute | solution.py:377
  41.7 10.7 %copy-start = (bf16[4,192,512]{2,1,0:T(8,128)(2,1)}, bf16[4,192,512]{2,1,0:T(8,128)(2,1)S(1)}, u32[]{:S(2)}) copy-start(bf16[4,192,512]{2,1,0:T(8,128)(2,1)S(1)} %get-tuple-element.45.y_ref) | copy-start | bytes 2359300
  41.7 19.6 %collective-permute-start.1 = (bf16[4,192,512]{2,1,0:T(8,128)(2,1)S(1)}, bf16[4,192,512]{2,1,0:T(8,128)(2,1)S(1)}, u32[]{:S(2)}, u32[]{:S(2)}) collective-permute-start(bf16[4,192,512]{2,1,0:T(8,128)(2,1)S(1)} %get-tuple-element.49.x_ref), channel_id=1, source_target_pairs={{0,2},{1,3},{2,0},{3,1},{4,6},{5,7},{6,4},{7,5},{8,10},{9,11},{10,... | collective-permute-start | bytes 2359304 | tf_op jit(solution)/shard_map/ppermute | solution.py:377
  43.2 19.3 %collective-permute-start.2 = (bf16[4,192,512]{2,1,0:T(8,128)(2,1)S(1)}, bf16[4,192,512]{2,1,0:T(8,128)(2,1)S(1)}, u32[]{:S(2)}, u32[]{:S(2)}) collective-permute-start(bf16[4,192,512]{2,1,0:T(8,128)(2,1)S(1)} %get-tuple-element.45.y_ref), channel_id=1, source_target_pairs={{0,4},{1,5},{2,6},{3,7},{4,0},{5,1},{6,2},{7,3},{8,12},{9,13},{10,... | collective-permute-start | bytes 2359304 | tf_op jit(solution)/shard_map/ppermute | solution.py:377
  62.6 33.4 %all-to-all-start.1 = ((bf16[32,2,16,384]{3,2,1,0:T(8,128)(2,1)}), bf16[32,2,16,384]{3,2,1,0:T(8,128)(2,1)S(1)}, u32[]{:S(2)}, u32[]{:S(2)}) async-start(bf16[32,2,16,384]{3,2,1,0:T(8,128)(2,1)} %shard_map.78), calls=%async_computation.1 | async-start | bytes 1572864 | tf_op jit(solution)/shard_map/all_to_all | solution.py:429
  65.6 18.9 %collective-permute-start.4 = (bf16[2,192,512]{2,1,0:T(8,128)(2,1)S(1)}, bf16[2,192,512]{2,1,0:T(8,128)(2,1)S(1)}, u32[]{:S(2)}, u32[]{:S(2)}) collective-permute-start(bf16[2,192,512]{2,1,0:T(8,128)(2,1)S(1)} %slice.7), channel_id=1, source_target_pairs={{0,4},{1,5},{2,6},{3,7},{4,0},{5,1},{6,2},{7,3},{8,12},{9,13},{10,... | collective-permute-start | bytes 1179656 | tf_op jit(solution)/shard_map/ppermute | solution.py:377
  67.2 17.5 %collective-permute-start.3 = (bf16[2,192,512]{2,1,0:T(8,128)(2,1)S(1)}, bf16[2,192,512]{2,1,0:T(8,128)(2,1)S(1)}, u32[]{:S(2)}, u32[]{:S(2)}) collective-permute-start(bf16[2,192,512]{2,1,0:T(8,128)(2,1)S(1)} %slice.6), channel_id=1, source_target_pairs={{0,2},{1,3},{2,0},{3,1},{4,6},{5,7},{6,4},{7,5},{8,10},{9,11},{10,... | collective-permute-start | bytes 1179656 | tf_op jit(solution)/shard_map/ppermute | solution.py:377
  68.7 1.1 %copy-start.1 = (bf16[4,192,512]{2,1,0:T(8,128)(2,1)S(1)}, bf16[4,192,512]{2,1,0:T(8,128)(2,1)}, u32[]{:S(2)}) copy-start(bf16[4,192,512]{2,1,0:T(8,128)(2,1)} %copy-done) | copy-start | bytes 2359300
  87.7 4.6 %collective-permute-start.5 = (bf16[112,384]{1,0:T(8,128)(2,1)S(1)}, bf16[112,384]{1,0:T(8,128)(2,1)S(1)}, u32[]{:S(2)}, u32[]{:S(2)}) collective-permute-start(bf16[112,384]{1,0:T(8,128)(2,1)S(1)} %get-tuple-element.53), channel_id=1, source_target_pairs={{0,1},{1,0},{8,9},{9,8},{16,17},{17,16},{24,25},{25,24},{2,3},{3,2... | collective-permute-start | bytes 258056 | tf_op jit(solution)/shard_map/ppermute | solution.py:460
  87.8 8.1 %collective-permute-start.6 = (bf16[112,384]{1,0:T(8,128)(2,1)S(1)}, bf16[112,384]{1,0:T(8,128)(2,1)S(1)}, u32[]{:S(2)}, u32[]{:S(2)}) collective-permute-start(bf16[112,384]{1,0:T(8,128)(2,1)S(1)} %get-tuple-element.54), channel_id=1, source_target_pairs={{0,8},{1,9},{8,0},{9,1},{16,24},{17,25},{24,16},{25,17},{2,10},{3,... | collective-permute-start | bytes 258056 | tf_op jit(solution)/shard_map/ppermute | solution.py:460
  89.2 8.3 %collective-permute-start.7 = (bf16[112,384]{1,0:T(8,128)(2,1)S(1)}, bf16[112,384]{1,0:T(8,128)(2,1)S(1)}, u32[]{:S(2)}, u32[]{:S(2)}) collective-permute-start(bf16[112,384]{1,0:T(8,128)(2,1)S(1)} %get-tuple-element.55), channel_id=1, source_target_pairs={{0,9},{1,8},{8,1},{9,0},{16,25},{17,24},{24,17},{25,16},{2,11},{3,... | collective-permute-start | bytes 258056 | tf_op jit(solution)/shard_map/ppermute | solution.py:460
  89.6 7.8 %collective-permute-start.8 = (bf16[112,384]{1,0:T(8,128)(2,1)S(1)}, bf16[112,384]{1,0:T(8,128)(2,1)S(1)}, u32[]{:S(2)}, u32[]{:S(2)}) collective-permute-start(bf16[112,384]{1,0:T(8,128)(2,1)S(1)} %get-tuple-element.56), channel_id=1, source_target_pairs={{0,16},{1,17},{8,24},{9,25},{16,0},{17,1},{24,8},{25,9},{2,18},{3,... | collective-permute-start | bytes 258056 | tf_op jit(solution)/shard_map/ppermute | solution.py:460
  92.3 12.9 %collective-permute-start.9 = (bf16[112,384]{1,0:T(8,128)(2,1)S(1)}, bf16[112,384]{1,0:T(8,128)(2,1)S(1)}, u32[]{:S(2)}, u32[]{:S(2)}) collective-permute-start(bf16[112,384]{1,0:T(8,128)(2,1)S(1)} %get-tuple-element.57), channel_id=1, source_target_pairs={{0,17},{1,16},{8,25},{9,24},{16,1},{17,0},{24,9},{25,8},{2,19},{3,... | collective-permute-start | bytes 258056 | tf_op jit(solution)/shard_map/ppermute | solution.py:460
  92.3 12.9 %collective-permute-start.10 = (bf16[112,384]{1,0:T(8,128)(2,1)S(1)}, bf16[112,384]{1,0:T(8,128)(2,1)S(1)}, u32[]{:S(2)}, u32[]{:S(2)}) collective-permute-start(bf16[112,384]{1,0:T(8,128)(2,1)S(1)} %get-tuple-element.58), channel_id=1, source_target_pairs={{0,24},{1,25},{8,16},{9,17},{16,8},{17,9},{24,0},{25,1},{2,26},{3,... | collective-permute-start | bytes 258056 | tf_op jit(solution)/shard_map/ppermute | solution.py:460
  95.9 9.4 %collective-permute-start.11 = (bf16[112,384]{1,0:T(8,128)(2,1)S(1)}, bf16[112,384]{1,0:T(8,128)(2,1)S(1)}, u32[]{:S(2)}, u32[]{:S(2)}) collective-permute-start(bf16[112,384]{1,0:T(8,128)(2,1)S(1)} %get-tuple-element.59), channel_id=1, source_target_pairs={{0,25},{1,24},{8,17},{9,16},{16,9},{17,8},{24,1},{25,0},{2,27},{3,... | collective-permute-start | bytes 258056 | tf_op jit(solution)/shard_map/ppermute | solution.py:460

commit v10 on v9

--- a/solution.py
+++ b/solution.py
@@ -123,10 +123,9 @@
         stack_ref[band + cells :, columns] = part[0:band]
 
 
-def convolved(stack_ref, weight_ref, band, cells, copies):
+def convolved(stack_ref, weight_ref, band, cells):
     total = None
     for b in range(3):
-        copies[b].wait()
         channels = weight_ref.shape[2]
         tap = weight_ref[:, b].reshape(3 * channels, channels)
         term = jnp.dot(stack_ref[b * band : b * band + cells, :], tap, preferred_element_type=F32)
@@ -134,10 +133,9 @@
     return total
 
 
-def convolved_back(stack_ref, weight_ref, band, cells, copies):
+def convolved_back(stack_ref, weight_ref, band, cells):
     total = None
     for b in range(3):
-        copies[b].wait()
         tap = jnp.concatenate([weight_ref[2 - a, 2 - b] for a in range(3)], axis=1)
         term = lax.dot_general(
             stack_ref[b * band : b * band + cells, :],
@@ -185,16 +183,12 @@
     return copies
 
 
-def by_tap(weight_ref, held_ref, sems, order):
-    return fetched([(weight_ref.at[:, b], held_ref.at[:, b]) for b in order], sems)
-
-
 def inner_kernel(band, step, place_ref, own_ref, one_ref, two_ref,
                  hidden_ref, pre_ref, mine_ref, give_ref,
-                 one_held, two_held, stack_ref, first_ref, slope_ref, turned_ref, sems):
+                 one_held, two_held, stack_ref, cot_stack_ref, first_ref, up_ref, slope_ref, turned_ref, sems):
     x, y, core = place_ref[0], place_ref[1], place_ref[2]
     cells, channels = first_ref.shape
-    first_weight = by_tap(one_ref, one_held, sems.at[0], range(3))
+    fetch = fetched(((one_ref, one_held),), sems.at[0])
     half, rows = channels // 2, 32
     deep = half // 4
 
@@ -207,25 +201,24 @@
 
     source = own_ref[:, 0].reshape(cells, channels)
     write_stack(source, stack_ref, band, step)
-    first_ref[...] = convolved(stack_ref, one_held, band, cells, first_weight)
-    second_weight = by_tap(two_ref, two_held, sems.at[1], (2, 1, 0))
+    fetch[0].wait()
+    later = fetched(((two_ref, two_held),), sems.at[1])[0]
+    first_ref[...] = convolved(stack_ref, one_held, band, cells)
+    cot = own_ref[:, 1].reshape(cells, channels)
+    write_stack(cot, cot_stack_ref, band, step)
     turn(0, source)
-
-    def activate(at, carry):
-        span = pl.ds(pl.multiple_of(at * rows, rows), rows)
+    turn(3, cot)
+    later.wait()
+    up_ref[...] = convolved_back(cot_stack_ref, two_held, band, cells)
+    for begin in range(0, cells, rows):
+        span = slice(begin, begin + rows)
         first = first_ref[span, :]
         cdf = 0.5 * (1.0 + lax.erf(first * (0.5**0.5)))
         density = jnp.exp(-0.5 * first * first) * ((2.0 * jnp.pi) ** -0.5)
         hidden_ref[span, :] = (first * cdf).astype(BF16)
         slope_ref[span, :] = cdf + first * density
-        return carry
-
-    lax.fori_loop(0, cells // rows, activate, 0)
     turn(1, hidden_ref[...])
-    cot = own_ref[:, 1].reshape(cells, channels)
-    write_stack(cot, stack_ref, band, step)
-    turn(3, cot)
-    pre_ref[...] = (slope_ref[...] * convolved_back(stack_ref, two_held, band, cells, second_weight)).astype(BF16)
+    pre_ref[...] = (slope_ref[...] * up_ref[...]).astype(BF16)
     turn(2, pre_ref[...])
 
     for ref, of in ((mine_ref, core), (give_ref, 1 - core)):
@@ -247,14 +240,16 @@
                  one_held, two_held, stack_ref, sems):
     cells, channels = hidden_ref.shape
     shape = (out_ref.shape[0],) + out_ref.shape[2:]
-    second_weight = by_tap(two_ref, two_held, sems.at[1], range(3))
+    fetch = fetched(((two_ref, two_held),), sems.at[1])[0]
+    later = fetched(((one_ref, one_held),), sems.at[0])[0]
     write_stack(hidden_ref[...], stack_ref, band, step)
-    second = convolved(stack_ref, two_held, band, cells, second_weight)
-    first_weight = by_tap(one_ref, one_held, sems.at[0], (2, 1, 0))
+    fetch.wait()
+    second = convolved(stack_ref, two_held, band, cells)
     source = own_ref[:, 0].reshape(cells, channels)
     out_ref[:, 0] = (source.astype(F32) + second).astype(BF16).reshape(shape)
     write_stack(pre_ref[...], stack_ref, band, step)
-    back = convolved_back(stack_ref, one_held, band, cells, first_weight)
+    later.wait()
+    back = convolved_back(stack_ref, one_held, band, cells)
     cot = own_ref[:, 1].reshape(cells, channels)
     out_ref[:, 1] = (cot.astype(F32) + back).astype(BF16).reshape(shape)
 
@@ -391,7 +386,7 @@
     own = lax.all_to_all(own, every, 0, 0, tiled=True)
     place = jnp.stack([lax.axis_index(axis) for axis in ("x", "y", "core", "z")]).astype(jnp.int32)
     one, two = (pltpu.with_memory_space_constraint(w, pltpu.HBM) for w in (conv1_weight, conv2_weight))
-    taps = pltpu.SemaphoreType.DMA((2, 3))
+    taps = pltpu.SemaphoreType.DMA((2, 1))
     pieces = held(4, half, cells)
     hidden, pre_grad, mine, give = kernel(
         functools.partial(inner_kernel, band, step),
@@ -402,6 +397,8 @@
             weights,
             weights,
             stack,
+            stack,
+            held(cells, channels, kind=F32),
             held(cells, channels, kind=F32),
             held(cells, channels, kind=F32),
             held(8, half, cells),
@@ -437,7 +434,7 @@
         (x_given, y_given, x_got, y_got),
         sums,
         [held(3 * half, 6 * cells), held(3, half, 6 * cells)],
-        5 * flops,
+        3 * flops,
         6,
     )
     terms = kernel(
@@ -452,7 +449,7 @@
             held(8, height, channels),
             pltpu.SemaphoreType.DMA((8,)),
         ],
-        5 * flops,
+        3 * flops,
         4,
     )
     parts = list(terms)

time: 109 us -> 110 us (level)
  no operation moved by 1% of the time
where the time goes in v10:
time: 110 us; the launch traced here: 108 us
  waiting for transfers between devices  52.9 us (48%)
  Pallas kernels  27.9 us (25%)
  starting transfers between devices  24.7 us (22%)
  local copies, waits for them, and re-layouts  1.19 us (1%)
    pallas_call x8, Pallas kernels, kernel(): pl.pallas_call(body, out_shape=out_shape, in_specs=specs, out_specs=jax.t...  27.9 us
    ppermute x5, waiting for transfers between devices, passed(): return lax.ppermute(piece, ('y', 'x', 'core'), pairs)  24.6 us
    all_to_all x1, waiting for transfers between devices, fast_local(): own = lax.all_to_all(own, every, 0, 0, tiled=True)  20.5 us
    ppermute x7, starting transfers between devices, fast_local(): lax.ppermute(terms[away], ('z', 'core'), [(i, i ^ away) for i in range(8)])  8.3 us
    ppermute x7, waiting for transfers between devices, fast_local(): lax.ppermute(terms[away], ('z', 'core'), [(i, i ^ away) for i in range(8)])  7.78 us
    all_to_all x1, starting transfers between devices, fast_local(): own = lax.all_to_all(own, every, 0, 0, tiled=True)  7.3 us
    ppermute x5, starting transfers between devices, passed(): return lax.ppermute(piece, ('y', 'x', 'core'), pairs)  6.22 us
    all_to_all x1, starting transfers between devices, fast_local(): fields = lax.all_to_all(fields, every, 0, 0, tiled=True)  2.91 us
  transfers between devices with their start and end apart: 14, of which 7 were waited for; matrix products, arithmetic and copies ran while one was open for 0% of the time, Pallas kernels for 14%

profile of v10, /device:TPU:0, one launch (start us, length us, event | category | flops | bytes accessed | tf_op | source)
XLA Modules:
  0.0 107.5 jit_solution(3684867970969350313)
XLA Ops:
  0.6 2.8 %shard_map.75 = bf16[32,2,16,384]{3,2,1,0:T(8,128)(2,1)} custom-call(bf16[8,64,384]{2,1,0:T(8,128)(2,1)} %inputs_ref.1, bf16[8,64,384]{2,1,0:T(8,128)(2,1)} %cot_ref.1), custom_call_target="tpu_custom_call" | custom-call | flops 1000000000 | bytes 3145728 | tf_op jit(solution)/shard_map/pallas_call | solution.py:360
  3.4 7.3 %all-to-all-start = ((bf16[32,2,16,384]{3,2,1,0:T(8,128)(2,1)}), bf16[32,2,16,384]{3,2,1,0:T(8,128)(2,1)S(1)}, u32[]{:S(2)}, u32[]{:S(2)}) async-start(bf16[32,2,16,384]{3,2,1,0:T(8,128)(2,1)} %shard_map.75), calls=%async_computation | async-start | bytes 1572864 | tf_op jit(solution)/shard_map/all_to_all | solution.py:386
  10.8 20.5 %all-to-all-done.own_ref = bf16[32,2,16,384]{3,2,1,0:T(8,128)(2,1)S(1)} async-done(((bf16[32,2,16,384]{3,2,1,0:T(8,128)(2,1)}), bf16[32,2,16,384]{3,2,1,0:T(8,128)(2,1)S(1)}, u32[]{:S(2)}, u32[]{:S(2)}) %all-to-all-start) | async-done | bytes 786464 | tf_op jit(solution)/shard_map/all_to_all | solution.py:386
  31.4 8.7 %shard_map.76 = (bf16[512,384]{1,0:T(8,128)(2,1)S(1)}, bf16[512,384]{1,0:T(8,128)(2,1)S(1)}, bf16[4,192,512]{2,1,0:T(8,128)(2,1)S(1)}, bf16[4,192,512]{2,1,0:T(8,128)(2,1)S(1)}) custom-call(s32[4]{0:T(128)S(1)} %pad_add_fusion.place_ref, bf16[32,2,16,384]{3,2,1,0:T(8,128)(2,1)S(1)} %all-to-all-done.own_ref, bf16[3,3,384,384]{3,2,1,0:T(8,128)(2,1)} %one_ref.3, ...), custom_call_target="tpu_custom_call" | custom-call | flops 2717908992 | bytes 10485760 | tf_op jit(solution)/shard_map/pallas_call | solution.py:360
  40.2 2.3 %collective-permute-done.got_ref = bf16[4,192,512]{2,1,0:T(8,128)(2,1)S(1)} collective-permute-done((bf16[4,192,512]{2,1,0:T(8,128)(2,1)S(1)}, bf16[4,192,512]{2,1,0:T(8,128)(2,1)S(1)}, u32[]{:S(2)}, u32[]{:S(2)}) %collective-permute-start) | collective-permute-done | bytes 786464 | tf_op jit(solution)/shard_map/ppermute | solution.py:372
  42.5 1.5 %collective-permute-start.1 = (bf16[4,192,512]{2,1,0:T(8,128)(2,1)S(1)}, bf16[4,192,512]{2,1,0:T(8,128)(2,1)S(1)}, u32[]{:S(2)}, u32[]{:S(2)}) collective-permute-start(bf16[4,192,512]{2,1,0:T(8,128)(2,1)S(1)} %get-tuple-element.49.x_ref), channel_id=1, source_target_pairs={{0,2},{1,3},{2,0},{3,1},{4,6},{5,7},{6,4},{7,5},{8,10},{9,11},{10,... | collective-permute-start | bytes 2359304 | tf_op jit(solution)/shard_map/ppermute | solution.py:372
  44.1 1.5 %collective-permute-start.2 = (bf16[4,192,512]{2,1,0:T(8,128)(2,1)S(1)}, bf16[4,192,512]{2,1,0:T(8,128)(2,1)S(1)}, u32[]{:S(2)}, u32[]{:S(2)}) collective-permute-start(bf16[4,192,512]{2,1,0:T(8,128)(2,1)S(1)} %get-tuple-element.45.y_ref), channel_id=1, source_target_pairs={{0,4},{1,5},{2,6},{3,7},{4,0},{5,1},{6,2},{7,3},{8,12},{9,13},{10,... | collective-permute-start | bytes 2359304 | tf_op jit(solution)/shard_map/ppermute | solution.py:372
  45.6 7.2 %shard_map.78 = bf16[32,2,16,384]{3,2,1,0:T(8,128)(2,1)} custom-call(bf16[32,2,16,384]{3,2,1,0:T(8,128)(2,1)S(1)} %all-to-all-done.own_ref, bf16[512,384]{1,0:T(8,128)(2,1)S(1)} %get-tuple-element.43.hidden_ref, bf16[512,384]{1,0:T(8,128)(2,1)S(1)} %get-tuple-element.44.pre_ref, bf16[3,3,384,384]{3,2,1,0:T(8,128)(2,1)} %one_ref.3, ...), custom_call_target="tpu_custom_call" | custom-call | flops 2717908992 | bytes 9437184 | tf_op jit(solution)/shard_map/pallas_call | solution.py:360
  52.8 9.4 %collective-permute-done.1.x_got_ref = bf16[4,192,512]{2,1,0:T(8,128)(2,1)S(1)} collective-permute-done((bf16[4,192,512]{2,1,0:T(8,128)(2,1)S(1)}, bf16[4,192,512]{2,1,0:T(8,128)(2,1)S(1)}, u32[]{:S(2)}, u32[]{:S(2)}) %collective-permute-start.1) | collective-permute-done | bytes 786464 | tf_op jit(solution)/shard_map/ppermute | solution.py:372
  62.2 1.2 %collective-permute-done.2.y_got_ref = bf16[4,192,512]{2,1,0:T(8,128)(2,1)S(1)} collective-permute-done((bf16[4,192,512]{2,1,0:T(8,128)(2,1)S(1)}, bf16[4,192,512]{2,1,0:T(8,128)(2,1)S(1)}, u32[]{:S(2)}, u32[]{:S(2)}) %collective-permute-start.2) | collective-permute-done | bytes 786464 | tf_op jit(solution)/shard_map/ppermute | solution.py:372
  63.4 2.9 %all-to-all-start.1 = ((bf16[32,2,16,384]{3,2,1,0:T(8,128)(2,1)}), bf16[32,2,16,384]{3,2,1,0:T(8,128)(2,1)S(1)}, u32[]{:S(2)}, u32[]{:S(2)}) async-start(bf16[32,2,16,384]{3,2,1,0:T(8,128)(2,1)} %shard_map.78), calls=%async_computation.1 | async-start | bytes 1572864 | tf_op jit(solution)/shard_map/all_to_all | solution.py:426
  66.4 1.7 %collective-permute-start.4 = (bf16[2,192,512]{2,1,0:T(8,128)(2,1)S(1)}, bf16[2,192,512]{2,1,0:T(8,128)(2,1)S(1)}, u32[]{:S(2)}, u32[]{:S(2)}) collective-permute-start(bf16[2,192,512]{2,1,0:T(8,128)(2,1)S(1)} %slice.7), channel_id=1, source_target_pairs={{0,4},{1,5},{2,6},{3,7},{4,0},{5,1},{6,2},{7,3},{8,12},{9,13},{10,... | collective-permute-start | bytes 1179656 | tf_op jit(solution)/shard_map/ppermute | solution.py:372
  68.1 1.5 %collective-permute-start.3 = (bf16[2,192,512]{2,1,0:T(8,128)(2,1)S(1)}, bf16[2,192,512]{2,1,0:T(8,128)(2,1)S(1)}, u32[]{:S(2)}, u32[]{:S(2)}) collective-permute-start(bf16[2,192,512]{2,1,0:T(8,128)(2,1)S(1)} %slice.6), channel_id=1, source_target_pairs={{0,2},{1,3},{2,0},{3,1},{4,6},{5,7},{6,4},{7,5},{8,10},{9,11},{10,... | collective-permute-start | bytes 1179656 | tf_op jit(solution)/shard_map/ppermute | solution.py:372
  69.5 1.1 %copy-done.1 = bf16[4,192,512]{2,1,0:T(8,128)(2,1)S(1)} copy-done((bf16[4,192,512]{2,1,0:T(8,128)(2,1)S(1)}, bf16[4,192,512]{2,1,0:T(8,128)(2,1)}, u32[]{:S(2)}) %copy-start.1) | copy-done | bytes 786456
  70.7 3.2 %shard_map.80.near_ref = f32[3,576,192]{2,1,0:T(8,128)S(1)} custom-call(bf16[4,192,512]{2,1,0:T(8,128)(2,1)S(1)} %get-tuple-element.49.x_ref, bf16[4,192,512]{2,1,0:T(8,128)(2,1)S(1)} %copy-done.1, bf16[4,192,512]{2,1,0:T(8,128)(2,1)S(1)} %collective-permute-done.1.x_got_ref, bf16[4,192,512]{2,1,0:T(8,128)(2,1)S(1)} %collective-permute-done.2.y_got_ref), custom_call_target="tpu_custom_call" | custom-call | flops 4076863488 | bytes 6291456 | tf_op jit(solution)/shard_map/pallas_call | solution.py:360
  73.8 11.4 %collective-permute-done.4.right_ref = bf16[2,192,512]{2,1,0:T(8,128)(2,1)S(1)} collective-permute-done((bf16[2,192,512]{2,1,0:T(8,128)(2,1)S(1)}, bf16[2,192,512]{2,1,0:T(8,128)(2,1)S(1)}, u32[]{:S(2)}, u32[]{:S(2)}) %collective-permute-start.4) | collective-permute-done | bytes 393248 | tf_op jit(solution)/shard_map/ppermute | solution.py:372
  85.6 2.9 %shard_map.81 = (bf16[112,384]{1,0:T(8,128)(2,1)S(1)}, bf16[112,384]{1,0:T(8,128)(2,1)S(1)}, bf16[112,384]{1,0:T(8,128)(2,1)S(1)}, bf16[112,384]{1,0:T(8,128)(2,...) custom-call(s32[4]{0:T(128)S(1)} %pad_add_fusion.place_ref, ...), custom_call_target="tpu_custom_call" | custom-call | flops 4076863488 | bytes 4194304 | tf_op jit(solution)/shard_map/pallas_call | solution.py:360
  88.6 1.4 %collective-permute-start.6 = (bf16[112,384]{1,0:T(8,128)(2,1)S(1)}, bf16[112,384]{1,0:T(8,128)(2,1)S(1)}, u32[]{:S(2)}, u32[]{:S(2)}) collective-permute-start(bf16[112,384]{1,0:T(8,128)(2,1)S(1)} %get-tuple-element.54), channel_id=1, source_target_pairs={{0,8},{1,9},{8,0},{9,1},{16,24},{17,25},{24,16},{25,17},{2,10},{3,... | collective-permute-start | bytes 258056 | tf_op jit(solution)/shard_map/ppermute | solution.py:457
  90.0 0.5 collective-permute-start.7
  90.5 2.7 %collective-permute-start.8 = (bf16[112,384]{1,0:T(8,128)(2,1)S(1)}, bf16[112,384]{1,0:T(8,128)(2,1)S(1)}, u32[]{:S(2)}, u32[]{:S(2)}) collective-permute-start(bf16[112,384]{1,0:T(8,128)(2,1)S(1)} %get-tuple-element.56), channel_id=1, source_target_pairs={{0,16},{1,17},{8,24},{9,25},{16,0},{17,1},{24,8},{25,9},{2,18},{3,... | collective-permute-start | bytes 258056 | tf_op jit(solution)/shard_map/ppermute | solution.py:457
  93.1 3.6 %collective-permute-start.10 = (bf16[112,384]{1,0:T(8,128)(2,1)S(1)}, bf16[112,384]{1,0:T(8,128)(2,1)S(1)}, u32[]{:S(2)}, u32[]{:S(2)}) collective-permute-start(bf16[112,384]{1,0:T(8,128)(2,1)S(1)} %get-tuple-element.58), channel_id=1, source_target_pairs={{0,24},{1,25},{8,16},{9,17},{16,8},{17,9},{24,0},{25,1},{2,26},{3,... | collective-permute-start | bytes 258056 | tf_op jit(solution)/shard_map/ppermute | solution.py:457
  96.8 1.5 %shard_map.79 = (bf16[8,64,384]{2,1,0:T(8,128)(2,1)}, bf16[8,64,384]{2,1,0:T(8,128)(2,1)}) custom-call(bf16[32,2,16,384]{3,2,1,0:T(8,128)(2,1)S(1)} %all-to-all-done.1.fields_ref), custom_call_target="tpu_custom_call" | custom-call | flops 1000000000 | bytes 3145728 | tf_op jit(solution)/shard_map/pallas_call | solution.py:360
  98.3 7.8 %collective-permute-done.9.refs_5_ = bf16[112,384]{1,0:T(8,128)(2,1)S(1)} collective-permute-done((bf16[112,384]{1,0:T(8,128)(2,1)S(1)}, bf16[112,384]{1,0:T(8,128)(2,1)S(1)}, u32[]{:S(2)}, u32[]{:S(2)}) %collective-permute-start.9) | collective-permute-done | bytes 86048 | tf_op jit(solution)/shard_map/ppermute | solution.py:457
  106.1 1.5 %shard_map.82 = (f32[3,3,48,96]{3,2,1,0:T(8,128)}, f32[3,3,48,96]{3,2,1,0:T(8,128)}) custom-call(s32[4]{0:T(128)S(1)} %pad_add_fusion.place_ref, bf16[112,384]{1,0:T(8,128)(2,1)S(1)} %get-tuple-element.62.refs_0_, bf16[112,384]{1,0:T(8,128)(2,1)S(1)} %collective-permute-done.5.refs_1_, bf16[112,384]{1,0:T(8,128)(2,1)S(1)} %collective-permute-done.6.refs_2_, ...), custom_call_target="tpu_custom_call" | custom-call | flops 1000000 | bytes 2097152 | tf_op jit(solution)/shard_map/pallas_call | solution.py:360
  (19 shorter events, 0.8 us)
Async XLA Ops:
  3.4 27.9 %all-to-all-start = ((bf16[32,2,16,384]{3,2,1,0:T(8,128)(2,1)}), bf16[32,2,16,384]{3,2,1,0:T(8,128)(2,1)S(1)}, u32[]{:S(2)}, u32[]{:S(2)}) async-start(bf16[32,2,16,384]{3,2,1,0:T(8,128)(2,1)} %shard_map.75), calls=%async_computation | async-start | bytes 1572864 | tf_op jit(solution)/shard_map/all_to_all | solution.py:386
  40.1 2.4 %collective-permute-start = (bf16[4,192,512]{2,1,0:T(8,128)(2,1)S(1)}, bf16[4,192,512]{2,1,0:T(8,128)(2,1)S(1)}, u32[]{:S(2)}, u32[]{:S(2)}) collective-permute-start(bf16[4,192,512]{2,1,0:T(8,128)(2,1)S(1)} %get-tuple-element.41), channel_id=1, source_target_pairs={{0,1},{1,0},{2,3},{3,2},{4,5},{5,4},{6,7},{7,6},{8,9},{9,8},{10,11... | collective-permute-start | bytes 2359304 | tf_op jit(solution)/shard_map/ppermute | solution.py:372
  42.5 10.3 %copy-start = (bf16[4,192,512]{2,1,0:T(8,128)(2,1)}, bf16[4,192,512]{2,1,0:T(8,128)(2,1)S(1)}, u32[]{:S(2)}) copy-start(bf16[4,192,512]{2,1,0:T(8,128)(2,1)S(1)} %get-tuple-element.45.y_ref) | copy-start | bytes 2359300
  42.5 19.6 %collective-permute-start.1 = (bf16[4,192,512]{2,1,0:T(8,128)(2,1)S(1)}, bf16[4,192,512]{2,1,0:T(8,128)(2,1)S(1)}, u32[]{:S(2)}, u32[]{:S(2)}) collective-permute-start(bf16[4,192,512]{2,1,0:T(8,128)(2,1)S(1)} %get-tuple-element.49.x_ref), channel_id=1, source_target_pairs={{0,2},{1,3},{2,0},{3,1},{4,6},{5,7},{6,4},{7,5},{8,10},{9,11},{10,... | collective-permute-start | bytes 2359304 | tf_op jit(solution)/shard_map/ppermute | solution.py:372
  44.1 19.3 %collective-permute-start.2 = (bf16[4,192,512]{2,1,0:T(8,128)(2,1)S(1)}, bf16[4,192,512]{2,1,0:T(8,128)(2,1)S(1)}, u32[]{:S(2)}, u32[]{:S(2)}) collective-permute-start(bf16[4,192,512]{2,1,0:T(8,128)(2,1)S(1)} %get-tuple-element.45.y_ref), channel_id=1, source_target_pairs={{0,4},{1,5},{2,6},{3,7},{4,0},{5,1},{6,2},{7,3},{8,12},{9,13},{10,... | collective-permute-start | bytes 2359304 | tf_op jit(solution)/shard_map/ppermute | solution.py:372
  63.4 33.4 %all-to-all-start.1 = ((bf16[32,2,16,384]{3,2,1,0:T(8,128)(2,1)}), bf16[32,2,16,384]{3,2,1,0:T(8,128)(2,1)S(1)}, u32[]{:S(2)}, u32[]{:S(2)}) async-start(bf16[32,2,16,384]{3,2,1,0:T(8,128)(2,1)} %shard_map.78), calls=%async_computation.1 | async-start | bytes 1572864 | tf_op jit(solution)/shard_map/all_to_all | solution.py:426
  66.4 18.9 %collective-permute-start.4 = (bf16[2,192,512]{2,1,0:T(8,128)(2,1)S(1)}, bf16[2,192,512]{2,1,0:T(8,128)(2,1)S(1)}, u32[]{:S(2)}, u32[]{:S(2)}) collective-permute-start(bf16[2,192,512]{2,1,0:T(8,128)(2,1)S(1)} %slice.7), channel_id=1, source_target_pairs={{0,4},{1,5},{2,6},{3,7},{4,0},{5,1},{6,2},{7,3},{8,12},{9,13},{10,... | collective-permute-start | bytes 1179656 | tf_op jit(solution)/shard_map/ppermute | solution.py:372
  68.1 17.5 %collective-permute-start.3 = (bf16[2,192,512]{2,1,0:T(8,128)(2,1)S(1)}, bf16[2,192,512]{2,1,0:T(8,128)(2,1)S(1)}, u32[]{:S(2)}, u32[]{:S(2)}) collective-permute-start(bf16[2,192,512]{2,1,0:T(8,128)(2,1)S(1)} %slice.6), channel_id=1, source_target_pairs={{0,2},{1,3},{2,0},{3,1},{4,6},{5,7},{6,4},{7,5},{8,10},{9,11},{10,... | collective-permute-start | bytes 1179656 | tf_op jit(solution)/shard_map/ppermute | solution.py:372
  69.5 1.1 %copy-start.1 = (bf16[4,192,512]{2,1,0:T(8,128)(2,1)S(1)}, bf16[4,192,512]{2,1,0:T(8,128)(2,1)}, u32[]{:S(2)}) copy-start(bf16[4,192,512]{2,1,0:T(8,128)(2,1)} %copy-done) | copy-start | bytes 2359300
  88.5 4.6 %collective-permute-start.5 = (bf16[112,384]{1,0:T(8,128)(2,1)S(1)}, bf16[112,384]{1,0:T(8,128)(2,1)S(1)}, u32[]{:S(2)}, u32[]{:S(2)}) collective-permute-start(bf16[112,384]{1,0:T(8,128)(2,1)S(1)} %get-tuple-element.53), channel_id=1, source_target_pairs={{0,1},{1,0},{8,9},{9,8},{16,17},{17,16},{24,25},{25,24},{2,3},{3,2... | collective-permute-start | bytes 258056 | tf_op jit(solution)/shard_map/ppermute | solution.py:457
  88.6 8.1 %collective-permute-start.6 = (bf16[112,384]{1,0:T(8,128)(2,1)S(1)}, bf16[112,384]{1,0:T(8,128)(2,1)S(1)}, u32[]{:S(2)}, u32[]{:S(2)}) collective-permute-start(bf16[112,384]{1,0:T(8,128)(2,1)S(1)} %get-tuple-element.54), channel_id=1, source_target_pairs={{0,8},{1,9},{8,0},{9,1},{16,24},{17,25},{24,16},{25,17},{2,10},{3,... | collective-permute-start | bytes 258056 | tf_op jit(solution)/shard_map/ppermute | solution.py:457
  90.0 8.3 %collective-permute-start.7 = (bf16[112,384]{1,0:T(8,128)(2,1)S(1)}, bf16[112,384]{1,0:T(8,128)(2,1)S(1)}, u32[]{:S(2)}, u32[]{:S(2)}) collective-permute-start(bf16[112,384]{1,0:T(8,128)(2,1)S(1)} %get-tuple-element.55), channel_id=1, source_target_pairs={{0,9},{1,8},{8,1},{9,0},{16,25},{17,24},{24,17},{25,16},{2,11},{3,... | collective-permute-start | bytes 258056 | tf_op jit(solution)/shard_map/ppermute | solution.py:457
  90.5 7.8 %collective-permute-start.8 = (bf16[112,384]{1,0:T(8,128)(2,1)S(1)}, bf16[112,384]{1,0:T(8,128)(2,1)S(1)}, u32[]{:S(2)}, u32[]{:S(2)}) collective-permute-start(bf16[112,384]{1,0:T(8,128)(2,1)S(1)} %get-tuple-element.56), channel_id=1, source_target_pairs={{0,16},{1,17},{8,24},{9,25},{16,0},{17,1},{24,8},{25,9},{2,18},{3,... | collective-permute-start | bytes 258056 | tf_op jit(solution)/shard_map/ppermute | solution.py:457
  93.1 12.9 %collective-permute-start.9 = (bf16[112,384]{1,0:T(8,128)(2,1)S(1)}, bf16[112,384]{1,0:T(8,128)(2,1)S(1)}, u32[]{:S(2)}, u32[]{:S(2)}) collective-permute-start(bf16[112,384]{1,0:T(8,128)(2,1)S(1)} %get-tuple-element.57), channel_id=1, source_target_pairs={{0,17},{1,16},{8,25},{9,24},{16,1},{17,0},{24,9},{25,8},{2,19},{3,... | collective-permute-start | bytes 258056 | tf_op jit(solution)/shard_map/ppermute | solution.py:457
  93.1 12.9 %collective-permute-start.10 = (bf16[112,384]{1,0:T(8,128)(2,1)S(1)}, bf16[112,384]{1,0:T(8,128)(2,1)S(1)}, u32[]{:S(2)}, u32[]{:S(2)}) collective-permute-start(bf16[112,384]{1,0:T(8,128)(2,1)S(1)} %get-tuple-element.58), channel_id=1, source_target_pairs={{0,24},{1,25},{8,16},{9,17},{16,8},{17,9},{24,0},{25,1},{2,26},{3,... | collective-permute-start | bytes 258056 | tf_op jit(solution)/shard_map/ppermute | solution.py:457
  96.7 9.4 %collective-permute-start.11 = (bf16[112,384]{1,0:T(8,128)(2,1)S(1)}, bf16[112,384]{1,0:T(8,128)(2,1)S(1)}, u32[]{:S(2)}, u32[]{:S(2)}) collective-permute-start(bf16[112,384]{1,0:T(8,128)(2,1)S(1)} %get-tuple-element.59), channel_id=1, source_target_pairs={{0,25},{1,24},{8,17},{9,16},{16,9},{17,8},{24,1},{25,0},{2,27},{3,... | collective-permute-start | bytes 258056 | tf_op jit(solution)/shard_map/ppermute | solution.py:457

commit v11 on v9

--- a/solution.py
+++ b/solution.py
@@ -424,7 +424,7 @@
         2 * flops,
         9,
     )
-    fields, x_got, y_got = lax.optimization_barrier((fields, x_got, y_got))
+    _, x_got, y_got = lax.optimization_barrier((fields, x_got, y_got))
     far = (passed(y_got[:2], 1, 0, 0), passed(x_got[:2], 0, 1, 0))
     fields = lax.all_to_all(fields, every, 0, 0, tiled=True)
     output, input_grad = kernel(
@@ -437,7 +437,7 @@
         (x_given, y_given, x_got, y_got),
         sums,
         [held(3 * half, 6 * cells), held(3, half, 6 * cells)],
-        5 * flops,
+        3 * flops,
         6,
     )
     terms = kernel(
@@ -452,7 +452,7 @@
             held(8, height, channels),
             pltpu.SemaphoreType.DMA((8,)),
         ],
-        5 * flops,
+        3 * flops,
         4,
     )
     parts = list(terms)

time: 109 us -> 103 us (0.945)
  the two profiles are of different devices: /device:TPU:0 before, /device:TPU:9 now
where the time goes in v11:
time: 103 us
  waiting for transfers between devices  49.6 us (48%)
  Pallas kernels  29.5 us (29%)
  starting transfers between devices  23 us (22%)
    pallas_call x8, Pallas kernels, kernel(): pl.pallas_call(body, out_shape=out_shape, in_specs=specs, out_specs=jax.t...  29.5 us
    all_to_all x1, waiting for transfers between devices, fast_local(): own = lax.all_to_all(own, every, 0, 0, tiled=True)  20 us
    ppermute x5, waiting for transfers between devices, passed(): return lax.ppermute(piece, ('y', 'x', 'core'), pairs)  17.7 us
    ppermute x7, waiting for transfers between devices, fast_local(): lax.ppermute(terms[away], ('z', 'core'), [(i, i ^ away) for i in range(8)])  11.9 us
    ppermute x7, starting transfers between devices, fast_local(): lax.ppermute(terms[away], ('z', 'core'), [(i, i ^ away) for i in range(8)])  8.11 us
    all_to_all x1, starting transfers between devices, fast_local(): own = lax.all_to_all(own, every, 0, 0, tiled=True)  6.36 us
    all_to_all x1, starting transfers between devices, fast_local(): fields = lax.all_to_all(fields, every, 0, 0, tiled=True)  4.9 us
    ppermute x5, starting transfers between devices, passed(): return lax.ppermute(piece, ('y', 'x', 'core'), pairs)  3.64 us
  transfers between devices with their start and end apart: 14, of which 9 were waited for; matrix products, arithmetic and copies ran while one was open for 0% of the time, Pallas kernels for 16%

profile of v11, /device:TPU:9, one launch (start us, length us, event | category | flops | bytes accessed | tf_op | source)
XLA Modules:
  0.0 102.9 jit_solution(6243609869361120791)
XLA Ops:
  0.6 2.8 %shard_map.75 = bf16[32,2,16,384]{3,2,1,0:T(8,128)(2,1)} custom-call(bf16[8,64,384]{2,1,0:T(8,128)(2,1)} %inputs_ref.1, bf16[8,64,384]{2,1,0:T(8,128)(2,1)} %cot_ref.1), custom_call_target="tpu_custom_call" | custom-call | flops 1000000000 | bytes 3145728 | tf_op jit(solution)/shard_map/pallas_call | solution.py:365
  3.4 6.4 %all-to-all-start = ((bf16[32,2,16,384]{3,2,1,0:T(8,128)(2,1)}), bf16[32,2,16,384]{3,2,1,0:T(8,128)(2,1)S(1)}, u32[]{:S(2)}, u32[]{:S(2)}) async-start(bf16[32,2,16,384]{3,2,1,0:T(8,128)(2,1)} %shard_map.75), calls=%async_computation | async-start | bytes 1572864 | tf_op jit(solution)/shard_map/all_to_all | solution.py:391
  9.9 20.0 %all-to-all-done.own_ref = bf16[32,2,16,384]{3,2,1,0:T(8,128)(2,1)S(1)} async-done(((bf16[32,2,16,384]{3,2,1,0:T(8,128)(2,1)}), bf16[32,2,16,384]{3,2,1,0:T(8,128)(2,1)S(1)}, u32[]{:S(2)}, u32[]{:S(2)}) %all-to-all-start) | async-done | bytes 786464 | tf_op jit(solution)/shard_map/all_to_all | solution.py:391
  29.9 7.9 %shard_map.76 = (bf16[512,384]{1,0:T(8,128)(2,1)S(1)}, bf16[512,384]{1,0:T(8,128)(2,1)S(1)}, bf16[4,192,512]{2,1,0:T(8,128)(2,1)S(1)}, bf16[4,192,512]{2,1,0:T(8,128)(2,1)S(1)}) custom-call(s32[4]{0:T(128)S(1)} %pad_add_fusion.place_ref, bf16[32,2,16,384]{3,2,1,0:T(8,128)(2,1)S(1)} %all-to-all-done.own_ref, bf16[3,3,384,384]{3,2,1,0:T(8,128)(2,1)} %one_ref.3, ...), custom_call_target="tpu_custom_call" | custom-call | flops 2717908992 | bytes 10485760 | tf_op jit(solution)/shard_map/pallas_call | solution.py:365
  38.3 1.9 %collective-permute-done.got_ref = bf16[4,192,512]{2,1,0:T(8,128)(2,1)S(1)} collective-permute-done((bf16[4,192,512]{2,1,0:T(8,128)(2,1)S(1)}, bf16[4,192,512]{2,1,0:T(8,128)(2,1)S(1)}, u32[]{:S(2)}, u32[]{:S(2)}) %collective-permute-start) | collective-permute-done | bytes 786464 | tf_op jit(solution)/shard_map/ppermute | solution.py:377
  40.3 1.0 shard_map.77
  42.3 7.6 %shard_map.78 = bf16[32,2,16,384]{3,2,1,0:T(8,128)(2,1)} custom-call(bf16[32,2,16,384]{3,2,1,0:T(8,128)(2,1)S(1)} %all-to-all-done.own_ref, bf16[512,384]{1,0:T(8,128)(2,1)S(1)} %get-tuple-element.42.hidden_ref, bf16[512,384]{1,0:T(8,128)(2,1)S(1)} %get-tuple-element.43.pre_ref, bf16[3,3,384,384]{3,2,1,0:T(8,128)(2,1)} %one_ref.3, ...), custom_call_target="tpu_custom_call" | custom-call | flops 2717908992 | bytes 9437184 | tf_op jit(solution)/shard_map/pallas_call | solution.py:365
  50.0 4.9 %all-to-all-start.1 = ((bf16[32,2,16,384]{3,2,1,0:T(8,128)(2,1)}), bf16[32,2,16,384]{3,2,1,0:T(8,128)(2,1)S(1)}, u32[]{:S(2)}, u32[]{:S(2)}) async-start(bf16[32,2,16,384]{3,2,1,0:T(8,128)(2,1)} %shard_map.78), calls=%async_computation.1 | async-start | bytes 1572864 | tf_op jit(solution)/shard_map/all_to_all | solution.py:429
  54.9 6.3 %collective-permute-done.1.x_got_ref = bf16[4,192,512]{2,1,0:T(8,128)(2,1)S(1)} collective-permute-done((bf16[4,192,512]{2,1,0:T(8,128)(2,1)S(1)}, bf16[4,192,512]{2,1,0:T(8,128)(2,1)S(1)}, u32[]{:S(2)}, u32[]{:S(2)}) %collective-permute-start.1) | collective-permute-done | bytes 786464 | tf_op jit(solution)/shard_map/ppermute | solution.py:377
  61.2 1.5 %collective-permute-done.2.y_got_ref = bf16[4,192,512]{2,1,0:T(8,128)(2,1)S(1)} collective-permute-done((bf16[4,192,512]{2,1,0:T(8,128)(2,1)}, bf16[4,192,512]{2,1,0:T(8,128)(2,1)S(1)}, u32[]{:S(2)}, u32[]{:S(2)}) %collective-permute-start.2) | collective-permute-done | bytes 786464 | tf_op jit(solution)/shard_map/ppermute | solution.py:377
  62.9 1.9 %collective-permute-start.3 = (bf16[2,192,512]{2,1,0:T(8,128)(2,1)S(1)}, bf16[2,192,512]{2,1,0:T(8,128)(2,1)S(1)}, u32[]{:S(2)}, u32[]{:S(2)}) collective-permute-start(bf16[2,192,512]{2,1,0:T(8,128)(2,1)S(1)} %slice.6), channel_id=1, source_target_pairs={{0,2},{1,3},{2,0},{3,1},{4,6},{5,7},{6,4},{7,5},{8,10},{9,11},{10,... | collective-permute-start | bytes 1179656 | tf_op jit(solution)/shard_map/ppermute | solution.py:377
  64.8 4.3 %shard_map.80.near_ref = f32[3,576,192]{2,1,0:T(8,128)S(1)} custom-call(bf16[4,192,512]{2,1,0:T(8,128)(2,1)S(1)} %get-tuple-element.46.x_ref, bf16[4,192,512]{2,1,0:T(8,128)(2,1)} %get-tuple-element.47.y_ref, bf16[4,192,512]{2,1,0:T(8,128)(2,1)S(1)} %collective-permute-done.1.x_got_ref, bf16[4,192,512]{2,1,0:T(8,128)(2,1)S(1)} %collective-permute-done.2.y_got_ref), custom_call_target="tpu_custom_call" | custom-call | flops 4076863488 | bytes 6291456 | tf_op jit(solution)/shard_map/pallas_call | solution.py:365
  69.1 8.0 %collective-permute-done.4.right_ref = bf16[2,192,512]{2,1,0:T(8,128)(2,1)S(1)} collective-permute-done((bf16[2,192,512]{2,1,0:T(8,128)(2,1)S(1)}, bf16[2,192,512]{2,1,0:T(8,128)(2,1)S(1)}, u32[]{:S(2)}, u32[]{:S(2)}) %collective-permute-start.4) | collective-permute-done | bytes 393248 | tf_op jit(solution)/shard_map/ppermute | solution.py:377
  77.1 2.9 %shard_map.81 = (bf16[112,384]{1,0:T(8,128)(2,1)S(1)}, bf16[112,384]{1,0:T(8,128)(2,1)S(1)}, bf16[112,384]{1,0:T(8,128)(2,1)S(1)}, bf16[112,384]{1,0:T(8,128)(2,...) custom-call(s32[4]{0:T(128)S(1)} %pad_add_fusion.place_ref, ...), custom_call_target="tpu_custom_call" | custom-call | flops 4076863488 | bytes 4194304 | tf_op jit(solution)/shard_map/pallas_call | solution.py:365
  80.0 2.0 %collective-permute-start.5 = (bf16[112,384]{1,0:T(8,128)(2,1)S(1)}, bf16[112,384]{1,0:T(8,128)(2,1)S(1)}, u32[]{:S(2)}, u32[]{:S(2)}) collective-permute-start(bf16[112,384]{1,0:T(8,128)(2,1)S(1)} %get-tuple-element.51), channel_id=1, source_target_pairs={{0,1},{1,0},{8,9},{9,8},{16,17},{17,16},{24,25},{25,24},{2,3},{3,2... | collective-permute-start | bytes 258056 | tf_op jit(solution)/shard_map/ppermute | solution.py:460
  82.0 0.9 collective-permute-start.6
  82.9 0.8 collective-permute-start.7
  84.6 1.9 %collective-permute-start.9 = (bf16[112,384]{1,0:T(8,128)(2,1)S(1)}, bf16[112,384]{1,0:T(8,128)(2,1)S(1)}, u32[]{:S(2)}, u32[]{:S(2)}) collective-permute-start(bf16[112,384]{1,0:T(8,128)(2,1)S(1)} %get-tuple-element.55), channel_id=1, source_target_pairs={{0,17},{1,16},{8,25},{9,24},{16,1},{17,0},{24,9},{25,8},{2,19},{3,... | collective-permute-start | bytes 258056 | tf_op jit(solution)/shard_map/ppermute | solution.py:460
  86.7 1.4 %collective-permute-start.11 = (bf16[112,384]{1,0:T(8,128)(2,1)S(1)}, bf16[112,384]{1,0:T(8,128)(2,1)S(1)}, u32[]{:S(2)}, u32[]{:S(2)}) collective-permute-start(bf16[112,384]{1,0:T(8,128)(2,1)S(1)} %get-tuple-element.57), channel_id=1, source_target_pairs={{0,25},{1,24},{8,17},{9,16},{16,9},{17,8},{24,1},{25,0},{2,27},{3,... | collective-permute-start | bytes 258056 | tf_op jit(solution)/shard_map/ppermute | solution.py:460
  88.1 1.5 %shard_map.79 = (bf16[8,64,384]{2,1,0:T(8,128)(2,1)}, bf16[8,64,384]{2,1,0:T(8,128)(2,1)}) custom-call(bf16[32,2,16,384]{3,2,1,0:T(8,128)(2,1)S(1)} %all-to-all-done.1.fields_ref), custom_call_target="tpu_custom_call" | custom-call | flops 1000000000 | bytes 3145728 | tf_op jit(solution)/shard_map/pallas_call | solution.py:365
  89.8 6.3 %collective-permute-done.9.refs_5_ = bf16[112,384]{1,0:T(8,128)(2,1)S(1)} collective-permute-done((bf16[112,384]{1,0:T(8,128)(2,1)S(1)}, bf16[112,384]{1,0:T(8,128)(2,1)S(1)}, u32[]{:S(2)}, u32[]{:S(2)}) %collective-permute-start.9) | collective-permute-done | bytes 86048 | tf_op jit(solution)/shard_map/ppermute | solution.py:460
  96.1 3.3 %collective-permute-done.10.refs_6_ = bf16[112,384]{1,0:T(8,128)(2,1)S(1)} collective-permute-done((bf16[112,384]{1,0:T(8,128)(2,1)S(1)}, bf16[112,384]{1,0:T(8,128)(2,1)S(1)}, u32[]{:S(2)}, u32[]{:S(2)}) %collective-permute-start.10) | collective-permute-done | bytes 86048 | tf_op jit(solution)/shard_map/ppermute | solution.py:460
  99.4 2.1 %collective-permute-done.11.refs_7_ = bf16[112,384]{1,0:T(8,128)(2,1)S(1)} collective-permute-done((bf16[112,384]{1,0:T(8,128)(2,1)S(1)}, bf16[112,384]{1,0:T(8,128)(2,1)S(1)}, u32[]{:S(2)}, u32[]{:S(2)}) %collective-permute-start.11) | collective-permute-done | bytes 86048 | tf_op jit(solution)/shard_map/ppermute | solution.py:460
  101.5 1.5 %shard_map.82 = (f32[3,3,48,96]{3,2,1,0:T(8,128)}, f32[3,3,48,96]{3,2,1,0:T(8,128)}) custom-call(s32[4]{0:T(128)S(1)} %pad_add_fusion.place_ref, bf16[112,384]{1,0:T(8,128)(2,1)S(1)} %get-tuple-element.60.refs_0_, bf16[112,384]{1,0:T(8,128)(2,1)S(1)} %collective-permute-done.5.refs_1_, bf16[112,384]{1,0:T(8,128)(2,1)S(1)} %collective-permute-done.6.refs_2_, ...), custom_call_target="tpu_custom_call" | custom-call | flops 1000000 | bytes 2097152 | tf_op jit(solution)/shard_map/pallas_call | solution.py:365
  (15 shorter events, 3.2 us)
Async XLA Ops:
  3.4 26.4 %all-to-all-start = ((bf16[32,2,16,384]{3,2,1,0:T(8,128)(2,1)}), bf16[32,2,16,384]{3,2,1,0:T(8,128)(2,1)S(1)}, u32[]{:S(2)}, u32[]{:S(2)}) async-start(bf16[32,2,16,384]{3,2,1,0:T(8,128)(2,1)} %shard_map.75), calls=%async_computation | async-start | bytes 1572864 | tf_op jit(solution)/shard_map/all_to_all | solution.py:391
  37.8 2.5 %collective-permute-start = (bf16[4,192,512]{2,1,0:T(8,128)(2,1)S(1)}, bf16[4,192,512]{2,1,0:T(8,128)(2,1)S(1)}, u32[]{:S(2)}, u32[]{:S(2)}) collective-permute-start(bf16[4,192,512]{2,1,0:T(8,128)(2,1)S(1)} %get-tuple-element.40), channel_id=1, source_target_pairs={{0,1},{1,0},{2,3},{3,2},{4,5},{5,4},{6,7},{7,6},{8,9},{9,8},{10,11... | collective-permute-start | bytes 2359304 | tf_op jit(solution)/shard_map/ppermute | solution.py:377
  41.3 19.9 %collective-permute-start.1 = (bf16[4,192,512]{2,1,0:T(8,128)(2,1)S(1)}, bf16[4,192,512]{2,1,0:T(8,128)(2,1)S(1)}, u32[]{:S(2)}, u32[]{:S(2)}) collective-permute-start(bf16[4,192,512]{2,1,0:T(8,128)(2,1)S(1)} %get-tuple-element.46.x_ref), channel_id=1, source_target_pairs={{0,2},{1,3},{2,0},{3,1},{4,6},{5,7},{6,4},{7,5},{8,10},{9,11},{10,... | collective-permute-start | bytes 2359304 | tf_op jit(solution)/shard_map/ppermute | solution.py:377
  42.0 20.7 %collective-permute-start.2 = (bf16[4,192,512]{2,1,0:T(8,128)(2,1)}, bf16[4,192,512]{2,1,0:T(8,128)(2,1)S(1)}, u32[]{:S(2)}, u32[]{:S(2)}) collective-permute-start(bf16[4,192,512]{2,1,0:T(8,128)(2,1)} %get-tuple-element.47.y_ref), channel_id=1, source_target_pairs={{0,4},{1,5},{2,6},{3,7},{4,0},{5,1},{6,2},{7,3},{8,12},{9,13},{10,... | collective-permute-start | bytes 2359304 | tf_op jit(solution)/shard_map/ppermute | solution.py:377
  50.0 38.2 %all-to-all-start.1 = ((bf16[32,2,16,384]{3,2,1,0:T(8,128)(2,1)}), bf16[32,2,16,384]{3,2,1,0:T(8,128)(2,1)S(1)}, u32[]{:S(2)}, u32[]{:S(2)}) async-start(bf16[32,2,16,384]{3,2,1,0:T(8,128)(2,1)} %shard_map.78), calls=%async_computation.1 | async-start | bytes 1572864 | tf_op jit(solution)/shard_map/all_to_all | solution.py:429
  62.7 14.3 %collective-permute-start.4 = (bf16[2,192,512]{2,1,0:T(8,128)(2,1)S(1)}, bf16[2,192,512]{2,1,0:T(8,128)(2,1)S(1)}, u32[]{:S(2)}, u32[]{:S(2)}) collective-permute-start(bf16[2,192,512]{2,1,0:T(8,128)(2,1)S(1)} %slice.7), channel_id=1, source_target_pairs={{0,4},{1,5},{2,6},{3,7},{4,0},{5,1},{6,2},{7,3},{8,12},{9,13},{10,... | collective-permute-start | bytes 1179656 | tf_op jit(solution)/shard_map/ppermute | solution.py:377
  62.9 14.2 %collective-permute-start.3 = (bf16[2,192,512]{2,1,0:T(8,128)(2,1)S(1)}, bf16[2,192,512]{2,1,0:T(8,128)(2,1)S(1)}, u32[]{:S(2)}, u32[]{:S(2)}) collective-permute-start(bf16[2,192,512]{2,1,0:T(8,128)(2,1)S(1)} %slice.6), channel_id=1, source_target_pairs={{0,2},{1,3},{2,0},{3,1},{4,6},{5,7},{6,4},{7,5},{8,10},{9,11},{10,... | collective-permute-start | bytes 1179656 | tf_op jit(solution)/shard_map/ppermute | solution.py:377
  80.0 6.4 %collective-permute-start.5 = (bf16[112,384]{1,0:T(8,128)(2,1)S(1)}, bf16[112,384]{1,0:T(8,128)(2,1)S(1)}, u32[]{:S(2)}, u32[]{:S(2)}) collective-permute-start(bf16[112,384]{1,0:T(8,128)(2,1)S(1)} %get-tuple-element.51), channel_id=1, source_target_pairs={{0,1},{1,0},{8,9},{9,8},{16,17},{17,16},{24,25},{25,24},{2,3},{3,2... | collective-permute-start | bytes 258056 | tf_op jit(solution)/shard_map/ppermute | solution.py:460
  82.0 4.7 %collective-permute-start.6 = (bf16[112,384]{1,0:T(8,128)(2,1)S(1)}, bf16[112,384]{1,0:T(8,128)(2,1)S(1)}, u32[]{:S(2)}, u32[]{:S(2)}) collective-permute-start(bf16[112,384]{1,0:T(8,128)(2,1)S(1)} %get-tuple-element.52), channel_id=1, source_target_pairs={{0,8},{1,9},{8,0},{9,1},{16,24},{17,25},{24,16},{25,17},{2,10},{3,... | collective-permute-start | bytes 258056 | tf_op jit(solution)/shard_map/ppermute | solution.py:460
  82.9 6.7 %collective-permute-start.7 = (bf16[112,384]{1,0:T(8,128)(2,1)S(1)}, bf16[112,384]{1,0:T(8,128)(2,1)S(1)}, u32[]{:S(2)}, u32[]{:S(2)}) collective-permute-start(bf16[112,384]{1,0:T(8,128)(2,1)S(1)} %get-tuple-element.53), channel_id=1, source_target_pairs={{0,9},{1,8},{8,1},{9,0},{16,25},{17,24},{24,17},{25,16},{2,11},{3,... | collective-permute-start | bytes 258056 | tf_op jit(solution)/shard_map/ppermute | solution.py:460
  83.7 6.1 %collective-permute-start.8 = (bf16[112,384]{1,0:T(8,128)(2,1)S(1)}, bf16[112,384]{1,0:T(8,128)(2,1)S(1)}, u32[]{:S(2)}, u32[]{:S(2)}) collective-permute-start(bf16[112,384]{1,0:T(8,128)(2,1)S(1)} %get-tuple-element.54), channel_id=1, source_target_pairs={{0,16},{1,17},{8,24},{9,25},{16,0},{17,1},{24,8},{25,9},{2,18},{3,... | collective-permute-start | bytes 258056 | tf_op jit(solution)/shard_map/ppermute | solution.py:460
  84.6 11.5 %collective-permute-start.9 = (bf16[112,384]{1,0:T(8,128)(2,1)S(1)}, bf16[112,384]{1,0:T(8,128)(2,1)S(1)}, u32[]{:S(2)}, u32[]{:S(2)}) collective-permute-start(bf16[112,384]{1,0:T(8,128)(2,1)S(1)} %get-tuple-element.55), channel_id=1, source_target_pairs={{0,17},{1,16},{8,25},{9,24},{16,1},{17,0},{24,9},{25,8},{2,19},{3,... | collective-permute-start | bytes 258056 | tf_op jit(solution)/shard_map/ppermute | solution.py:460
  86.4 12.9 %collective-permute-start.10 = (bf16[112,384]{1,0:T(8,128)(2,1)S(1)}, bf16[112,384]{1,0:T(8,128)(2,1)S(1)}, u32[]{:S(2)}, u32[]{:S(2)}) collective-permute-start(bf16[112,384]{1,0:T(8,128)(2,1)S(1)} %get-tuple-element.56), channel_id=1, source_target_pairs={{0,24},{1,25},{8,16},{9,17},{16,8},{17,9},{24,0},{25,1},{2,26},{3,... | collective-permute-start | bytes 258056 | tf_op jit(solution)/shard_map/ppermute | solution.py:460
  86.7 14.8 %collective-permute-start.11 = (bf16[112,384]{1,0:T(8,128)(2,1)S(1)}, bf16[112,384]{1,0:T(8,128)(2,1)S(1)}, u32[]{:S(2)}, u32[]{:S(2)}) collective-permute-start(bf16[112,384]{1,0:T(8,128)(2,1)S(1)} %get-tuple-element.57), channel_id=1, source_target_pairs={{0,25},{1,24},{8,17},{9,16},{16,9},{17,8},{24,1},{25,0},{2,27},{3,... | collective-permute-start | bytes 258056 | tf_op jit(solution)/shard_map/ppermute | solution.py:460

commit v12 on v11

--- a/solution.py
+++ b/solution.py
@@ -228,19 +228,11 @@
     pre_ref[...] = (slope_ref[...] * convolved_back(stack_ref, two_held, band, cells, second_weight)).astype(BF16)
     turn(2, pre_ref[...])
 
-    for ref, of in ((mine_ref, core), (give_ref, 1 - core)):
-        ref[0] = turned_ref[of * 2 + 1 - y]
-        ref[1] = turned_ref[of * 2 + y]
-        ref[2] = turned_ref[4 + of * 2 + 1 - x]
-        ref[3] = turned_ref[4 + of * 2 + x]
-
-
-def join_kernel(mine_ref, got_ref, x_ref, y_ref):
-    for at, ref in enumerate((mine_ref, got_ref)):
-        y_ref[at] = ref[0]
-        x_ref[2 + at] = ref[1]
-        x_ref[at] = ref[2]
-        y_ref[2 + at] = ref[3]
+    for ref, of, side in ((mine_ref, core, jnp.where(core == 0, x, y)), (give_ref, 1 - core, jnp.where(core == 0, y, x))):
+        ref[0] = turned_ref[6 * of]
+        ref[1] = turned_ref[6 * of + 1]
+        ref[2] = turned_ref[4 - 2 * of + 1 - side]
+        ref[3] = turned_ref[4 - 2 * of + side]
 
 
 def outer_kernel(band, step, own_ref, hidden_ref, pre_ref, one_ref, two_ref, out_ref,
@@ -265,51 +257,57 @@
         yield unit // count, (unit % count) * 16, (unit // 4) * 16, unit % 4
 
 
-def summed(band, step, lefts, rights, turned_ref, moved_ref, b):
-    half, cells = lefts[0].shape
-    if b == 0:
-        place = lax.broadcasted_iota(jnp.int32, (half, cells), 1) % band
-        for at, (left_ref, right_ref) in enumerate(zip(lefts, rights)):
-            columns = slice(at * cells, (at + 1) * cells)
-            field = left_ref[...]
-            wide = field.astype(F32)
-            turned_ref[0:half, columns] = jnp.where(place >= step, pltpu.roll(wide, step, 1), 0.0).astype(BF16)
-            turned_ref[half : 2 * half, columns] = field
-            turned_ref[2 * half :, columns] = jnp.where(
-                place < band - step, pltpu.roll(wide, cells - step, 1), 0.0
-            ).astype(BF16)
-            grad = right_ref[...]
-            wide = grad.astype(F32)
-            moved_ref[0, :, columns] = pltpu.roll(wide, cells - band, 1).astype(BF16)
-            moved_ref[1, :, columns] = grad
-            moved_ref[2, :, columns] = pltpu.roll(wide, band, 1).astype(BF16)
-    return lax.dot_general(turned_ref[...], moved_ref[b], (((1,), (1,)), ((), ())), preferred_element_type=F32)
-
-
-def near_kernel(band, step, x_ref, y_ref, x_got_ref, y_got_ref, sums_ref, turned_ref, moved_ref):
-    lefts = [x_ref.at[2], x_ref.at[3], x_got_ref.at[2], x_got_ref.at[3], y_got_ref.at[0], y_got_ref.at[1]]
-    rights = [y_ref.at[2], y_ref.at[3], x_got_ref.at[0], x_got_ref.at[1], y_got_ref.at[2], y_got_ref.at[3]]
-    for b in range(3):
-        sums_ref[b] = summed(band, step, lefts, rights, turned_ref, moved_ref, b)
-
-
-def far_kernel(band, step, place_ref, near_ref, left_ref, right_ref, *refs):
-    out_refs, (turned_ref, moved_ref, sums_ref, send_ref, sems) = refs[:-5], refs[-5:]
+def grads_kernel(band, step, place_ref, mine_ref, got_ref, far_ref, far_pair_ref, keep_ref, give_ref, whole_ref, moved_ref):
+    x, y, core = place_ref[0], place_ref[1], place_ref[2]
+    half, cells = mine_ref.shape[1:]
+    place = lax.broadcasted_iota(jnp.int32, (half, cells), 1) % band
+    for at, (ref, moving) in enumerate(((mine_ref, 3), (got_ref, 3), (far_ref, 2), (far_pair_ref, 2))):
+        columns = slice(at * cells, (at + 1) * cells)
+        whole_ref[0, :, columns] = ref[0]
+        whole_ref[1, :, columns] = ref[1]
+        wide = ref[moving].astype(F32)
+        for a in range(-1, 2):
+            for b in range(-1, 2):
+                shift = (-(b * band + a * step)) % cells
+                part = pltpu.roll(wide, shift, 1) if shift else wide
+                if a > 0:
+                    part = jnp.where(place < band - step, part, 0.0)
+                if a < 0:
+                    part = jnp.where(place >= step, part, 0.0)
+                tap = (a + 1) * 3 + b + 1
+                moved_ref[jnp.where(core == 0, 8 - tap, tap), :, columns] = part.astype(BF16)
+    moved = moved_ref[...].reshape(9 * half, 4 * cells)
+    stays = jnp.where(core == 0, y, x)
+    for ref, which in ((give_ref, 1 - stays), (keep_ref, stays)):
+        whole = whole_ref[which]
+
+        @pl.when(core == 0)
+        def _():
+            ref[...] = lax.dot_general(
+                whole, moved, (((1,), (1,)), ((), ())), preferred_element_type=F32
+            ).astype(ref.dtype)
+
+        @pl.when(core == 1)
+        def _():
+            terms = lax.dot_general(moved, whole, (((1,), (1,)), ((), ())), preferred_element_type=F32)
+            for tap in range(9):
+                rows = slice(tap * half, (tap + 1) * half)
+                ref[:, rows] = terms[rows].astype(ref.dtype)
+
+
+def pack_kernel(place_ref, keep_ref, got_ref, *refs):
+    out_refs, (sums_ref, send_ref, sems) = refs[:-3], refs[-3:]
     me = place_ref[3] * 2 + place_ref[2]
-    half = left_ref.shape[1]
-    lefts, rights = ([ref.at[at] for at in range(2)] for ref in (left_ref, right_ref))
-    for b in range(3):
-        sums_ref[b] = near_ref[b] + summed(band, step, lefts, rights, turned_ref, moved_ref, b)
+    half = keep_ref.shape[0]
+    sums_ref[...] = keep_ref[...] + got_ref[...].astype(F32)
     deep, quarter = half // 4, half // 2
     height = send_ref.shape[1]
     for z in range(4):
         for core in range(2):
             blocks = [[] for _ in range(height // 16)]
             for tap, row, to, _ in units(deep):
-                begin = (tap // 3) * half + z * deep + row
-                blocks[to // 16].append(
-                    sums_ref[tap % 3, begin : begin + 16, core * quarter : (core + 1) * quarter]
-                )
+                begin, first = z * deep + row, tap * half + core * quarter
+                blocks[to // 16].append(sums_ref[begin : begin + 16, first : first + quarter])
             for to, parts in enumerate(blocks):
                 while len(parts) < 4:
                     parts.append(jnp.zeros((16, quarter), F32))
@@ -368,12 +366,12 @@
             in_specs=specs,
             out_specs=jax.tree.map(lambda _: vmem, out_shape),
             scratch_shapes=scratch_shapes,
-            compiler_params=pltpu.CompilerParams(vmem_limit_bytes=20 * 2**20),
+            compiler_params=pltpu.CompilerParams(vmem_limit_bytes=32 * 2**20),
             cost_estimate=pl.CostEstimate(flops=work, bytes_accessed=megabytes * 2**20, transcendentals=0),
         )(*arguments)
 
     def passed(piece, x, y, core):
-        pairs = [(i, i ^ (4 * y + 2 * x + core)) for i in range(8)]
+        pairs = [(i, i ^ (4 * (i % 2 == y) + 2 * (i % 2 == x) + core)) for i in range(8)]
         return lax.ppermute(piece, ("y", "x", "core"), pairs)
 
     stack = held(cells + 2 * band, 3 * channels)
@@ -410,11 +408,9 @@
         2 * flops,
         10,
     )
-    x_given, y_given = kernel(
-        join_kernel, [vmem] * 2, (mine, passed(give, 0, 0, 1)), (pieces, pieces), [], 10**6, 4
-    )
-    x_got, y_got = passed(x_given, 1, 0, 0), passed(y_given, 0, 1, 0)
-    hidden, pre_grad, x_given = lax.optimization_barrier((hidden, pre_grad, x_given))
+    got = passed(give, None, None, 1)
+    far, far_pair = passed(mine[:3], 0, 1, 0), passed(got[:3], 0, 1, 0)
+    hidden, pre_grad, got = lax.optimization_barrier((hidden, pre_grad, got))
     fields = kernel(
         functools.partial(outer_kernel, band, step),
         [vmem] * 3 + [hbm] * 2,
@@ -424,35 +420,27 @@
         2 * flops,
         9,
     )
-    _, x_got, y_got = lax.optimization_barrier((fields, x_got, y_got))
-    far = (passed(y_got[:2], 1, 0, 0), passed(x_got[:2], 0, 1, 0))
+    _, far, far_pair = lax.optimization_barrier((fields, far, far_pair))
     fields = lax.all_to_all(fields, every, 0, 0, tiled=True)
     output, input_grad = kernel(
         functools.partial(gather_kernel, step), [vmem], (fields,), (shaped(*inputs.shape),) * 2, [], 10**9, 3
     )
-    sums = shaped(3, 3 * half, half, kind=F32)
-    near = kernel(
-        functools.partial(near_kernel, band, step),
-        [vmem] * 4,
-        (x_given, y_given, x_got, y_got),
-        sums,
-        [held(3 * half, 6 * cells), held(3, half, 6 * cells)],
-        3 * flops,
+    keep, give = kernel(
+        functools.partial(grads_kernel, band, step),
+        [smem] + [vmem] * 4,
+        (place, mine, got, far, far_pair),
+        (held(half, 9 * half, kind=F32), held(half, 9 * half)),
+        [held(2, half, 4 * cells), held(9, half, 4 * cells)],
+        4 * flops,
         6,
     )
     terms = kernel(
-        functools.partial(far_kernel, band, step),
-        [smem] + [vmem] * 3,
-        (place, near) + far,
-        (pltpu.VMEM((height, channels), BF16),) * 8,
-        [
-            held(3 * half, 2 * cells),
-            held(3, half, 2 * cells),
-            held(*sums.shape, kind=F32),
-            held(8, height, channels),
-            pltpu.SemaphoreType.DMA((8,)),
-        ],
-        3 * flops,
+        pack_kernel,
+        [smem] + [vmem] * 2,
+        (place, keep, passed(give, 1, 0, 0)),
+        (held(height, channels),) * 8,
+        [held(half, 9 * half, kind=F32), held(8, height, channels), pltpu.SemaphoreType.DMA((8,))],
+        2 * flops,
         4,
     )
     parts = list(terms)

time: 103 us -> 100 us (0.971)
  the two profiles are of different devices: /device:TPU:9 before, /device:TPU:0 now
where the time goes in v12:
time: 100 us; the launch traced here: 98.1 us
  waiting for transfers between devices  41.3 us (41%)
  Pallas kernels  31.3 us (31%)
  starting transfers between devices  23 us (23%)
  local copies, waits for them, and re-layouts  1.72 us (2%)
    pallas_call x7, Pallas kernels, kernel(): pl.pallas_call(body, out_shape=out_shape, in_specs=specs, out_specs=jax.t...  31.3 us
    all_to_all x1, waiting for transfers between devices, fast_local(): own = lax.all_to_all(own, every, 0, 0, tiled=True)  20.5 us
    ppermute x4, waiting for transfers between devices, passed(): return lax.ppermute(piece, ('y', 'x', 'core'), pairs)  13.4 us
    ppermute x7, starting transfers between devices, fast_local(): lax.ppermute(terms[away], ('z', 'core'), [(i, i ^ away) for i in range(8)])  8.12 us
    ppermute x7, waiting for transfers between devices, fast_local(): lax.ppermute(terms[away], ('z', 'core'), [(i, i ^ away) for i in range(8)])  7.39 us
    all_to_all x1, starting transfers between devices, fast_local(): own = lax.all_to_all(own, every, 0, 0, tiled=True)  7.3 us
    ppermute x4, starting transfers between devices, passed(): return lax.ppermute(piece, ('y', 'x', 'core'), pairs)  4.51 us
    all_to_all x1, starting transfers between devices, fast_local(): fields = lax.all_to_all(fields, every, 0, 0, tiled=True)  3.01 us
  transfers between devices with their start and end apart: 13, of which 4 were waited for; matrix products, arithmetic and copies ran while one was open for 2% of the time, Pallas kernels for 19%

profile of v12, /device:TPU:0, one launch (start us, length us, event | category | flops | bytes accessed | tf_op | source)
XLA Modules:
  0.0 98.1 jit_solution(12091107240293380514)
XLA Ops:
  0.6 2.8 %shard_map.75 = bf16[32,2,16,384]{3,2,1,0:T(8,128)(2,1)} custom-call(bf16[8,64,384]{2,1,0:T(8,128)(2,1)} %inputs_ref.1, bf16[8,64,384]{2,1,0:T(8,128)(2,1)} %cot_ref.1), custom_call_target="tpu_custom_call" | custom-call | flops 1000000000 | bytes 3145728 | tf_op jit(solution)/shard_map/pallas_call | solution.py:363
  3.4 7.3 %all-to-all-start = ((bf16[32,2,16,384]{3,2,1,0:T(8,128)(2,1)}), bf16[32,2,16,384]{3,2,1,0:T(8,128)(2,1)S(1)}, u32[]{:S(2)}, u32[]{:S(2)}) async-start(bf16[32,2,16,384]{3,2,1,0:T(8,128)(2,1)} %shard_map.75), calls=%async_computation | async-start | bytes 1572864 | tf_op jit(solution)/shard_map/all_to_all | solution.py:389
  10.8 20.5 %all-to-all-done.own_ref = bf16[32,2,16,384]{3,2,1,0:T(8,128)(2,1)S(1)} async-done(((bf16[32,2,16,384]{3,2,1,0:T(8,128)(2,1)}), bf16[32,2,16,384]{3,2,1,0:T(8,128)(2,1)S(1)}, u32[]{:S(2)}, u32[]{:S(2)}) %all-to-all-start) | async-done | bytes 786464 | tf_op jit(solution)/shard_map/all_to_all | solution.py:389
  31.3 7.9 %shard_map.76 = (bf16[512,384]{1,0:T(8,128)(2,1)S(1)}, bf16[512,384]{1,0:T(8,128)(2,1)S(1)}, bf16[4,192,512]{2,1,0:T(8,128)(2,1)S(1)}, bf16[4,192,512]{2,1,0:T(8,128)(2,1)S(1)}) custom-call(s32[4]{0:T(128)S(1)} %pad_add_fusion.place_ref, bf16[32,2,16,384]{3,2,1,0:T(8,128)(2,1)S(1)} %all-to-all-done.own_ref, bf16[3,3,384,384]{3,2,1,0:T(8,128)(2,1)} %one_ref.3, ...), custom_call_target="tpu_custom_call" | custom-call | flops 2717908992 | bytes 10485760 | tf_op jit(solution)/shard_map/pallas_call | solution.py:363
  39.3 0.9 slice.6
  40.2 1.6 %collective-permute-start.1 = (bf16[3,192,512]{2,1,0:T(8,128)(2,1)}, bf16[3,192,512]{2,1,0:T(8,128)(2,1)S(1)}, u32[]{:S(2)}, u32[]{:S(2)}) collective-permute-start(bf16[3,192,512]{2,1,0:T(8,128)(2,1)} %slice.6), channel_id=1, source_target_pairs={{0,2},{1,5},{2,0},{3,7},{4,6},{5,1},{6,4},{7,3},{8,10},{9,13},{10,... | collective-permute-start | bytes 1769480 | tf_op jit(solution)/shard_map/ppermute | solution.py:375
  41.8 0.9 slice.8
  42.7 1.2 %collective-permute-start.2 = (bf16[3,192,512]{2,1,0:T(8,128)(2,1)}, bf16[3,192,512]{2,1,0:T(8,128)(2,1)S(1)}, u32[]{:S(2)}, u32[]{:S(2)}) collective-permute-start(bf16[3,192,512]{2,1,0:T(8,128)(2,1)} %slice.8), channel_id=1, source_target_pairs={{0,2},{1,5},{2,0},{3,7},{4,6},{5,1},{6,4},{7,3},{8,10},{9,13},{10,... | collective-permute-start | bytes 1769480 | tf_op jit(solution)/shard_map/ppermute | solution.py:375
  43.9 7.7 %shard_map.77 = bf16[32,2,16,384]{3,2,1,0:T(8,128)(2,1)} custom-call(bf16[32,2,16,384]{3,2,1,0:T(8,128)(2,1)S(1)} %all-to-all-done.own_ref, bf16[512,384]{1,0:T(8,128)(2,1)S(1)} %get-tuple-element.40.hidden_ref, bf16[512,384]{1,0:T(8,128)(2,1)S(1)} %get-tuple-element.41.pre_ref, bf16[3,3,384,384]{3,2,1,0:T(8,128)(2,1)} %one_ref.3, ...), custom_call_target="tpu_custom_call" | custom-call | flops 2717908992 | bytes 9437184 | tf_op jit(solution)/shard_map/pallas_call | solution.py:363
  51.6 3.0 %all-to-all-start.1 = ((bf16[32,2,16,384]{3,2,1,0:T(8,128)(2,1)}), bf16[32,2,16,384]{3,2,1,0:T(8,128)(2,1)S(1)}, u32[]{:S(2)}, u32[]{:S(2)}) async-start(bf16[32,2,16,384]{3,2,1,0:T(8,128)(2,1)} %shard_map.77), calls=%async_computation.1 | async-start | bytes 1572864 | tf_op jit(solution)/shard_map/all_to_all | solution.py:424
  54.6 2.0 %collective-permute-done.2.far_pair_ref = bf16[3,192,512]{2,1,0:T(8,128)(2,1)S(1)} collective-permute-done((bf16[3,192,512]{2,1,0:T(8,128)(2,1)}, bf16[3,192,512]{2,1,0:T(8,128)(2,1)S(1)}, u32[]{:S(2)}, u32[]{:S(2)}) %collective-permute-start.2) | collective-permute-done | bytes 589856 | tf_op jit(solution)/shard_map/ppermute | solution.py:375
  56.6 8.1 %shard_map.79 = (f32[192,1728]{1,0:T(8,128)S(1)}, bf16[192,1728]{1,0:T(8,128)(2,1)S(1)}) custom-call(s32[4]{0:T(128)S(1)} %pad_add_fusion.place_ref, bf16[4,192,512]{2,1,0:T(8,128)(2,1)S(1)} %get-tuple-element.44.mine_ref, bf16[4,192,512]{2,1,0:T(8,128)(2,1)S(1)} %collective-permute-done.got_ref, bf16[3,192,512]{2,1,0:T(8,128)(2,1)S(1)} %collective-permute-done.1.far_ref, ...), custom_call_target="tpu_custom_call" | custom-call | flops 5435817984 | bytes 6291456 | tf_op jit(solution)/shard_map/pallas_call | solution.py:363
  64.7 1.6 %collective-permute-start.3 = (bf16[192,1728]{1,0:T(8,128)(2,1)S(1)}, bf16[192,1728]{1,0:T(8,128)(2,1)S(1)}, u32[]{:S(2)}, u32[]{:S(2)}) collective-permute-start(bf16[192,1728]{1,0:T(8,128)(2,1)S(1)} %get-tuple-element.49), channel_id=1, source_target_pairs={{0,4},{1,3},{2,6},{3,1},{4,0},{5,7},{6,2},{7,5},{8,12},{9,11},{10,... | collective-permute-start | bytes 1990664 | tf_op jit(solution)/shard_map/ppermute | solution.py:375
  66.3 11.4 %collective-permute-done.3.got_ref = bf16[192,1728]{1,0:T(8,128)(2,1)S(1)} collective-permute-done((bf16[192,1728]{1,0:T(8,128)(2,1)S(1)}, bf16[192,1728]{1,0:T(8,128)(2,1)S(1)}, u32[]{:S(2)}, u32[]{:S(2)}) %collective-permute-start.3) | collective-permute-done | bytes 663584 | tf_op jit(solution)/shard_map/ppermute | solution.py:375
  77.7 1.9 %shard_map.80 = (bf16[112,384]{1,0:T(8,128)(2,1)S(1)}, bf16[112,384]{1,0:T(8,128)(2,1)S(1)}, bf16[112,384]{1,0:T(8,128)(2,1)S(1)}, bf16[112,384]{1,0:T(8,128)(2,...) custom-call(s32[4]{0:T(128)S(1)} %pad_add_fusion.place_ref, ...), custom_call_target="tpu_custom_call" | custom-call | flops 2717908992 | bytes 4194304 | tf_op jit(solution)/shard_map/pallas_call | solution.py:363
  79.7 1.7 %collective-permute-start.5 = (bf16[112,384]{1,0:T(8,128)(2,1)S(1)}, bf16[112,384]{1,0:T(8,128)(2,1)S(1)}, u32[]{:S(2)}, u32[]{:S(2)}) collective-permute-start(bf16[112,384]{1,0:T(8,128)(2,1)S(1)} %get-tuple-element.52), channel_id=1, source_target_pairs={{0,8},{1,9},{8,0},{9,1},{16,24},{17,25},{24,16},{25,17},{2,10},{3,... | collective-permute-start | bytes 258056 | tf_op jit(solution)/shard_map/ppermute | solution.py:448
  81.4 0.1 collective-permute-start.6
  81.6 2.1 %collective-permute-start.7 = (bf16[112,384]{1,0:T(8,128)(2,1)S(1)}, bf16[112,384]{1,0:T(8,128)(2,1)S(1)}, u32[]{:S(2)}, u32[]{:S(2)}) collective-permute-start(bf16[112,384]{1,0:T(8,128)(2,1)S(1)} %get-tuple-element.54), channel_id=1, source_target_pairs={{0,16},{1,17},{8,24},{9,25},{16,0},{17,1},{24,8},{25,9},{2,18},{3,... | collective-permute-start | bytes 258056 | tf_op jit(solution)/shard_map/ppermute | solution.py:448
  83.6 0.5 collective-permute-start.8
  84.2 1.6 %collective-permute-start.9 = (bf16[112,384]{1,0:T(8,128)(2,1)S(1)}, bf16[112,384]{1,0:T(8,128)(2,1)S(1)}, u32[]{:S(2)}, u32[]{:S(2)}) collective-permute-start(bf16[112,384]{1,0:T(8,128)(2,1)S(1)} %get-tuple-element.56), channel_id=1, source_target_pairs={{0,24},{1,25},{8,16},{9,17},{16,8},{17,9},{24,0},{25,1},{2,26},{3,... | collective-permute-start | bytes 258056 | tf_op jit(solution)/shard_map/ppermute | solution.py:448
  85.8 2.0 %collective-permute-start.10 = (bf16[112,384]{1,0:T(8,128)(2,1)S(1)}, bf16[112,384]{1,0:T(8,128)(2,1)S(1)}, u32[]{:S(2)}, u32[]{:S(2)}) collective-permute-start(bf16[112,384]{1,0:T(8,128)(2,1)S(1)} %get-tuple-element.57), channel_id=1, source_target_pairs={{0,25},{1,24},{8,17},{9,16},{16,9},{17,8},{24,1},{25,0},{2,27},{3,... | collective-permute-start | bytes 258056 | tf_op jit(solution)/shard_map/ppermute | solution.py:448
  87.8 1.5 %shard_map.78 = (bf16[8,64,384]{2,1,0:T(8,128)(2,1)}, bf16[8,64,384]{2,1,0:T(8,128)(2,1)}) custom-call(bf16[32,2,16,384]{3,2,1,0:T(8,128)(2,1)S(1)} %all-to-all-done.1.fields_ref), custom_call_target="tpu_custom_call" | custom-call | flops 1000000000 | bytes 3145728 | tf_op jit(solution)/shard_map/pallas_call | solution.py:363
  89.2 7.4 %collective-permute-done.8.refs_5_ = bf16[112,384]{1,0:T(8,128)(2,1)S(1)} collective-permute-done((bf16[112,384]{1,0:T(8,128)(2,1)S(1)}, bf16[112,384]{1,0:T(8,128)(2,1)S(1)}, u32[]{:S(2)}, u32[]{:S(2)}) %collective-permute-start.8) | collective-permute-done | bytes 86048 | tf_op jit(solution)/shard_map/ppermute | solution.py:448
  96.6 1.5 %shard_map.81 = (f32[3,3,48,96]{3,2,1,0:T(8,128)}, f32[3,3,48,96]{3,2,1,0:T(8,128)}) custom-call(s32[4]{0:T(128)S(1)} %pad_add_fusion.place_ref, bf16[112,384]{1,0:T(8,128)(2,1)S(1)} %get-tuple-element.60.refs_0_, bf16[112,384]{1,0:T(8,128)(2,1)S(1)} %collective-permute-done.4.refs_1_, bf16[112,384]{1,0:T(8,128)(2,1)S(1)} %collective-permute-done.5.refs_2_, ...), custom_call_target="tpu_custom_call" | custom-call | flops 1000000 | bytes 2097152 | tf_op jit(solution)/shard_map/pallas_call | solution.py:363
  (12 shorter events, 0.2 us)
Async XLA Ops:
  3.4 27.9 %all-to-all-start = ((bf16[32,2,16,384]{3,2,1,0:T(8,128)(2,1)}), bf16[32,2,16,384]{3,2,1,0:T(8,128)(2,1)S(1)}, u32[]{:S(2)}, u32[]{:S(2)}) async-start(bf16[32,2,16,384]{3,2,1,0:T(8,128)(2,1)} %shard_map.75), calls=%async_computation | async-start | bytes 1572864 | tf_op jit(solution)/shard_map/all_to_all | solution.py:389
  39.2 2.6 %collective-permute-start = (bf16[4,192,512]{2,1,0:T(8,128)(2,1)S(1)}, bf16[4,192,512]{2,1,0:T(8,128)(2,1)S(1)}, u32[]{:S(2)}, u32[]{:S(2)}) collective-permute-start(bf16[4,192,512]{2,1,0:T(8,128)(2,1)S(1)} %get-tuple-element.39), channel_id=1, source_target_pairs={{0,1},{1,0},{2,3},{3,2},{4,5},{5,4},{6,7},{7,6},{8,9},{9,8},{10,11... | collective-permute-start | bytes 2359304 | tf_op jit(solution)/shard_map/ppermute | solution.py:375
  40.2 14.4 %collective-permute-start.1 = (bf16[3,192,512]{2,1,0:T(8,128)(2,1)}, bf16[3,192,512]{2,1,0:T(8,128)(2,1)S(1)}, u32[]{:S(2)}, u32[]{:S(2)}) collective-permute-start(bf16[3,192,512]{2,1,0:T(8,128)(2,1)} %slice.6), channel_id=1, source_target_pairs={{0,2},{1,5},{2,0},{3,7},{4,6},{5,1},{6,4},{7,3},{8,10},{9,13},{10,... | collective-permute-start | bytes 1769480 | tf_op jit(solution)/shard_map/ppermute | solution.py:375
  42.7 13.9 %collective-permute-start.2 = (bf16[3,192,512]{2,1,0:T(8,128)(2,1)}, bf16[3,192,512]{2,1,0:T(8,128)(2,1)S(1)}, u32[]{:S(2)}, u32[]{:S(2)}) collective-permute-start(bf16[3,192,512]{2,1,0:T(8,128)(2,1)} %slice.8), channel_id=1, source_target_pairs={{0,2},{1,5},{2,0},{3,7},{4,6},{5,1},{6,4},{7,3},{8,10},{9,13},{10,... | collective-permute-start | bytes 1769480 | tf_op jit(solution)/shard_map/ppermute | solution.py:375
  51.6 36.2 %all-to-all-start.1 = ((bf16[32,2,16,384]{3,2,1,0:T(8,128)(2,1)}), bf16[32,2,16,384]{3,2,1,0:T(8,128)(2,1)S(1)}, u32[]{:S(2)}, u32[]{:S(2)}) async-start(bf16[32,2,16,384]{3,2,1,0:T(8,128)(2,1)} %shard_map.77), calls=%async_computation.1 | async-start | bytes 1572864 | tf_op jit(solution)/shard_map/all_to_all | solution.py:424
  64.7 13.0 %collective-permute-start.3 = (bf16[192,1728]{1,0:T(8,128)(2,1)S(1)}, bf16[192,1728]{1,0:T(8,128)(2,1)S(1)}, u32[]{:S(2)}, u32[]{:S(2)}) collective-permute-start(bf16[192,1728]{1,0:T(8,128)(2,1)S(1)} %get-tuple-element.49), channel_id=1, source_target_pairs={{0,4},{1,3},{2,6},{3,1},{4,0},{5,7},{6,2},{7,5},{8,12},{9,11},{10,... | collective-permute-start | bytes 1990664 | tf_op jit(solution)/shard_map/ppermute | solution.py:375
  79.6 4.5 %collective-permute-start.4 = (bf16[112,384]{1,0:T(8,128)(2,1)S(1)}, bf16[112,384]{1,0:T(8,128)(2,1)S(1)}, u32[]{:S(2)}, u32[]{:S(2)}) collective-permute-start(bf16[112,384]{1,0:T(8,128)(2,1)S(1)} %get-tuple-element.51), channel_id=1, source_target_pairs={{0,1},{1,0},{8,9},{9,8},{16,17},{17,16},{24,25},{25,24},{2,3},{3,2... | collective-permute-start | bytes 258056 | tf_op jit(solution)/shard_map/ppermute | solution.py:448
  79.7 6.1 %collective-permute-start.5 = (bf16[112,384]{1,0:T(8,128)(2,1)S(1)}, bf16[112,384]{1,0:T(8,128)(2,1)S(1)}, u32[]{:S(2)}, u32[]{:S(2)}) collective-permute-start(bf16[112,384]{1,0:T(8,128)(2,1)S(1)} %get-tuple-element.52), channel_id=1, source_target_pairs={{0,8},{1,9},{8,0},{9,1},{16,24},{17,25},{24,16},{25,17},{2,10},{3,... | collective-permute-start | bytes 258056 | tf_op jit(solution)/shard_map/ppermute | solution.py:448
  81.4 7.8 %collective-permute-start.6 = (bf16[112,384]{1,0:T(8,128)(2,1)S(1)}, bf16[112,384]{1,0:T(8,128)(2,1)S(1)}, u32[]{:S(2)}, u32[]{:S(2)}) collective-permute-start(bf16[112,384]{1,0:T(8,128)(2,1)S(1)} %get-tuple-element.53), channel_id=1, source_target_pairs={{0,9},{1,8},{8,1},{9,0},{16,25},{17,24},{24,17},{25,16},{2,11},{3,... | collective-permute-start | bytes 258056 | tf_op jit(solution)/shard_map/ppermute | solution.py:448
  81.6 7.7 %collective-permute-start.7 = (bf16[112,384]{1,0:T(8,128)(2,1)S(1)}, bf16[112,384]{1,0:T(8,128)(2,1)S(1)}, u32[]{:S(2)}, u32[]{:S(2)}) collective-permute-start(bf16[112,384]{1,0:T(8,128)(2,1)S(1)} %get-tuple-element.54), channel_id=1, source_target_pairs={{0,16},{1,17},{8,24},{9,25},{16,0},{17,1},{24,8},{25,9},{2,18},{3,... | collective-permute-start | bytes 258056 | tf_op jit(solution)/shard_map/ppermute | solution.py:448
  83.6 13.0 %collective-permute-start.8 = (bf16[112,384]{1,0:T(8,128)(2,1)S(1)}, bf16[112,384]{1,0:T(8,128)(2,1)S(1)}, u32[]{:S(2)}, u32[]{:S(2)}) collective-permute-start(bf16[112,384]{1,0:T(8,128)(2,1)S(1)} %get-tuple-element.55), channel_id=1, source_target_pairs={{0,17},{1,16},{8,25},{9,24},{16,1},{17,0},{24,9},{25,8},{2,19},{3,... | collective-permute-start | bytes 258056 | tf_op jit(solution)/shard_map/ppermute | solution.py:448
  84.2 12.4 %collective-permute-start.9 = (bf16[112,384]{1,0:T(8,128)(2,1)S(1)}, bf16[112,384]{1,0:T(8,128)(2,1)S(1)}, u32[]{:S(2)}, u32[]{:S(2)}) collective-permute-start(bf16[112,384]{1,0:T(8,128)(2,1)S(1)} %get-tuple-element.56), channel_id=1, source_target_pairs={{0,24},{1,25},{8,16},{9,17},{16,8},{17,9},{24,0},{25,1},{2,26},{3,... | collective-permute-start | bytes 258056 | tf_op jit(solution)/shard_map/ppermute | solution.py:448
  85.8 10.8 %collective-permute-start.10 = (bf16[112,384]{1,0:T(8,128)(2,1)S(1)}, bf16[112,384]{1,0:T(8,128)(2,1)S(1)}, u32[]{:S(2)}, u32[]{:S(2)}) collective-permute-start(bf16[112,384]{1,0:T(8,128)(2,1)S(1)} %get-tuple-element.57), channel_id=1, source_target_pairs={{0,25},{1,24},{8,17},{9,16},{16,9},{17,8},{24,1},{25,0},{2,27},{3,... | collective-permute-start | bytes 258056 | tf_op jit(solution)/shard_map/ppermute | solution.py:448

commit v13 on v12

--- a/solution.py
+++ b/solution.py
@@ -123,10 +123,11 @@
         stack_ref[band + cells :, columns] = part[0:band]
 
 
-def convolved(stack_ref, weight_ref, band, cells, copies):
+def convolved(stack_ref, weight_ref, band, cells, copies=None):
     total = None
     for b in range(3):
-        copies[b].wait()
+        if copies:
+            copies[b].wait()
         channels = weight_ref.shape[2]
         tap = weight_ref[:, b].reshape(3 * channels, channels)
         term = jnp.dot(stack_ref[b * band : b * band + cells, :], tap, preferred_element_type=F32)
@@ -134,10 +135,11 @@
     return total
 
 
-def convolved_back(stack_ref, weight_ref, band, cells, copies):
+def convolved_back(stack_ref, weight_ref, band, cells, copies=None):
     total = None
     for b in range(3):
-        copies[b].wait()
+        if copies:
+            copies[b].wait()
         tap = jnp.concatenate([weight_ref[2 - a, 2 - b] for a in range(3)], axis=1)
         term = lax.dot_general(
             stack_ref[b * band : b * band + cells, :],
@@ -190,7 +192,7 @@
 
 
 def inner_kernel(band, step, place_ref, own_ref, one_ref, two_ref,
-                 hidden_ref, pre_ref, mine_ref, give_ref,
+                 hidden_ref, pre_ref, mine_ref, kept_ref, give_ref,
                  one_held, two_held, stack_ref, first_ref, slope_ref, turned_ref, sems):
     x, y, core = place_ref[0], place_ref[1], place_ref[2]
     cells, channels = first_ref.shape
@@ -228,25 +230,25 @@
     pre_ref[...] = (slope_ref[...] * convolved_back(stack_ref, two_held, band, cells, second_weight)).astype(BF16)
     turn(2, pre_ref[...])
 
-    for ref, of, side in ((mine_ref, core, jnp.where(core == 0, x, y)), (give_ref, 1 - core, jnp.where(core == 0, y, x))):
+    for ref, last_ref, of, side in (
+        (mine_ref, kept_ref, core, jnp.where(core == 0, x, y)),
+        (give_ref, give_ref.at[3], 1 - core, jnp.where(core == 0, y, x)),
+    ):
         ref[0] = turned_ref[6 * of]
         ref[1] = turned_ref[6 * of + 1]
         ref[2] = turned_ref[4 - 2 * of + 1 - side]
-        ref[3] = turned_ref[4 - 2 * of + side]
-
-
-def outer_kernel(band, step, own_ref, hidden_ref, pre_ref, one_ref, two_ref, out_ref,
-                 one_held, two_held, stack_ref, sems):
+        last_ref[...] = turned_ref[4 - 2 * of + side]
+
+
+def outer_kernel(band, step, own_ref, hidden_ref, pre_ref, one_ref, two_ref, out_ref, stack_ref, back_ref):
     cells, channels = hidden_ref.shape
     shape = (out_ref.shape[0],) + out_ref.shape[2:]
-    second_weight = by_tap(two_ref, two_held, sems.at[1], range(3))
     write_stack(hidden_ref[...], stack_ref, band, step)
-    second = convolved(stack_ref, two_held, band, cells, second_weight)
-    first_weight = by_tap(one_ref, one_held, sems.at[0], (2, 1, 0))
+    write_stack(pre_ref[...], back_ref, band, step)
+    second = convolved(stack_ref, two_ref, band, cells)
     source = own_ref[:, 0].reshape(cells, channels)
     out_ref[:, 0] = (source.astype(F32) + second).astype(BF16).reshape(shape)
-    write_stack(pre_ref[...], stack_ref, band, step)
-    back = convolved_back(stack_ref, one_held, band, cells, first_weight)
+    back = convolved_back(back_ref, one_ref, band, cells)
     cot = own_ref[:, 1].reshape(cells, channels)
     out_ref[:, 1] = (cot.astype(F32) + back).astype(BF16).reshape(shape)
 
@@ -257,42 +259,61 @@
         yield unit // count, (unit % count) * 16, (unit // 4) * 16, unit % 4
 
 
-def grads_kernel(band, step, place_ref, mine_ref, got_ref, far_ref, far_pair_ref, keep_ref, give_ref, whole_ref, moved_ref):
+def terms_of(band, step, place_ref, sources, whole_ref, moved_ref, write):
     x, y, core = place_ref[0], place_ref[1], place_ref[2]
-    half, cells = mine_ref.shape[1:]
+    half, cells = sources[0][1].shape
     place = lax.broadcasted_iota(jnp.int32, (half, cells), 1) % band
-    for at, (ref, moving) in enumerate(((mine_ref, 3), (got_ref, 3), (far_ref, 2), (far_pair_ref, 2))):
+    inside = {
+        1: jnp.where(place < band - step, 1.0, 0.0).astype(BF16),
+        -1: jnp.where(place >= step, 1.0, 0.0).astype(BF16),
+    }
+    for at, (ref, moving_ref) in enumerate(sources):
         columns = slice(at * cells, (at + 1) * cells)
         whole_ref[0, :, columns] = ref[0]
         whole_ref[1, :, columns] = ref[1]
-        wide = ref[moving].astype(F32)
+        field = moving_ref[...]
         for a in range(-1, 2):
             for b in range(-1, 2):
                 shift = (-(b * band + a * step)) % cells
-                part = pltpu.roll(wide, shift, 1) if shift else wide
-                if a > 0:
-                    part = jnp.where(place < band - step, part, 0.0)
-                if a < 0:
-                    part = jnp.where(place >= step, part, 0.0)
+                part = pltpu.roll(field, shift, 1) if shift else field
+                if a:
+                    part = part * inside[a]
                 tap = (a + 1) * 3 + b + 1
-                moved_ref[jnp.where(core == 0, 8 - tap, tap), :, columns] = part.astype(BF16)
-    moved = moved_ref[...].reshape(9 * half, 4 * cells)
+                moved_ref[jnp.where(core == 0, 8 - tap, tap), :, columns] = part
+    moved = moved_ref[...].reshape(9 * half, len(sources) * cells)
     stays = jnp.where(core == 0, y, x)
-    for ref, which in ((give_ref, 1 - stays), (keep_ref, stays)):
+    for at, which in enumerate((1 - stays, stays)):
         whole = whole_ref[which]
 
         @pl.when(core == 0)
         def _():
-            ref[...] = lax.dot_general(
+            write(at, slice(None), lax.dot_general(
                 whole, moved, (((1,), (1,)), ((), ())), preferred_element_type=F32
-            ).astype(ref.dtype)
+            ))
 
         @pl.when(core == 1)
         def _():
             terms = lax.dot_general(moved, whole, (((1,), (1,)), ((), ())), preferred_element_type=F32)
             for tap in range(9):
                 rows = slice(tap * half, (tap + 1) * half)
-                ref[:, rows] = terms[rows].astype(ref.dtype)
+                write(at, rows, terms[rows])
+
+
+def near_kernel(band, step, place_ref, mine_ref, kept_ref, got_ref, sums_ref, whole_ref, moved_ref):
+    def write(at, columns, terms):
+        sums_ref[at, :, columns] = terms
+
+    sources = ((mine_ref, kept_ref), (got_ref, got_ref.at[3]))
+    terms_of(band, step, place_ref, sources, whole_ref, moved_ref, write)
+
+
+def far_kernel(band, step, place_ref, sums_ref, far_ref, pair_ref, keep_ref, give_ref, whole_ref, moved_ref):
+    def write(at, columns, terms):
+        ref = (give_ref, keep_ref)[at]
+        ref[:, columns] = (sums_ref[at, :, columns] + terms).astype(ref.dtype)
+
+    sources = ((far_ref, far_ref.at[2]), (pair_ref, pair_ref.at[2]))
+    terms_of(band, step, place_ref, sources, whole_ref, moved_ref, write)
 
 
 def pack_kernel(place_ref, keep_ref, got_ref, *refs):
@@ -366,7 +387,7 @@
             in_specs=specs,
             out_specs=jax.tree.map(lambda _: vmem, out_shape),
             scratch_shapes=scratch_shapes,
-            compiler_params=pltpu.CompilerParams(vmem_limit_bytes=32 * 2**20),
+            compiler_params=pltpu.CompilerParams(vmem_limit_bytes=24 * 2**20),
             cost_estimate=pl.CostEstimate(flops=work, bytes_accessed=megabytes * 2**20, transcendentals=0),
         )(*arguments)
 
@@ -390,12 +411,17 @@
     place = jnp.stack([lax.axis_index(axis) for axis in ("x", "y", "core", "z")]).astype(jnp.int32)
     one, two = (pltpu.with_memory_space_constraint(w, pltpu.HBM) for w in (conv1_weight, conv2_weight))
     taps = pltpu.SemaphoreType.DMA((2, 3))
-    pieces = held(4, half, cells)
-    hidden, pre_grad, mine, give = kernel(
+    hidden, pre_grad, mine, kept, give = kernel(
         functools.partial(inner_kernel, band, step),
         [smem, vmem, hbm, hbm],
         (place, own, one, two),
-        (held(cells, channels), held(cells, channels), pieces, pieces),
+        (
+            held(cells, channels),
+            held(cells, channels),
+            held(3, half, cells),
+            held(half, cells),
+            held(4, half, cells),
+        ),
         [
             weights,
             weights,
@@ -409,14 +435,14 @@
         10,
     )
     got = passed(give, None, None, 1)
-    far, far_pair = passed(mine[:3], 0, 1, 0), passed(got[:3], 0, 1, 0)
+    far, far_pair = passed(mine, 0, 1, 0), passed(got[:3], 0, 1, 0)
     hidden, pre_grad, got = lax.optimization_barrier((hidden, pre_grad, got))
     fields = kernel(
         functools.partial(outer_kernel, band, step),
-        [vmem] * 3 + [hbm] * 2,
-        (own, hidden, pre_grad, one, two),
+        [vmem] * 5,
+        (own, hidden, pre_grad, conv1_weight, conv2_weight),
         dealt,
-        [weights, weights, stack, taps],
+        [stack, stack],
         2 * flops,
         9,
     )
@@ -425,13 +451,23 @@
     output, input_grad = kernel(
         functools.partial(gather_kernel, step), [vmem], (fields,), (shaped(*inputs.shape),) * 2, [], 10**9, 3
     )
+    room = [held(2, half, 2 * cells), held(9, half, 2 * cells)]
+    near = kernel(
+        functools.partial(near_kernel, band, step),
+        [smem] + [vmem] * 3,
+        (place, mine, kept, got),
+        held(2, half, 9 * half, kind=F32),
+        room,
+        2 * flops,
+        6,
+    )
     keep, give = kernel(
-        functools.partial(grads_kernel, band, step),
-        [smem] + [vmem] * 4,
-        (place, mine, got, far, far_pair),
+        functools.partial(far_kernel, band, step),
+        [smem] + [vmem] * 3,
+        (place, near, far, far_pair),
         (held(half, 9 * half, kind=F32), held(half, 9 * half)),
-        [held(2, half, 4 * cells), held(9, half, 4 * cells)],
-        4 * flops,
+        room,
+        3 * flops,
         6,
     )
     terms = kernel(

time: 100 us -> 98 us (0.980)
  the two profiles are of different devices: /device:TPU:0 before, /device:TPU:11 now
where the time goes in v13:
time: 98 us; the launch traced here: 97.7 us
  waiting for transfers between devices  46.1 us (47%)
  Pallas kernels  28.8 us (29%)
  starting transfers between devices  21.1 us (22%)
    pallas_call x8, Pallas kernels, kernel(): pl.pallas_call(body, out_shape=out_shape, in_specs=specs, out_specs=jax.t...  28.8 us
    all_to_all x1, waiting for transfers between devices, fast_local(): own = lax.all_to_all(own, every, 0, 0, tiled=True)  19.7 us
    ppermute x4, waiting for transfers between devices, passed(): return lax.ppermute(piece, ('y', 'x', 'core'), pairs)  13.9 us
    ppermute x7, waiting for transfers between devices, fast_local(): lax.ppermute(terms[away], ('z', 'core'), [(i, i ^ away) for i in range(8)])  12.6 us
    ppermute x7, starting transfers between devices, fast_local(): lax.ppermute(terms[away], ('z', 'core'), [(i, i ^ away) for i in range(8)])  8.59 us
    all_to_all x1, starting transfers between devices, fast_local(): own = lax.all_to_all(own, every, 0, 0, tiled=True)  6.34 us
    all_to_all x1, starting transfers between devices, fast_local(): fields = lax.all_to_all(fields, every, 0, 0, tiled=True)  4.78 us
  transfers between devices with their start and end apart: 13, of which 7 were waited for; matrix products, arithmetic and copies ran while one was open for 1% of the time, Pallas kernels for 17%

profile of v13, /device:TPU:11, one launch (start us, length us, event | category | flops | bytes accessed | tf_op | source)
XLA Modules:
  0.0 97.7 jit_solution(14975576067307437596)
XLA Ops:
  0.6 2.8 %shard_map.75 = bf16[32,2,16,384]{3,2,1,0:T(8,128)(2,1)} custom-call(bf16[8,64,384]{2,1,0:T(8,128)(2,1)} %inputs_ref.1, bf16[8,64,384]{2,1,0:T(8,128)(2,1)} %cot_ref.1), custom_call_target="tpu_custom_call" | custom-call | flops 1000000000 | bytes 3145728 | tf_op jit(solution)/shard_map/pallas_call | solution.py:384
  3.4 6.3 %all-to-all-start = ((bf16[32,2,16,384]{3,2,1,0:T(8,128)(2,1)}), bf16[32,2,16,384]{3,2,1,0:T(8,128)(2,1)S(1)}, u32[]{:S(2)}, u32[]{:S(2)}) async-start(bf16[32,2,16,384]{3,2,1,0:T(8,128)(2,1)} %shard_map.75), calls=%async_computation | async-start | bytes 1572864 | tf_op jit(solution)/shard_map/all_to_all | solution.py:410
  9.8 19.7 %all-to-all-done.own_ref = bf16[32,2,16,384]{3,2,1,0:T(8,128)(2,1)S(1)} async-done(((bf16[32,2,16,384]{3,2,1,0:T(8,128)(2,1)}), bf16[32,2,16,384]{3,2,1,0:T(8,128)(2,1)S(1)}, u32[]{:S(2)}, u32[]{:S(2)}) %all-to-all-start) | async-done | bytes 786464 | tf_op jit(solution)/shard_map/all_to_all | solution.py:410
  29.5 8.2 %shard_map.76 = (bf16[512,384]{1,0:T(8,128)(2,1)S(1)}, bf16[512,384]{1,0:T(8,128)(2,1)S(1)}, bf16[3,192,512]{2,1,0:T(8,128)(2,1)S(1)}, bf16[192,512]{1,0:T(8,128)(2,1)S(1)}, bf16[4,192,512]{2,1,0:T(8,128)(2,1)S(1)}) custom-call(s32[4]{0:T(128)S(1)} %pad_add_fusion.place_ref, bf16[32,2,16,384]{3,2,1,0:T(8,128)(2,1)S(1)} %all-to-all-done.own_ref, ...), custom_call_target="tpu_custom_call" | custom-call | flops 2717908992 | bytes 10485760 | tf_op jit(solution)/shard_map/pallas_call | solution.py:384
  37.8 0.7 collective-permute-start.1
  38.4 1.6 %collective-permute-done.got_ref = bf16[4,192,512]{2,1,0:T(8,128)(2,1)S(1)} collective-permute-done((bf16[4,192,512]{2,1,0:T(8,128)(2,1)S(1)}, bf16[4,192,512]{2,1,0:T(8,128)(2,1)S(1)}, u32[]{:S(2)}, u32[]{:S(2)}) %collective-permute-start) | collective-permute-done | bytes 786464 | tf_op jit(solution)/shard_map/ppermute | solution.py:396
  40.0 0.9 slice.4
  41.2 5.0 %shard_map.77 = bf16[32,2,16,384]{3,2,1,0:T(8,128)(2,1)} custom-call(bf16[32,2,16,384]{3,2,1,0:T(8,128)(2,1)S(1)} %all-to-all-done.own_ref, bf16[512,384]{1,0:T(8,128)(2,1)S(1)} %get-tuple-element.41.hidden_ref, bf16[512,384]{1,0:T(8,128)(2,1)S(1)} %get-tuple-element.42.pre_ref, bf16[3,3,384,384]{3,2,1,0:T(8,128)(2,1)S(1)} %copy-done, ...), custom_call_target="tpu_custom_call" | custom-call | flops 2717908992 | bytes 9437184 | tf_op jit(solution)/shard_map/pallas_call | solution.py:384
  46.2 4.8 %all-to-all-start.1 = ((bf16[32,2,16,384]{3,2,1,0:T(8,128)(2,1)}), bf16[32,2,16,384]{3,2,1,0:T(8,128)(2,1)S(1)}, u32[]{:S(2)}, u32[]{:S(2)}) async-start(bf16[32,2,16,384]{3,2,1,0:T(8,128)(2,1)} %shard_map.77), calls=%async_computation.1 | async-start | bytes 1572864 | tf_op jit(solution)/shard_map/all_to_all | solution.py:450
  51.0 4.1 %shard_map.79.sums_ref = f32[2,192,1728]{2,1,0:T(8,128)S(1)} custom-call(s32[4]{0:T(128)S(1)} %pad_add_fusion.place_ref, bf16[3,192,512]{2,1,0:T(8,128)(2,1)S(1)} %get-tuple-element.45.mine_ref, bf16[192,512]{1,0:T(8,128)(2,1)S(1)} %get-tuple-element.46.kept_ref, bf16[4,192,512]{2,1,0:T(8,128)(2,1)S(1)} %collective-permute-done.got_ref), custom_call_target="tpu_custom_call" | custom-call | flops 2717908992 | bytes 6291456 | tf_op jit(solution)/shard_map/pallas_call | solution.py:384
  55.1 4.0 %shard_map.80 = (f32[192,1728]{1,0:T(8,128)S(1)}, bf16[192,1728]{1,0:T(8,128)(2,1)S(1)}) custom-call(s32[4]{0:T(128)S(1)} %pad_add_fusion.place_ref, f32[2,192,1728]{2,1,0:T(8,128)S(1)} %shard_map.79.sums_ref, bf16[3,192,512]{2,1,0:T(8,128)(2,1)S(1)} %collective-permute-done.1.far_ref, bf16[3,192,512]{2,1,0:T(8,128)(2,1)S(1)} %collective-permute-done.2.pair_ref), custom_call_target="tpu_custom_call" | custom-call | flops 4076863488 | bytes 6291456 | tf_op jit(solution)/shard_map/pallas_call | solution.py:384
  59.1 0.3 collective-permute-start.3
  59.5 12.2 %collective-permute-done.3.got_ref = bf16[192,1728]{1,0:T(8,128)(2,1)S(1)} collective-permute-done((bf16[192,1728]{1,0:T(8,128)(2,1)S(1)}, bf16[192,1728]{1,0:T(8,128)(2,1)S(1)}, u32[]{:S(2)}, u32[]{:S(2)}) %collective-permute-start.3) | collective-permute-done | bytes 663584 | tf_op jit(solution)/shard_map/ppermute | solution.py:396
  71.7 1.9 %shard_map.81 = (bf16[112,384]{1,0:T(8,128)(2,1)S(1)}, bf16[112,384]{1,0:T(8,128)(2,1)S(1)}, bf16[112,384]{1,0:T(8,128)(2,1)S(1)}, bf16[112,384]{1,0:T(8,128)(2,...) custom-call(s32[4]{0:T(128)S(1)} %pad_add_fusion.place_ref, ...), custom_call_target="tpu_custom_call" | custom-call | flops 2717908992 | bytes 4194304 | tf_op jit(solution)/shard_map/pallas_call | solution.py:384
  73.6 2.5 %collective-permute-start.4 = (bf16[112,384]{1,0:T(8,128)(2,1)S(1)}, bf16[112,384]{1,0:T(8,128)(2,1)S(1)}, u32[]{:S(2)}, u32[]{:S(2)}) collective-permute-start(bf16[112,384]{1,0:T(8,128)(2,1)S(1)} %get-tuple-element.53), channel_id=1, source_target_pairs={{0,1},{1,0},{8,9},{9,8},{16,17},{17,16},{24,25},{25,24},{2,3},{3,2... | collective-permute-start | bytes 258056 | tf_op jit(solution)/shard_map/ppermute | solution.py:484
  76.1 1.6 %collective-permute-start.5 = (bf16[112,384]{1,0:T(8,128)(2,1)S(1)}, bf16[112,384]{1,0:T(8,128)(2,1)S(1)}, u32[]{:S(2)}, u32[]{:S(2)}) collective-permute-start(bf16[112,384]{1,0:T(8,128)(2,1)S(1)} %get-tuple-element.54), channel_id=1, source_target_pairs={{0,8},{1,9},{8,0},{9,1},{16,24},{17,25},{24,16},{25,17},{2,10},{3,... | collective-permute-start | bytes 258056 | tf_op jit(solution)/shard_map/ppermute | solution.py:484
  77.8 1.0 collective-permute-start.7
  78.8 1.8 %collective-permute-start.8 = (bf16[112,384]{1,0:T(8,128)(2,1)S(1)}, bf16[112,384]{1,0:T(8,128)(2,1)S(1)}, u32[]{:S(2)}, u32[]{:S(2)}) collective-permute-start(bf16[112,384]{1,0:T(8,128)(2,1)S(1)} %get-tuple-element.57), channel_id=1, source_target_pairs={{0,17},{1,16},{8,25},{9,24},{16,1},{17,0},{24,9},{25,8},{2,19},{3,... | collective-permute-start | bytes 258056 | tf_op jit(solution)/shard_map/ppermute | solution.py:484
  80.8 1.4 %collective-permute-start.10 = (bf16[112,384]{1,0:T(8,128)(2,1)S(1)}, bf16[112,384]{1,0:T(8,128)(2,1)S(1)}, u32[]{:S(2)}, u32[]{:S(2)}) collective-permute-start(bf16[112,384]{1,0:T(8,128)(2,1)S(1)} %get-tuple-element.59), channel_id=1, source_target_pairs={{0,25},{1,24},{8,17},{9,16},{16,9},{17,8},{24,1},{25,0},{2,27},{3,... | collective-permute-start | bytes 258056 | tf_op jit(solution)/shard_map/ppermute | solution.py:484
  82.2 1.5 %shard_map.78 = (bf16[8,64,384]{2,1,0:T(8,128)(2,1)}, bf16[8,64,384]{2,1,0:T(8,128)(2,1)}) custom-call(bf16[32,2,16,384]{3,2,1,0:T(8,128)(2,1)S(1)} %all-to-all-done.1.fields_ref), custom_call_target="tpu_custom_call" | custom-call | flops 1000000000 | bytes 3145728 | tf_op jit(solution)/shard_map/pallas_call | solution.py:384
  83.9 6.4 %collective-permute-done.8.refs_5_ = bf16[112,384]{1,0:T(8,128)(2,1)S(1)} collective-permute-done((bf16[112,384]{1,0:T(8,128)(2,1)S(1)}, bf16[112,384]{1,0:T(8,128)(2,1)S(1)}, u32[]{:S(2)}, u32[]{:S(2)}) %collective-permute-start.8) | collective-permute-done | bytes 86048 | tf_op jit(solution)/shard_map/ppermute | solution.py:484
  90.3 4.0 %collective-permute-done.9.refs_6_ = bf16[112,384]{1,0:T(8,128)(2,1)S(1)} collective-permute-done((bf16[112,384]{1,0:T(8,128)(2,1)S(1)}, bf16[112,384]{1,0:T(8,128)(2,1)S(1)}, u32[]{:S(2)}, u32[]{:S(2)}) %collective-permute-start.9) | collective-permute-done | bytes 86048 | tf_op jit(solution)/shard_map/ppermute | solution.py:484
  94.3 1.9 %collective-permute-done.10.refs_7_ = bf16[112,384]{1,0:T(8,128)(2,1)S(1)} collective-permute-done((bf16[112,384]{1,0:T(8,128)(2,1)S(1)}, bf16[112,384]{1,0:T(8,128)(2,1)S(1)}, u32[]{:S(2)}, u32[]{:S(2)}) %collective-permute-start.10) | collective-permute-done | bytes 86048 | tf_op jit(solution)/shard_map/ppermute | solution.py:484
  96.2 1.5 %shard_map.82 = (f32[3,3,48,96]{3,2,1,0:T(8,128)}, f32[3,3,48,96]{3,2,1,0:T(8,128)}) custom-call(s32[4]{0:T(128)S(1)} %pad_add_fusion.place_ref, bf16[112,384]{1,0:T(8,128)(2,1)S(1)} %get-tuple-element.62.refs_0_, bf16[112,384]{1,0:T(8,128)(2,1)S(1)} %collective-permute-done.4.refs_1_, bf16[112,384]{1,0:T(8,128)(2,1)S(1)} %collective-permute-done.5.refs_2_, ...), custom_call_target="tpu_custom_call" | custom-call | flops 1000000 | bytes 2097152 | tf_op jit(solution)/shard_map/pallas_call | solution.py:384
  (16 shorter events, 1.0 us)
Async XLA Ops:
  3.4 26.1 %all-to-all-start = ((bf16[32,2,16,384]{3,2,1,0:T(8,128)(2,1)}), bf16[32,2,16,384]{3,2,1,0:T(8,128)(2,1)S(1)}, u32[]{:S(2)}, u32[]{:S(2)}) async-start(bf16[32,2,16,384]{3,2,1,0:T(8,128)(2,1)} %shard_map.75), calls=%async_computation | async-start | bytes 1572864 | tf_op jit(solution)/shard_map/all_to_all | solution.py:410
  29.5 11.7 %copy-start = (bf16[3,3,384,384]{3,2,1,0:T(8,128)(2,1)S(1)}, bf16[3,3,384,384]{3,2,1,0:T(8,128)(2,1)}, u32[]{:S(2)}) copy-start(bf16[3,3,384,384]{3,2,1,0:T(8,128)(2,1)} %one_ref.3) | copy-start | bytes 7962628
  29.5 11.7 %copy-start.1 = (bf16[3,3,384,384]{3,2,1,0:T(8,128)(2,1)S(1)}, bf16[3,3,384,384]{3,2,1,0:T(8,128)(2,1)}, u32[]{:S(2)}) copy-start(bf16[3,3,384,384]{3,2,1,0:T(8,128)(2,1)} %two_ref.3) | copy-start | bytes 7962628
  37.7 2.4 %collective-permute-start = (bf16[4,192,512]{2,1,0:T(8,128)(2,1)S(1)}, bf16[4,192,512]{2,1,0:T(8,128)(2,1)S(1)}, u32[]{:S(2)}, u32[]{:S(2)}) collective-permute-start(bf16[4,192,512]{2,1,0:T(8,128)(2,1)S(1)} %get-tuple-element.40), channel_id=1, source_target_pairs={{0,1},{1,0},{2,3},{3,2},{4,5},{5,4},{6,7},{7,6},{8,9},{9,8},{10,11... | collective-permute-start | bytes 2359304 | tf_op jit(solution)/shard_map/ppermute | solution.py:396
  37.8 17.4 %collective-permute-start.1 = (bf16[3,192,512]{2,1,0:T(8,128)(2,1)S(1)}, bf16[3,192,512]{2,1,0:T(8,128)(2,1)S(1)}, u32[]{:S(2)}, u32[]{:S(2)}) collective-permute-start(bf16[3,192,512]{2,1,0:T(8,128)(2,1)S(1)} %get-tuple-element.45.mine_ref), channel_id=1, source_target_pairs={{0,2},{1,5},{2,0},{3,7},{4,6},{5,1},{6,4},{7,3},{8,10},{9,13},{10,... | collective-permute-start | bytes 1769480 | tf_op jit(solution)/shard_map/ppermute | solution.py:396
  40.9 14.2 %collective-permute-start.2 = (bf16[3,192,512]{2,1,0:T(8,128)(2,1)}, bf16[3,192,512]{2,1,0:T(8,128)(2,1)S(1)}, u32[]{:S(2)}, u32[]{:S(2)}) collective-permute-start(bf16[3,192,512]{2,1,0:T(8,128)(2,1)} %slice.4), channel_id=1, source_target_pairs={{0,2},{1,5},{2,0},{3,7},{4,6},{5,1},{6,4},{7,3},{8,10},{9,13},{10,... | collective-permute-start | bytes 1769480 | tf_op jit(solution)/shard_map/ppermute | solution.py:396
  46.2 36.0 %all-to-all-start.1 = ((bf16[32,2,16,384]{3,2,1,0:T(8,128)(2,1)}), bf16[32,2,16,384]{3,2,1,0:T(8,128)(2,1)S(1)}, u32[]{:S(2)}, u32[]{:S(2)}) async-start(bf16[32,2,16,384]{3,2,1,0:T(8,128)(2,1)} %shard_map.77), calls=%async_computation.1 | async-start | bytes 1572864 | tf_op jit(solution)/shard_map/all_to_all | solution.py:450
  59.1 12.6 %collective-permute-start.3 = (bf16[192,1728]{1,0:T(8,128)(2,1)S(1)}, bf16[192,1728]{1,0:T(8,128)(2,1)S(1)}, u32[]{:S(2)}, u32[]{:S(2)}) collective-permute-start(bf16[192,1728]{1,0:T(8,128)(2,1)S(1)} %get-tuple-element.51), channel_id=1, source_target_pairs={{0,4},{1,3},{2,6},{3,1},{4,0},{5,7},{6,2},{7,5},{8,12},{9,11},{10,... | collective-permute-start | bytes 1990664 | tf_op jit(solution)/shard_map/ppermute | solution.py:396
  73.6 7.0 %collective-permute-start.4 = (bf16[112,384]{1,0:T(8,128)(2,1)S(1)}, bf16[112,384]{1,0:T(8,128)(2,1)S(1)}, u32[]{:S(2)}, u32[]{:S(2)}) collective-permute-start(bf16[112,384]{1,0:T(8,128)(2,1)S(1)} %get-tuple-element.53), channel_id=1, source_target_pairs={{0,1},{1,0},{8,9},{9,8},{16,17},{17,16},{24,25},{25,24},{2,3},{3,2... | collective-permute-start | bytes 258056 | tf_op jit(solution)/shard_map/ppermute | solution.py:484
  76.1 4.7 %collective-permute-start.5 = (bf16[112,384]{1,0:T(8,128)(2,1)S(1)}, bf16[112,384]{1,0:T(8,128)(2,1)S(1)}, u32[]{:S(2)}, u32[]{:S(2)}) collective-permute-start(bf16[112,384]{1,0:T(8,128)(2,1)S(1)} %get-tuple-element.54), channel_id=1, source_target_pairs={{0,8},{1,9},{8,0},{9,1},{16,24},{17,25},{24,16},{25,17},{2,10},{3,... | collective-permute-start | bytes 258056 | tf_op jit(solution)/shard_map/ppermute | solution.py:484
  77.7 6.0 %collective-permute-start.6 = (bf16[112,384]{1,0:T(8,128)(2,1)S(1)}, bf16[112,384]{1,0:T(8,128)(2,1)S(1)}, u32[]{:S(2)}, u32[]{:S(2)}) collective-permute-start(bf16[112,384]{1,0:T(8,128)(2,1)S(1)} %get-tuple-element.55), channel_id=1, source_target_pairs={{0,9},{1,8},{8,1},{9,0},{16,25},{17,24},{24,17},{25,16},{2,11},{3,... | collective-permute-start | bytes 258056 | tf_op jit(solution)/shard_map/ppermute | solution.py:484
  77.8 6.1 %collective-permute-start.7 = (bf16[112,384]{1,0:T(8,128)(2,1)S(1)}, bf16[112,384]{1,0:T(8,128)(2,1)S(1)}, u32[]{:S(2)}, u32[]{:S(2)}) collective-permute-start(bf16[112,384]{1,0:T(8,128)(2,1)S(1)} %get-tuple-element.56), channel_id=1, source_target_pairs={{0,16},{1,17},{8,24},{9,25},{16,0},{17,1},{24,8},{25,9},{2,18},{3,... | collective-permute-start | bytes 258056 | tf_op jit(solution)/shard_map/ppermute | solution.py:484
  78.8 11.5 %collective-permute-start.8 = (bf16[112,384]{1,0:T(8,128)(2,1)S(1)}, bf16[112,384]{1,0:T(8,128)(2,1)S(1)}, u32[]{:S(2)}, u32[]{:S(2)}) collective-permute-start(bf16[112,384]{1,0:T(8,128)(2,1)S(1)} %get-tuple-element.57), channel_id=1, source_target_pairs={{0,17},{1,16},{8,25},{9,24},{16,1},{17,0},{24,9},{25,8},{2,19},{3,... | collective-permute-start | bytes 258056 | tf_op jit(solution)/shard_map/ppermute | solution.py:484
  80.6 13.7 %collective-permute-start.9 = (bf16[112,384]{1,0:T(8,128)(2,1)S(1)}, bf16[112,384]{1,0:T(8,128)(2,1)S(1)}, u32[]{:S(2)}, u32[]{:S(2)}) collective-permute-start(bf16[112,384]{1,0:T(8,128)(2,1)S(1)} %get-tuple-element.58), channel_id=1, source_target_pairs={{0,24},{1,25},{8,16},{9,17},{16,8},{17,9},{24,0},{25,1},{2,26},{3,... | collective-permute-start | bytes 258056 | tf_op jit(solution)/shard_map/ppermute | solution.py:484
  80.8 15.4 %collective-permute-start.10 = (bf16[112,384]{1,0:T(8,128)(2,1)S(1)}, bf16[112,384]{1,0:T(8,128)(2,1)S(1)}, u32[]{:S(2)}, u32[]{:S(2)}) collective-permute-start(bf16[112,384]{1,0:T(8,128)(2,1)S(1)} %get-tuple-element.59), channel_id=1, source_target_pairs={{0,25},{1,24},{8,17},{9,16},{16,9},{17,8},{24,1},{25,0},{2,27},{3,... | collective-permute-start | bytes 258056 | tf_op jit(solution)/shard_map/ppermute | solution.py:484

commit v14 on v13

--- a/solution.py
+++ b/solution.py
@@ -123,11 +123,9 @@
         stack_ref[band + cells :, columns] = part[0:band]
 
 
-def convolved(stack_ref, weight_ref, band, cells, copies=None):
+def convolved(stack_ref, weight_ref, band, cells):
     total = None
     for b in range(3):
-        if copies:
-            copies[b].wait()
         channels = weight_ref.shape[2]
         tap = weight_ref[:, b].reshape(3 * channels, channels)
         term = jnp.dot(stack_ref[b * band : b * band + cells, :], tap, preferred_element_type=F32)
@@ -135,11 +133,9 @@
     return total
 
 
-def convolved_back(stack_ref, weight_ref, band, cells, copies=None):
+def convolved_back(stack_ref, weight_ref, band, cells):
     total = None
     for b in range(3):
-        if copies:
-            copies[b].wait()
         tap = jnp.concatenate([weight_ref[2 - a, 2 - b] for a in range(3)], axis=1)
         term = lax.dot_general(
             stack_ref[b * band : b * band + cells, :],
@@ -155,7 +151,8 @@
     to = lax.broadcasted_iota(jnp.int32, (cells, cells), 1 if back else 0)
     source = lax.broadcasted_iota(jnp.int32, (cells, cells), 0 if back else 1)
     rows = cells // (devices * step)
-    device, row, column = to // (rows * step), (to // step) % rows, to % step
+    device, inner = lax.div(to, rows * step), lax.rem(to, rows * step)
+    row, column = lax.div(inner, step), lax.rem(inner, step)
     return (source == (row * devices + device) * step + column).astype(BF16)
 
 
@@ -187,16 +184,11 @@
     return copies
 
 
-def by_tap(weight_ref, held_ref, sems, order):
-    return fetched([(weight_ref.at[:, b], held_ref.at[:, b]) for b in order], sems)
-
-
 def inner_kernel(band, step, place_ref, own_ref, one_ref, two_ref,
                  hidden_ref, pre_ref, mine_ref, kept_ref, give_ref,
-                 one_held, two_held, stack_ref, first_ref, slope_ref, turned_ref, sems):
+                 stack_ref, first_ref, slope_ref, turned_ref):
     x, y, core = place_ref[0], place_ref[1], place_ref[2]
     cells, channels = first_ref.shape
-    first_weight = by_tap(one_ref, one_held, sems.at[0], range(3))
     half, rows = channels // 2, 32
     deep = half // 4
 
@@ -209,8 +201,7 @@
 
     source = own_ref[:, 0].reshape(cells, channels)
     write_stack(source, stack_ref, band, step)
-    first_ref[...] = convolved(stack_ref, one_held, band, cells, first_weight)
-    second_weight = by_tap(two_ref, two_held, sems.at[1], (2, 1, 0))
+    first_ref[...] = convolved(stack_ref, one_ref, band, cells)
     turn(0, source)
 
     def activate(at, carry):
@@ -227,7 +218,7 @@
     cot = own_ref[:, 1].reshape(cells, channels)
     write_stack(cot, stack_ref, band, step)
     turn(3, cot)
-    pre_ref[...] = (slope_ref[...] * convolved_back(stack_ref, two_held, band, cells, second_weight)).astype(BF16)
+    pre_ref[...] = (slope_ref[...] * convolved_back(stack_ref, two_ref, band, cells)).astype(BF16)
     turn(2, pre_ref[...])
 
     for ref, last_ref, of, side in (
@@ -396,7 +387,6 @@
         return lax.ppermute(piece, ("y", "x", "core"), pairs)
 
     stack = held(cells + 2 * band, 3 * channels)
-    weights = held(*conv1_weight.shape)
     dealt = shaped(devices, 2, rows * step, channels)
     own = kernel(
         functools.partial(deal_kernel, step),
@@ -409,12 +399,10 @@
     )
     own = lax.all_to_all(own, every, 0, 0, tiled=True)
     place = jnp.stack([lax.axis_index(axis) for axis in ("x", "y", "core", "z")]).astype(jnp.int32)
-    one, two = (pltpu.with_memory_space_constraint(w, pltpu.HBM) for w in (conv1_weight, conv2_weight))
-    taps = pltpu.SemaphoreType.DMA((2, 3))
     hidden, pre_grad, mine, kept, give = kernel(
         functools.partial(inner_kernel, band, step),
-        [smem, vmem, hbm, hbm],
-        (place, own, one, two),
+        [smem] + [vmem] * 3,
+        (place, own, conv1_weight, conv2_weight),
         (
             held(cells, channels),
             held(cells, channels),
@@ -423,13 +411,10 @@
             held(4, half, cells),
         ),
         [
-            weights,
-            weights,
             stack,
             held(cells, channels, kind=F32),
             held(cells, channels, kind=F32),
             held(8, half, cells),
-            taps,
         ],
         2 * flops,
         10,

time: 98 us -> 99.3 us (1.013)
  local copies, waits for them, and re-layouts: 0.89 us -> 4.38 us
  Pallas kernels: 28.8 us -> 26.5 us
    unnamed x4, local copies, waits for them, and re-layouts: 0.01 us -> 3.5 us
    pallas_call x8, Pallas kernels: 28.8 us -> 26.5 us  [kernel(): pl.pallas_call(body, out_shape=out_shape, in_specs=specs, out_specs=jax.t...]
where the time goes in v14:
time: 99.3 us; the launch traced here: 98.9 us
  waiting for transfers between devices  46.1 us (46%)
  Pallas kernels  26.5 us (27%)
  starting transfers between devices  21.1 us (21%)
  local copies, waits for them, and re-layouts  4.38 us (4%)
    pallas_call x8, Pallas kernels, kernel(): pl.pallas_call(body, out_shape=out_shape, in_specs=specs, out_specs=jax.t...  26.5 us
    all_to_all x1, waiting for transfers between devices, fast_local(): own = lax.all_to_all(own, every, 0, 0, tiled=True)  19.7 us
    ppermute x4, waiting for transfers between devices, passed(): return lax.ppermute(piece, ('y', 'x', 'core'), pairs)  13.9 us
    ppermute x7, waiting for transfers between devices, fast_local(): lax.ppermute(terms[away], ('z', 'core'), [(i, i ^ away) for i in range(8)])  12.6 us
    ppermute x7, starting transfers between devices, fast_local(): lax.ppermute(terms[away], ('z', 'core'), [(i, i ^ away) for i in range(8)])  8.62 us
    all_to_all x1, starting transfers between devices, fast_local(): own = lax.all_to_all(own, every, 0, 0, tiled=True)  6.34 us
    all_to_all x1, starting transfers between devices, fast_local(): fields = lax.all_to_all(fields, every, 0, 0, tiled=True)  4.78 us
    unnamed x4, local copies, waits for them, and re-layouts  3.5 us
  transfers between devices with their start and end apart: 13, of which 7 were waited for; matrix products, arithmetic and copies ran while one was open for 1% of the time, Pallas kernels for 17%

profile of v14, /device:TPU:11, one launch (start us, length us, event | category | flops | bytes accessed | tf_op | source)
XLA Modules:
  0.0 98.9 jit_solution(13304393112309119119)
XLA Ops:
  0.6 2.8 %shard_map.75 = bf16[32,2,16,384]{3,2,1,0:T(8,128)(2,1)} custom-call(bf16[8,64,384]{2,1,0:T(8,128)(2,1)} %inputs_ref.1, bf16[8,64,384]{2,1,0:T(8,128)(2,1)} %cot_ref.1), custom_call_target="tpu_custom_call" | custom-call | flops 1000000000 | bytes 3145728 | tf_op jit(solution)/shard_map/pallas_call | solution.py:375
  3.4 6.3 %all-to-all-start = ((bf16[32,2,16,384]{3,2,1,0:T(8,128)(2,1)}), bf16[32,2,16,384]{3,2,1,0:T(8,128)(2,1)S(1)}, u32[]{:S(2)}, u32[]{:S(2)}) async-start(bf16[32,2,16,384]{3,2,1,0:T(8,128)(2,1)} %shard_map.75), calls=%async_computation | async-start | bytes 1572864 | tf_op jit(solution)/shard_map/all_to_all | solution.py:400
  9.8 19.7 %all-to-all-done.own_ref = bf16[32,2,16,384]{3,2,1,0:T(8,128)(2,1)S(1)} async-done(((bf16[32,2,16,384]{3,2,1,0:T(8,128)(2,1)}), bf16[32,2,16,384]{3,2,1,0:T(8,128)(2,1)S(1)}, u32[]{:S(2)}, u32[]{:S(2)}) %all-to-all-start) | async-done | bytes 786464 | tf_op jit(solution)/shard_map/all_to_all | solution.py:400
  29.5 1.7 %copy-done = bf16[3,3,384,384]{3,2,1,0:T(8,128)(2,1)S(1)} copy-done((bf16[3,3,384,384]{3,2,1,0:T(8,128)(2,1)S(1)}, bf16[3,3,384,384]{3,2,1,0:T(8,128)(2,1)}, u32[]{:S(2)}) %copy-start) | copy-done | bytes 2654232
  31.3 1.7 %copy-done.1 = bf16[3,3,384,384]{3,2,1,0:T(8,128)(2,1)S(1)} copy-done((bf16[3,3,384,384]{3,2,1,0:T(8,128)(2,1)S(1)}, bf16[3,3,384,384]{3,2,1,0:T(8,128)(2,1)}, u32[]{:S(2)}) %copy-start.1) | copy-done | bytes 2654232
  33.0 5.9 %shard_map.76 = (bf16[512,384]{1,0:T(8,128)(2,1)S(1)}, bf16[512,384]{1,0:T(8,128)(2,1)S(1)}, bf16[3,192,512]{2,1,0:T(8,128)(2,1)S(1)}, bf16[192,512]{1,0:T(8,128)(2,1)S(1)}, bf16[4,192,512]{2,1,0:T(8,128)(2,1)S(1)}) custom-call(s32[4]{0:T(128)S(1)} %pad_add_fusion.place_ref, bf16[32,2,16,384]{3,2,1,0:T(8,128)(2,1)S(1)} %all-to-all-done.own_ref, ...), custom_call_target="tpu_custom_call" | custom-call | flops 2717908992 | bytes 10485760 | tf_op jit(solution)/shard_map/pallas_call | solution.py:375
  39.6 1.6 %collective-permute-done.got_ref = bf16[4,192,512]{2,1,0:T(8,128)(2,1)S(1)} collective-permute-done((bf16[4,192,512]{2,1,0:T(8,128)(2,1)S(1)}, bf16[4,192,512]{2,1,0:T(8,128)(2,1)S(1)}, u32[]{:S(2)}, u32[]{:S(2)}) %collective-permute-start) | collective-permute-done | bytes 786464 | tf_op jit(solution)/shard_map/ppermute | solution.py:387
  41.2 0.9 slice.4
  42.4 5.0 %shard_map.77 = bf16[32,2,16,384]{3,2,1,0:T(8,128)(2,1)} custom-call(bf16[32,2,16,384]{3,2,1,0:T(8,128)(2,1)S(1)} %all-to-all-done.own_ref, bf16[512,384]{1,0:T(8,128)(2,1)S(1)} %get-tuple-element.41.hidden_ref, bf16[512,384]{1,0:T(8,128)(2,1)S(1)} %get-tuple-element.42.pre_ref, bf16[3,3,384,384]{3,2,1,0:T(8,128)(2,1)S(1)} %copy-done, ...), custom_call_target="tpu_custom_call" | custom-call | flops 2717908992 | bytes 9437184 | tf_op jit(solution)/shard_map/pallas_call | solution.py:375
  47.4 4.8 %all-to-all-start.1 = ((bf16[32,2,16,384]{3,2,1,0:T(8,128)(2,1)}), bf16[32,2,16,384]{3,2,1,0:T(8,128)(2,1)S(1)}, u32[]{:S(2)}, u32[]{:S(2)}) async-start(bf16[32,2,16,384]{3,2,1,0:T(8,128)(2,1)} %shard_map.77), calls=%async_computation.1 | async-start | bytes 1572864 | tf_op jit(solution)/shard_map/all_to_all | solution.py:435
  52.2 4.1 %shard_map.79.sums_ref = f32[2,192,1728]{2,1,0:T(8,128)S(1)} custom-call(s32[4]{0:T(128)S(1)} %pad_add_fusion.place_ref, bf16[3,192,512]{2,1,0:T(8,128)(2,1)S(1)} %get-tuple-element.45.mine_ref, bf16[192,512]{1,0:T(8,128)(2,1)S(1)} %get-tuple-element.46.kept_ref, bf16[4,192,512]{2,1,0:T(8,128)(2,1)S(1)} %collective-permute-done.got_ref), custom_call_target="tpu_custom_call" | custom-call | flops 2717908992 | bytes 6291456 | tf_op jit(solution)/shard_map/pallas_call | solution.py:375
  56.3 4.0 %shard_map.80 = (f32[192,1728]{1,0:T(8,128)S(1)}, bf16[192,1728]{1,0:T(8,128)(2,1)S(1)}) custom-call(s32[4]{0:T(128)S(1)} %pad_add_fusion.place_ref, f32[2,192,1728]{2,1,0:T(8,128)S(1)} %shard_map.79.sums_ref, bf16[3,192,512]{2,1,0:T(8,128)(2,1)S(1)} %collective-permute-done.1.far_ref, bf16[3,192,512]{2,1,0:T(8,128)(2,1)S(1)} %collective-permute-done.2.pair_ref), custom_call_target="tpu_custom_call" | custom-call | flops 4076863488 | bytes 6291456 | tf_op jit(solution)/shard_map/pallas_call | solution.py:375
  60.6 12.2 %collective-permute-done.3.got_ref = bf16[192,1728]{1,0:T(8,128)(2,1)S(1)} collective-permute-done((bf16[192,1728]{1,0:T(8,128)(2,1)S(1)}, bf16[192,1728]{1,0:T(8,128)(2,1)S(1)}, u32[]{:S(2)}, u32[]{:S(2)}) %collective-permute-start.3) | collective-permute-done | bytes 663584 | tf_op jit(solution)/shard_map/ppermute | solution.py:387
  72.9 1.9 %shard_map.81 = (bf16[112,384]{1,0:T(8,128)(2,1)S(1)}, bf16[112,384]{1,0:T(8,128)(2,1)S(1)}, bf16[112,384]{1,0:T(8,128)(2,1)S(1)}, bf16[112,384]{1,0:T(8,128)(2,...) custom-call(s32[4]{0:T(128)S(1)} %pad_add_fusion.place_ref, ...), custom_call_target="tpu_custom_call" | custom-call | flops 2717908992 | bytes 4194304 | tf_op jit(solution)/shard_map/pallas_call | solution.py:375
  74.8 2.5 %collective-permute-start.4 = (bf16[112,384]{1,0:T(8,128)(2,1)S(1)}, bf16[112,384]{1,0:T(8,128)(2,1)S(1)}, u32[]{:S(2)}, u32[]{:S(2)}) collective-permute-start(bf16[112,384]{1,0:T(8,128)(2,1)S(1)} %get-tuple-element.53), channel_id=1, source_target_pairs={{0,1},{1,0},{8,9},{9,8},{16,17},{17,16},{24,25},{25,24},{2,3},{3,2... | collective-permute-start | bytes 258056 | tf_op jit(solution)/shard_map/ppermute | solution.py:469
  77.3 1.6 %collective-permute-start.5 = (bf16[112,384]{1,0:T(8,128)(2,1)S(1)}, bf16[112,384]{1,0:T(8,128)(2,1)S(1)}, u32[]{:S(2)}, u32[]{:S(2)}) collective-permute-start(bf16[112,384]{1,0:T(8,128)(2,1)S(1)} %get-tuple-element.54), channel_id=1, source_target_pairs={{0,8},{1,9},{8,0},{9,1},{16,24},{17,25},{24,16},{25,17},{2,10},{3,... | collective-permute-start | bytes 258056 | tf_op jit(solution)/shard_map/ppermute | solution.py:469
  79.0 0.9 collective-permute-start.7
  79.9 1.9 %collective-permute-start.8 = (bf16[112,384]{1,0:T(8,128)(2,1)S(1)}, bf16[112,384]{1,0:T(8,128)(2,1)S(1)}, u32[]{:S(2)}, u32[]{:S(2)}) collective-permute-start(bf16[112,384]{1,0:T(8,128)(2,1)S(1)} %get-tuple-element.57), channel_id=1, source_target_pairs={{0,17},{1,16},{8,25},{9,24},{16,1},{17,0},{24,9},{25,8},{2,19},{3,... | collective-permute-start | bytes 258056 | tf_op jit(solution)/shard_map/ppermute | solution.py:469
  82.0 1.5 %collective-permute-start.10 = (bf16[112,384]{1,0:T(8,128)(2,1)S(1)}, bf16[112,384]{1,0:T(8,128)(2,1)S(1)}, u32[]{:S(2)}, u32[]{:S(2)}) collective-permute-start(bf16[112,384]{1,0:T(8,128)(2,1)S(1)} %get-tuple-element.59), channel_id=1, source_target_pairs={{0,25},{1,24},{8,17},{9,16},{16,9},{17,8},{24,1},{25,0},{2,27},{3,... | collective-permute-start | bytes 258056 | tf_op jit(solution)/shard_map/ppermute | solution.py:469
  83.4 1.5 %shard_map.78 = (bf16[8,64,384]{2,1,0:T(8,128)(2,1)}, bf16[8,64,384]{2,1,0:T(8,128)(2,1)}) custom-call(bf16[32,2,16,384]{3,2,1,0:T(8,128)(2,1)S(1)} %all-to-all-done.1.fields_ref), custom_call_target="tpu_custom_call" | custom-call | flops 1000000000 | bytes 3145728 | tf_op jit(solution)/shard_map/pallas_call | solution.py:375
  85.1 6.4 %collective-permute-done.8.refs_5_ = bf16[112,384]{1,0:T(8,128)(2,1)S(1)} collective-permute-done((bf16[112,384]{1,0:T(8,128)(2,1)S(1)}, bf16[112,384]{1,0:T(8,128)(2,1)S(1)}, u32[]{:S(2)}, u32[]{:S(2)}) %collective-permute-start.8) | collective-permute-done | bytes 86048 | tf_op jit(solution)/shard_map/ppermute | solution.py:469
  91.4 4.1 %collective-permute-done.9.refs_6_ = bf16[112,384]{1,0:T(8,128)(2,1)S(1)} collective-permute-done((bf16[112,384]{1,0:T(8,128)(2,1)S(1)}, bf16[112,384]{1,0:T(8,128)(2,1)S(1)}, u32[]{:S(2)}, u32[]{:S(2)}) %collective-permute-start.9) | collective-permute-done | bytes 86048 | tf_op jit(solution)/shard_map/ppermute | solution.py:469
  95.5 1.9 %collective-permute-done.10.refs_7_ = bf16[112,384]{1,0:T(8,128)(2,1)S(1)} collective-permute-done((bf16[112,384]{1,0:T(8,128)(2,1)S(1)}, bf16[112,384]{1,0:T(8,128)(2,1)S(1)}, u32[]{:S(2)}, u32[]{:S(2)}) %collective-permute-start.10) | collective-permute-done | bytes 86048 | tf_op jit(solution)/shard_map/ppermute | solution.py:469
  97.5 1.5 %shard_map.82 = (f32[3,3,48,96]{3,2,1,0:T(8,128)}, f32[3,3,48,96]{3,2,1,0:T(8,128)}) custom-call(s32[4]{0:T(128)S(1)} %pad_add_fusion.place_ref, bf16[112,384]{1,0:T(8,128)(2,1)S(1)} %get-tuple-element.62.refs_0_, bf16[112,384]{1,0:T(8,128)(2,1)S(1)} %collective-permute-done.4.refs_1_, bf16[112,384]{1,0:T(8,128)(2,1)S(1)} %collective-permute-done.5.refs_2_, ...), custom_call_target="tpu_custom_call" | custom-call | flops 1000000 | bytes 2097152 | tf_op jit(solution)/shard_map/pallas_call | solution.py:375
  (16 shorter events, 1.9 us)
Async XLA Ops:
  3.4 26.1 %all-to-all-start = ((bf16[32,2,16,384]{3,2,1,0:T(8,128)(2,1)}), bf16[32,2,16,384]{3,2,1,0:T(8,128)(2,1)S(1)}, u32[]{:S(2)}, u32[]{:S(2)}) async-start(bf16[32,2,16,384]{3,2,1,0:T(8,128)(2,1)} %shard_map.75), calls=%async_computation | async-start | bytes 1572864 | tf_op jit(solution)/shard_map/all_to_all | solution.py:400
  29.5 1.8 %copy-start = (bf16[3,3,384,384]{3,2,1,0:T(8,128)(2,1)S(1)}, bf16[3,3,384,384]{3,2,1,0:T(8,128)(2,1)}, u32[]{:S(2)}) copy-start(bf16[3,3,384,384]{3,2,1,0:T(8,128)(2,1)} %one_ref.3) | copy-start | bytes 7962628
  31.2 1.7 %copy-start.1 = (bf16[3,3,384,384]{3,2,1,0:T(8,128)(2,1)S(1)}, bf16[3,3,384,384]{3,2,1,0:T(8,128)(2,1)}, u32[]{:S(2)}) copy-start(bf16[3,3,384,384]{3,2,1,0:T(8,128)(2,1)} %two_ref.3) | copy-start | bytes 7962628
  38.9 2.4 %collective-permute-start = (bf16[4,192,512]{2,1,0:T(8,128)(2,1)S(1)}, bf16[4,192,512]{2,1,0:T(8,128)(2,1)S(1)}, u32[]{:S(2)}, u32[]{:S(2)}) collective-permute-start(bf16[4,192,512]{2,1,0:T(8,128)(2,1)S(1)} %get-tuple-element.40), channel_id=1, source_target_pairs={{0,1},{1,0},{2,3},{3,2},{4,5},{5,4},{6,7},{7,6},{8,9},{9,8},{10,11... | collective-permute-start | bytes 2359304 | tf_op jit(solution)/shard_map/ppermute | solution.py:387
  39.0 17.3 %collective-permute-start.1 = (bf16[3,192,512]{2,1,0:T(8,128)(2,1)S(1)}, bf16[3,192,512]{2,1,0:T(8,128)(2,1)S(1)}, u32[]{:S(2)}, u32[]{:S(2)}) collective-permute-start(bf16[3,192,512]{2,1,0:T(8,128)(2,1)S(1)} %get-tuple-element.45.mine_ref), channel_id=1, source_target_pairs={{0,2},{1,5},{2,0},{3,7},{4,6},{5,1},{6,4},{7,3},{8,10},{9,13},{10,... | collective-permute-start | bytes 1769480 | tf_op jit(solution)/shard_map/ppermute | solution.py:387
  42.1 14.2 %collective-permute-start.2 = (bf16[3,192,512]{2,1,0:T(8,128)(2,1)}, bf16[3,192,512]{2,1,0:T(8,128)(2,1)S(1)}, u32[]{:S(2)}, u32[]{:S(2)}) collective-permute-start(bf16[3,192,512]{2,1,0:T(8,128)(2,1)} %slice.4), channel_id=1, source_target_pairs={{0,2},{1,5},{2,0},{3,7},{4,6},{5,1},{6,4},{7,3},{8,10},{9,13},{10,... | collective-permute-start | bytes 1769480 | tf_op jit(solution)/shard_map/ppermute | solution.py:387
  47.4 36.0 %all-to-all-start.1 = ((bf16[32,2,16,384]{3,2,1,0:T(8,128)(2,1)}), bf16[32,2,16,384]{3,2,1,0:T(8,128)(2,1)S(1)}, u32[]{:S(2)}, u32[]{:S(2)}) async-start(bf16[32,2,16,384]{3,2,1,0:T(8,128)(2,1)} %shard_map.77), calls=%async_computation.1 | async-start | bytes 1572864 | tf_op jit(solution)/shard_map/all_to_all | solution.py:435
  60.3 12.6 %collective-permute-start.3 = (bf16[192,1728]{1,0:T(8,128)(2,1)S(1)}, bf16[192,1728]{1,0:T(8,128)(2,1)S(1)}, u32[]{:S(2)}, u32[]{:S(2)}) collective-permute-start(bf16[192,1728]{1,0:T(8,128)(2,1)S(1)} %get-tuple-element.51), channel_id=1, source_target_pairs={{0,4},{1,3},{2,6},{3,1},{4,0},{5,7},{6,2},{7,5},{8,12},{9,11},{10,... | collective-permute-start | bytes 1990664 | tf_op jit(solution)/shard_map/ppermute | solution.py:387
  74.8 7.1 %collective-permute-start.4 = (bf16[112,384]{1,0:T(8,128)(2,1)S(1)}, bf16[112,384]{1,0:T(8,128)(2,1)S(1)}, u32[]{:S(2)}, u32[]{:S(2)}) collective-permute-start(bf16[112,384]{1,0:T(8,128)(2,1)S(1)} %get-tuple-element.53), channel_id=1, source_target_pairs={{0,1},{1,0},{8,9},{9,8},{16,17},{17,16},{24,25},{25,24},{2,3},{3,2... | collective-permute-start | bytes 258056 | tf_op jit(solution)/shard_map/ppermute | solution.py:469
  77.3 4.6 %collective-permute-start.5 = (bf16[112,384]{1,0:T(8,128)(2,1)S(1)}, bf16[112,384]{1,0:T(8,128)(2,1)S(1)}, u32[]{:S(2)}, u32[]{:S(2)}) collective-permute-start(bf16[112,384]{1,0:T(8,128)(2,1)S(1)} %get-tuple-element.54), channel_id=1, source_target_pairs={{0,8},{1,9},{8,0},{9,1},{16,24},{17,25},{24,16},{25,17},{2,10},{3,... | collective-permute-start | bytes 258056 | tf_op jit(solution)/shard_map/ppermute | solution.py:469
  78.9 6.0 %collective-permute-start.6 = (bf16[112,384]{1,0:T(8,128)(2,1)S(1)}, bf16[112,384]{1,0:T(8,128)(2,1)S(1)}, u32[]{:S(2)}, u32[]{:S(2)}) collective-permute-start(bf16[112,384]{1,0:T(8,128)(2,1)S(1)} %get-tuple-element.55), channel_id=1, source_target_pairs={{0,9},{1,8},{8,1},{9,0},{16,25},{17,24},{24,17},{25,16},{2,11},{3,... | collective-permute-start | bytes 258056 | tf_op jit(solution)/shard_map/ppermute | solution.py:469
  79.0 6.0 %collective-permute-start.7 = (bf16[112,384]{1,0:T(8,128)(2,1)S(1)}, bf16[112,384]{1,0:T(8,128)(2,1)S(1)}, u32[]{:S(2)}, u32[]{:S(2)}) collective-permute-start(bf16[112,384]{1,0:T(8,128)(2,1)S(1)} %get-tuple-element.56), channel_id=1, source_target_pairs={{0,16},{1,17},{8,24},{9,25},{16,0},{17,1},{24,8},{25,9},{2,18},{3,... | collective-permute-start | bytes 258056 | tf_op jit(solution)/shard_map/ppermute | solution.py:469
  79.9 11.5 %collective-permute-start.8 = (bf16[112,384]{1,0:T(8,128)(2,1)S(1)}, bf16[112,384]{1,0:T(8,128)(2,1)S(1)}, u32[]{:S(2)}, u32[]{:S(2)}) collective-permute-start(bf16[112,384]{1,0:T(8,128)(2,1)S(1)} %get-tuple-element.57), channel_id=1, source_target_pairs={{0,17},{1,16},{8,25},{9,24},{16,1},{17,0},{24,9},{25,8},{2,19},{3,... | collective-permute-start | bytes 258056 | tf_op jit(solution)/shard_map/ppermute | solution.py:469
  81.8 13.7 %collective-permute-start.9 = (bf16[112,384]{1,0:T(8,128)(2,1)S(1)}, bf16[112,384]{1,0:T(8,128)(2,1)S(1)}, u32[]{:S(2)}, u32[]{:S(2)}) collective-permute-start(bf16[112,384]{1,0:T(8,128)(2,1)S(1)} %get-tuple-element.58), channel_id=1, source_target_pairs={{0,24},{1,25},{8,16},{9,17},{16,8},{17,9},{24,0},{25,1},{2,26},{3,... | collective-permute-start | bytes 258056 | tf_op jit(solution)/shard_map/ppermute | solution.py:469
  82.0 15.5 %collective-permute-start.10 = (bf16[112,384]{1,0:T(8,128)(2,1)S(1)}, bf16[112,384]{1,0:T(8,128)(2,1)S(1)}, u32[]{:S(2)}, u32[]{:S(2)}) collective-permute-start(bf16[112,384]{1,0:T(8,128)(2,1)S(1)} %get-tuple-element.59), channel_id=1, source_target_pairs={{0,25},{1,24},{8,17},{9,16},{16,9},{17,8},{24,1},{25,0},{2,27},{3,... | collective-permute-start | bytes 258056 | tf_op jit(solution)/shard_map/ppermute | solution.py:469

commit v15 on v13

--- a/solution.py
+++ b/solution.py
@@ -193,7 +193,7 @@
 
 def inner_kernel(band, step, place_ref, own_ref, one_ref, two_ref,
                  hidden_ref, pre_ref, mine_ref, kept_ref, give_ref,
-                 one_held, two_held, stack_ref, first_ref, slope_ref, turned_ref, sems):
+                 one_held, two_held, stack_ref, cot_stack_ref, first_ref, slope_ref, turned_ref, sems):
     x, y, core = place_ref[0], place_ref[1], place_ref[2]
     cells, channels = first_ref.shape
     first_weight = by_tap(one_ref, one_held, sems.at[0], range(3))
@@ -208,10 +208,13 @@
                 turned_ref[at * 2 + h, z * deep : (z + 1) * deep, :] = turned[begin : begin + deep]
 
     source = own_ref[:, 0].reshape(cells, channels)
+    cot = own_ref[:, 1].reshape(cells, channels)
     write_stack(source, stack_ref, band, step)
+    write_stack(cot, cot_stack_ref, band, step)
+    turn(0, source)
+    turn(3, cot)
     first_ref[...] = convolved(stack_ref, one_held, band, cells, first_weight)
     second_weight = by_tap(two_ref, two_held, sems.at[1], (2, 1, 0))
-    turn(0, source)
 
     def activate(at, carry):
         span = pl.ds(pl.multiple_of(at * rows, rows), rows)
@@ -224,10 +227,7 @@
 
     lax.fori_loop(0, cells // rows, activate, 0)
     turn(1, hidden_ref[...])
-    cot = own_ref[:, 1].reshape(cells, channels)
-    write_stack(cot, stack_ref, band, step)
-    turn(3, cot)
-    pre_ref[...] = (slope_ref[...] * convolved_back(stack_ref, two_held, band, cells, second_weight)).astype(BF16)
+    pre_ref[...] = (slope_ref[...] * convolved_back(cot_stack_ref, two_held, band, cells, second_weight)).astype(BF16)
     turn(2, pre_ref[...])
 
     for ref, last_ref, of, side in (
@@ -320,7 +320,7 @@
     out_refs, (sums_ref, send_ref, sems) = refs[:-3], refs[-3:]
     me = place_ref[3] * 2 + place_ref[2]
     half = keep_ref.shape[0]
-    sums_ref[...] = keep_ref[...] + got_ref[...].astype(F32)
+    sums_ref[...] = (keep_ref[...] + got_ref[...].astype(F32)).astype(BF16)
     deep, quarter = half // 4, half // 2
     height = send_ref.shape[1]
     for z in range(4):
@@ -331,8 +331,8 @@
                 blocks[to // 16].append(sums_ref[begin : begin + 16, first : first + quarter])
             for to, parts in enumerate(blocks):
                 while len(parts) < 4:
-                    parts.append(jnp.zeros((16, quarter), F32))
-                send_ref[z * 2 + core, to * 16 : (to + 1) * 16, :] = jnp.concatenate(parts, axis=1).astype(BF16)
+                    parts.append(jnp.zeros((16, quarter), BF16))
+                send_ref[z * 2 + core, to * 16 : (to + 1) * 16, :] = jnp.concatenate(parts, axis=1)
     pairs = [(send_ref.at[me ^ away], ref) for away, ref in enumerate(out_refs)]
     for copy in fetched(pairs, sems):
         copy.wait()
@@ -426,6 +426,7 @@
             weights,
             weights,
             stack,
+            stack,
             held(cells, channels, kind=F32),
             held(cells, channels, kind=F32),
             held(8, half, cells),
@@ -475,7 +476,7 @@
         [smem] + [vmem] * 2,
         (place, keep, passed(give, 1, 0, 0)),
         (held(height, channels),) * 8,
-        [held(half, 9 * half, kind=F32), held(8, height, channels), pltpu.SemaphoreType.DMA((8,))],
+        [held(half, 9 * half), held(8, height, channels), pltpu.SemaphoreType.DMA((8,))],
         2 * flops,
         4,
     )

time: 98 us -> 98.3 us (level)
  no operation moved by 1% of the time
where the time goes in v15:
time: 98.3 us; the launch traced here: 98 us
  waiting for transfers between devices  46.1 us (47%)
  Pallas kernels  29.1 us (30%)
  starting transfers between devices  21.1 us (21%)
    pallas_call x8, Pallas kernels, kernel(): pl.pallas_call(body, out_shape=out_shape, in_specs=specs, out_specs=jax.t...  29.1 us
    all_to_all x1, waiting for transfers between devices, fast_local(): own = lax.all_to_all(own, every, 0, 0, tiled=True)  19.7 us
    ppermute x4, waiting for transfers between devices, passed(): return lax.ppermute(piece, ('y', 'x', 'core'), pairs)  13.8 us
    ppermute x7, waiting for transfers between devices, fast_local(): lax.ppermute(terms[away], ('z', 'core'), [(i, i ^ away) for i in range(8)])  12.6 us
    ppermute x7, starting transfers between devices, fast_local(): lax.ppermute(terms[away], ('z', 'core'), [(i, i ^ away) for i in range(8)])  8.58 us
    all_to_all x1, starting transfers between devices, fast_local(): own = lax.all_to_all(own, every, 0, 0, tiled=True)  6.34 us
    all_to_all x1, starting transfers between devices, fast_local(): fields = lax.all_to_all(fields, every, 0, 0, tiled=True)  4.79 us
  transfers between devices with their start and end apart: 13, of which 7 were waited for; matrix products, arithmetic and copies ran while one was open for 1% of the time, Pallas kernels for 17%

profile of v15, /device:TPU:11, one launch (start us, length us, event | category | flops | bytes accessed | tf_op | source)
XLA Modules:
  0.0 98.0 jit_solution(17246696047650494447)
XLA Ops:
  0.6 2.8 %shard_map.75 = bf16[32,2,16,384]{3,2,1,0:T(8,128)(2,1)} custom-call(bf16[8,64,384]{2,1,0:T(8,128)(2,1)} %inputs_ref.1, bf16[8,64,384]{2,1,0:T(8,128)(2,1)} %cot_ref.1), custom_call_target="tpu_custom_call" | custom-call | flops 1000000000 | bytes 3145728 | tf_op jit(solution)/shard_map/pallas_call | solution.py:384
  3.4 6.3 %all-to-all-start = ((bf16[32,2,16,384]{3,2,1,0:T(8,128)(2,1)}), bf16[32,2,16,384]{3,2,1,0:T(8,128)(2,1)S(1)}, u32[]{:S(2)}, u32[]{:S(2)}) async-start(bf16[32,2,16,384]{3,2,1,0:T(8,128)(2,1)} %shard_map.75), calls=%async_computation | async-start | bytes 1572864 | tf_op jit(solution)/shard_map/all_to_all | solution.py:410
  9.8 19.7 %all-to-all-done.own_ref = bf16[32,2,16,384]{3,2,1,0:T(8,128)(2,1)S(1)} async-done(((bf16[32,2,16,384]{3,2,1,0:T(8,128)(2,1)}), bf16[32,2,16,384]{3,2,1,0:T(8,128)(2,1)S(1)}, u32[]{:S(2)}, u32[]{:S(2)}) %all-to-all-start) | async-done | bytes 786464 | tf_op jit(solution)/shard_map/all_to_all | solution.py:410
  29.5 8.5 %shard_map.76 = (bf16[512,384]{1,0:T(8,128)(2,1)S(1)}, bf16[512,384]{1,0:T(8,128)(2,1)S(1)}, bf16[3,192,512]{2,1,0:T(8,128)(2,1)S(1)}, bf16[192,512]{1,0:T(8,128)(2,1)S(1)}, bf16[4,192,512]{2,1,0:T(8,128)(2,1)S(1)}) custom-call(s32[4]{0:T(128)S(1)} %pad_add_fusion.place_ref, bf16[32,2,16,384]{3,2,1,0:T(8,128)(2,1)S(1)} %all-to-all-done.own_ref, ...), custom_call_target="tpu_custom_call" | custom-call | flops 2717908992 | bytes 10485760 | tf_op jit(solution)/shard_map/pallas_call | solution.py:384
  38.1 0.7 collective-permute-start.1
  38.8 1.6 %collective-permute-done.got_ref = bf16[4,192,512]{2,1,0:T(8,128)(2,1)S(1)} collective-permute-done((bf16[4,192,512]{2,1,0:T(8,128)(2,1)S(1)}, bf16[4,192,512]{2,1,0:T(8,128)(2,1)S(1)}, u32[]{:S(2)}, u32[]{:S(2)}) %collective-permute-start) | collective-permute-done | bytes 786464 | tf_op jit(solution)/shard_map/ppermute | solution.py:396
  40.3 0.9 slice.4
  41.5 5.0 %shard_map.77 = bf16[32,2,16,384]{3,2,1,0:T(8,128)(2,1)} custom-call(bf16[32,2,16,384]{3,2,1,0:T(8,128)(2,1)S(1)} %all-to-all-done.own_ref, bf16[512,384]{1,0:T(8,128)(2,1)S(1)} %get-tuple-element.41.hidden_ref, bf16[512,384]{1,0:T(8,128)(2,1)S(1)} %get-tuple-element.42.pre_ref, bf16[3,3,384,384]{3,2,1,0:T(8,128)(2,1)S(1)} %copy-done, ...), custom_call_target="tpu_custom_call" | custom-call | flops 2717908992 | bytes 9437184 | tf_op jit(solution)/shard_map/pallas_call | solution.py:384
  46.6 4.8 %all-to-all-start.1 = ((bf16[32,2,16,384]{3,2,1,0:T(8,128)(2,1)}), bf16[32,2,16,384]{3,2,1,0:T(8,128)(2,1)S(1)}, u32[]{:S(2)}, u32[]{:S(2)}) async-start(bf16[32,2,16,384]{3,2,1,0:T(8,128)(2,1)} %shard_map.77), calls=%async_computation.1 | async-start | bytes 1572864 | tf_op jit(solution)/shard_map/all_to_all | solution.py:451
  51.4 4.1 %shard_map.79.sums_ref = f32[2,192,1728]{2,1,0:T(8,128)S(1)} custom-call(s32[4]{0:T(128)S(1)} %pad_add_fusion.place_ref, bf16[3,192,512]{2,1,0:T(8,128)(2,1)S(1)} %get-tuple-element.45.mine_ref, bf16[192,512]{1,0:T(8,128)(2,1)S(1)} %get-tuple-element.46.kept_ref, bf16[4,192,512]{2,1,0:T(8,128)(2,1)S(1)} %collective-permute-done.got_ref), custom_call_target="tpu_custom_call" | custom-call | flops 2717908992 | bytes 6291456 | tf_op jit(solution)/shard_map/pallas_call | solution.py:384
  55.5 4.0 %shard_map.80 = (f32[192,1728]{1,0:T(8,128)S(1)}, bf16[192,1728]{1,0:T(8,128)(2,1)S(1)}) custom-call(s32[4]{0:T(128)S(1)} %pad_add_fusion.place_ref, f32[2,192,1728]{2,1,0:T(8,128)S(1)} %shard_map.79.sums_ref, bf16[3,192,512]{2,1,0:T(8,128)(2,1)S(1)} %collective-permute-done.1.far_ref, bf16[3,192,512]{2,1,0:T(8,128)(2,1)S(1)} %collective-permute-done.2.pair_ref), custom_call_target="tpu_custom_call" | custom-call | flops 4076863488 | bytes 6291456 | tf_op jit(solution)/shard_map/pallas_call | solution.py:384
  59.5 0.3 collective-permute-start.3
  59.8 12.2 %collective-permute-done.3.got_ref = bf16[192,1728]{1,0:T(8,128)(2,1)S(1)} collective-permute-done((bf16[192,1728]{1,0:T(8,128)(2,1)S(1)}, bf16[192,1728]{1,0:T(8,128)(2,1)S(1)}, u32[]{:S(2)}, u32[]{:S(2)}) %collective-permute-start.3) | collective-permute-done | bytes 663584 | tf_op jit(solution)/shard_map/ppermute | solution.py:396
  72.1 1.9 %shard_map.81 = (bf16[112,384]{1,0:T(8,128)(2,1)S(1)}, bf16[112,384]{1,0:T(8,128)(2,1)S(1)}, bf16[112,384]{1,0:T(8,128)(2,1)S(1)}, bf16[112,384]{1,0:T(8,128)(2,...) custom-call(s32[4]{0:T(128)S(1)} %pad_add_fusion.place_ref, ...), custom_call_target="tpu_custom_call" | custom-call | flops 2717908992 | bytes 4194304 | tf_op jit(solution)/shard_map/pallas_call | solution.py:384
  73.9 2.5 %collective-permute-start.4 = (bf16[112,384]{1,0:T(8,128)(2,1)S(1)}, bf16[112,384]{1,0:T(8,128)(2,1)S(1)}, u32[]{:S(2)}, u32[]{:S(2)}) collective-permute-start(bf16[112,384]{1,0:T(8,128)(2,1)S(1)} %get-tuple-element.53), channel_id=1, source_target_pairs={{0,1},{1,0},{8,9},{9,8},{16,17},{17,16},{24,25},{25,24},{2,3},{3,2... | collective-permute-start | bytes 258056 | tf_op jit(solution)/shard_map/ppermute | solution.py:485
  76.4 1.6 %collective-permute-start.5 = (bf16[112,384]{1,0:T(8,128)(2,1)S(1)}, bf16[112,384]{1,0:T(8,128)(2,1)S(1)}, u32[]{:S(2)}, u32[]{:S(2)}) collective-permute-start(bf16[112,384]{1,0:T(8,128)(2,1)S(1)} %get-tuple-element.54), channel_id=1, source_target_pairs={{0,8},{1,9},{8,0},{9,1},{16,24},{17,25},{24,16},{25,17},{2,10},{3,... | collective-permute-start | bytes 258056 | tf_op jit(solution)/shard_map/ppermute | solution.py:485
  78.1 1.0 collective-permute-start.7
  79.1 1.8 %collective-permute-start.8 = (bf16[112,384]{1,0:T(8,128)(2,1)S(1)}, bf16[112,384]{1,0:T(8,128)(2,1)S(1)}, u32[]{:S(2)}, u32[]{:S(2)}) collective-permute-start(bf16[112,384]{1,0:T(8,128)(2,1)S(1)} %get-tuple-element.57), channel_id=1, source_target_pairs={{0,17},{1,16},{8,25},{9,24},{16,1},{17,0},{24,9},{25,8},{2,19},{3,... | collective-permute-start | bytes 258056 | tf_op jit(solution)/shard_map/ppermute | solution.py:485
  81.1 1.4 %collective-permute-start.10 = (bf16[112,384]{1,0:T(8,128)(2,1)S(1)}, bf16[112,384]{1,0:T(8,128)(2,1)S(1)}, u32[]{:S(2)}, u32[]{:S(2)}) collective-permute-start(bf16[112,384]{1,0:T(8,128)(2,1)S(1)} %get-tuple-element.59), channel_id=1, source_target_pairs={{0,25},{1,24},{8,17},{9,16},{16,9},{17,8},{24,1},{25,0},{2,27},{3,... | collective-permute-start | bytes 258056 | tf_op jit(solution)/shard_map/ppermute | solution.py:485
  82.5 1.5 %shard_map.78 = (bf16[8,64,384]{2,1,0:T(8,128)(2,1)}, bf16[8,64,384]{2,1,0:T(8,128)(2,1)}) custom-call(bf16[32,2,16,384]{3,2,1,0:T(8,128)(2,1)S(1)} %all-to-all-done.1.fields_ref), custom_call_target="tpu_custom_call" | custom-call | flops 1000000000 | bytes 3145728 | tf_op jit(solution)/shard_map/pallas_call | solution.py:384
  84.2 6.4 %collective-permute-done.8.refs_5_ = bf16[112,384]{1,0:T(8,128)(2,1)S(1)} collective-permute-done((bf16[112,384]{1,0:T(8,128)(2,1)S(1)}, bf16[112,384]{1,0:T(8,128)(2,1)S(1)}, u32[]{:S(2)}, u32[]{:S(2)}) %collective-permute-start.8) | collective-permute-done | bytes 86048 | tf_op jit(solution)/shard_map/ppermute | solution.py:485
  90.6 4.0 %collective-permute-done.9.refs_6_ = bf16[112,384]{1,0:T(8,128)(2,1)S(1)} collective-permute-done((bf16[112,384]{1,0:T(8,128)(2,1)S(1)}, bf16[112,384]{1,0:T(8,128)(2,1)S(1)}, u32[]{:S(2)}, u32[]{:S(2)}) %collective-permute-start.9) | collective-permute-done | bytes 86048 | tf_op jit(solution)/shard_map/ppermute | solution.py:485
  94.6 1.9 %collective-permute-done.10.refs_7_ = bf16[112,384]{1,0:T(8,128)(2,1)S(1)} collective-permute-done((bf16[112,384]{1,0:T(8,128)(2,1)S(1)}, bf16[112,384]{1,0:T(8,128)(2,1)S(1)}, u32[]{:S(2)}, u32[]{:S(2)}) %collective-permute-start.10) | collective-permute-done | bytes 86048 | tf_op jit(solution)/shard_map/ppermute | solution.py:485
  96.6 1.5 %shard_map.82 = (f32[3,3,48,96]{3,2,1,0:T(8,128)}, f32[3,3,48,96]{3,2,1,0:T(8,128)}) custom-call(s32[4]{0:T(128)S(1)} %pad_add_fusion.place_ref, bf16[112,384]{1,0:T(8,128)(2,1)S(1)} %get-tuple-element.62.refs_0_, bf16[112,384]{1,0:T(8,128)(2,1)S(1)} %collective-permute-done.4.refs_1_, bf16[112,384]{1,0:T(8,128)(2,1)S(1)} %collective-permute-done.5.refs_2_, ...), custom_call_target="tpu_custom_call" | custom-call | flops 1000000 | bytes 2097152 | tf_op jit(solution)/shard_map/pallas_call | solution.py:384
  (16 shorter events, 1.0 us)
Async XLA Ops:
  3.4 26.1 %all-to-all-start = ((bf16[32,2,16,384]{3,2,1,0:T(8,128)(2,1)}), bf16[32,2,16,384]{3,2,1,0:T(8,128)(2,1)S(1)}, u32[]{:S(2)}, u32[]{:S(2)}) async-start(bf16[32,2,16,384]{3,2,1,0:T(8,128)(2,1)} %shard_map.75), calls=%async_computation | async-start | bytes 1572864 | tf_op jit(solution)/shard_map/all_to_all | solution.py:410
  29.5 12.0 %copy-start = (bf16[3,3,384,384]{3,2,1,0:T(8,128)(2,1)S(1)}, bf16[3,3,384,384]{3,2,1,0:T(8,128)(2,1)}, u32[]{:S(2)}) copy-start(bf16[3,3,384,384]{3,2,1,0:T(8,128)(2,1)} %one_ref.3) | copy-start | bytes 7962628
  29.5 12.0 %copy-start.1 = (bf16[3,3,384,384]{3,2,1,0:T(8,128)(2,1)S(1)}, bf16[3,3,384,384]{3,2,1,0:T(8,128)(2,1)}, u32[]{:S(2)}) copy-start(bf16[3,3,384,384]{3,2,1,0:T(8,128)(2,1)} %two_ref.3) | copy-start | bytes 7962628
  38.0 2.4 %collective-permute-start = (bf16[4,192,512]{2,1,0:T(8,128)(2,1)S(1)}, bf16[4,192,512]{2,1,0:T(8,128)(2,1)S(1)}, u32[]{:S(2)}, u32[]{:S(2)}) collective-permute-start(bf16[4,192,512]{2,1,0:T(8,128)(2,1)S(1)} %get-tuple-element.40), channel_id=1, source_target_pairs={{0,1},{1,0},{2,3},{3,2},{4,5},{5,4},{6,7},{7,6},{8,9},{9,8},{10,11... | collective-permute-start | bytes 2359304 | tf_op jit(solution)/shard_map/ppermute | solution.py:396
  38.1 17.4 %collective-permute-start.1 = (bf16[3,192,512]{2,1,0:T(8,128)(2,1)S(1)}, bf16[3,192,512]{2,1,0:T(8,128)(2,1)S(1)}, u32[]{:S(2)}, u32[]{:S(2)}) collective-permute-start(bf16[3,192,512]{2,1,0:T(8,128)(2,1)S(1)} %get-tuple-element.45.mine_ref), channel_id=1, source_target_pairs={{0,2},{1,5},{2,0},{3,7},{4,6},{5,1},{6,4},{7,3},{8,10},{9,13},{10,... | collective-permute-start | bytes 1769480 | tf_op jit(solution)/shard_map/ppermute | solution.py:396
  41.2 14.2 %collective-permute-start.2 = (bf16[3,192,512]{2,1,0:T(8,128)(2,1)}, bf16[3,192,512]{2,1,0:T(8,128)(2,1)S(1)}, u32[]{:S(2)}, u32[]{:S(2)}) collective-permute-start(bf16[3,192,512]{2,1,0:T(8,128)(2,1)} %slice.4), channel_id=1, source_target_pairs={{0,2},{1,5},{2,0},{3,7},{4,6},{5,1},{6,4},{7,3},{8,10},{9,13},{10,... | collective-permute-start | bytes 1769480 | tf_op jit(solution)/shard_map/ppermute | solution.py:396
  46.6 36.0 %all-to-all-start.1 = ((bf16[32,2,16,384]{3,2,1,0:T(8,128)(2,1)}), bf16[32,2,16,384]{3,2,1,0:T(8,128)(2,1)S(1)}, u32[]{:S(2)}, u32[]{:S(2)}) async-start(bf16[32,2,16,384]{3,2,1,0:T(8,128)(2,1)} %shard_map.77), calls=%async_computation.1 | async-start | bytes 1572864 | tf_op jit(solution)/shard_map/all_to_all | solution.py:451
  59.5 12.6 %collective-permute-start.3 = (bf16[192,1728]{1,0:T(8,128)(2,1)S(1)}, bf16[192,1728]{1,0:T(8,128)(2,1)S(1)}, u32[]{:S(2)}, u32[]{:S(2)}) collective-permute-start(bf16[192,1728]{1,0:T(8,128)(2,1)S(1)} %get-tuple-element.51), channel_id=1, source_target_pairs={{0,4},{1,3},{2,6},{3,1},{4,0},{5,7},{6,2},{7,5},{8,12},{9,11},{10,... | collective-permute-start | bytes 1990664 | tf_op jit(solution)/shard_map/ppermute | solution.py:396
  73.9 7.0 %collective-permute-start.4 = (bf16[112,384]{1,0:T(8,128)(2,1)S(1)}, bf16[112,384]{1,0:T(8,128)(2,1)S(1)}, u32[]{:S(2)}, u32[]{:S(2)}) collective-permute-start(bf16[112,384]{1,0:T(8,128)(2,1)S(1)} %get-tuple-element.53), channel_id=1, source_target_pairs={{0,1},{1,0},{8,9},{9,8},{16,17},{17,16},{24,25},{25,24},{2,3},{3,2... | collective-permute-start | bytes 258056 | tf_op jit(solution)/shard_map/ppermute | solution.py:485
  76.4 4.7 %collective-permute-start.5 = (bf16[112,384]{1,0:T(8,128)(2,1)S(1)}, bf16[112,384]{1,0:T(8,128)(2,1)S(1)}, u32[]{:S(2)}, u32[]{:S(2)}) collective-permute-start(bf16[112,384]{1,0:T(8,128)(2,1)S(1)} %get-tuple-element.54), channel_id=1, source_target_pairs={{0,8},{1,9},{8,0},{9,1},{16,24},{17,25},{24,16},{25,17},{2,10},{3,... | collective-permute-start | bytes 258056 | tf_op jit(solution)/shard_map/ppermute | solution.py:485
  78.0 6.0 %collective-permute-start.6 = (bf16[112,384]{1,0:T(8,128)(2,1)S(1)}, bf16[112,384]{1,0:T(8,128)(2,1)S(1)}, u32[]{:S(2)}, u32[]{:S(2)}) collective-permute-start(bf16[112,384]{1,0:T(8,128)(2,1)S(1)} %get-tuple-element.55), channel_id=1, source_target_pairs={{0,9},{1,8},{8,1},{9,0},{16,25},{17,24},{24,17},{25,16},{2,11},{3,... | collective-permute-start | bytes 258056 | tf_op jit(solution)/shard_map/ppermute | solution.py:485
  78.1 6.1 %collective-permute-start.7 = (bf16[112,384]{1,0:T(8,128)(2,1)S(1)}, bf16[112,384]{1,0:T(8,128)(2,1)S(1)}, u32[]{:S(2)}, u32[]{:S(2)}) collective-permute-start(bf16[112,384]{1,0:T(8,128)(2,1)S(1)} %get-tuple-element.56), channel_id=1, source_target_pairs={{0,16},{1,17},{8,24},{9,25},{16,0},{17,1},{24,8},{25,9},{2,18},{3,... | collective-permute-start | bytes 258056 | tf_op jit(solution)/shard_map/ppermute | solution.py:485
  79.1 11.5 %collective-permute-start.8 = (bf16[112,384]{1,0:T(8,128)(2,1)S(1)}, bf16[112,384]{1,0:T(8,128)(2,1)S(1)}, u32[]{:S(2)}, u32[]{:S(2)}) collective-permute-start(bf16[112,384]{1,0:T(8,128)(2,1)S(1)} %get-tuple-element.57), channel_id=1, source_target_pairs={{0,17},{1,16},{8,25},{9,24},{16,1},{17,0},{24,9},{25,8},{2,19},{3,... | collective-permute-start | bytes 258056 | tf_op jit(solution)/shard_map/ppermute | solution.py:485
  80.9 13.7 %collective-permute-start.9 = (bf16[112,384]{1,0:T(8,128)(2,1)S(1)}, bf16[112,384]{1,0:T(8,128)(2,1)S(1)}, u32[]{:S(2)}, u32[]{:S(2)}) collective-permute-start(bf16[112,384]{1,0:T(8,128)(2,1)S(1)} %get-tuple-element.58), channel_id=1, source_target_pairs={{0,24},{1,25},{8,16},{9,17},{16,8},{17,9},{24,0},{25,1},{2,26},{3,... | collective-permute-start | bytes 258056 | tf_op jit(solution)/shard_map/ppermute | solution.py:485
  81.1 15.4 %collective-permute-start.10 = (bf16[112,384]{1,0:T(8,128)(2,1)S(1)}, bf16[112,384]{1,0:T(8,128)(2,1)S(1)}, u32[]{:S(2)}, u32[]{:S(2)}) collective-permute-start(bf16[112,384]{1,0:T(8,128)(2,1)S(1)} %get-tuple-element.59), channel_id=1, source_target_pairs={{0,25},{1,24},{8,17},{9,16},{16,9},{17,8},{24,1},{25,0},{2,27},{3,... | collective-permute-start | bytes 258056 | tf_op jit(solution)/shard_map/ppermute | solution.py:485

commit v16 on v13

--- a/solution.py
+++ b/solution.py
@@ -192,7 +192,7 @@
 
 
 def inner_kernel(band, step, place_ref, own_ref, one_ref, two_ref,
-                 hidden_ref, pre_ref, mine_ref, kept_ref, give_ref,
+                 hidden_ref, pre_ref, mine_ref, kept_ref, give_ref, cross_ref,
                  one_held, two_held, stack_ref, first_ref, slope_ref, turned_ref, sems):
     x, y, core = place_ref[0], place_ref[1], place_ref[2]
     cells, channels = first_ref.shape
@@ -230,14 +230,15 @@
     pre_ref[...] = (slope_ref[...] * convolved_back(stack_ref, two_held, band, cells, second_weight)).astype(BF16)
     turn(2, pre_ref[...])
 
-    for ref, last_ref, of, side in (
-        (mine_ref, kept_ref, core, jnp.where(core == 0, x, y)),
-        (give_ref, give_ref.at[3], 1 - core, jnp.where(core == 0, y, x)),
+    for ref, of, half_of in (
+        (mine_ref, core, jnp.where(core == 0, 1 - x, 1 - y)),
+        (give_ref, 1 - core, jnp.where(core == 0, y, x)),
+        (cross_ref, 1 - core, jnp.where(core == 0, 1 - y, 1 - x)),
     ):
         ref[0] = turned_ref[6 * of]
         ref[1] = turned_ref[6 * of + 1]
-        ref[2] = turned_ref[4 - 2 * of + 1 - side]
-        last_ref[...] = turned_ref[4 - 2 * of + side]
+        ref[2] = turned_ref[4 - 2 * of + half_of]
+    kept_ref[...] = turned_ref[4 - 2 * core + jnp.where(core == 0, x, y)]
 
 
 def outer_kernel(band, step, own_ref, hidden_ref, pre_ref, one_ref, two_ref, out_ref, stack_ref, back_ref):
@@ -303,7 +304,7 @@
     def write(at, columns, terms):
         sums_ref[at, :, columns] = terms
 
-    sources = ((mine_ref, kept_ref), (got_ref, got_ref.at[3]))
+    sources = ((mine_ref, kept_ref), (got_ref, got_ref.at[2]))
     terms_of(band, step, place_ref, sources, whole_ref, moved_ref, write)
 
 
@@ -320,7 +321,7 @@
     out_refs, (sums_ref, send_ref, sems) = refs[:-3], refs[-3:]
     me = place_ref[3] * 2 + place_ref[2]
     half = keep_ref.shape[0]
-    sums_ref[...] = keep_ref[...] + got_ref[...].astype(F32)
+    sums_ref[...] = (keep_ref[...] + got_ref[...].astype(F32)).astype(BF16)
     deep, quarter = half // 4, half // 2
     height = send_ref.shape[1]
     for z in range(4):
@@ -331,8 +332,8 @@
                 blocks[to // 16].append(sums_ref[begin : begin + 16, first : first + quarter])
             for to, parts in enumerate(blocks):
                 while len(parts) < 4:
-                    parts.append(jnp.zeros((16, quarter), F32))
-                send_ref[z * 2 + core, to * 16 : (to + 1) * 16, :] = jnp.concatenate(parts, axis=1).astype(BF16)
+                    parts.append(jnp.zeros((16, quarter), BF16))
+                send_ref[z * 2 + core, to * 16 : (to + 1) * 16, :] = jnp.concatenate(parts, axis=1)
     pairs = [(send_ref.at[me ^ away], ref) for away, ref in enumerate(out_refs)]
     for copy in fetched(pairs, sems):
         copy.wait()
@@ -411,7 +412,7 @@
     place = jnp.stack([lax.axis_index(axis) for axis in ("x", "y", "core", "z")]).astype(jnp.int32)
     one, two = (pltpu.with_memory_space_constraint(w, pltpu.HBM) for w in (conv1_weight, conv2_weight))
     taps = pltpu.SemaphoreType.DMA((2, 3))
-    hidden, pre_grad, mine, kept, give = kernel(
+    hidden, pre_grad, mine, kept, give, cross = kernel(
         functools.partial(inner_kernel, band, step),
         [smem, vmem, hbm, hbm],
         (place, own, one, two),
@@ -420,7 +421,8 @@
             held(cells, channels),
             held(3, half, cells),
             held(half, cells),
-            held(4, half, cells),
+            held(3, half, cells),
+            held(3, half, cells),
         ),
         [
             weights,
@@ -435,7 +437,7 @@
         10,
     )
     got = passed(give, None, None, 1)
-    far, far_pair = passed(mine, 0, 1, 0), passed(got[:3], 0, 1, 0)
+    far, far_pair = passed(mine, 0, 1, 0), passed(cross, 1, 0, 1)
     hidden, pre_grad, got = lax.optimization_barrier((hidden, pre_grad, got))
     fields = kernel(
         functools.partial(outer_kernel, band, step),
@@ -475,7 +477,7 @@
         [smem] + [vmem] * 2,
         (place, keep, passed(give, 1, 0, 0)),
         (held(height, channels),) * 8,
-        [held(half, 9 * half, kind=F32), held(8, height, channels), pltpu.SemaphoreType.DMA((8,))],
+        [held(half, 9 * half), held(8, height, channels), pltpu.SemaphoreType.DMA((8,))],
         2 * flops,
         4,
     )

time: 98 us -> 103 us (1.051)
  waiting for transfers between devices: 46.1 us -> 50.1 us
  starting transfers between devices: 21.1 us -> 22.2 us
    ppermute x4, waiting for transfers between devices: 13.9 us -> 17.8 us  [passed(): return lax.ppermute(piece, ('y', 'x', 'core'), pairs)]
  transfers between devices with their start and end apart: 13 -> 13, of which waited for: 7 -> 8; matrix products, arithmetic and copies ran while one was open for 1% -> 0% of each run, Pallas kernels for 17% -> 16%
where the time goes in v16:
time: 103 us
  waiting for transfers between devices  50.1 us (49%)
  Pallas kernels  29.7 us (29%)
  starting transfers between devices  22.2 us (22%)
    pallas_call x8, Pallas kernels, kernel(): pl.pallas_call(body, out_shape=out_shape, in_specs=specs, out_specs=jax.t...  29.7 us
    all_to_all x1, waiting for transfers between devices, fast_local(): own = lax.all_to_all(own, every, 0, 0, tiled=True)  19.7 us
    ppermute x4, waiting for transfers between devices, passed(): return lax.ppermute(piece, ('y', 'x', 'core'), pairs)  17.8 us
    ppermute x7, waiting for transfers between devices, fast_local(): lax.ppermute(terms[away], ('z', 'core'), [(i, i ^ away) for i in range(8)])  12.6 us
    ppermute x7, starting transfers between devices, fast_local(): lax.ppermute(terms[away], ('z', 'core'), [(i, i ^ away) for i in range(8)])  9.08 us
    all_to_all x1, starting transfers between devices, fast_local(): own = lax.all_to_all(own, every, 0, 0, tiled=True)  6.34 us
    all_to_all x1, starting transfers between devices, fast_local(): fields = lax.all_to_all(fields, every, 0, 0, tiled=True)  4.5 us
    ppermute x4, starting transfers between devices, passed(): return lax.ppermute(piece, ('y', 'x', 'core'), pairs)  2.33 us
  transfers between devices with their start and end apart: 13, of which 8 were waited for; matrix products, arithmetic and copies ran while one was open for 0% of the time, Pallas kernels for 16%

profile of v16, /device:TPU:11, one launch (start us, length us, event | category | flops | bytes accessed | tf_op | source)
XLA Modules:
  0.0 102.8 jit_solution(2528254993156474824)
XLA Ops:
  0.6 2.8 %shard_map.75 = bf16[32,2,16,384]{3,2,1,0:T(8,128)(2,1)} custom-call(bf16[8,64,384]{2,1,0:T(8,128)(2,1)} %inputs_ref.1, bf16[8,64,384]{2,1,0:T(8,128)(2,1)} %cot_ref.1), custom_call_target="tpu_custom_call" | custom-call | flops 1000000000 | bytes 3145728 | tf_op jit(solution)/shard_map/pallas_call | solution.py:385
  3.4 6.3 %all-to-all-start = ((bf16[32,2,16,384]{3,2,1,0:T(8,128)(2,1)}), bf16[32,2,16,384]{3,2,1,0:T(8,128)(2,1)S(1)}, u32[]{:S(2)}, u32[]{:S(2)}) async-start(bf16[32,2,16,384]{3,2,1,0:T(8,128)(2,1)} %shard_map.75), calls=%async_computation | async-start | bytes 1572864 | tf_op jit(solution)/shard_map/all_to_all | solution.py:411
  9.8 19.7 %all-to-all-done.own_ref = bf16[32,2,16,384]{3,2,1,0:T(8,128)(2,1)S(1)} async-done(((bf16[32,2,16,384]{3,2,1,0:T(8,128)(2,1)}), bf16[32,2,16,384]{3,2,1,0:T(8,128)(2,1)S(1)}, u32[]{:S(2)}, u32[]{:S(2)}) %all-to-all-start) | async-done | bytes 786464 | tf_op jit(solution)/shard_map/all_to_all | solution.py:411
  29.5 9.0 %shard_map.76 = (bf16[512,384]{1,0:T(8,128)(2,1)S(1)}, bf16[512,384]{1,0:T(8,128)(2,1)S(1)}, bf16[3,192,512]{2,1,0:T(8,128)(2,1)S(1)}, bf16[192,512]{1,0:T(8,128...) custom-call(s32[4]{0:T(128)S(1)} %pad_add_fusion.place_ref, ...), custom_call_target="tpu_custom_call" | custom-call | flops 2717908992 | bytes 10485760 | tf_op jit(solution)/shard_map/pallas_call | solution.py:385
  38.6 1.1 %collective-permute-start.2 = (bf16[3,192,512]{2,1,0:T(8,128)(2,1)}, bf16[3,192,512]{2,1,0:T(8,128)(2,1)S(1)}, u32[]{:S(2)}, u32[]{:S(2)}) collective-permute-start(bf16[3,192,512]{2,1,0:T(8,128)(2,1)} %get-tuple-element.49), channel_id=1, source_target_pairs={{0,5},{1,2},{2,7},{3,0},{4,1},{5,6},{6,3},{7,4},{8,13},{9,10},{10,... | collective-permute-start | bytes 1769480 | tf_op jit(solution)/shard_map/ppermute | solution.py:397
  39.7 0.7 collective-permute-start.1
  40.6 5.0 %shard_map.77 = bf16[32,2,16,384]{3,2,1,0:T(8,128)(2,1)} custom-call(bf16[32,2,16,384]{3,2,1,0:T(8,128)(2,1)S(1)} %all-to-all-done.own_ref, bf16[512,384]{1,0:T(8,128)(2,1)S(1)} %get-tuple-element.42.hidden_ref, bf16[512,384]{1,0:T(8,128)(2,1)S(1)} %get-tuple-element.43.pre_ref, bf16[3,3,384,384]{3,2,1,0:T(8,128)(2,1)S(1)} %copy-done, ...), custom_call_target="tpu_custom_call" | custom-call | flops 2717908992 | bytes 9437184 | tf_op jit(solution)/shard_map/pallas_call | solution.py:385
  45.6 4.5 %all-to-all-start.1 = ((bf16[32,2,16,384]{3,2,1,0:T(8,128)(2,1)}), bf16[32,2,16,384]{3,2,1,0:T(8,128)(2,1)S(1)}, u32[]{:S(2)}, u32[]{:S(2)}) async-start(bf16[32,2,16,384]{3,2,1,0:T(8,128)(2,1)} %shard_map.77), calls=%async_computation.1 | async-start | bytes 1572864 | tf_op jit(solution)/shard_map/all_to_all | solution.py:452
  50.1 6.1 %collective-permute-done.2.pair_ref = bf16[3,192,512]{2,1,0:T(8,128)(2,1)S(1)} collective-permute-done((bf16[3,192,512]{2,1,0:T(8,128)(2,1)}, bf16[3,192,512]{2,1,0:T(8,128)(2,1)S(1)}, u32[]{:S(2)}, u32[]{:S(2)}) %collective-permute-start.2) | collective-permute-done | bytes 589856 | tf_op jit(solution)/shard_map/ppermute | solution.py:397
  56.2 1.7 %collective-permute-done.1.far_ref = bf16[3,192,512]{2,1,0:T(8,128)(2,1)S(1)} collective-permute-done((bf16[3,192,512]{2,1,0:T(8,128)(2,1)S(1)}, bf16[3,192,512]{2,1,0:T(8,128)(2,1)S(1)}, u32[]{:S(2)}, u32[]{:S(2)}) %collective-permute-start.1) | collective-permute-done | bytes 589856 | tf_op jit(solution)/shard_map/ppermute | solution.py:397
  57.9 4.1 %shard_map.79.sums_ref = f32[2,192,1728]{2,1,0:T(8,128)S(1)} custom-call(s32[4]{0:T(128)S(1)} %pad_add_fusion.place_ref, bf16[3,192,512]{2,1,0:T(8,128)(2,1)S(1)} %get-tuple-element.46.mine_ref, bf16[192,512]{1,0:T(8,128)(2,1)S(1)} %get-tuple-element.47.kept_ref, bf16[3,192,512]{2,1,0:T(8,128)(2,1)S(1)} %collective-permute-done.got_ref), custom_call_target="tpu_custom_call" | custom-call | flops 2717908992 | bytes 6291456 | tf_op jit(solution)/shard_map/pallas_call | solution.py:385
  62.0 4.0 %shard_map.80 = (f32[192,1728]{1,0:T(8,128)S(1)}, bf16[192,1728]{1,0:T(8,128)(2,1)S(1)}) custom-call(s32[4]{0:T(128)S(1)} %pad_add_fusion.place_ref, f32[2,192,1728]{2,1,0:T(8,128)S(1)} %shard_map.79.sums_ref, bf16[3,192,512]{2,1,0:T(8,128)(2,1)S(1)} %collective-permute-done.1.far_ref, bf16[3,192,512]{2,1,0:T(8,128)(2,1)S(1)} %collective-permute-done.2.pair_ref), custom_call_target="tpu_custom_call" | custom-call | flops 4076863488 | bytes 6291456 | tf_op jit(solution)/shard_map/pallas_call | solution.py:385
  66.5 9.7 %collective-permute-done.3.got_ref = bf16[192,1728]{1,0:T(8,128)(2,1)S(1)} collective-permute-done((bf16[192,1728]{1,0:T(8,128)(2,1)S(1)}, bf16[192,1728]{1,0:T(8,128)(2,1)S(1)}, u32[]{:S(2)}, u32[]{:S(2)}) %collective-permute-start.3) | collective-permute-done | bytes 663584 | tf_op jit(solution)/shard_map/ppermute | solution.py:397
  76.2 1.9 %shard_map.81 = (bf16[112,384]{1,0:T(8,128)(2,1)S(1)}, bf16[112,384]{1,0:T(8,128)(2,1)S(1)}, bf16[112,384]{1,0:T(8,128)(2,1)S(1)}, bf16[112,384]{1,0:T(8,128)(2,...) custom-call(s32[4]{0:T(128)S(1)} %pad_add_fusion.place_ref, ...), custom_call_target="tpu_custom_call" | custom-call | flops 2717908992 | bytes 4194304 | tf_op jit(solution)/shard_map/pallas_call | solution.py:385
  78.1 1.8 %collective-permute-start.4 = (bf16[112,384]{1,0:T(8,128)(2,1)S(1)}, bf16[112,384]{1,0:T(8,128)(2,1)S(1)}, u32[]{:S(2)}, u32[]{:S(2)}) collective-permute-start(bf16[112,384]{1,0:T(8,128)(2,1)S(1)} %get-tuple-element.55), channel_id=1, source_target_pairs={{0,1},{1,0},{8,9},{9,8},{16,17},{17,16},{24,25},{25,24},{2,3},{3,2... | collective-permute-start | bytes 258056 | tf_op jit(solution)/shard_map/ppermute | solution.py:486
  79.9 2.8 %collective-permute-start.5 = (bf16[112,384]{1,0:T(8,128)(2,1)S(1)}, bf16[112,384]{1,0:T(8,128)(2,1)S(1)}, u32[]{:S(2)}, u32[]{:S(2)}) collective-permute-start(bf16[112,384]{1,0:T(8,128)(2,1)S(1)} %get-tuple-element.56), channel_id=1, source_target_pairs={{0,8},{1,9},{8,0},{9,1},{16,24},{17,25},{24,16},{25,17},{2,10},{3,... | collective-permute-start | bytes 258056 | tf_op jit(solution)/shard_map/ppermute | solution.py:486
  82.8 0.8 collective-permute-start.7
  83.7 2.1 %collective-permute-start.8 = (bf16[112,384]{1,0:T(8,128)(2,1)S(1)}, bf16[112,384]{1,0:T(8,128)(2,1)S(1)}, u32[]{:S(2)}, u32[]{:S(2)}) collective-permute-start(bf16[112,384]{1,0:T(8,128)(2,1)S(1)} %get-tuple-element.59), channel_id=1, source_target_pairs={{0,17},{1,16},{8,25},{9,24},{16,1},{17,0},{24,9},{25,8},{2,19},{3,... | collective-permute-start | bytes 258056 | tf_op jit(solution)/shard_map/ppermute | solution.py:486
  85.7 1.5 %collective-permute-start.10 = (bf16[112,384]{1,0:T(8,128)(2,1)S(1)}, bf16[112,384]{1,0:T(8,128)(2,1)S(1)}, u32[]{:S(2)}, u32[]{:S(2)}) collective-permute-start(bf16[112,384]{1,0:T(8,128)(2,1)S(1)} %get-tuple-element.61), channel_id=1, source_target_pairs={{0,25},{1,24},{8,17},{9,16},{16,9},{17,8},{24,1},{25,0},{2,27},{3,... | collective-permute-start | bytes 258056 | tf_op jit(solution)/shard_map/ppermute | solution.py:486
  87.2 1.5 %shard_map.78 = (bf16[8,64,384]{2,1,0:T(8,128)(2,1)}, bf16[8,64,384]{2,1,0:T(8,128)(2,1)}) custom-call(bf16[32,2,16,384]{3,2,1,0:T(8,128)(2,1)S(1)} %all-to-all-done.1.fields_ref), custom_call_target="tpu_custom_call" | custom-call | flops 1000000000 | bytes 3145728 | tf_op jit(solution)/shard_map/pallas_call | solution.py:385
  88.7 6.7 %collective-permute-done.8.refs_5_ = bf16[112,384]{1,0:T(8,128)(2,1)S(1)} collective-permute-done((bf16[112,384]{1,0:T(8,128)(2,1)S(1)}, bf16[112,384]{1,0:T(8,128)(2,1)S(1)}, u32[]{:S(2)}, u32[]{:S(2)}) %collective-permute-start.8) | collective-permute-done | bytes 86048 | tf_op jit(solution)/shard_map/ppermute | solution.py:486
  95.4 4.1 %collective-permute-done.9.refs_6_ = bf16[112,384]{1,0:T(8,128)(2,1)S(1)} collective-permute-done((bf16[112,384]{1,0:T(8,128)(2,1)S(1)}, bf16[112,384]{1,0:T(8,128)(2,1)S(1)}, u32[]{:S(2)}, u32[]{:S(2)}) %collective-permute-start.9) | collective-permute-done | bytes 86048 | tf_op jit(solution)/shard_map/ppermute | solution.py:486
  99.5 1.8 %collective-permute-done.10.refs_7_ = bf16[112,384]{1,0:T(8,128)(2,1)S(1)} collective-permute-done((bf16[112,384]{1,0:T(8,128)(2,1)S(1)}, bf16[112,384]{1,0:T(8,128)(2,1)S(1)}, u32[]{:S(2)}, u32[]{:S(2)}) %collective-permute-start.10) | collective-permute-done | bytes 86048 | tf_op jit(solution)/shard_map/ppermute | solution.py:486
  101.3 1.5 %shard_map.82 = (f32[3,3,48,96]{3,2,1,0:T(8,128)}, f32[3,3,48,96]{3,2,1,0:T(8,128)}) custom-call(s32[4]{0:T(128)S(1)} %pad_add_fusion.place_ref, bf16[112,384]{1,0:T(8,128)(2,1)S(1)} %get-tuple-element.64.refs_0_, bf16[112,384]{1,0:T(8,128)(2,1)S(1)} %collective-permute-done.4.refs_1_, bf16[112,384]{1,0:T(8,128)(2,1)S(1)} %collective-permute-done.5.refs_2_, ...), custom_call_target="tpu_custom_call" | custom-call | flops 1000000 | bytes 2097152 | tf_op jit(solution)/shard_map/pallas_call | solution.py:385
  (15 shorter events, 1.0 us)
Async XLA Ops:
  3.4 26.1 %all-to-all-start = ((bf16[32,2,16,384]{3,2,1,0:T(8,128)(2,1)}), bf16[32,2,16,384]{3,2,1,0:T(8,128)(2,1)S(1)}, u32[]{:S(2)}, u32[]{:S(2)}) async-start(bf16[32,2,16,384]{3,2,1,0:T(8,128)(2,1)} %shard_map.75), calls=%async_computation | async-start | bytes 1572864 | tf_op jit(solution)/shard_map/all_to_all | solution.py:411
  29.5 11.1 %copy-start = (bf16[3,3,384,384]{3,2,1,0:T(8,128)(2,1)S(1)}, bf16[3,3,384,384]{3,2,1,0:T(8,128)(2,1)}, u32[]{:S(2)}) copy-start(bf16[3,3,384,384]{3,2,1,0:T(8,128)(2,1)} %one_ref.3) | copy-start | bytes 7962628
  29.5 11.1 %copy-start.1 = (bf16[3,3,384,384]{3,2,1,0:T(8,128)(2,1)S(1)}, bf16[3,3,384,384]{3,2,1,0:T(8,128)(2,1)}, u32[]{:S(2)}) copy-start(bf16[3,3,384,384]{3,2,1,0:T(8,128)(2,1)} %two_ref.3) | copy-start | bytes 7962628
  38.5 2.1 %collective-permute-start = (bf16[3,192,512]{2,1,0:T(8,128)(2,1)S(1)}, bf16[3,192,512]{2,1,0:T(8,128)(2,1)S(1)}, u32[]{:S(2)}, u32[]{:S(2)}) collective-permute-start(bf16[3,192,512]{2,1,0:T(8,128)(2,1)S(1)} %get-tuple-element.41), channel_id=1, source_target_pairs={{0,1},{1,0},{2,3},{3,2},{4,5},{5,4},{6,7},{7,6},{8,9},{9,8},{10,11... | collective-permute-start | bytes 1769480 | tf_op jit(solution)/shard_map/ppermute | solution.py:397
  38.6 17.6 %collective-permute-start.2 = (bf16[3,192,512]{2,1,0:T(8,128)(2,1)}, bf16[3,192,512]{2,1,0:T(8,128)(2,1)S(1)}, u32[]{:S(2)}, u32[]{:S(2)}) collective-permute-start(bf16[3,192,512]{2,1,0:T(8,128)(2,1)} %get-tuple-element.49), channel_id=1, source_target_pairs={{0,5},{1,2},{2,7},{3,0},{4,1},{5,6},{6,3},{7,4},{8,13},{9,10},{10,... | collective-permute-start | bytes 1769480 | tf_op jit(solution)/shard_map/ppermute | solution.py:397
  39.7 18.2 %collective-permute-start.1 = (bf16[3,192,512]{2,1,0:T(8,128)(2,1)S(1)}, bf16[3,192,512]{2,1,0:T(8,128)(2,1)S(1)}, u32[]{:S(2)}, u32[]{:S(2)}) collective-permute-start(bf16[3,192,512]{2,1,0:T(8,128)(2,1)S(1)} %get-tuple-element.46.mine_ref), channel_id=1, source_target_pairs={{0,2},{1,5},{2,0},{3,7},{4,6},{5,1},{6,4},{7,3},{8,10},{9,13},{10,... | collective-permute-start | bytes 1769480 | tf_op jit(solution)/shard_map/ppermute | solution.py:397
  45.6 41.6 %all-to-all-start.1 = ((bf16[32,2,16,384]{3,2,1,0:T(8,128)(2,1)}), bf16[32,2,16,384]{3,2,1,0:T(8,128)(2,1)S(1)}, u32[]{:S(2)}, u32[]{:S(2)}) async-start(bf16[32,2,16,384]{3,2,1,0:T(8,128)(2,1)} %shard_map.77), calls=%async_computation.1 | async-start | bytes 1572864 | tf_op jit(solution)/shard_map/all_to_all | solution.py:452
  66.0 10.2 %collective-permute-start.3 = (bf16[192,1728]{1,0:T(8,128)(2,1)S(1)}, bf16[192,1728]{1,0:T(8,128)(2,1)S(1)}, u32[]{:S(2)}, u32[]{:S(2)}) collective-permute-start(bf16[192,1728]{1,0:T(8,128)(2,1)S(1)} %get-tuple-element.53), channel_id=1, source_target_pairs={{0,4},{1,3},{2,6},{3,1},{4,0},{5,7},{6,2},{7,5},{8,12},{9,11},{10,... | collective-permute-start | bytes 1990664 | tf_op jit(solution)/shard_map/ppermute | solution.py:397
  78.1 7.6 %collective-permute-start.4 = (bf16[112,384]{1,0:T(8,128)(2,1)S(1)}, bf16[112,384]{1,0:T(8,128)(2,1)S(1)}, u32[]{:S(2)}, u32[]{:S(2)}) collective-permute-start(bf16[112,384]{1,0:T(8,128)(2,1)S(1)} %get-tuple-element.55), channel_id=1, source_target_pairs={{0,1},{1,0},{8,9},{9,8},{16,17},{17,16},{24,25},{25,24},{2,3},{3,2... | collective-permute-start | bytes 258056 | tf_op jit(solution)/shard_map/ppermute | solution.py:486
  79.9 5.8 %collective-permute-start.5 = (bf16[112,384]{1,0:T(8,128)(2,1)S(1)}, bf16[112,384]{1,0:T(8,128)(2,1)S(1)}, u32[]{:S(2)}, u32[]{:S(2)}) collective-permute-start(bf16[112,384]{1,0:T(8,128)(2,1)S(1)} %get-tuple-element.56), channel_id=1, source_target_pairs={{0,8},{1,9},{8,0},{9,1},{16,24},{17,25},{24,16},{25,17},{2,10},{3,... | collective-permute-start | bytes 258056 | tf_op jit(solution)/shard_map/ppermute | solution.py:486
  82.8 5.9 %collective-permute-start.6 = (bf16[112,384]{1,0:T(8,128)(2,1)S(1)}, bf16[112,384]{1,0:T(8,128)(2,1)S(1)}, u32[]{:S(2)}, u32[]{:S(2)}) collective-permute-start(bf16[112,384]{1,0:T(8,128)(2,1)S(1)} %get-tuple-element.57), channel_id=1, source_target_pairs={{0,9},{1,8},{8,1},{9,0},{16,25},{17,24},{24,17},{25,16},{2,11},{3,... | collective-permute-start | bytes 258056 | tf_op jit(solution)/shard_map/ppermute | solution.py:486
  82.8 5.9 %collective-permute-start.7 = (bf16[112,384]{1,0:T(8,128)(2,1)S(1)}, bf16[112,384]{1,0:T(8,128)(2,1)S(1)}, u32[]{:S(2)}, u32[]{:S(2)}) collective-permute-start(bf16[112,384]{1,0:T(8,128)(2,1)S(1)} %get-tuple-element.58), channel_id=1, source_target_pairs={{0,16},{1,17},{8,24},{9,25},{16,0},{17,1},{24,8},{25,9},{2,18},{3,... | collective-permute-start | bytes 258056 | tf_op jit(solution)/shard_map/ppermute | solution.py:486
  83.7 11.7 %collective-permute-start.8 = (bf16[112,384]{1,0:T(8,128)(2,1)S(1)}, bf16[112,384]{1,0:T(8,128)(2,1)S(1)}, u32[]{:S(2)}, u32[]{:S(2)}) collective-permute-start(bf16[112,384]{1,0:T(8,128)(2,1)S(1)} %get-tuple-element.59), channel_id=1, source_target_pairs={{0,17},{1,16},{8,25},{9,24},{16,1},{17,0},{24,9},{25,8},{2,19},{3,... | collective-permute-start | bytes 258056 | tf_op jit(solution)/shard_map/ppermute | solution.py:486
  85.7 13.8 %collective-permute-start.9 = (bf16[112,384]{1,0:T(8,128)(2,1)S(1)}, bf16[112,384]{1,0:T(8,128)(2,1)S(1)}, u32[]{:S(2)}, u32[]{:S(2)}) collective-permute-start(bf16[112,384]{1,0:T(8,128)(2,1)S(1)} %get-tuple-element.60), channel_id=1, source_target_pairs={{0,24},{1,25},{8,16},{9,17},{16,8},{17,9},{24,0},{25,1},{2,26},{3,... | collective-permute-start | bytes 258056 | tf_op jit(solution)/shard_map/ppermute | solution.py:486
  85.7 15.6 %collective-permute-start.10 = (bf16[112,384]{1,0:T(8,128)(2,1)S(1)}, bf16[112,384]{1,0:T(8,128)(2,1)S(1)}, u32[]{:S(2)}, u32[]{:S(2)}) collective-permute-start(bf16[112,384]{1,0:T(8,128)(2,1)S(1)} %get-tuple-element.61), channel_id=1, source_target_pairs={{0,25},{1,24},{8,17},{9,16},{16,9},{17,8},{24,1},{25,0},{2,27},{3,... | collective-permute-start | bytes 258056 | tf_op jit(solution)/shard_map/ppermute | solution.py:486

commit v17 on v16

--- a/solution.py
+++ b/solution.py
@@ -438,21 +438,6 @@
     )
     got = passed(give, None, None, 1)
     far, far_pair = passed(mine, 0, 1, 0), passed(cross, 1, 0, 1)
-    hidden, pre_grad, got = lax.optimization_barrier((hidden, pre_grad, got))
-    fields = kernel(
-        functools.partial(outer_kernel, band, step),
-        [vmem] * 5,
-        (own, hidden, pre_grad, conv1_weight, conv2_weight),
-        dealt,
-        [stack, stack],
-        2 * flops,
-        9,
-    )
-    _, far, far_pair = lax.optimization_barrier((fields, far, far_pair))
-    fields = lax.all_to_all(fields, every, 0, 0, tiled=True)
-    output, input_grad = kernel(
-        functools.partial(gather_kernel, step), [vmem], (fields,), (shaped(*inputs.shape),) * 2, [], 10**9, 3
-    )
     room = [held(2, half, 2 * cells), held(9, half, 2 * cells)]
     near = kernel(
         functools.partial(near_kernel, band, step),
@@ -462,6 +447,21 @@
         room,
         2 * flops,
         6,
+    )
+    hidden, pre_grad, near = lax.optimization_barrier((hidden, pre_grad, near))
+    fields = kernel(
+        functools.partial(outer_kernel, band, step),
+        [vmem] * 5,
+        (own, hidden, pre_grad, conv1_weight, conv2_weight),
+        dealt,
+        [stack, stack],
+        2 * flops,
+        9,
+    )
+    _, far, far_pair = lax.optimization_barrier((fields, far, far_pair))
+    fields = lax.all_to_all(fields, every, 0, 0, tiled=True)
+    output, input_grad = kernel(
+        functools.partial(gather_kernel, step), [vmem], (fields,), (shaped(*inputs.shape),) * 2, [], 10**9, 3
     )
     keep, give = kernel(
         functools.partial(far_kernel, band, step),

time: 103 us -> 98.3 us (0.954)
  the two profiles are of different devices: /device:TPU:11 before, /device:TPU:0 now
where the time goes in v17:
time: 98.3 us; the launch traced here: 98 us
  waiting for transfers between devices  41.2 us (42%)
  Pallas kernels  29.2 us (30%)
  starting transfers between devices  23.5 us (24%)
  local copies, waits for them, and re-layouts  3.32 us (3%)
    pallas_call x8, Pallas kernels, kernel(): pl.pallas_call(body, out_shape=out_shape, in_specs=specs, out_specs=jax.t...  29.2 us
    all_to_all x1, waiting for transfers between devices, fast_local(): own = lax.all_to_all(own, every, 0, 0, tiled=True)  20.5 us
    ppermute x4, waiting for transfers between devices, passed(): return lax.ppermute(piece, ('y', 'x', 'core'), pairs)  12.8 us
    ppermute x7, starting transfers between devices, fast_local(): lax.ppermute(terms[away], ('z', 'core'), [(i, i ^ away) for i in range(8)])  8.85 us
    ppermute x7, waiting for transfers between devices, fast_local(): lax.ppermute(terms[away], ('z', 'core'), [(i, i ^ away) for i in range(8)])  7.82 us
    all_to_all x1, starting transfers between devices, fast_local(): own = lax.all_to_all(own, every, 0, 0, tiled=True)  7.3 us
    ppermute x4, starting transfers between devices, passed(): return lax.ppermute(piece, ('y', 'x', 'core'), pairs)  3.75 us
    all_to_all x1, starting transfers between devices, fast_local(): fields = lax.all_to_all(fields, every, 0, 0, tiled=True)  3.62 us
  transfers between devices with their start and end apart: 13, of which 6 were waited for; matrix products, arithmetic and copies ran while one was open for 0% of the time, Pallas kernels for 17%

profile of v17, /device:TPU:0, one launch (start us, length us, event | category | flops | bytes accessed | tf_op | source)
XLA Modules:
  0.0 98.0 jit_solution(10506137338909038396)
XLA Ops:
  0.6 2.8 %shard_map.75 = bf16[32,2,16,384]{3,2,1,0:T(8,128)(2,1)} custom-call(bf16[8,64,384]{2,1,0:T(8,128)(2,1)} %inputs_ref.1, bf16[8,64,384]{2,1,0:T(8,128)(2,1)} %cot_ref.1), custom_call_target="tpu_custom_call" | custom-call | flops 1000000000 | bytes 3145728 | tf_op jit(solution)/shard_map/pallas_call | solution.py:385
  3.4 7.3 %all-to-all-start = ((bf16[32,2,16,384]{3,2,1,0:T(8,128)(2,1)}), bf16[32,2,16,384]{3,2,1,0:T(8,128)(2,1)S(1)}, u32[]{:S(2)}, u32[]{:S(2)}) async-start(bf16[32,2,16,384]{3,2,1,0:T(8,128)(2,1)} %shard_map.75), calls=%async_computation | async-start | bytes 1572864 | tf_op jit(solution)/shard_map/all_to_all | solution.py:411
  10.8 20.5 %all-to-all-done.own_ref = bf16[32,2,16,384]{3,2,1,0:T(8,128)(2,1)S(1)} async-done(((bf16[32,2,16,384]{3,2,1,0:T(8,128)(2,1)}), bf16[32,2,16,384]{3,2,1,0:T(8,128)(2,1)S(1)}, u32[]{:S(2)}, u32[]{:S(2)}) %all-to-all-start) | async-done | bytes 786464 | tf_op jit(solution)/shard_map/all_to_all | solution.py:411
  31.3 7.9 %shard_map.76 = (bf16[512,384]{1,0:T(8,128)(2,1)S(1)}, bf16[512,384]{1,0:T(8,128)(2,1)S(1)}, bf16[3,192,512]{2,1,0:T(8,128)(2,1)S(1)}, bf16[192,512]{1,0:T(8,128...) custom-call(s32[4]{0:T(128)S(1)} %pad_add_fusion.place_ref, ...), custom_call_target="tpu_custom_call" | custom-call | flops 2717908992 | bytes 10485760 | tf_op jit(solution)/shard_map/pallas_call | solution.py:385
  39.4 1.6 %collective-permute-start.1 = (bf16[3,192,512]{2,1,0:T(8,128)(2,1)S(1)}, bf16[3,192,512]{2,1,0:T(8,128)(2,1)S(1)}, u32[]{:S(2)}, u32[]{:S(2)}) collective-permute-start(bf16[3,192,512]{2,1,0:T(8,128)(2,1)S(1)} %get-tuple-element.41.mine_ref), channel_id=1, source_target_pairs={{0,2},{1,5},{2,0},{3,7},{4,6},{5,1},{6,4},{7,3},{8,10},{9,13},{10,... | collective-permute-start | bytes 1769480 | tf_op jit(solution)/shard_map/ppermute | solution.py:397
  41.4 4.4 %shard_map.77.sums_ref = f32[2,192,1728]{2,1,0:T(8,128)S(1)} custom-call(s32[4]{0:T(128)S(1)} %pad_add_fusion.place_ref, bf16[3,192,512]{2,1,0:T(8,128)(2,1)S(1)} %get-tuple-element.41.mine_ref, bf16[192,512]{1,0:T(8,128)(2,1)S(1)} %get-tuple-element.42.kept_ref, bf16[3,192,512]{2,1,0:T(8,128)(2,1)S(1)} %collective-permute-done.got_ref), custom_call_target="tpu_custom_call" | custom-call | flops 2717908992 | bytes 6291456 | tf_op jit(solution)/shard_map/pallas_call | solution.py:385
  45.8 1.5 %copy-done.2 = f32[2,192,1728]{2,1,0:T(8,128)} copy-done((f32[2,192,1728]{2,1,0:T(8,128)}, f32[2,192,1728]{2,1,0:T(8,128)S(1)}, u32[]{:S(2)}) %copy-start.2) | copy-done | bytes 2654232
  47.3 5.0 %shard_map.78 = bf16[32,2,16,384]{3,2,1,0:T(8,128)(2,1)} custom-call(bf16[32,2,16,384]{3,2,1,0:T(8,128)(2,1)S(1)} %all-to-all-done.own_ref, bf16[512,384]{1,0:T(8,128)(2,1)S(1)} %get-tuple-element.44.hidden_ref, bf16[512,384]{1,0:T(8,128)(2,1)S(1)} %get-tuple-element.45.pre_ref, bf16[3,3,384,384]{3,2,1,0:T(8,128)(2,1)S(1)} %copy-done, ...), custom_call_target="tpu_custom_call" | custom-call | flops 2717908992 | bytes 9437184 | tf_op jit(solution)/shard_map/pallas_call | solution.py:385
  52.3 3.6 %all-to-all-start.1 = ((bf16[32,2,16,384]{3,2,1,0:T(8,128)(2,1)}), bf16[32,2,16,384]{3,2,1,0:T(8,128)(2,1)S(1)}, u32[]{:S(2)}, u32[]{:S(2)}) async-start(bf16[32,2,16,384]{3,2,1,0:T(8,128)(2,1)} %shard_map.78), calls=%async_computation.1 | async-start | bytes 1572864 | tf_op jit(solution)/shard_map/all_to_all | solution.py:462
  56.0 1.8 %copy-done.3 = f32[2,192,1728]{2,1,0:T(8,128)S(1)} copy-done((f32[2,192,1728]{2,1,0:T(8,128)S(1)}, f32[2,192,1728]{2,1,0:T(8,128)}, u32[]{:S(2)}) %copy-start.3) | copy-done | bytes 2654232
  57.7 4.2 %shard_map.80 = (f32[192,1728]{1,0:T(8,128)S(1)}, bf16[192,1728]{1,0:T(8,128)(2,1)S(1)}) custom-call(s32[4]{0:T(128)S(1)} %pad_add_fusion.place_ref, f32[2,192,1728]{2,1,0:T(8,128)S(1)} %copy-done.3, bf16[3,192,512]{2,1,0:T(8,128)(2,1)S(1)} %collective-permute-done.1.far_ref, bf16[3,192,512]{2,1,0:T(8,128)(2,1)S(1)} %collective-permute-done.2.pair_ref), custom_call_target="tpu_custom_call" | custom-call | flops 4076863488 | bytes 6291456 | tf_op jit(solution)/shard_map/pallas_call | solution.py:385
  62.0 1.8 %collective-permute-start.3 = (bf16[192,1728]{1,0:T(8,128)(2,1)S(1)}, bf16[192,1728]{1,0:T(8,128)(2,1)S(1)}, u32[]{:S(2)}, u32[]{:S(2)}) collective-permute-start(bf16[192,1728]{1,0:T(8,128)(2,1)S(1)} %get-tuple-element.53), channel_id=1, source_target_pairs={{0,4},{1,3},{2,6},{3,1},{4,0},{5,7},{6,2},{7,5},{8,12},{9,11},{10,... | collective-permute-start | bytes 1990664 | tf_op jit(solution)/shard_map/ppermute | solution.py:397
  63.8 12.7 %collective-permute-done.3.got_ref = bf16[192,1728]{1,0:T(8,128)(2,1)S(1)} collective-permute-done((bf16[192,1728]{1,0:T(8,128)(2,1)S(1)}, bf16[192,1728]{1,0:T(8,128)(2,1)S(1)}, u32[]{:S(2)}, u32[]{:S(2)}) %collective-permute-start.3) | collective-permute-done | bytes 663584 | tf_op jit(solution)/shard_map/ppermute | solution.py:397
  76.5 1.9 %shard_map.81 = (bf16[112,384]{1,0:T(8,128)(2,1)S(1)}, bf16[112,384]{1,0:T(8,128)(2,1)S(1)}, bf16[112,384]{1,0:T(8,128)(2,1)S(1)}, bf16[112,384]{1,0:T(8,128)(2,...) custom-call(s32[4]{0:T(128)S(1)} %pad_add_fusion.place_ref, ...), custom_call_target="tpu_custom_call" | custom-call | flops 2717908992 | bytes 4194304 | tf_op jit(solution)/shard_map/pallas_call | solution.py:385
  78.4 1.7 %collective-permute-start.10 = (bf16[112,384]{1,0:T(8,128)(2,1)S(1)}, bf16[112,384]{1,0:T(8,128)(2,1)S(1)}, u32[]{:S(2)}, u32[]{:S(2)}) collective-permute-start(bf16[112,384]{1,0:T(8,128)(2,1)S(1)} %get-tuple-element.61), channel_id=1, source_target_pairs={{0,25},{1,24},{8,17},{9,16},{16,9},{17,8},{24,1},{25,0},{2,27},{3,... | collective-permute-start | bytes 258056 | tf_op jit(solution)/shard_map/ppermute | solution.py:486
  80.1 1.7 %collective-permute-start.4 = (bf16[112,384]{1,0:T(8,128)(2,1)S(1)}, bf16[112,384]{1,0:T(8,128)(2,1)S(1)}, u32[]{:S(2)}, u32[]{:S(2)}) collective-permute-start(bf16[112,384]{1,0:T(8,128)(2,1)S(1)} %get-tuple-element.55), channel_id=1, source_target_pairs={{0,1},{1,0},{8,9},{9,8},{16,17},{17,16},{24,25},{25,24},{2,3},{3,2... | collective-permute-start | bytes 258056 | tf_op jit(solution)/shard_map/ppermute | solution.py:486
  82.0 1.2 %collective-permute-start.6 = (bf16[112,384]{1,0:T(8,128)(2,1)S(1)}, bf16[112,384]{1,0:T(8,128)(2,1)S(1)}, u32[]{:S(2)}, u32[]{:S(2)}) collective-permute-start(bf16[112,384]{1,0:T(8,128)(2,1)S(1)} %get-tuple-element.57), channel_id=1, source_target_pairs={{0,9},{1,8},{8,1},{9,0},{16,25},{17,24},{24,17},{25,16},{2,11},{3,... | collective-permute-start | bytes 258056 | tf_op jit(solution)/shard_map/ppermute | solution.py:486
  83.6 1.6 %collective-permute-done.10.refs_7_ = bf16[112,384]{1,0:T(8,128)(2,1)S(1)} collective-permute-done((bf16[112,384]{1,0:T(8,128)(2,1)S(1)}, bf16[112,384]{1,0:T(8,128)(2,1)S(1)}, u32[]{:S(2)}, u32[]{:S(2)}) %collective-permute-start.10) | collective-permute-done | bytes 86048 | tf_op jit(solution)/shard_map/ppermute | solution.py:486
  85.3 1.3 %collective-permute-start.8 = (bf16[112,384]{1,0:T(8,128)(2,1)S(1)}, bf16[112,384]{1,0:T(8,128)(2,1)S(1)}, u32[]{:S(2)}, u32[]{:S(2)}) collective-permute-start(bf16[112,384]{1,0:T(8,128)(2,1)S(1)} %get-tuple-element.59), channel_id=1, source_target_pairs={{0,17},{1,16},{8,25},{9,24},{16,1},{17,0},{24,9},{25,8},{2,19},{3,... | collective-permute-start | bytes 258056 | tf_op jit(solution)/shard_map/ppermute | solution.py:486
  86.6 2.3 %collective-permute-start.9 = (bf16[112,384]{1,0:T(8,128)(2,1)S(1)}, bf16[112,384]{1,0:T(8,128)(2,1)S(1)}, u32[]{:S(2)}, u32[]{:S(2)}) collective-permute-start(bf16[112,384]{1,0:T(8,128)(2,1)S(1)} %get-tuple-element.60), channel_id=1, source_target_pairs={{0,24},{1,25},{8,16},{9,17},{16,8},{17,9},{24,0},{25,1},{2,26},{3,... | collective-permute-start | bytes 258056 | tf_op jit(solution)/shard_map/ppermute | solution.py:486
  88.9 1.5 %shard_map.79 = (bf16[8,64,384]{2,1,0:T(8,128)(2,1)}, bf16[8,64,384]{2,1,0:T(8,128)(2,1)}) custom-call(bf16[32,2,16,384]{3,2,1,0:T(8,128)(2,1)S(1)} %all-to-all-done.1.fields_ref), custom_call_target="tpu_custom_call" | custom-call | flops 1000000000 | bytes 3145728 | tf_op jit(solution)/shard_map/pallas_call | solution.py:385
  90.4 4.7 %collective-permute-done.7.refs_4_ = bf16[112,384]{1,0:T(8,128)(2,1)S(1)} collective-permute-done((bf16[112,384]{1,0:T(8,128)(2,1)S(1)}, bf16[112,384]{1,0:T(8,128)(2,1)S(1)}, u32[]{:S(2)}, u32[]{:S(2)}) %collective-permute-start.7) | collective-permute-done | bytes 86048 | tf_op jit(solution)/shard_map/ppermute | solution.py:486
  95.0 1.5 %collective-permute-done.8.refs_5_ = bf16[112,384]{1,0:T(8,128)(2,1)S(1)} collective-permute-done((bf16[112,384]{1,0:T(8,128)(2,1)S(1)}, bf16[112,384]{1,0:T(8,128)(2,1)S(1)}, u32[]{:S(2)}, u32[]{:S(2)}) %collective-permute-start.8) | collective-permute-done | bytes 86048 | tf_op jit(solution)/shard_map/ppermute | solution.py:486
  96.5 1.5 %shard_map.82 = (f32[3,3,48,96]{3,2,1,0:T(8,128)}, f32[3,3,48,96]{3,2,1,0:T(8,128)}) custom-call(s32[4]{0:T(128)S(1)} %pad_add_fusion.place_ref, bf16[112,384]{1,0:T(8,128)(2,1)S(1)} %get-tuple-element.64.refs_0_, bf16[112,384]{1,0:T(8,128)(2,1)S(1)} %collective-permute-done.4.refs_1_, bf16[112,384]{1,0:T(8,128)(2,1)S(1)} %collective-permute-done.5.refs_2_, ...), custom_call_target="tpu_custom_call" | custom-call | flops 1000000 | bytes 2097152 | tf_op jit(solution)/shard_map/pallas_call | solution.py:385
  (19 shorter events, 1.2 us)
Async XLA Ops:
  3.4 27.9 %all-to-all-start = ((bf16[32,2,16,384]{3,2,1,0:T(8,128)(2,1)}), bf16[32,2,16,384]{3,2,1,0:T(8,128)(2,1)S(1)}, u32[]{:S(2)}, u32[]{:S(2)}) async-start(bf16[32,2,16,384]{3,2,1,0:T(8,128)(2,1)} %shard_map.75), calls=%async_computation | async-start | bytes 1572864 | tf_op jit(solution)/shard_map/all_to_all | solution.py:411
  39.3 2.1 %collective-permute-start = (bf16[3,192,512]{2,1,0:T(8,128)(2,1)S(1)}, bf16[3,192,512]{2,1,0:T(8,128)(2,1)S(1)}, u32[]{:S(2)}, u32[]{:S(2)}) collective-permute-start(bf16[3,192,512]{2,1,0:T(8,128)(2,1)S(1)} %get-tuple-element.43), channel_id=1, source_target_pairs={{0,1},{1,0},{2,3},{3,2},{4,5},{5,4},{6,7},{7,6},{8,9},{9,8},{10,11... | collective-permute-start | bytes 1769480 | tf_op jit(solution)/shard_map/ppermute | solution.py:397
  39.4 16.6 %collective-permute-start.1 = (bf16[3,192,512]{2,1,0:T(8,128)(2,1)S(1)}, bf16[3,192,512]{2,1,0:T(8,128)(2,1)S(1)}, u32[]{:S(2)}, u32[]{:S(2)}) collective-permute-start(bf16[3,192,512]{2,1,0:T(8,128)(2,1)S(1)} %get-tuple-element.41.mine_ref), channel_id=1, source_target_pairs={{0,2},{1,5},{2,0},{3,7},{4,6},{5,1},{6,4},{7,3},{8,10},{9,13},{10,... | collective-permute-start | bytes 1769480 | tf_op jit(solution)/shard_map/ppermute | solution.py:397
  41.0 15.0 %collective-permute-start.2 = (bf16[3,192,512]{2,1,0:T(8,128)(2,1)S(1)}, bf16[3,192,512]{2,1,0:T(8,128)(2,1)S(1)}, u32[]{:S(2)}, u32[]{:S(2)}) collective-permute-start(bf16[3,192,512]{2,1,0:T(8,128)(2,1)S(1)} %get-tuple-element.49), channel_id=1, source_target_pairs={{0,5},{1,2},{2,7},{3,0},{4,1},{5,6},{6,3},{7,4},{8,13},{9,10},{10,... | collective-permute-start | bytes 1769480 | tf_op jit(solution)/shard_map/ppermute | solution.py:397
  41.3 6.0 %copy-start = (bf16[3,3,384,384]{3,2,1,0:T(8,128)(2,1)S(1)}, bf16[3,3,384,384]{3,2,1,0:T(8,128)(2,1)}, u32[]{:S(2)}) copy-start(bf16[3,3,384,384]{3,2,1,0:T(8,128)(2,1)} %one_ref.3) | copy-start | bytes 7962628
  41.3 6.0 %copy-start.1 = (bf16[3,3,384,384]{3,2,1,0:T(8,128)(2,1)S(1)}, bf16[3,3,384,384]{3,2,1,0:T(8,128)(2,1)}, u32[]{:S(2)}) copy-start(bf16[3,3,384,384]{3,2,1,0:T(8,128)(2,1)} %two_ref.3) | copy-start | bytes 7962628
  45.8 1.5 %copy-start.2 = (f32[2,192,1728]{2,1,0:T(8,128)}, f32[2,192,1728]{2,1,0:T(8,128)S(1)}, u32[]{:S(2)}) copy-start(f32[2,192,1728]{2,1,0:T(8,128)S(1)} %shard_map.77.sums_ref) | copy-start | bytes 7962628
  52.3 36.6 %all-to-all-start.1 = ((bf16[32,2,16,384]{3,2,1,0:T(8,128)(2,1)}), bf16[32,2,16,384]{3,2,1,0:T(8,128)(2,1)S(1)}, u32[]{:S(2)}, u32[]{:S(2)}) async-start(bf16[32,2,16,384]{3,2,1,0:T(8,128)(2,1)} %shard_map.78), calls=%async_computation.1 | async-start | bytes 1572864 | tf_op jit(solution)/shard_map/all_to_all | solution.py:462
  56.0 1.8 %copy-start.3 = (f32[2,192,1728]{2,1,0:T(8,128)S(1)}, f32[2,192,1728]{2,1,0:T(8,128)}, u32[]{:S(2)}) copy-start(f32[2,192,1728]{2,1,0:T(8,128)} %copy-done.2) | copy-start | bytes 7962628
  62.0 14.5 %collective-permute-start.3 = (bf16[192,1728]{1,0:T(8,128)(2,1)S(1)}, bf16[192,1728]{1,0:T(8,128)(2,1)S(1)}, u32[]{:S(2)}, u32[]{:S(2)}) collective-permute-start(bf16[192,1728]{1,0:T(8,128)(2,1)S(1)} %get-tuple-element.53), channel_id=1, source_target_pairs={{0,4},{1,3},{2,6},{3,1},{4,0},{5,7},{6,2},{7,5},{8,12},{9,11},{10,... | collective-permute-start | bytes 1990664 | tf_op jit(solution)/shard_map/ppermute | solution.py:397
  78.4 6.9 %collective-permute-start.10 = (bf16[112,384]{1,0:T(8,128)(2,1)S(1)}, bf16[112,384]{1,0:T(8,128)(2,1)S(1)}, u32[]{:S(2)}, u32[]{:S(2)}) collective-permute-start(bf16[112,384]{1,0:T(8,128)(2,1)S(1)} %get-tuple-element.61), channel_id=1, source_target_pairs={{0,25},{1,24},{8,17},{9,16},{16,9},{17,8},{24,1},{25,0},{2,27},{3,... | collective-permute-start | bytes 258056 | tf_op jit(solution)/shard_map/ppermute | solution.py:486
  80.1 6.5 %collective-permute-start.4 = (bf16[112,384]{1,0:T(8,128)(2,1)S(1)}, bf16[112,384]{1,0:T(8,128)(2,1)S(1)}, u32[]{:S(2)}, u32[]{:S(2)}) collective-permute-start(bf16[112,384]{1,0:T(8,128)(2,1)S(1)} %get-tuple-element.55), channel_id=1, source_target_pairs={{0,1},{1,0},{8,9},{9,8},{16,17},{17,16},{24,25},{25,24},{2,3},{3,2... | collective-permute-start | bytes 258056 | tf_op jit(solution)/shard_map/ppermute | solution.py:486
  81.8 8.5 %collective-permute-start.5 = (bf16[112,384]{1,0:T(8,128)(2,1)S(1)}, bf16[112,384]{1,0:T(8,128)(2,1)S(1)}, u32[]{:S(2)}, u32[]{:S(2)}) collective-permute-start(bf16[112,384]{1,0:T(8,128)(2,1)S(1)} %get-tuple-element.56), channel_id=1, source_target_pairs={{0,8},{1,9},{8,0},{9,1},{16,24},{17,25},{24,16},{25,17},{2,10},{3,... | collective-permute-start | bytes 258056 | tf_op jit(solution)/shard_map/ppermute | solution.py:486
  82.0 8.4 %collective-permute-start.6 = (bf16[112,384]{1,0:T(8,128)(2,1)S(1)}, bf16[112,384]{1,0:T(8,128)(2,1)S(1)}, u32[]{:S(2)}, u32[]{:S(2)}) collective-permute-start(bf16[112,384]{1,0:T(8,128)(2,1)S(1)} %get-tuple-element.57), channel_id=1, source_target_pairs={{0,9},{1,8},{8,1},{9,0},{16,25},{17,24},{24,17},{25,16},{2,11},{3,... | collective-permute-start | bytes 258056 | tf_op jit(solution)/shard_map/ppermute | solution.py:486
  83.2 11.9 %collective-permute-start.7 = (bf16[112,384]{1,0:T(8,128)(2,1)S(1)}, bf16[112,384]{1,0:T(8,128)(2,1)S(1)}, u32[]{:S(2)}, u32[]{:S(2)}) collective-permute-start(bf16[112,384]{1,0:T(8,128)(2,1)S(1)} %get-tuple-element.58), channel_id=1, source_target_pairs={{0,16},{1,17},{8,24},{9,25},{16,0},{17,1},{24,8},{25,9},{2,18},{3,... | collective-permute-start | bytes 258056 | tf_op jit(solution)/shard_map/ppermute | solution.py:486
  85.3 11.3 %collective-permute-start.8 = (bf16[112,384]{1,0:T(8,128)(2,1)S(1)}, bf16[112,384]{1,0:T(8,128)(2,1)S(1)}, u32[]{:S(2)}, u32[]{:S(2)}) collective-permute-start(bf16[112,384]{1,0:T(8,128)(2,1)S(1)} %get-tuple-element.59), channel_id=1, source_target_pairs={{0,17},{1,16},{8,25},{9,24},{16,1},{17,0},{24,9},{25,8},{2,19},{3,... | collective-permute-start | bytes 258056 | tf_op jit(solution)/shard_map/ppermute | solution.py:486
  86.6 10.0 %collective-permute-start.9 = (bf16[112,384]{1,0:T(8,128)(2,1)S(1)}, bf16[112,384]{1,0:T(8,128)(2,1)S(1)}, u32[]{:S(2)}, u32[]{:S(2)}) collective-permute-start(bf16[112,384]{1,0:T(8,128)(2,1)S(1)} %get-tuple-element.60), channel_id=1, source_target_pairs={{0,24},{1,25},{8,16},{9,17},{16,8},{17,9},{24,0},{25,1},{2,26},{3,... | collective-permute-start | bytes 258056 | tf_op jit(solution)/shard_map/ppermute | solution.py:486

commit v18 on v17

--- a/solution.py
+++ b/solution.py
@@ -388,7 +388,7 @@
             in_specs=specs,
             out_specs=jax.tree.map(lambda _: vmem, out_shape),
             scratch_shapes=scratch_shapes,
-            compiler_params=pltpu.CompilerParams(vmem_limit_bytes=24 * 2**20),
+            compiler_params=pltpu.CompilerParams(vmem_limit_bytes=15 * 2**20),
             cost_estimate=pl.CostEstimate(flops=work, bytes_accessed=megabytes * 2**20, transcendentals=0),
         )(*arguments)
 

time: 98.3 us -> 98.3 us (level)
  no operation moved by 1% of the time
where the time goes in v18:
time: 98.3 us; the launch traced here: 98 us
  waiting for transfers between devices  41.2 us (42%)
  Pallas kernels  29.2 us (30%)
  starting transfers between devices  23.5 us (24%)
  local copies, waits for them, and re-layouts  3.32 us (3%)
    pallas_call x8, Pallas kernels, kernel(): pl.pallas_call(body, out_shape=out_shape, in_specs=specs, out_specs=jax.t...  29.2 us
    all_to_all x1, waiting for transfers between devices, fast_local(): own = lax.all_to_all(own, every, 0, 0, tiled=True)  20.5 us
    ppermute x4, waiting for transfers between devices, passed(): return lax.ppermute(piece, ('y', 'x', 'core'), pairs)  12.8 us
    ppermute x7, starting transfers between devices, fast_local(): lax.ppermute(terms[away], ('z', 'core'), [(i, i ^ away) for i in range(8)])  8.85 us
    ppermute x7, waiting for transfers between devices, fast_local(): lax.ppermute(terms[away], ('z', 'core'), [(i, i ^ away) for i in range(8)])  7.82 us
    all_to_all x1, starting transfers between devices, fast_local(): own = lax.all_to_all(own, every, 0, 0, tiled=True)  7.3 us
    ppermute x4, starting transfers between devices, passed(): return lax.ppermute(piece, ('y', 'x', 'core'), pairs)  3.75 us
    all_to_all x1, starting transfers between devices, fast_local(): fields = lax.all_to_all(fields, every, 0, 0, tiled=True)  3.62 us
  transfers between devices with their start and end apart: 13, of which 6 were waited for; matrix products, arithmetic and copies ran while one was open for 0% of the time, Pallas kernels for 17%

profile of v18, /device:TPU:0, one launch (start us, length us, event | category | flops | bytes accessed | tf_op | source)
XLA Modules:
  0.0 98.0 jit_solution(13055311590634902494)
XLA Ops:
  0.6 2.8 %shard_map.75 = bf16[32,2,16,384]{3,2,1,0:T(8,128)(2,1)} custom-call(bf16[8,64,384]{2,1,0:T(8,128)(2,1)} %inputs_ref.1, bf16[8,64,384]{2,1,0:T(8,128)(2,1)} %cot_ref.1), custom_call_target="tpu_custom_call" | custom-call | flops 1000000000 | bytes 3145728 | tf_op jit(solution)/shard_map/pallas_call | solution.py:385
  3.4 7.3 %all-to-all-start = ((bf16[32,2,16,384]{3,2,1,0:T(8,128)(2,1)}), bf16[32,2,16,384]{3,2,1,0:T(8,128)(2,1)S(1)}, u32[]{:S(2)}, u32[]{:S(2)}) async-start(bf16[32,2,16,384]{3,2,1,0:T(8,128)(2,1)} %shard_map.75), calls=%async_computation | async-start | bytes 1572864 | tf_op jit(solution)/shard_map/all_to_all | solution.py:411
  10.8 20.5 %all-to-all-done.own_ref = bf16[32,2,16,384]{3,2,1,0:T(8,128)(2,1)S(1)} async-done(((bf16[32,2,16,384]{3,2,1,0:T(8,128)(2,1)}), bf16[32,2,16,384]{3,2,1,0:T(8,128)(2,1)S(1)}, u32[]{:S(2)}, u32[]{:S(2)}) %all-to-all-start) | async-done | bytes 786464 | tf_op jit(solution)/shard_map/all_to_all | solution.py:411
  31.3 7.9 %shard_map.76 = (bf16[512,384]{1,0:T(8,128)(2,1)S(1)}, bf16[512,384]{1,0:T(8,128)(2,1)S(1)}, bf16[3,192,512]{2,1,0:T(8,128)(2,1)S(1)}, bf16[192,512]{1,0:T(8,128...) custom-call(s32[4]{0:T(128)S(1)} %pad_add_fusion.place_ref, ...), custom_call_target="tpu_custom_call" | custom-call | flops 2717908992 | bytes 10485760 | tf_op jit(solution)/shard_map/pallas_call | solution.py:385
  39.4 1.6 %collective-permute-start.1 = (bf16[3,192,512]{2,1,0:T(8,128)(2,1)S(1)}, bf16[3,192,512]{2,1,0:T(8,128)(2,1)S(1)}, u32[]{:S(2)}, u32[]{:S(2)}) collective-permute-start(bf16[3,192,512]{2,1,0:T(8,128)(2,1)S(1)} %get-tuple-element.41.mine_ref), channel_id=1, source_target_pairs={{0,2},{1,5},{2,0},{3,7},{4,6},{5,1},{6,4},{7,3},{8,10},{9,13},{10,... | collective-permute-start | bytes 1769480 | tf_op jit(solution)/shard_map/ppermute | solution.py:397
  41.4 4.4 %shard_map.77.sums_ref = f32[2,192,1728]{2,1,0:T(8,128)S(1)} custom-call(s32[4]{0:T(128)S(1)} %pad_add_fusion.place_ref, bf16[3,192,512]{2,1,0:T(8,128)(2,1)S(1)} %get-tuple-element.41.mine_ref, bf16[192,512]{1,0:T(8,128)(2,1)S(1)} %get-tuple-element.42.kept_ref, bf16[3,192,512]{2,1,0:T(8,128)(2,1)S(1)} %collective-permute-done.got_ref), custom_call_target="tpu_custom_call" | custom-call | flops 2717908992 | bytes 6291456 | tf_op jit(solution)/shard_map/pallas_call | solution.py:385
  45.8 1.5 %copy-done.2 = f32[2,192,1728]{2,1,0:T(8,128)} copy-done((f32[2,192,1728]{2,1,0:T(8,128)}, f32[2,192,1728]{2,1,0:T(8,128)S(1)}, u32[]{:S(2)}) %copy-start.2) | copy-done | bytes 2654232
  47.3 5.0 %shard_map.78 = bf16[32,2,16,384]{3,2,1,0:T(8,128)(2,1)} custom-call(bf16[32,2,16,384]{3,2,1,0:T(8,128)(2,1)S(1)} %all-to-all-done.own_ref, bf16[512,384]{1,0:T(8,128)(2,1)S(1)} %get-tuple-element.44.hidden_ref, bf16[512,384]{1,0:T(8,128)(2,1)S(1)} %get-tuple-element.45.pre_ref, bf16[3,3,384,384]{3,2,1,0:T(8,128)(2,1)S(1)} %copy-done, ...), custom_call_target="tpu_custom_call" | custom-call | flops 2717908992 | bytes 9437184 | tf_op jit(solution)/shard_map/pallas_call | solution.py:385
  52.3 3.6 %all-to-all-start.1 = ((bf16[32,2,16,384]{3,2,1,0:T(8,128)(2,1)}), bf16[32,2,16,384]{3,2,1,0:T(8,128)(2,1)S(1)}, u32[]{:S(2)}, u32[]{:S(2)}) async-start(bf16[32,2,16,384]{3,2,1,0:T(8,128)(2,1)} %shard_map.78), calls=%async_computation.1 | async-start | bytes 1572864 | tf_op jit(solution)/shard_map/all_to_all | solution.py:462
  56.0 1.8 %copy-done.3 = f32[2,192,1728]{2,1,0:T(8,128)S(1)} copy-done((f32[2,192,1728]{2,1,0:T(8,128)S(1)}, f32[2,192,1728]{2,1,0:T(8,128)}, u32[]{:S(2)}) %copy-start.3) | copy-done | bytes 2654232
  57.7 4.2 %shard_map.80 = (f32[192,1728]{1,0:T(8,128)S(1)}, bf16[192,1728]{1,0:T(8,128)(2,1)S(1)}) custom-call(s32[4]{0:T(128)S(1)} %pad_add_fusion.place_ref, f32[2,192,1728]{2,1,0:T(8,128)S(1)} %copy-done.3, bf16[3,192,512]{2,1,0:T(8,128)(2,1)S(1)} %collective-permute-done.1.far_ref, bf16[3,192,512]{2,1,0:T(8,128)(2,1)S(1)} %collective-permute-done.2.pair_ref), custom_call_target="tpu_custom_call" | custom-call | flops 4076863488 | bytes 6291456 | tf_op jit(solution)/shard_map/pallas_call | solution.py:385
  62.0 1.8 %collective-permute-start.3 = (bf16[192,1728]{1,0:T(8,128)(2,1)S(1)}, bf16[192,1728]{1,0:T(8,128)(2,1)S(1)}, u32[]{:S(2)}, u32[]{:S(2)}) collective-permute-start(bf16[192,1728]{1,0:T(8,128)(2,1)S(1)} %get-tuple-element.53), channel_id=1, source_target_pairs={{0,4},{1,3},{2,6},{3,1},{4,0},{5,7},{6,2},{7,5},{8,12},{9,11},{10,... | collective-permute-start | bytes 1990664 | tf_op jit(solution)/shard_map/ppermute | solution.py:397
  63.8 12.7 %collective-permute-done.3.got_ref = bf16[192,1728]{1,0:T(8,128)(2,1)S(1)} collective-permute-done((bf16[192,1728]{1,0:T(8,128)(2,1)S(1)}, bf16[192,1728]{1,0:T(8,128)(2,1)S(1)}, u32[]{:S(2)}, u32[]{:S(2)}) %collective-permute-start.3) | collective-permute-done | bytes 663584 | tf_op jit(solution)/shard_map/ppermute | solution.py:397
  76.5 1.9 %shard_map.81 = (bf16[112,384]{1,0:T(8,128)(2,1)S(1)}, bf16[112,384]{1,0:T(8,128)(2,1)S(1)}, bf16[112,384]{1,0:T(8,128)(2,1)S(1)}, bf16[112,384]{1,0:T(8,128)(2,...) custom-call(s32[4]{0:T(128)S(1)} %pad_add_fusion.place_ref, ...), custom_call_target="tpu_custom_call" | custom-call | flops 2717908992 | bytes 4194304 | tf_op jit(solution)/shard_map/pallas_call | solution.py:385
  78.4 1.7 %collective-permute-start.10 = (bf16[112,384]{1,0:T(8,128)(2,1)S(1)}, bf16[112,384]{1,0:T(8,128)(2,1)S(1)}, u32[]{:S(2)}, u32[]{:S(2)}) collective-permute-start(bf16[112,384]{1,0:T(8,128)(2,1)S(1)} %get-tuple-element.61), channel_id=1, source_target_pairs={{0,25},{1,24},{8,17},{9,16},{16,9},{17,8},{24,1},{25,0},{2,27},{3,... | collective-permute-start | bytes 258056 | tf_op jit(solution)/shard_map/ppermute | solution.py:486
  80.1 1.7 %collective-permute-start.4 = (bf16[112,384]{1,0:T(8,128)(2,1)S(1)}, bf16[112,384]{1,0:T(8,128)(2,1)S(1)}, u32[]{:S(2)}, u32[]{:S(2)}) collective-permute-start(bf16[112,384]{1,0:T(8,128)(2,1)S(1)} %get-tuple-element.55), channel_id=1, source_target_pairs={{0,1},{1,0},{8,9},{9,8},{16,17},{17,16},{24,25},{25,24},{2,3},{3,2... | collective-permute-start | bytes 258056 | tf_op jit(solution)/shard_map/ppermute | solution.py:486
  82.0 1.2 %collective-permute-start.6 = (bf16[112,384]{1,0:T(8,128)(2,1)S(1)}, bf16[112,384]{1,0:T(8,128)(2,1)S(1)}, u32[]{:S(2)}, u32[]{:S(2)}) collective-permute-start(bf16[112,384]{1,0:T(8,128)(2,1)S(1)} %get-tuple-element.57), channel_id=1, source_target_pairs={{0,9},{1,8},{8,1},{9,0},{16,25},{17,24},{24,17},{25,16},{2,11},{3,... | collective-permute-start | bytes 258056 | tf_op jit(solution)/shard_map/ppermute | solution.py:486
  83.6 1.6 %collective-permute-done.10.refs_7_ = bf16[112,384]{1,0:T(8,128)(2,1)S(1)} collective-permute-done((bf16[112,384]{1,0:T(8,128)(2,1)S(1)}, bf16[112,384]{1,0:T(8,128)(2,1)S(1)}, u32[]{:S(2)}, u32[]{:S(2)}) %collective-permute-start.10) | collective-permute-done | bytes 86048 | tf_op jit(solution)/shard_map/ppermute | solution.py:486
  85.3 1.3 %collective-permute-start.8 = (bf16[112,384]{1,0:T(8,128)(2,1)S(1)}, bf16[112,384]{1,0:T(8,128)(2,1)S(1)}, u32[]{:S(2)}, u32[]{:S(2)}) collective-permute-start(bf16[112,384]{1,0:T(8,128)(2,1)S(1)} %get-tuple-element.59), channel_id=1, source_target_pairs={{0,17},{1,16},{8,25},{9,24},{16,1},{17,0},{24,9},{25,8},{2,19},{3,... | collective-permute-start | bytes 258056 | tf_op jit(solution)/shard_map/ppermute | solution.py:486
  86.6 2.3 %collective-permute-start.9 = (bf16[112,384]{1,0:T(8,128)(2,1)S(1)}, bf16[112,384]{1,0:T(8,128)(2,1)S(1)}, u32[]{:S(2)}, u32[]{:S(2)}) collective-permute-start(bf16[112,384]{1,0:T(8,128)(2,1)S(1)} %get-tuple-element.60), channel_id=1, source_target_pairs={{0,24},{1,25},{8,16},{9,17},{16,8},{17,9},{24,0},{25,1},{2,26},{3,... | collective-permute-start | bytes 258056 | tf_op jit(solution)/shard_map/ppermute | solution.py:486
  88.9 1.5 %shard_map.79 = (bf16[8,64,384]{2,1,0:T(8,128)(2,1)}, bf16[8,64,384]{2,1,0:T(8,128)(2,1)}) custom-call(bf16[32,2,16,384]{3,2,1,0:T(8,128)(2,1)S(1)} %all-to-all-done.1.fields_ref), custom_call_target="tpu_custom_call" | custom-call | flops 1000000000 | bytes 3145728 | tf_op jit(solution)/shard_map/pallas_call | solution.py:385
  90.4 4.7 %collective-permute-done.7.refs_4_ = bf16[112,384]{1,0:T(8,128)(2,1)S(1)} collective-permute-done((bf16[112,384]{1,0:T(8,128)(2,1)S(1)}, bf16[112,384]{1,0:T(8,128)(2,1)S(1)}, u32[]{:S(2)}, u32[]{:S(2)}) %collective-permute-start.7) | collective-permute-done | bytes 86048 | tf_op jit(solution)/shard_map/ppermute | solution.py:486
  95.0 1.5 %collective-permute-done.8.refs_5_ = bf16[112,384]{1,0:T(8,128)(2,1)S(1)} collective-permute-done((bf16[112,384]{1,0:T(8,128)(2,1)S(1)}, bf16[112,384]{1,0:T(8,128)(2,1)S(1)}, u32[]{:S(2)}, u32[]{:S(2)}) %collective-permute-start.8) | collective-permute-done | bytes 86048 | tf_op jit(solution)/shard_map/ppermute | solution.py:486
  96.5 1.5 %shard_map.82 = (f32[3,3,48,96]{3,2,1,0:T(8,128)}, f32[3,3,48,96]{3,2,1,0:T(8,128)}) custom-call(s32[4]{0:T(128)S(1)} %pad_add_fusion.place_ref, bf16[112,384]{1,0:T(8,128)(2,1)S(1)} %get-tuple-element.64.refs_0_, bf16[112,384]{1,0:T(8,128)(2,1)S(1)} %collective-permute-done.4.refs_1_, bf16[112,384]{1,0:T(8,128)(2,1)S(1)} %collective-permute-done.5.refs_2_, ...), custom_call_target="tpu_custom_call" | custom-call | flops 1000000 | bytes 2097152 | tf_op jit(solution)/shard_map/pallas_call | solution.py:385
  (19 shorter events, 1.2 us)
Async XLA Ops:
  3.4 27.9 %all-to-all-start = ((bf16[32,2,16,384]{3,2,1,0:T(8,128)(2,1)}), bf16[32,2,16,384]{3,2,1,0:T(8,128)(2,1)S(1)}, u32[]{:S(2)}, u32[]{:S(2)}) async-start(bf16[32,2,16,384]{3,2,1,0:T(8,128)(2,1)} %shard_map.75), calls=%async_computation | async-start | bytes 1572864 | tf_op jit(solution)/shard_map/all_to_all | solution.py:411
  39.3 2.1 %collective-permute-start = (bf16[3,192,512]{2,1,0:T(8,128)(2,1)S(1)}, bf16[3,192,512]{2,1,0:T(8,128)(2,1)S(1)}, u32[]{:S(2)}, u32[]{:S(2)}) collective-permute-start(bf16[3,192,512]{2,1,0:T(8,128)(2,1)S(1)} %get-tuple-element.43), channel_id=1, source_target_pairs={{0,1},{1,0},{2,3},{3,2},{4,5},{5,4},{6,7},{7,6},{8,9},{9,8},{10,11... | collective-permute-start | bytes 1769480 | tf_op jit(solution)/shard_map/ppermute | solution.py:397
  39.4 16.6 %collective-permute-start.1 = (bf16[3,192,512]{2,1,0:T(8,128)(2,1)S(1)}, bf16[3,192,512]{2,1,0:T(8,128)(2,1)S(1)}, u32[]{:S(2)}, u32[]{:S(2)}) collective-permute-start(bf16[3,192,512]{2,1,0:T(8,128)(2,1)S(1)} %get-tuple-element.41.mine_ref), channel_id=1, source_target_pairs={{0,2},{1,5},{2,0},{3,7},{4,6},{5,1},{6,4},{7,3},{8,10},{9,13},{10,... | collective-permute-start | bytes 1769480 | tf_op jit(solution)/shard_map/ppermute | solution.py:397
  41.0 15.0 %collective-permute-start.2 = (bf16[3,192,512]{2,1,0:T(8,128)(2,1)S(1)}, bf16[3,192,512]{2,1,0:T(8,128)(2,1)S(1)}, u32[]{:S(2)}, u32[]{:S(2)}) collective-permute-start(bf16[3,192,512]{2,1,0:T(8,128)(2,1)S(1)} %get-tuple-element.49), channel_id=1, source_target_pairs={{0,5},{1,2},{2,7},{3,0},{4,1},{5,6},{6,3},{7,4},{8,13},{9,10},{10,... | collective-permute-start | bytes 1769480 | tf_op jit(solution)/shard_map/ppermute | solution.py:397
  41.3 6.0 %copy-start = (bf16[3,3,384,384]{3,2,1,0:T(8,128)(2,1)S(1)}, bf16[3,3,384,384]{3,2,1,0:T(8,128)(2,1)}, u32[]{:S(2)}) copy-start(bf16[3,3,384,384]{3,2,1,0:T(8,128)(2,1)} %one_ref.3) | copy-start | bytes 7962628
  41.3 6.0 %copy-start.1 = (bf16[3,3,384,384]{3,2,1,0:T(8,128)(2,1)S(1)}, bf16[3,3,384,384]{3,2,1,0:T(8,128)(2,1)}, u32[]{:S(2)}) copy-start(bf16[3,3,384,384]{3,2,1,0:T(8,128)(2,1)} %two_ref.3) | copy-start | bytes 7962628
  45.8 1.5 %copy-start.2 = (f32[2,192,1728]{2,1,0:T(8,128)}, f32[2,192,1728]{2,1,0:T(8,128)S(1)}, u32[]{:S(2)}) copy-start(f32[2,192,1728]{2,1,0:T(8,128)S(1)} %shard_map.77.sums_ref) | copy-start | bytes 7962628
  52.3 36.6 %all-to-all-start.1 = ((bf16[32,2,16,384]{3,2,1,0:T(8,128)(2,1)}), bf16[32,2,16,384]{3,2,1,0:T(8,128)(2,1)S(1)}, u32[]{:S(2)}, u32[]{:S(2)}) async-start(bf16[32,2,16,384]{3,2,1,0:T(8,128)(2,1)} %shard_map.78), calls=%async_computation.1 | async-start | bytes 1572864 | tf_op jit(solution)/shard_map/all_to_all | solution.py:462
  56.0 1.8 %copy-start.3 = (f32[2,192,1728]{2,1,0:T(8,128)S(1)}, f32[2,192,1728]{2,1,0:T(8,128)}, u32[]{:S(2)}) copy-start(f32[2,192,1728]{2,1,0:T(8,128)} %copy-done.2) | copy-start | bytes 7962628
  62.0 14.5 %collective-permute-start.3 = (bf16[192,1728]{1,0:T(8,128)(2,1)S(1)}, bf16[192,1728]{1,0:T(8,128)(2,1)S(1)}, u32[]{:S(2)}, u32[]{:S(2)}) collective-permute-start(bf16[192,1728]{1,0:T(8,128)(2,1)S(1)} %get-tuple-element.53), channel_id=1, source_target_pairs={{0,4},{1,3},{2,6},{3,1},{4,0},{5,7},{6,2},{7,5},{8,12},{9,11},{10,... | collective-permute-start | bytes 1990664 | tf_op jit(solution)/shard_map/ppermute | solution.py:397
  78.4 6.9 %collective-permute-start.10 = (bf16[112,384]{1,0:T(8,128)(2,1)S(1)}, bf16[112,384]{1,0:T(8,128)(2,1)S(1)}, u32[]{:S(2)}, u32[]{:S(2)}) collective-permute-start(bf16[112,384]{1,0:T(8,128)(2,1)S(1)} %get-tuple-element.61), channel_id=1, source_target_pairs={{0,25},{1,24},{8,17},{9,16},{16,9},{17,8},{24,1},{25,0},{2,27},{3,... | collective-permute-start | bytes 258056 | tf_op jit(solution)/shard_map/ppermute | solution.py:486
  80.1 6.5 %collective-permute-start.4 = (bf16[112,384]{1,0:T(8,128)(2,1)S(1)}, bf16[112,384]{1,0:T(8,128)(2,1)S(1)}, u32[]{:S(2)}, u32[]{:S(2)}) collective-permute-start(bf16[112,384]{1,0:T(8,128)(2,1)S(1)} %get-tuple-element.55), channel_id=1, source_target_pairs={{0,1},{1,0},{8,9},{9,8},{16,17},{17,16},{24,25},{25,24},{2,3},{3,2... | collective-permute-start | bytes 258056 | tf_op jit(solution)/shard_map/ppermute | solution.py:486
  81.8 8.5 %collective-permute-start.5 = (bf16[112,384]{1,0:T(8,128)(2,1)S(1)}, bf16[112,384]{1,0:T(8,128)(2,1)S(1)}, u32[]{:S(2)}, u32[]{:S(2)}) collective-permute-start(bf16[112,384]{1,0:T(8,128)(2,1)S(1)} %get-tuple-element.56), channel_id=1, source_target_pairs={{0,8},{1,9},{8,0},{9,1},{16,24},{17,25},{24,16},{25,17},{2,10},{3,... | collective-permute-start | bytes 258056 | tf_op jit(solution)/shard_map/ppermute | solution.py:486
  82.0 8.4 %collective-permute-start.6 = (bf16[112,384]{1,0:T(8,128)(2,1)S(1)}, bf16[112,384]{1,0:T(8,128)(2,1)S(1)}, u32[]{:S(2)}, u32[]{:S(2)}) collective-permute-start(bf16[112,384]{1,0:T(8,128)(2,1)S(1)} %get-tuple-element.57), channel_id=1, source_target_pairs={{0,9},{1,8},{8,1},{9,0},{16,25},{17,24},{24,17},{25,16},{2,11},{3,... | collective-permute-start | bytes 258056 | tf_op jit(solution)/shard_map/ppermute | solution.py:486
  83.2 11.9 %collective-permute-start.7 = (bf16[112,384]{1,0:T(8,128)(2,1)S(1)}, bf16[112,384]{1,0:T(8,128)(2,1)S(1)}, u32[]{:S(2)}, u32[]{:S(2)}) collective-permute-start(bf16[112,384]{1,0:T(8,128)(2,1)S(1)} %get-tuple-element.58), channel_id=1, source_target_pairs={{0,16},{1,17},{8,24},{9,25},{16,0},{17,1},{24,8},{25,9},{2,18},{3,... | collective-permute-start | bytes 258056 | tf_op jit(solution)/shard_map/ppermute | solution.py:486
  85.3 11.3 %collective-permute-start.8 = (bf16[112,384]{1,0:T(8,128)(2,1)S(1)}, bf16[112,384]{1,0:T(8,128)(2,1)S(1)}, u32[]{:S(2)}, u32[]{:S(2)}) collective-permute-start(bf16[112,384]{1,0:T(8,128)(2,1)S(1)} %get-tuple-element.59), channel_id=1, source_target_pairs={{0,17},{1,16},{8,25},{9,24},{16,1},{17,0},{24,9},{25,8},{2,19},{3,... | collective-permute-start | bytes 258056 | tf_op jit(solution)/shard_map/ppermute | solution.py:486
  86.6 10.0 %collective-permute-start.9 = (bf16[112,384]{1,0:T(8,128)(2,1)S(1)}, bf16[112,384]{1,0:T(8,128)(2,1)S(1)}, u32[]{:S(2)}, u32[]{:S(2)}) collective-permute-start(bf16[112,384]{1,0:T(8,128)(2,1)S(1)} %get-tuple-element.60), channel_id=1, source_target_pairs={{0,24},{1,25},{8,16},{9,17},{16,8},{17,9},{24,0},{25,1},{2,26},{3,... | collective-permute-start | bytes 258056 | tf_op jit(solution)/shard_map/ppermute | solution.py:486
